TPU v7x, 32 devices: a whole 2x2x4 slice. The times are simulated.
32 devices in a mesh: region: 16 (over z, y, x), tile: 2 (over core).
Axes of the slice: x: 2, y: 2, z: 4, core: 2. Of those that a mesh axis runs over, the one named last changes fastest.
Arguments:
- innovations: float32 [64, 16384], P(None, ('region', 'tile')), may hold values from -6 to 6
- obs_geometry: float32 [3, 16384], P(None, ('region', 'tile')), may hold values from 0 to 32, as said below
- obs_error: float32 [16384], P(('region', 'tile')), may hold values from 0.25 to 1
- tile_owner: int32 [16, 7], P('region'), may hold values from -1 to 1, as said below
Outputs:
- weights: float32 [64, 16384], P(None, ('region', 'tile'))
- residual: float32 [64, 16384], P(None, ('region', 'tile'))
Inputs may be any that keep to these rules, and one draw needn't show every extreme that they name: tile_owner[i, k] names the device along tile that computes the tile of regions i and i + k, or is -1 where that pair is not listed. A region lists the offsets 0 to e - 1 for some e of 1 to 7, and i + k is a region for every listed pair. No device owns more than 4 tiles of its region, and some device owns exactly 4. `obs_geometry`: the standard deviations lie between 0.5 and 2. The operator A built from these positions and the listed tiles is symmetric positive definite.
All inputs are finite; a program needn't handle non-finite values.
Results may differ from a plain program's by a relative error of at most 0.0098.
Values may be sent and summed in bfloat16 or wider, within the bound.
No kernel may reach another device: no remote copies, remote signals or barrier semaphores. Data moves between devices by JAX's collectives and lax.ppermute only.
A program may use at most 128 MiB of HBM per device.

v0:
```python
import jax
import jax.numpy as jnp
from jax import lax
from jax.sharding import PartitionSpec as P

ITERS = 2


gc_length = 0.5


def from_behind(block, axis, distance):
    devices = range(lax.axis_size(axis))
    route = [(i - distance, i) for i in devices if i - distance in devices]
    return lax.ppermute(block, axis, route)


def gaspari_cohn(distance):
    scaled = distance / gc_length
    bounded = jnp.maximum(scaled, 1.0)
    near_part = (
        ((-0.25 * scaled + 0.5) * scaled + 0.625) * scaled - 5.0 / 3.0
    ) * scaled * scaled + 1.0
    far_part = (
        ((((scaled / 12.0 - 0.5) * scaled + 0.625) * scaled + 5.0 / 3.0) * scaled - 5.0) * scaled
        + 4.0
        - 2.0 / (3.0 * bounded)
    )
    return jnp.where(scaled <= 1.0, near_part, jnp.where(scaled <= 2.0, far_part, 0.0))


def build_tile(home_rows, far_rows):
    across_x = home_rows[0][:, None] - far_rows[0][None, :]
    across_y = home_rows[1][:, None] - far_rows[1][None, :]
    distance = jnp.sqrt(across_x * across_x + across_y * across_y)
    return (home_rows[2][:, None] * far_rows[2][None, :] * gaspari_cohn(distance)).astype(
        jnp.bfloat16
    )


def empty_tile(home_rows, far_rows):
    return jnp.zeros((home_rows.shape[1], far_rows.shape[1]), jnp.bfloat16)


def home_term(tile_block, far_block):
    return lax.dot_general(
        far_block, tile_block, (((1,), (1,)), ((), ())), preferred_element_type=jnp.float32
    )


def skip_home(tile_block, far_block):
    return jnp.zeros((far_block.shape[0], tile_block.shape[0]), jnp.float32)


def both_terms(tile_block, home_block, far_block):
    to_partner = jnp.dot(home_block, tile_block, preferred_element_type=jnp.float32)
    return (home_term(tile_block, far_block), to_partner)


def skip_both(tile_block, home_block, far_block):
    return (
        skip_home(tile_block, far_block),
        jnp.zeros((home_block.shape[0], tile_block.shape[1]), jnp.float32),
    )


def gram_matrix(left_rows, right_rows):
    return jnp.dot(
        left_rows, right_rows.T, precision=lax.Precision.HIGHEST, preferred_element_type=jnp.float32
    )


def gram_solve(gram_value, target):
    symmetric = 0.5 * (gram_value + gram_value.T)
    factor = jnp.linalg.cholesky(symmetric)
    interim = lax.linalg.triangular_solve(factor, target, left_side=True, lower=True)
    return lax.linalg.triangular_solve(
        factor, interim, left_side=True, lower=True, transpose_a=True
    )


def shards(innovations, obs_geometry, obs_error, tile_owner):
    tile_place = lax.axis_index("tile")
    tile_reach = tile_owner.shape[1]
    owning = tile_owner[0]
    shifted = [obs_geometry]
    for offset in range(1, tile_reach):
        shifted.append(from_behind(obs_geometry, "region", -offset))
    places = lax.all_gather(jnp.stack(shifted), "tile", axis=2, tiled=True)
    owned_flags = []
    tiles = []
    for offset in range(tile_reach):
        is_mine = owning[offset] == tile_place
        owned_flags.append(is_mine)
        tiles.append(lax.cond(is_mine, build_tile, empty_tile, places[0], places[offset]))
    weights = jnp.zeros_like(innovations)
    residual = innovations
    direction = innovations
    squares = lax.psum(gram_matrix(residual, residual), ("region", "tile"))
    for iteration in range(ITERS):
        rounded = direction.astype(jnp.bfloat16)
        pieces = [rounded]
        for apply_offset in range(1, tile_reach):
            pieces.append(from_behind(rounded, "region", -apply_offset))
        blocks = lax.all_gather(jnp.stack(pieces), "tile", axis=2, tiled=True)
        home_total = lax.cond(owned_flags[0], home_term, skip_home, tiles[0], blocks[0])
        outgoing = []
        for apply_offset in range(1, tile_reach):
            to_home, to_partner = lax.cond(
                owned_flags[apply_offset],
                both_terms,
                skip_both,
                tiles[apply_offset],
                blocks[0],
                blocks[apply_offset],
            )
            home_total = home_total + to_home
            outgoing.append(to_partner)
        total_block = home_total
        for apply_offset in range(1, tile_reach):
            total_block = total_block + from_behind(
                outgoing[apply_offset - 1], "region", apply_offset
            )
        summed = lax.psum_scatter(total_block, "tile", scatter_dimension=1, tiled=True)
        image_block = obs_error[None, :] * direction + summed
        curvature, cross_gram, image_gram = lax.psum(
            (
                gram_matrix(direction, image_block),
                gram_matrix(residual, image_block),
                gram_matrix(image_block, image_block),
            ),
            ("region", "tile"),
        )
        step_size = gram_solve(curvature, squares)
        weights = weights + jnp.dot(step_size.T, direction, precision=lax.Precision.HIGHEST)
        residual = residual - jnp.dot(step_size.T, image_block, precision=lax.Precision.HIGHEST)
        if iteration + 1 < ITERS:
            cross_step = jnp.dot(cross_gram, step_size, precision=lax.Precision.HIGHEST)
            image_step = jnp.dot(image_gram, step_size, precision=lax.Precision.HIGHEST)
            next_squares = (
                squares
                - cross_step
                - cross_step.T
                + jnp.dot(step_size.T, image_step, precision=lax.Precision.HIGHEST)
            )
            conjugacy = gram_solve(squares, next_squares)
            direction = residual + jnp.dot(conjugacy.T, direction, precision=lax.Precision.HIGHEST)
            squares = next_squares
    return (weights, residual)


def solution(mesh):
    return jax.shard_map(
        shards,
        mesh=mesh,
        in_specs=(
            P(None, ("region", "tile")),
            P(None, ("region", "tile")),
            P(("region", "tile")),
            P("region", None),
        ),
        out_specs=(P(None, ("region", "tile")), P(None, ("region", "tile"))),
        check_vma=False,
    )
```

profile of v0, /device:TPU:0, one launch (start us, length us, event | category | flops | bytes accessed | tf_op | source)
XLA Modules:
  0.0 404.8 jit_solution(94424359007091014)
XLA Ops:
  15.9 1.6 fusion.112
  18.2 3.1 collective-permute-done.6
  22.5 6.5 %collective-permute-done.7 = f32[3,512]{1,0:T(4,128)S(1)} collective-permute-done((f32[3,512]{1,0:T(4,128)}, f32[3,512]{1,0:T(4,128)S(1)}, u32[]{:S(2)}, u32[]{:S(2)}) %collective-permute-start.7) | collective-permute-done | bytes 6176 | tf_op jit(solution)/shard_map/ppermute | solution.py:15
  30.4 8.4 %collective-permute-done.8 = f32[3,512]{1,0:T(4,128)S(1)} collective-permute-done((f32[3,512]{1,0:T(4,128)}, f32[3,512]{1,0:T(4,128)S(1)}, u32[]{:S(2)}, u32[]{:S(2)}) %collective-permute-start.8) | collective-permute-done | bytes 6176 | tf_op jit(solution)/shard_map/ppermute | solution.py:15
  40.1 6.8 %collective-permute-done.9 = f32[3,512]{1,0:T(4,128)S(1)} collective-permute-done((f32[3,512]{1,0:T(4,128)}, f32[3,512]{1,0:T(4,128)S(1)}, u32[]{:S(2)}, u32[]{:S(2)}) %collective-permute-start.9) | collective-permute-done | bytes 6176 | tf_op jit(solution)/shard_map/ppermute | solution.py:15
  48.2 5.3 %collective-permute-done.10 = f32[3,512]{1,0:T(4,128)S(1)} collective-permute-done((f32[3,512]{1,0:T(4,128)}, f32[3,512]{1,0:T(4,128)S(1)}, u32[]{:S(2)}, u32[]{:S(2)}) %collective-permute-start.10) | collective-permute-done | bytes 6176 | tf_op jit(solution)/shard_map/ppermute | solution.py:15
  54.8 6.0 %collective-permute-done.11 = f32[3,512]{1,0:T(4,128)S(1)} collective-permute-done((f32[3,512]{1,0:T(4,128)}, f32[3,512]{1,0:T(4,128)S(1)}, u32[]{:S(2)}, u32[]{:S(2)}) %collective-permute-start.11) | collective-permute-done | bytes 6176 | tf_op jit(solution)/shard_map/ppermute | solution.py:15
  62.1 1.9 all_gather.10
  68.7 12.8 %collective-permute-done.5 = bf16[64,512]{1,0:T(8,128)(2,1)S(1)} collective-permute-done((bf16[64,512]{1,0:T(8,128)(2,1)S(1)}, bf16[64,512]{1,0:T(8,128)(2,1)S(1)}, u32[]{:S(2)}, u32[]{:S(2)}) %collective-permute-start.5) | collective-permute-done | bytes 65568 | tf_op jit(solution)/shard_map/ppermute | solution.py:15
  82.1 2.7 all_gather.9
  85.6 4.1 %collective-permute-start.12 = (f32[64,1024]{1,0:T(8,128)}, f32[64,1024]{1,0:T(8,128)}, u32[]{:S(2)}, u32[]{:S(2)}) collective-permute-start(f32[64,1024]{1,0:T(8,128)} %get-tuple-element.256), channel_id=1, source_target_pairs={{0,2},{2,4},{4,6},{6,8},{8,10},{10,12},{12,14},{14,16},{16,18},{18... | collective-permute-start | bytes 786440 | tf_op jit(solution)/shard_map/ppermute | solution.py:15
  92.8 1.6 conditional.25
  92.8 1.6 broadcast.287
  94.4 1.6 conditional.27
  94.4 1.6 broadcast.298
  96.0 7.9 %conditional.29 = (bf16[1024,1024]{1,0:T(8,128)(2,1)}) conditional(s32[]{:T(128)} %convert_element_type.67, () %tuple.174, (f32[3,1024]{1,0:T(4,128)S(1)}, f32[7,3,1024]{2,1,0:T(4,128)S(1)}) %tuple.165), branch_computations={%region_16.17_spmd, %region_17.18_spmd} | conditional | flops 37748736 | bytes 2170888 | solution.py:95
  96.0 7.9 %fusion.32 = bf16[1024,1024]{1,0:T(8,128)(2,1)} fusion(f32[1024]{0:T(1024)S(1)} %bitcast.282, f32[1024]{0:T(1024)S(1)} %bitcast.264, f32[1024]{0:T(1024)S(1)} %bitcast.283, f32[1024]{0:T(1024)S(1)} %bitcast.265, f32[1024]{0:T(1024)S(1)} %bitcast.281, f32[1024]{0:T(1024)S(1)} %bitcast.263), kind=kLoop, calls=%fused_computation.49 | loop fusion | flops 37748736 | bytes 2121728 | tf_op jit(solution)/shard_map/cond/branch_1_fun/convert_element_type | solution.py:36
  103.9 8.1 %conditional.31 = (bf16[1024,1024]{1,0:T(8,128)(2,1)}) conditional(s32[]{:T(128)} %convert_element_type.68, () %tuple.177, (f32[3,1024]{1,0:T(4,128)S(1)}, f32[7,3,1024]{2,1,0:T(4,128)S(1)}) %tuple.165), branch_computations={%region_20.21_spmd, %region_21.22_spmd} | conditional | flops 37748736 | bytes 2170888 | solution.py:95
  104.1 7.9 %fusion.40 = bf16[1024,1024]{1,0:T(8,128)(2,1)} fusion(f32[1024]{0:T(1024)S(1)} %bitcast.285, f32[1024]{0:T(1024)S(1)} %bitcast.267, f32[1024]{0:T(1024)S(1)} %bitcast.286, f32[1024]{0:T(1024)S(1)} %bitcast.268, f32[1024]{0:T(1024)S(1)} %bitcast.284, f32[1024]{0:T(1024)S(1)} %bitcast.266), kind=kLoop, calls=%fused_computation.61 | loop fusion | flops 37748736 | bytes 2121728 | tf_op jit(solution)/shard_map/cond/branch_1_fun/convert_element_type | solution.py:36
  112.0 7.9 %conditional.33 = (bf16[1024,1024]{1,0:T(8,128)(2,1)}) conditional(s32[]{:T(128)} %convert_element_type.69, () %tuple.180, (f32[3,1024]{1,0:T(4,128)S(1)}, f32[7,3,1024]{2,1,0:T(4,128)S(1)}) %tuple.165), branch_computations={%region_24.25_spmd, %region_25.26_spmd} | conditional | flops 37748736 | bytes 2170888 | solution.py:95
  112.0 7.9 %fusion.48 = bf16[1024,1024]{1,0:T(8,128)(2,1)} fusion(f32[1024]{0:T(1024)S(1)} %bitcast.288, f32[1024]{0:T(1024)S(1)} %bitcast.270, f32[1024]{0:T(1024)S(1)} %bitcast.289, f32[1024]{0:T(1024)S(1)} %bitcast.271, f32[1024]{0:T(1024)S(1)} %bitcast.287, f32[1024]{0:T(1024)S(1)} %bitcast.269), kind=kLoop, calls=%fused_computation.73 | loop fusion | flops 37748736 | bytes 2121728 | tf_op jit(solution)/shard_map/cond/branch_1_fun/convert_element_type | solution.py:36
  120.7 2.0 collective-permute-start.13
  123.4 5.6 %collective-permute-start.14 = (f32[64,1024]{1,0:T(8,128)}, f32[64,1024]{1,0:T(8,128)}, u32[]{:S(2)}, u32[]{:S(2)}) collective-permute-start(f32[64,1024]{1,0:T(8,128)} %get-tuple-element.258), channel_id=1, source_target_pairs={{0,6},{2,8},{4,10},{6,12},{8,14},{10,16},{12,18},{14,20},{16,22},{... | collective-permute-start | bytes 786440 | tf_op jit(solution)/shard_map/ppermute | solution.py:15
  129.0 3.7 conditional.30
  129.0 2.9 fusion.118
  132.7 4.9 %collective-permute-start.15 = (f32[64,1024]{1,0:T(8,128)}, f32[64,1024]{1,0:T(8,128)}, u32[]{:S(2)}, u32[]{:S(2)}) collective-permute-start(f32[64,1024]{1,0:T(8,128)} %get-tuple-element.259), channel_id=1, source_target_pairs={{0,8},{2,10},{4,12},{6,14},{8,16},{10,18},{12,20},{14,22},{16,24},... | collective-permute-start | bytes 786440 | tf_op jit(solution)/shard_map/ppermute | solution.py:15
  137.6 3.7 conditional.32
  137.6 2.9 fusion.119
  141.3 3.5 collective-permute-start.16
  144.8 4.4 %conditional.34 = (f32[64,1024]{1,0:T(8,128)}, f32[64,1024]{1,0:T(8,128)}) conditional(s32[]{:T(128)} %convert_element_type.69, () %tuple.179, (bf16[7,64,1024]{2,1,0:T(8,128)(2,1)S(1)}, bf16[1024,1024]{1,0:T(8,128)(2,1)}, bf16[64,1024]{1,0:T(8,128)(2,1)S(1)}) %tuple.181), branch_computations={%region_26.27_spmd, %region_27.28_spmd} | conditional | flops 268435456 | bytes 13369388 | solution.py:109
  144.8 2.9 fusion.120
  149.2 2.0 collective-permute-start.17
  151.8 1.6 conditional.21
  154.2 3.3 collective-permute-done.17
  157.5 2.6 add_add_fusion.1
  160.7 19.4 %reduce-scatter.3.cloned.1.call-done = f32[64,512]{1,0:T(8,128)} async-done(((f32[64,1024]{1,0:T(8,128)}), f32[64,512]{1,0:T(8,128)}) %reduce-scatter.3.cloned.1.call-update) | async-done | bytes 131088 | tf_op jit(solution)/shard_map/reduce_scatter | solution.py:124
  182.6 41.6 %all-reduce = (f32[64,64]{1,0:T(8,128)S(1)}, f32[64,64]{1,0:T(8,128)S(1)}, f32[64,64]{1,0:T(8,128)S(1)}) all-reduce(f32[64,64]{1,0:T(8,128)S(1)} %fusion.127, f32[64,64]{1,0:T(8,128)S(1)} %convolution_bitcast_fusion, f32[64,64]{1,0:T(8,128)S(1)} %fusion.72), channel_id=1, replica_groups=mesh['region'=16,'tile'=2] {'region','tile'}, use_global_device_ids=true, to_apply=%region_32.34 | all-reduce | flops 12288 | bytes 98304 | tf_op jit(solution)/shard_map/psum | solution.py:99
  224.5 5.8 %cholesky.70 = f32[64,64]{1,0:T(8,128)S(1)} custom-call(f32[64,64]{1,0:T(8,128)S(1)} %fusion.91), custom_call_target="Cholesky" | custom-call | tf_op jit(solution)/shard_map/jit(cholesky)/cholesky | solution.py:75
  231.7 4.9 %custom-call.15 = f32[1,64,64]{1,2,0:T(8,128)S(1)} custom-call(f32[1,64,64]{2,1,0:T(8,128)S(1)} %fusion.79), custom_call_target="InvertDiagBlocksLowerTriangular" | custom-call | tf_op jit(solution)/shard_map/triangular_solve/custom-call.2 | solution.py:77
  236.7 5.8 %cholesky.59 = f32[64,64]{1,0:T(8,128)S(1)} custom-call(f32[64,64]{1,0:T(8,128)S(1)} %fusion.97), custom_call_target="Cholesky" | custom-call | tf_op jit(solution)/shard_map/jit(cholesky)/cholesky | solution.py:75
  243.9 4.9 %custom-call.13 = f32[1,64,64]{1,2,0:T(8,128)S(1)} custom-call(f32[1,64,64]{2,1,0:T(8,128)S(1)} %fusion.78), custom_call_target="InvertDiagBlocksLowerTriangular" | custom-call | tf_op jit(solution)/shard_map/triangular_solve/custom-call.2 | solution.py:77
  259.0 2.1 collective-permute-done.19
  261.2 1.7 collective-permute-done.20
  262.8 4.1 %collective-permute-done.21 = bf16[64,512]{1,0:T(8,128)(2,1)S(1)} collective-permute-done((bf16[64,512]{1,0:T(8,128)(2,1)S(1)}, bf16[64,512]{1,0:T(8,128)(2,1)S(1)}, u32[]{:S(2)}, u32[]{:S(2)}) %collective-permute-start.21) | collective-permute-done | bytes 65568 | tf_op jit(solution)/shard_map/ppermute | solution.py:15
  266.9 2.1 collective-permute-done.22
  270.1 2.5 all_gather.11
  273.3 5.5 %collective-permute-start.24 = (f32[64,1024]{1,0:T(8,128)}, f32[64,1024]{1,0:T(8,128)}, u32[]{:S(2)}, u32[]{:S(2)}) collective-permute-start(f32[64,1024]{1,0:T(8,128)} %get-tuple-element.268), channel_id=1, source_target_pairs={{0,2},{2,4},{4,6},{6,8},{8,10},{10,12},{12,14},{14,16},{16,18},{18... | collective-permute-start | bytes 786440 | tf_op jit(solution)/shard_map/ppermute | solution.py:15
  279.6 7.6 %collective-permute-start.25 = (f32[64,1024]{1,0:T(8,128)}, f32[64,1024]{1,0:T(8,128)}, u32[]{:S(2)}, u32[]{:S(2)}) collective-permute-start(f32[64,1024]{1,0:T(8,128)} %get-tuple-element.269), channel_id=1, source_target_pairs={{0,4},{2,6},{4,8},{6,10},{8,12},{10,14},{12,16},{14,18},{16,20},{1... | collective-permute-start | bytes 786440 | tf_op jit(solution)/shard_map/ppermute | solution.py:15
  287.9 6.0 %collective-permute-start.26 = (f32[64,1024]{1,0:T(8,128)}, f32[64,1024]{1,0:T(8,128)}, u32[]{:S(2)}, u32[]{:S(2)}) collective-permute-start(f32[64,1024]{1,0:T(8,128)} %get-tuple-element.270), channel_id=1, source_target_pairs={{0,6},{2,8},{4,10},{6,12},{8,14},{10,16},{12,18},{14,20},{16,22},{... | collective-permute-start | bytes 786440 | tf_op jit(solution)/shard_map/ppermute | solution.py:15
  293.9 3.7 conditional.39
  293.9 2.9 fusion.124
  297.6 2.0 collective-permute-start.27
  299.6 3.7 conditional.40
  299.6 2.9 fusion.125
  303.3 2.0 collective-permute-start.28
  305.3 3.9 conditional.41
  305.6 2.9 fusion.126
  311.3 6.5 %collective-permute-done.29 = f32[64,1024]{1,0:T(8,128)S(1)} collective-permute-done((f32[64,1024]{1,0:T(8,128)}, f32[64,1024]{1,0:T(8,128)S(1)}, u32[]{:S(2)}, u32[]{:S(2)}) %collective-permute-start.29) | collective-permute-done | bytes 262176 | tf_op jit(solution)/shard_map/ppermute | solution.py:15
  317.8 2.3 add_add_fusion
  320.5 19.6 %reduce-scatter.5.cloned.1.call-done = f32[64,512]{1,0:T(8,128)} async-done(((f32[64,1024]{1,0:T(8,128)}), f32[64,512]{1,0:T(8,128)}) %reduce-scatter.5.cloned.1.call-update) | async-done | bytes 131088 | tf_op jit(solution)/shard_map/reduce_scatter | solution.py:124
  341.3 40.7 %psum.34 = f32[64,64]{1,0:T(8,128)S(1)} all-reduce(f32[64,64]{1,0:T(8,128)S(1)} %fusion.71), channel_id=1, replica_groups=mesh['region'=16,'tile'=2] {'region','tile'}, use_global_device_ids=true, to_apply=%region_49.53 | all-reduce | flops 4096 | bytes 32768 | tf_op jit(solution)/shard_map/psum | solution.py:126
  382.1 5.8 %cholesky.81 = f32[64,64]{1,0:T(8,128)S(1)} custom-call(f32[64,64]{1,0:T(8,128)S(1)} %fusion.85), custom_call_target="Cholesky" | custom-call | tf_op jit(solution)/shard_map/jit(cholesky)/cholesky | solution.py:75
  389.3 4.9 %custom-call.17 = f32[1,64,64]{1,2,0:T(8,128)S(1)} custom-call(f32[1,64,64]{2,1,0:T(8,128)S(1)} %fusion.80), custom_call_target="InvertDiagBlocksLowerTriangular" | custom-call | tf_op jit(solution)/shard_map/triangular_solve/custom-call.2 | solution.py:77
  395.6 1.9 convolution_subtract_fusion
  (200 shorter events, 63.0 us)
Async XLA Ops:
  7.2 173.0 %reduce-scatter.3.cloned.1.call-start = ((), (), s32[]{:S(2)}) async-start(), calls=%async_computation.2 | async-start | bytes 393216 | tf_op jit(solution)/shard_map/reduce_scatter | solution.py:124
  8.7 55.5 %collective-permute-start = (bf16[64,512]{1,0:T(8,128)(2,1)S(1)}, bf16[64,512]{1,0:T(8,128)(2,1)S(1)}, u32[]{:S(2)}, u32[]{:S(2)}) collective-permute-start(bf16[64,512]{1,0:T(8,128)(2,1)S(1)} %get-tuple-element.280), channel_id=1, source_target_pairs={{2,0},{4,2},{6,4},{8,6},{10,8},{12,10},{14,12},{16,14},{18,16},{20... | collective-permute-start | bytes 196616 | tf_op jit(solution)/shard_map/ppermute | solution.py:15
  10.0 56.2 %collective-permute-start.1 = (bf16[64,512]{1,0:T(8,128)(2,1)S(1)}, bf16[64,512]{1,0:T(8,128)(2,1)S(1)}, u32[]{:S(2)}, u32[]{:S(2)}) collective-permute-start(bf16[64,512]{1,0:T(8,128)(2,1)S(1)} %get-tuple-element.280), channel_id=1, source_target_pairs={{4,0},{6,2},{8,4},{10,6},{12,8},{14,10},{16,12},{18,14},{20,16},{2... | collective-permute-start | bytes 196616 | tf_op jit(solution)/shard_map/ppermute | solution.py:15
  11.3 55.5 %collective-permute-start.2 = (bf16[64,512]{1,0:T(8,128)(2,1)S(1)}, bf16[64,512]{1,0:T(8,128)(2,1)S(1)}, u32[]{:S(2)}, u32[]{:S(2)}) collective-permute-start(bf16[64,512]{1,0:T(8,128)(2,1)S(1)} %get-tuple-element.280), channel_id=1, source_target_pairs={{6,0},{8,2},{10,4},{12,6},{14,8},{16,10},{18,12},{20,14},{22,16},{... | collective-permute-start | bytes 196616 | tf_op jit(solution)/shard_map/ppermute | solution.py:15
  12.6 54.8 %collective-permute-start.3 = (bf16[64,512]{1,0:T(8,128)(2,1)S(1)}, bf16[64,512]{1,0:T(8,128)(2,1)S(1)}, u32[]{:S(2)}, u32[]{:S(2)}) collective-permute-start(bf16[64,512]{1,0:T(8,128)(2,1)S(1)} %get-tuple-element.280), channel_id=1, source_target_pairs={{8,0},{10,2},{12,4},{14,6},{16,8},{18,10},{20,12},{22,14},{24,16},... | collective-permute-start | bytes 196616 | tf_op jit(solution)/shard_map/ppermute | solution.py:15
  13.9 7.3 %collective-permute-start.6 = (f32[3,512]{1,0:T(4,128)}, f32[3,512]{1,0:T(4,128)S(1)}, u32[]{:S(2)}, u32[]{:S(2)}) collective-permute-start(f32[3,512]{1,0:T(4,128)} %param.52), channel_id=1, source_target_pairs={{2,0},{4,2},{6,4},{8,6},{10,8},{12,10},{14,12},{16,14},{18,16},{20... | collective-permute-start | bytes 18440 | tf_op jit(solution)/shard_map/ppermute | solution.py:15
  21.2 7.8 %collective-permute-start.7 = (f32[3,512]{1,0:T(4,128)}, f32[3,512]{1,0:T(4,128)S(1)}, u32[]{:S(2)}, u32[]{:S(2)}) collective-permute-start(f32[3,512]{1,0:T(4,128)} %param.52), channel_id=1, source_target_pairs={{4,0},{6,2},{8,4},{10,6},{12,8},{14,10},{16,12},{18,14},{20,16},{2... | collective-permute-start | bytes 18440 | tf_op jit(solution)/shard_map/ppermute | solution.py:15
  29.1 9.7 %collective-permute-start.8 = (f32[3,512]{1,0:T(4,128)}, f32[3,512]{1,0:T(4,128)S(1)}, u32[]{:S(2)}, u32[]{:S(2)}) collective-permute-start(f32[3,512]{1,0:T(4,128)} %param.52), channel_id=1, source_target_pairs={{6,0},{8,2},{10,4},{12,6},{14,8},{16,10},{18,12},{20,14},{22,16},{... | collective-permute-start | bytes 18440 | tf_op jit(solution)/shard_map/ppermute | solution.py:15
  38.8 8.1 %collective-permute-start.9 = (f32[3,512]{1,0:T(4,128)}, f32[3,512]{1,0:T(4,128)S(1)}, u32[]{:S(2)}, u32[]{:S(2)}) collective-permute-start(f32[3,512]{1,0:T(4,128)} %param.52), channel_id=1, source_target_pairs={{8,0},{10,2},{12,4},{14,6},{16,8},{18,10},{20,12},{22,14},{24,16},... | collective-permute-start | bytes 18440 | tf_op jit(solution)/shard_map/ppermute | solution.py:15
  46.9 6.6 %collective-permute-start.10 = (f32[3,512]{1,0:T(4,128)}, f32[3,512]{1,0:T(4,128)S(1)}, u32[]{:S(2)}, u32[]{:S(2)}) collective-permute-start(f32[3,512]{1,0:T(4,128)} %param.52), channel_id=1, source_target_pairs={{10,0},{12,2},{14,4},{16,6},{18,8},{20,10},{22,12},{24,14},{26,16}... | collective-permute-start | bytes 18440 | tf_op jit(solution)/shard_map/ppermute | solution.py:15
  53.5 7.3 %collective-permute-start.11 = (f32[3,512]{1,0:T(4,128)}, f32[3,512]{1,0:T(4,128)S(1)}, u32[]{:S(2)}, u32[]{:S(2)}) collective-permute-start(f32[3,512]{1,0:T(4,128)} %param.52), channel_id=1, source_target_pairs={{12,0},{14,2},{16,4},{18,6},{20,8},{22,10},{24,12},{26,14},{28,16}... | collective-permute-start | bytes 18440 | tf_op jit(solution)/shard_map/ppermute | solution.py:15
  60.8 7.3 %collective-permute-start.4 = (bf16[64,512]{1,0:T(8,128)(2,1)S(1)}, bf16[64,512]{1,0:T(8,128)(2,1)S(1)}, u32[]{:S(2)}, u32[]{:S(2)}) collective-permute-start(bf16[64,512]{1,0:T(8,128)(2,1)S(1)} %get-tuple-element.280), channel_id=1, source_target_pairs={{10,0},{12,2},{14,4},{16,6},{18,8},{20,10},{22,12},{24,14},{26,16}... | collective-permute-start | bytes 196616 | tf_op jit(solution)/shard_map/ppermute | solution.py:15
  64.3 17.2 %collective-permute-start.5 = (bf16[64,512]{1,0:T(8,128)(2,1)S(1)}, bf16[64,512]{1,0:T(8,128)(2,1)S(1)}, u32[]{:S(2)}, u32[]{:S(2)}) collective-permute-start(bf16[64,512]{1,0:T(8,128)(2,1)S(1)} %get-tuple-element.280), channel_id=1, source_target_pairs={{12,0},{14,2},{16,4},{18,6},{20,8},{22,10},{24,12},{26,14},{28,16}... | collective-permute-start | bytes 196616 | tf_op jit(solution)/shard_map/ppermute | solution.py:15
  85.6 63.6 %collective-permute-start.12 = (f32[64,1024]{1,0:T(8,128)}, f32[64,1024]{1,0:T(8,128)}, u32[]{:S(2)}, u32[]{:S(2)}) collective-permute-start(f32[64,1024]{1,0:T(8,128)} %get-tuple-element.256), channel_id=1, source_target_pairs={{0,2},{2,4},{4,6},{6,8},{8,10},{10,12},{12,14},{14,16},{16,18},{18... | collective-permute-start | bytes 786440 | tf_op jit(solution)/shard_map/ppermute | solution.py:15
  120.7 2.0 copy-start.14
  120.7 33.5 %collective-permute-start.13 = (f32[64,1024]{1,0:T(8,128)}, f32[64,1024]{1,0:T(8,128)}, u32[]{:S(2)}, u32[]{:S(2)}) collective-permute-start(f32[64,1024]{1,0:T(8,128)} %get-tuple-element.257), channel_id=1, source_target_pairs={{0,4},{2,6},{4,8},{6,10},{8,12},{10,14},{12,16},{14,18},{16,20},{1... | collective-permute-start | bytes 786440 | tf_op jit(solution)/shard_map/ppermute | solution.py:15
  123.4 5.6 %copy-start.16 = (f32[64,1024]{1,0:T(8,128)}, f32[64,1024]{1,0:T(8,128)S(1)}, u32[]{:S(2)}) copy-start(f32[64,1024]{1,0:T(8,128)S(1)} %get-tuple-element.252) | copy-start | bytes 786436
  123.4 30.7 %collective-permute-start.14 = (f32[64,1024]{1,0:T(8,128)}, f32[64,1024]{1,0:T(8,128)}, u32[]{:S(2)}, u32[]{:S(2)}) collective-permute-start(f32[64,1024]{1,0:T(8,128)} %get-tuple-element.258), channel_id=1, source_target_pairs={{0,6},{2,8},{4,10},{6,12},{8,14},{10,16},{12,18},{14,20},{16,22},{... | collective-permute-start | bytes 786440 | tf_op jit(solution)/shard_map/ppermute | solution.py:15
  129.0 2.9 copy-start.4
  132.7 4.9 %copy-start.18 = (f32[64,1024]{1,0:T(8,128)}, f32[64,1024]{1,0:T(8,128)S(1)}, u32[]{:S(2)}) copy-start(f32[64,1024]{1,0:T(8,128)S(1)} %get-tuple-element.253) | copy-start | bytes 786436
  132.7 21.5 %collective-permute-start.15 = (f32[64,1024]{1,0:T(8,128)}, f32[64,1024]{1,0:T(8,128)}, u32[]{:S(2)}, u32[]{:S(2)}) collective-permute-start(f32[64,1024]{1,0:T(8,128)} %get-tuple-element.259), channel_id=1, source_target_pairs={{0,8},{2,10},{4,12},{6,14},{8,16},{10,18},{12,20},{14,22},{16,24},... | collective-permute-start | bytes 786440 | tf_op jit(solution)/shard_map/ppermute | solution.py:15
  137.6 2.9 copy-start.6
  141.3 3.5 copy-start.20
  141.3 12.9 %collective-permute-start.16 = (f32[64,1024]{1,0:T(8,128)}, f32[64,1024]{1,0:T(8,128)}, u32[]{:S(2)}, u32[]{:S(2)}) collective-permute-start(f32[64,1024]{1,0:T(8,128)} %get-tuple-element.260), channel_id=1, source_target_pairs={{0,10},{2,12},{4,14},{6,16},{8,18},{10,20},{12,22},{14,24},{16,26}... | collective-permute-start | bytes 786440 | tf_op jit(solution)/shard_map/ppermute | solution.py:15
  144.8 2.9 copy-start.8
  149.2 8.3 %collective-permute-start.17 = (f32[64,1024]{1,0:T(8,128)}, f32[64,1024]{1,0:T(8,128)}, u32[]{:S(2)}, u32[]{:S(2)}) collective-permute-start(f32[64,1024]{1,0:T(8,128)} %get-tuple-element.261), channel_id=1, source_target_pairs={{0,12},{2,14},{4,16},{6,18},{8,20},{10,22},{12,24},{14,26},{16,28}... | collective-permute-start | bytes 786440 | tf_op jit(solution)/shard_map/ppermute | solution.py:15
  153.4 4.1 %copy-start.15 = (f32[64,1024]{1,0:T(8,128)S(1)}, f32[64,1024]{1,0:T(8,128)}, u32[]{:S(2)}) copy-start(f32[64,1024]{1,0:T(8,128)} %copy-done.14) | copy-start | bytes 786436
  153.4 4.1 %copy-start.17 = (f32[64,1024]{1,0:T(8,128)S(1)}, f32[64,1024]{1,0:T(8,128)}, u32[]{:S(2)}) copy-start(f32[64,1024]{1,0:T(8,128)} %copy-done.16) | copy-start | bytes 786436
  153.4 4.1 %copy-start.19 = (f32[64,1024]{1,0:T(8,128)S(1)}, f32[64,1024]{1,0:T(8,128)}, u32[]{:S(2)}) copy-start(f32[64,1024]{1,0:T(8,128)} %copy-done.18) | copy-start | bytes 786436
  154.2 6.3 %copy-start.10 = (f32[64,512]{1,0:T(8,128)S(1)}, f32[64,512]{1,0:T(8,128)}, u32[]{:S(2)}) copy-start(f32[64,512]{1,0:T(8,128)} %param.51) | copy-start | bytes 393220
  157.5 22.6 %copy-start.34 = (f32[512]{0:T(512)S(1)}, f32[512]{0:T(512)}, u32[]{:S(2)}) copy-start(f32[512]{0:T(512)} %param.53) | copy-start | bytes 6148
  160.2 179.9 %reduce-scatter.5.cloned.1.call-start = ((), (), s32[]{:S(2)}) async-start(), calls=%async_computation.3 | async-start | bytes 393216 | tf_op jit(solution)/shard_map/reduce_scatter | solution.py:124
  180.1 70.4 %copy-start.11 = (f32[64,512]{1,0:T(8,128)S(1)}, f32[64,512]{1,0:T(8,128)}, u32[]{:S(2)}) copy-start(f32[64,512]{1,0:T(8,128)} %reduce-scatter.3.cloned.1.call-done) | copy-start | bytes 393220
  249.2 20.8 %copy-start.12 = (f32[64,64]{1,0:T(8,128)}, f32[64,64]{1,0:T(8,128)S(1)}, u32[]{:S(2)}) copy-start(f32[64,64]{1,0:T(8,128)S(1)} %fusion.95) | copy-start | bytes 49156
  249.9 0.6 copy-start.32
  251.2 6.5 %collective-permute-start.18 = (bf16[64,512]{1,0:T(8,128)(2,1)S(1)}, bf16[64,512]{1,0:T(8,128)(2,1)S(1)}, u32[]{:S(2)}, u32[]{:S(2)}) collective-permute-start(bf16[64,512]{1,0:T(8,128)(2,1)S(1)} %get-tuple-element.278), channel_id=1, source_target_pairs={{2,0},{4,2},{6,4},{8,6},{10,8},{12,10},{14,12},{16,14},{18,16},{20... | collective-permute-start | bytes 196616 | tf_op jit(solution)/shard_map/ppermute | solution.py:15
  252.5 8.7 %collective-permute-start.19 = (bf16[64,512]{1,0:T(8,128)(2,1)S(1)}, bf16[64,512]{1,0:T(8,128)(2,1)S(1)}, u32[]{:S(2)}, u32[]{:S(2)}) collective-permute-start(bf16[64,512]{1,0:T(8,128)(2,1)S(1)} %get-tuple-element.278), channel_id=1, source_target_pairs={{4,0},{6,2},{8,4},{10,6},{12,8},{14,10},{16,12},{18,14},{20,16},{2... | collective-permute-start | bytes 196616 | tf_op jit(solution)/shard_map/ppermute | solution.py:15
  253.8 9.0 %collective-permute-start.20 = (bf16[64,512]{1,0:T(8,128)(2,1)S(1)}, bf16[64,512]{1,0:T(8,128)(2,1)S(1)}, u32[]{:S(2)}, u32[]{:S(2)}) collective-permute-start(bf16[64,512]{1,0:T(8,128)(2,1)S(1)} %get-tuple-element.278), channel_id=1, source_target_pairs={{6,0},{8,2},{10,4},{12,6},{14,8},{16,10},{18,12},{20,14},{22,16},{... | collective-permute-start | bytes 196616 | tf_op jit(solution)/shard_map/ppermute | solution.py:15
  255.1 11.8 %collective-permute-start.21 = (bf16[64,512]{1,0:T(8,128)(2,1)S(1)}, bf16[64,512]{1,0:T(8,128)(2,1)S(1)}, u32[]{:S(2)}, u32[]{:S(2)}) collective-permute-start(bf16[64,512]{1,0:T(8,128)(2,1)S(1)} %get-tuple-element.278), channel_id=1, source_target_pairs={{8,0},{10,2},{12,4},{14,6},{16,8},{18,10},{20,12},{22,14},{24,16},... | collective-permute-start | bytes 196616 | tf_op jit(solution)/shard_map/ppermute | solution.py:15
  256.4 12.6 %collective-permute-start.22 = (bf16[64,512]{1,0:T(8,128)(2,1)S(1)}, bf16[64,512]{1,0:T(8,128)(2,1)S(1)}, u32[]{:S(2)}, u32[]{:S(2)}) collective-permute-start(bf16[64,512]{1,0:T(8,128)(2,1)S(1)} %get-tuple-element.278), channel_id=1, source_target_pairs={{10,0},{12,2},{14,4},{16,6},{18,8},{20,10},{22,12},{24,14},{26,16}... | collective-permute-start | bytes 196616 | tf_op jit(solution)/shard_map/ppermute | solution.py:15
  257.7 12.4 %collective-permute-start.23 = (bf16[64,512]{1,0:T(8,128)(2,1)S(1)}, bf16[64,512]{1,0:T(8,128)(2,1)S(1)}, u32[]{:S(2)}, u32[]{:S(2)}) collective-permute-start(bf16[64,512]{1,0:T(8,128)(2,1)S(1)} %get-tuple-element.278), channel_id=1, source_target_pairs={{12,0},{14,2},{16,4},{18,6},{20,8},{22,10},{24,12},{26,14},{28,16}... | collective-permute-start | bytes 196616 | tf_op jit(solution)/shard_map/ppermute | solution.py:15
  273.3 5.5 %copy-start.21 = (f32[64,1024]{1,0:T(8,128)}, f32[64,1024]{1,0:T(8,128)S(1)}, u32[]{:S(2)}) copy-start(f32[64,1024]{1,0:T(8,128)S(1)} %get-tuple-element.262) | copy-start | bytes 786436
  273.3 36.0 %collective-permute-start.24 = (f32[64,1024]{1,0:T(8,128)}, f32[64,1024]{1,0:T(8,128)}, u32[]{:S(2)}, u32[]{:S(2)}) collective-permute-start(f32[64,1024]{1,0:T(8,128)} %get-tuple-element.268), channel_id=1, source_target_pairs={{0,2},{2,4},{4,6},{6,8},{8,10},{10,12},{12,14},{14,16},{16,18},{18... | collective-permute-start | bytes 786440 | tf_op jit(solution)/shard_map/ppermute | solution.py:15
  279.6 7.6 %copy-start.23 = (f32[64,1024]{1,0:T(8,128)}, f32[64,1024]{1,0:T(8,128)S(1)}, u32[]{:S(2)}) copy-start(f32[64,1024]{1,0:T(8,128)S(1)} %get-tuple-element.263) | copy-start | bytes 786436
  279.6 31.3 %collective-permute-start.25 = (f32[64,1024]{1,0:T(8,128)}, f32[64,1024]{1,0:T(8,128)}, u32[]{:S(2)}, u32[]{:S(2)}) collective-permute-start(f32[64,1024]{1,0:T(8,128)} %get-tuple-element.269), channel_id=1, source_target_pairs={{0,4},{2,6},{4,8},{6,10},{8,12},{10,14},{12,16},{14,18},{16,20},{1... | collective-permute-start | bytes 786440 | tf_op jit(solution)/shard_map/ppermute | solution.py:15
  287.9 6.0 %copy-start.25 = (f32[64,1024]{1,0:T(8,128)}, f32[64,1024]{1,0:T(8,128)S(1)}, u32[]{:S(2)}) copy-start(f32[64,1024]{1,0:T(8,128)S(1)} %get-tuple-element.264) | copy-start | bytes 786436
  287.9 23.0 %collective-permute-start.26 = (f32[64,1024]{1,0:T(8,128)}, f32[64,1024]{1,0:T(8,128)}, u32[]{:S(2)}, u32[]{:S(2)}) collective-permute-start(f32[64,1024]{1,0:T(8,128)} %get-tuple-element.270), channel_id=1, source_target_pairs={{0,6},{2,8},{4,10},{6,12},{8,14},{10,16},{12,18},{14,20},{16,22},{... | collective-permute-start | bytes 786440 | tf_op jit(solution)/shard_map/ppermute | solution.py:15
  293.9 2.9 copy-start.5
  297.6 2.0 copy-start.27
  297.6 13.3 %collective-permute-start.27 = (f32[64,1024]{1,0:T(8,128)}, f32[64,1024]{1,0:T(8,128)}, u32[]{:S(2)}, u32[]{:S(2)}) collective-permute-start(f32[64,1024]{1,0:T(8,128)} %get-tuple-element.271), channel_id=1, source_target_pairs={{0,8},{2,10},{4,12},{6,14},{8,16},{10,18},{12,20},{14,22},{16,24},... | collective-permute-start | bytes 786440 | tf_op jit(solution)/shard_map/ppermute | solution.py:15
  299.6 2.9 copy-start.7
  303.3 2.0 copy-start.29
  303.3 8.0 %collective-permute-start.28 = (f32[64,1024]{1,0:T(8,128)}, f32[64,1024]{1,0:T(8,128)}, u32[]{:S(2)}, u32[]{:S(2)}) collective-permute-start(f32[64,1024]{1,0:T(8,128)} %get-tuple-element.272), channel_id=1, source_target_pairs={{0,10},{2,12},{4,14},{6,16},{8,18},{10,20},{12,22},{14,24},{16,26}... | collective-permute-start | bytes 786440 | tf_op jit(solution)/shard_map/ppermute | solution.py:15
  305.6 2.9 copy-start.9
  309.3 1.5 copy-start.31
  309.3 8.5 %copy-start.22 = (f32[64,1024]{1,0:T(8,128)S(1)}, f32[64,1024]{1,0:T(8,128)}, u32[]{:S(2)}) copy-start(f32[64,1024]{1,0:T(8,128)} %copy-done.21) | copy-start | bytes 786436
  309.3 8.5 %copy-start.24 = (f32[64,1024]{1,0:T(8,128)S(1)}, f32[64,1024]{1,0:T(8,128)}, u32[]{:S(2)}) copy-start(f32[64,1024]{1,0:T(8,128)} %copy-done.23) | copy-start | bytes 786436
  309.3 8.5 %copy-start.26 = (f32[64,1024]{1,0:T(8,128)S(1)}, f32[64,1024]{1,0:T(8,128)}, u32[]{:S(2)}) copy-start(f32[64,1024]{1,0:T(8,128)} %copy-done.25) | copy-start | bytes 786436
  309.3 8.5 %copy-start.28 = (f32[64,1024]{1,0:T(8,128)S(1)}, f32[64,1024]{1,0:T(8,128)}, u32[]{:S(2)}) copy-start(f32[64,1024]{1,0:T(8,128)} %copy-done.27) | copy-start | bytes 786436
  309.3 8.5 %copy-start.30 = (f32[64,1024]{1,0:T(8,128)S(1)}, f32[64,1024]{1,0:T(8,128)}, u32[]{:S(2)}) copy-start(f32[64,1024]{1,0:T(8,128)} %copy-done.29) | copy-start | bytes 786436
  309.3 8.5 %collective-permute-start.29 = (f32[64,1024]{1,0:T(8,128)}, f32[64,1024]{1,0:T(8,128)S(1)}, u32[]{:S(2)}, u32[]{:S(2)}) collective-permute-start(f32[64,1024]{1,0:T(8,128)} %get-tuple-element.273), channel_id=1, source_target_pairs={{0,12},{2,14},{4,16},{6,18},{8,20},{10,22},{12,24},{14,26},{16,28}... | collective-permute-start | bytes 786440 | tf_op jit(solution)/shard_map/ppermute | solution.py:15
  310.9 9.4 %copy-start.13 = (f32[64,64]{1,0:T(8,128)S(1)}, f32[64,64]{1,0:T(8,128)}, u32[]{:S(2)}) copy-start(f32[64,64]{1,0:T(8,128)} %copy-done.12) | copy-start | bytes 49156
  317.8 76.4 %copy-start.33 = (f32[64,64]{1,0:T(8,128)S(1)}, f32[64,64]{1,0:T(8,128)}, u32[]{:S(2)}) copy-start(f32[64,64]{1,0:T(8,128)} %copy-done.32) | copy-start | bytes 49156
Sparse Core Ops, SparseCore 0:
  160.3 19.7 reduce-scatter.2
  320.3 19.7 reduce-scatter.4
where the time goes:
time: 413 us; the launch traced here: 405 us
  waiting for transfers between devices  109 us (26%)
  blocking collectives  89.3 us (22%)
  starting transfers between devices  70.1 us (17%)
  other arithmetic  66.4 us (16%)
  matrix products  32.3 us (8%)
  between operations  19.5 us (5%)
  local copies, waits for them, and re-layouts  17.4 us (4%)
    ppermute x30, waiting for transfers between devices, from_behind(): return lax.ppermute(block, axis, route)  70.2 us
    ppermute x30, starting transfers between devices, from_behind(): return lax.ppermute(block, axis, route)  69.8 us
    psum x1, blocking collectives, shards(): squares = lax.psum(gram_matrix(residual, residual), ('region', 'tile'))  41.6 us
    psum x1, blocking collectives, shards(): lax.psum((gram_matrix(direction, image_block), gram_matrix(residual, imag...  40.7 us
    reduce_scatter x2, waiting for transfers between devices, shards(): lax.psum_scatter(total_block, 'tile', scatter_dimension=1, tiled=True)  39 us
    convert_element_type x3, other arithmetic, build_tile(): (home_rows[2][:, None] * far_rows[2][None, :] * gaspari_cohn(distance)).a...  23.6 us
    another operation x9, other arithmetic, gram_solve(): factor = jnp.linalg.cholesky(symmetric)  19.6 us
    dot_general x6, matrix products, both_terms(): jnp.dot(home_block, tile_block, preferred_element_type=jnp.float32)  17.6 us
  transfers between devices with their start and end apart: 32, of which 17 were waited for; matrix products, arithmetic and copies ran while one was open for 15% of the time, Pallas kernels for 0%

commit v1 on v0

v1 whole, which is shorter than its diff:
```python
import functools

import jax
import jax.numpy as jnp
from jax import lax
from jax.experimental import pallas as pl
from jax.experimental.pallas import tpu as pltpu
from jax.sharding import PartitionSpec as P

CUTOFF = 1.001
LANES = 128
ROWS = 64
BATCH = 4
GROUP = 4
RING = 4
VMEM = 60 * 1024 * 1024
HIGHEST = lax.Precision.HIGHEST


def whole_vmem(count):
    return [pl.BlockSpec(memory_space=pltpu.VMEM)] * count


def dot_nt(left, right, precision=None):
    return lax.dot_general(
        left, right, (((1,), (1,)), ((), ())), precision=precision, preferred_element_type=jnp.float32
    )


def dot_nn(left, right, precision=None):
    return lax.dot_general(
        left, right, (((1,), (0,)), ((), ())), precision=precision, preferred_element_type=jnp.float32
    )


def three_parts(value):
    high = value.astype(jnp.bfloat16)
    rest = value - high.astype(jnp.float32)
    middle = rest.astype(jnp.bfloat16)
    low = (rest - middle.astype(jnp.float32)).astype(jnp.bfloat16)
    return high, middle, low


def exchange(block, offsets, axis):
    count = lax.axis_size(axis)
    gathered = block[None]
    bit = count // 2
    while bit:
        other = lax.ppermute(gathered, axis, [(i, i ^ bit) for i in range(count)])
        gathered = jnp.concatenate([gathered, other], axis=0)
        bit //= 2
    return gathered


def slot_offsets(count):
    offsets = [0]
    bit = count // 2
    while bit:
        offsets = offsets + [o ^ bit for o in offsets]
        bit //= 2
    return offsets


def sum_over(block, axis):
    count = lax.axis_size(axis)
    bit = 1
    while bit < count:
        block = block + lax.ppermute(block, axis, [(i, i ^ bit) for i in range(count)])
        bit *= 2
    return block


def fill_order(rank, order_ref):
    n = order_ref.shape[0]
    step = 64

    def fill(block, carry):
        start = pl.multiple_of(block * step, step)
        place = (start + lax.broadcasted_iota(jnp.int32, (step, n), 0)).astype(jnp.float32)
        order_ref[pl.ds(start, step), :] = jnp.where(place == rank, 1.0, 0.0).astype(jnp.bfloat16)
        return carry

    lax.fori_loop(0, n // step, fill, 0)


def sort_kernel(places_ref, y_ref, block_ref, places_out, block_out, rounded_out, rank_out, order_ref):
    n = places_ref.shape[1]
    step = 64
    y_row = places_ref[1:2, :]
    index_row = lax.broadcasted_iota(jnp.int32, (step, n), 1)

    def count(block, total):
        start = pl.multiple_of(block * step, step)
        y_column = y_ref[pl.ds(start, step), :]
        index_column = start + lax.broadcasted_iota(jnp.int32, (step, n), 0)
        before = (y_column < y_row) | ((y_column == y_row) & (index_column < index_row))
        return total + jnp.sum(jnp.where(before, 1.0, 0.0).reshape(step // 8, 8, n), axis=0)

    total = lax.fori_loop(0, n // step, count, jnp.zeros((8, n), jnp.float32))
    rank = jnp.sum(total, axis=0, keepdims=True)
    rank_out[...] = rank
    fill_order(rank, order_ref)
    order = order_ref[...]
    places_out[...] = sum(dot_nt(part, order) for part in reversed(three_parts(places_ref[...])))
    sorted_block = sum(dot_nt(part, order) for part in reversed(three_parts(block_ref[...])))
    block_out[...] = sorted_block
    rounded_out[...] = sorted_block.astype(jnp.bfloat16)


def sort_region(places, block):
    n = places.shape[1]
    columns = block.shape[0]
    return pl.pallas_call(
        sort_kernel,
        out_shape=(
            jax.ShapeDtypeStruct(places.shape, jnp.float32),
            jax.ShapeDtypeStruct(block.shape, jnp.float32),
            jax.ShapeDtypeStruct(block.shape, jnp.bfloat16),
            jax.ShapeDtypeStruct((1, n), jnp.float32),
        ),
        in_specs=whole_vmem(3),
        out_specs=tuple(whole_vmem(4)),
        scratch_shapes=[pltpu.VMEM((n, n), jnp.bfloat16)],
        compiler_params=pltpu.CompilerParams(vmem_limit_bytes=VMEM),
        cost_estimate=pl.CostEstimate(
            flops=6 * n * n * (columns + 8), bytes_accessed=4 * n * n, transcendentals=0
        ),
        name="sort_region",
    )(places, places[1][:, None], block)


def unsort_kernel(rank_ref, block_ref, block_out, order_ref):
    fill_order(rank_ref[...], order_ref)
    order = order_ref[...]
    block_out[...] = sum(dot_nn(part, order) for part in reversed(three_parts(block_ref[...])))


def unsort(rank, block):
    n = block.shape[1]
    return pl.pallas_call(
        unsort_kernel,
        out_shape=jax.ShapeDtypeStruct(block.shape, jnp.float32),
        in_specs=whole_vmem(2),
        out_specs=whole_vmem(1)[0],
        scratch_shapes=[pltpu.VMEM((n, n), jnp.bfloat16)],
        compiler_params=pltpu.CompilerParams(vmem_limit_bytes=VMEM),
        cost_estimate=pl.CostEstimate(
            flops=6 * n * n * block.shape[0], bytes_accessed=4 * n * n, transcendentals=0
        ),
        name="unsort",
    )(rank, block)


def plan_blocks(own, everyone, listed, most):
    n = own.shape[1]
    slots = everyone.shape[0]
    chunks = n // LANES
    y = everyone[:, 1, :].reshape(slots * chunks, LANES)
    y_own = own[1].reshape(n // ROWS, ROWS)
    near = (y[None, :, 0] <= y_own[:, -1:] + CUTOFF) & (y[None, :, -1] >= y_own[:, :1] - CUTOFF)
    active = near & jnp.repeat(listed, chunks)[None, :]
    total = slots * chunks
    index = jnp.arange(total, dtype=jnp.int32)
    counted = active.astype(jnp.int32)
    place = jnp.sum(
        jnp.where(index[None, :, None] < index[None, None, :], counted[:, :, None], 0), axis=1
    )
    length = most * chunks
    spot = jnp.arange(length, dtype=jnp.int32)
    hit = active[:, :, None] & (place[:, :, None] == spot[None, None, :])
    ids = jnp.sum(jnp.where(hit, index[None, :, None] + 1, 0), axis=1) - 1
    batches = (jnp.sum(counted, axis=1) + BATCH - 1) // BATCH
    blocks = jnp.arange(n // ROWS, dtype=jnp.int32)
    base = jnp.sum(jnp.where(blocks[None, :] < blocks[:, None], batches[None, :], 0), axis=1)
    return ids.reshape(-1), jnp.concatenate([batches, base])


def gaspari_cohn(squared):
    squared = jnp.maximum(squared, 1e-12)
    inverse = lax.rsqrt(squared)
    scaled = squared * inverse
    near = (((-0.25 * scaled + 0.5) * scaled + 0.625) * scaled - 5.0 / 3.0) * squared + 1.0
    left = jnp.maximum(2.0 - scaled, 0.0)
    left = left * left
    far = (left * left) * ((scaled + 2.0) * scaled - 0.5) * (inverse * (1.0 / 12.0))
    return jnp.where(scaled <= 1.0, near, far)


def build_kernel(length, ids_ref, plan_ref, own_ref, all_ref, tiles_ref, wide_ref, ring_ref, sems):
    n = own_ref.shape[1]
    blocks = n // ROWS
    chunks = n // LANES
    column = jnp.transpose(own_ref[...])
    for row in range(3):
        wide_ref[row] = jnp.broadcast_to(column[:, row : row + 1], (n, LANES))

    def copy_out(slot, batch):
        return pltpu.make_async_copy(ring_ref.at[slot], tiles_ref.at[batch], sems.at[slot])

    def build_block(block, carry):
        start = pl.multiple_of(block * ROWS, ROWS)
        base = plan_ref[blocks + block]

        def build_batch(step, inner):
            batch = base + step
            slot = lax.rem(batch, RING)

            @pl.when(batch >= RING)
            def _():
                copy_out(slot, batch).wait()

            for part in range(BATCH):
                entry = ids_ref[block * length + step * BATCH + part]
                chunk = jnp.maximum(entry, 0)
                place = chunk // chunks
                lane = pl.multiple_of((chunk - place * chunks) * LANES, LANES)
                far = all_ref[place, :, pl.ds(lane, LANES)]
                across_x = 2.0 * wide_ref[0, pl.ds(start, ROWS), :] - 2.0 * far[0:1, :]
                across_y = 2.0 * wide_ref[1, pl.ds(start, ROWS), :] - 2.0 * far[1:2, :]
                value = gaspari_cohn(across_x * across_x + across_y * across_y)
                spread = jnp.where(entry >= 0, far[2:3, :], 0.0)
                value = wide_ref[2, pl.ds(start, ROWS), :] * spread * value
                ring_ref[slot, :, part * LANES : (part + 1) * LANES] = value.astype(jnp.bfloat16)
            copy_out(slot, batch).start()
            return inner

        return lax.fori_loop(0, plan_ref[block], build_batch, carry)

    lax.fori_loop(0, blocks, build_block, 0)
    total = plan_ref[blocks - 1] + plan_ref[2 * blocks - 1]
    for slot in range(RING):

        @pl.when(slot < total)
        def _():
            copy_out(slot, slot).wait()


def build_tiles(ids, plan, own, everyone, length, capacity):
    n = own.shape[1]
    smem = pl.BlockSpec(memory_space=pltpu.SMEM)
    return pl.pallas_call(
        functools.partial(build_kernel, length),
        out_shape=jax.ShapeDtypeStruct((capacity, ROWS, BATCH * LANES), jnp.bfloat16),
        in_specs=[smem, smem] + whole_vmem(2),
        out_specs=pl.BlockSpec(memory_space=pl.ANY),
        scratch_shapes=[
            pltpu.VMEM((3, n, LANES), jnp.float32),
            pltpu.VMEM((RING, ROWS, BATCH * LANES), jnp.bfloat16),
            pltpu.SemaphoreType.DMA((RING,)),
        ],
        compiler_params=pltpu.CompilerParams(vmem_limit_bytes=VMEM),
        cost_estimate=pl.CostEstimate(
            flops=40 * 3 * n * n, bytes_accessed=8 * n * n, transcendentals=3 * n * n
        ),
        name="build_tiles",
    )(ids, plan, own, everyone)


def apply_kernel(
    length, ids_ref, plan_ref, tiles_ref, all_ref, block_ref, scale_ref, out_ref, rounded_ref,
    held_ref, total_ref, sems,
):
    columns, n = block_ref.shape
    blocks = n // ROWS
    chunks = n // LANES
    total = plan_ref[blocks - 1] + plan_ref[2 * blocks - 1]
    groups = (total + GROUP - 1) // GROUP

    def copy_in(group):
        start = group * GROUP
        return pltpu.make_async_copy(
            tiles_ref.at[pl.ds(start, GROUP)], held_ref.at[pl.ds(start, GROUP)], sems.at[group]
        )

    def start_copy(group, carry):
        copy_in(group).start()
        return carry

    lax.fori_loop(0, groups, start_copy, 0)

    def apply_block(block, carry):
        base = plan_ref[blocks + block]

        def apply_batch(step, value):
            batch = base + step

            @pl.when(lax.rem(batch, GROUP) == 0)
            def _():
                copy_in(batch // GROUP).wait()

            parts = []
            for part in range(BATCH):
                chunk = jnp.maximum(ids_ref[block * length + step * BATCH + part], 0)
                place = chunk // chunks
                lane = pl.multiple_of((chunk - place * chunks) * LANES, LANES)
                parts.append(all_ref[place, :, pl.ds(lane, LANES)])
            return value + dot_nt(held_ref[batch], jnp.concatenate(parts, axis=1))

        value = lax.fori_loop(
            0, plan_ref[block], apply_batch, jnp.zeros((ROWS, columns), jnp.float32)
        )
        total_ref[pl.ds(pl.multiple_of(block * ROWS, ROWS), ROWS), :] = value
        return carry

    lax.fori_loop(0, blocks, apply_block, 0)
    result = jnp.transpose(total_ref[...]) + scale_ref[...] * block_ref[...]
    out_ref[...] = result
    rounded_ref[...] = result.astype(jnp.bfloat16)


def apply_tiles(ids, plan, tiles, everyone, block, scale, length):
    columns, n = block.shape
    smem = pl.BlockSpec(memory_space=pltpu.SMEM)
    return pl.pallas_call(
        functools.partial(apply_kernel, length),
        out_shape=(
            jax.ShapeDtypeStruct(block.shape, jnp.float32),
            jax.ShapeDtypeStruct(block.shape, jnp.bfloat16),
        ),
        in_specs=[smem, smem, pl.BlockSpec(memory_space=pl.ANY)] + whole_vmem(3),
        out_specs=tuple(whole_vmem(2)),
        scratch_shapes=[
            pltpu.VMEM(tiles.shape, jnp.bfloat16),
            pltpu.VMEM((n, columns), jnp.float32),
            pltpu.SemaphoreType.DMA((tiles.shape[0] // GROUP,)),
        ],
        compiler_params=pltpu.CompilerParams(vmem_limit_bytes=VMEM),
        cost_estimate=pl.CostEstimate(
            flops=6 * n * n * columns, bytes_accessed=8 * n * n, transcendentals=0
        ),
        name="apply_tiles",
    )(ids, plan, tiles, everyone, block, scale)


def solve_positive(matrix, target):
    n = matrix.shape[0]
    table = jnp.concatenate([0.5 * (matrix + jnp.transpose(matrix)), target], axis=1)
    bands = [table[k : k + 8, :] for k in range(0, n, 8)]
    row_index = lax.broadcasted_iota(jnp.int32, (8, 1), 0)
    for k in range(0, n, 2):
        own, row = k // 8, k % 8
        firsts = [band[:, k : k + 1] for band in bands]
        seconds = [band[:, k + 1 : k + 2] for band in bands]
        a, b = firsts[own][row : row + 1, :], seconds[own][row : row + 1, :]
        c, d = firsts[own][row + 1 : row + 2, :], seconds[own][row + 1 : row + 2, :]
        determinant = a * d - b * c
        inverse = lax.rsqrt(determinant)
        inverse = inverse * inverse
        inverse = inverse * (2.0 - determinant * inverse)
        upper, lower = bands[own][row : row + 1, :], bands[own][row + 1 : row + 2, :]
        new_upper = (d * upper - b * lower) * inverse
        new_lower = (a * lower - c * upper) * inverse
        bands = [
            band - (first * new_upper + second * new_lower)
            for band, first, second in zip(bands, firsts, seconds)
        ]
        bands[own] = jnp.where(
            row_index == row, new_upper, jnp.where(row_index == row + 1, new_lower, bands[own])
        )
    return jnp.concatenate([band[:, n:] for band in bands], axis=0)


def gram_kernel(left_ref, right_ref, out_ref):
    left, right = left_ref[...], right_ref[...]
    out_ref[0] = dot_nt(left, left, HIGHEST)
    out_ref[1] = dot_nt(left, right, HIGHEST)
    out_ref[2] = dot_nt(right, right, HIGHEST)


def gram_matrices(left, right):
    n = left.shape[0]
    return pl.pallas_call(
        gram_kernel,
        out_shape=jax.ShapeDtypeStruct((3, n, n), jnp.float32),
        in_specs=whole_vmem(2),
        out_specs=whole_vmem(1)[0],
        name="gram_matrices",
    )(left, right)


def cross_kernel(left_ref, right_ref, out_ref):
    out_ref[...] = dot_nt(left_ref[...], right_ref[...], HIGHEST)


def cross_gram(left, right):
    return pl.pallas_call(
        cross_kernel,
        out_shape=jax.ShapeDtypeStruct((left.shape[0], right.shape[0]), jnp.float32),
        in_specs=whole_vmem(2),
        out_specs=whole_vmem(1)[0],
        name="cross_gram",
    )(left, right)


def first_kernel(grams_ref, out_ref):
    squares, mixed, images = grams_ref[0], grams_ref[1], grams_ref[2]
    n = squares.shape[0]
    step = solve_positive(mixed, squares)
    step_t = jnp.transpose(step)
    cross = dot_nn(mixed, step, HIGHEST)
    after = squares - cross - jnp.transpose(cross) + dot_nn(step_t, dot_nn(images, step, HIGHEST), HIGHEST)
    turn = solve_positive(squares, after)
    eye = (
        lax.broadcasted_iota(jnp.int32, (n, n), 0) == lax.broadcasted_iota(jnp.int32, (n, n), 1)
    ).astype(jnp.float32)
    lead = eye + jnp.transpose(turn)
    part = dot_nn(lead, dot_nn(images, step, HIGHEST), HIGHEST)
    known = dot_nt(dot_nn(lead, mixed, HIGHEST), lead, HIGHEST) - part - jnp.transpose(part)
    out_ref[0] = step_t
    out_ref[1] = lead
    out_ref[2] = after
    out_ref[3] = known


def first_step(grams):
    n = grams.shape[1]
    return pl.pallas_call(
        first_kernel,
        out_shape=jax.ShapeDtypeStruct((4, n, n), jnp.float32),
        in_specs=whole_vmem(1),
        out_specs=whole_vmem(1)[0],
        name="first_step",
    )(grams)


def last_kernel(first_ref, cross_ref, start_ref, image_ref, second_ref, weights_ref, residual_ref):
    step_t, lead, after, known = first_ref[0], first_ref[1], first_ref[2], first_ref[3]
    curvature = known + dot_nt(dot_nn(step_t, cross_ref[...], HIGHEST), step_t, HIGHEST)
    last_t = jnp.transpose(solve_positive(curvature, after))
    outer = step_t + dot_nn(last_t, lead, HIGHEST)
    inner = dot_nn(last_t, step_t, HIGHEST)
    start, image = start_ref[...], image_ref[...]
    weights_ref[...] = dot_nn(outer, start, HIGHEST) - dot_nn(inner, image, HIGHEST)
    residual_ref[...] = start - dot_nn(outer, image, HIGHEST) + dot_nn(inner, second_ref[...], HIGHEST)


def last_step(first, cross, start, image, second):
    return pl.pallas_call(
        last_kernel,
        out_shape=(jax.ShapeDtypeStruct(start.shape, jnp.float32),) * 2,
        in_specs=whole_vmem(5),
        out_specs=tuple(whole_vmem(2)),
        name="last_step",
    )(first, cross, start, image, second)


def shards(innovations, obs_geometry, obs_error, tile_owner):
    regions = lax.axis_size("region")
    reach = tile_owner.shape[1]
    here = lax.axis_index("region")
    offsets = slot_offsets(regions)

    def to_columns(block):
        return lax.all_to_all(block, "tile", 0, 1, tiled=True)

    def to_rows(block):
        return lax.all_to_all(block, "tile", 1, 0, tiled=True)

    places = lax.all_gather(
        jnp.concatenate([obs_geometry, obs_error[None, :]], axis=0), "tile", axis=1, tiled=True
    )
    n = places.shape[1]
    chunks = n // LANES
    places, start, rounded, rank = sort_region(places, to_columns(innovations))
    scale = places[3:4]

    flags = jnp.where(tile_owner[0] >= 0, 1.0, 0.0).astype(jnp.float32)
    flag_row = jnp.zeros((1, n), jnp.float32).at[0, :reach].set(flags)
    message = jnp.concatenate([places[:3], flag_row], axis=0)
    everyone = exchange(message, offsets, "region")
    region = here ^ jnp.array(offsets, jnp.int32)
    distance = region - here
    ahead = jnp.arange(reach, dtype=jnp.int32)
    own_flag = jnp.sum(jnp.where(distance[:, None] == ahead[None, :], flags[None, :], 0.0), axis=1)
    far_flag = jnp.sum(
        jnp.where(-distance[:, None] == ahead[None, :], everyone[:, 3, :reach], 0.0), axis=1
    )
    listed = (own_flag + far_flag) > 0.5

    most = min(regions, 2 * reach - 1)
    length = -(-most * chunks // BATCH) * BATCH
    capacity = (n // ROWS) * (length // BATCH)
    capacity = -(-capacity // GROUP) * GROUP
    ids, plan = plan_blocks(places, everyone, listed, most)
    tiles = build_tiles(ids, plan, places, everyone, length, capacity)

    apply = functools.partial(apply_tiles, ids, plan, tiles, length=length)
    image, image_rounded = apply(exchange(rounded, offsets, "region"), start, scale)
    image_all = lax.all_gather(image, "tile", axis=0, tiled=True)
    image_rows = to_rows(unsort(rank, image))
    grams = lax.psum(gram_matrices(innovations, image_rows), ("region", "tile"))

    second, _ = apply(exchange(image_rounded, offsets, "region"), image, scale)
    cross = sum_over(cross_gram(image_all, second), "region")
    cross = lax.all_gather(cross, "tile", axis=1, tiled=True)
    second_rows = to_rows(unsort(rank, second))
    first = first_step(grams)
    return last_step(first, cross, innovations, image_rows, second_rows)


def solution(mesh):
    return jax.shard_map(
        shards,
        mesh=mesh,
        in_specs=(
            P(None, ("region", "tile")),
            P(None, ("region", "tile")),
            P(("region", "tile")),
            P("region", None),
        ),
        out_specs=(P(None, ("region", "tile")), P(None, ("region", "tile"))),
        check_vma=False,
    )
```

time: 413 us -> 250 us (0.61); the launches traced: 405 us -> 248 us
  Pallas kernels: 0 us -> 88.3 us
  waiting for transfers between devices: 109 us -> 30 us
  other arithmetic: 66.4 us -> 12.1 us
  blocking collectives: 89.3 us -> 50.9 us
  matrix products: 32.3 us -> 0 us
  between operations: 19.5 us -> 0.93 us
  starting transfers between devices: 70.1 us -> 53.8 us
  local copies, waits for them, and re-layouts: 17.4 us -> 12.3 us
    pallas_call x0 -> x10, Pallas kernels: none -> 88.3 us  [the longest x2 27.9 us: apply_tiles(): pl.pallas_call(functools.partial(apply_kernel, length), out_shape=(jax.Sh...]
    psum x2 -> x1, blocking collectives: 82.3 us -> 38.9 us  [shards(): grams = lax.psum(gram_matrices(innovations, image_rows), ('region', 'tile'))]
    ppermute x30 -> x16, waiting for transfers between devices: 70.2 us -> 30 us  [the longest x12 26.9 us: exchange(): other = lax.ppermute(gathered, axis, [(i, i ^ bit) for i in range(count)])]
    reduce_scatter x2 -> x0, waiting for transfers between devices: 39 us -> none  [shards(): lax.psum_scatter(total_block, 'tile', scatter_dimension=1, tiled=True)]
    another operation x15 -> x2, other arithmetic: 36.2 us -> 2.07 us  [the longest x9 19.6 us: gram_solve(): factor = jnp.linalg.cholesky(symmetric)]
    dot_general x24 -> x0, matrix products: 31.1 us -> none  [the longest x6 17.6 us: both_terms(): jnp.dot(home_block, tile_block, preferred_element_type=jnp.float32)]
    convert_element_type x3 -> x1, other arithmetic: 23.6 us -> 0.01 us  [plan_blocks(): counted = active.astype(jnp.int32)]
    ppermute x30 -> x16, starting transfers between devices: 69.8 us -> 47.1 us  [the longest x12 34.3 us: exchange(): other = lax.ppermute(gathered, axis, [(i, i ^ bit) for i in range(count)])]
  transfers between devices with their start and end apart: 32 -> 18, of which waited for: 17 -> 9; matrix products, arithmetic and copies ran while one was open for 15% -> 6% of each run, Pallas kernels for 0% -> 16%
where the time goes in v1:
time: 250 us; the launch traced here: 248 us
  Pallas kernels  88.3 us (35%)
  starting transfers between devices  53.8 us (22%)
  blocking collectives  50.9 us (20%)
  waiting for transfers between devices  30 us (12%)
  local copies, waits for them, and re-layouts  12.3 us (5%)
  other arithmetic  12.1 us (5%)
    psum x1, blocking collectives, shards(): grams = lax.psum(gram_matrices(innovations, image_rows), ('region', 'tile'))  38.9 us
    ppermute x12, starting transfers between devices, exchange(): other = lax.ppermute(gathered, axis, [(i, i ^ bit) for i in range(count)])  34.3 us
    pallas_call x2, Pallas kernels, apply_tiles(): pl.pallas_call(functools.partial(apply_kernel, length), out_shape=(jax.Sh...  27.9 us
    ppermute x12, waiting for transfers between devices, exchange(): other = lax.ppermute(gathered, axis, [(i, i ^ bit) for i in range(count)])  26.9 us
    pallas_call x1, Pallas kernels, first_step(): pl.pallas_call(first_kernel, out_shape=jax.ShapeDtypeStruct((4, n, n), jn...  17.5 us
    pallas_call x1, Pallas kernels, build_tiles(): pl.pallas_call(functools.partial(build_kernel, length), out_shape=jax.Sha...  13.6 us
    ppermute x4, starting transfers between devices, sum_over(): lax.ppermute(block, axis, [(i, i ^ bit) for i in range(count)])  12.7 us
    pallas_call x1, Pallas kernels, last_step(): pl.pallas_call(last_kernel, out_shape=(jax.ShapeDtypeStruct(start.shape,...  10.5 us
  transfers between devices with their start and end apart: 18, of which 9 were waited for; matrix products, arithmetic and copies ran while one was open for 6% of the time, Pallas kernels for 16%

profile of v1, /device:TPU:0, one launch (start us, length us, event | category | flops | bytes accessed | tf_op | source)
XLA Modules:
  0.0 248.4 jit_solution(16949699210310413158)
XLA Ops:
  0.6 3.4 %all-to-all-start = ((f32[2,32,512]{2,1,0:T(8,128)}), f32[2,32,512]{2,1,0:T(8,128)S(1)}, u32[]{:S(2)}, u32[]{:S(2)}) async-start(f32[2,32,512]{2,1,0:T(8,128)} %bitcast.40), calls=%async_computation | async-start | bytes 262144 | tf_op jit(solution)/shard_map/all_to_all | solution.py:454
  4.0 0.7 compare_reduce_fusion
  4.7 0.7 pad_maximum_fusion.9
  5.5 2.0 all_gather.9.places_ref
  7.4 1.0 copy.36.y_ref
  8.5 0.7 copy.52
  9.2 8.3 %sort_region.1 = (f32[4,1024]{1,0:T(4,128)}, f32[32,1024]{1,0:T(8,128)}, bf16[32,1024]{1,0:T(8,128)(2,1)}, f32[1,1024]{1,0:T(1,128)}) custom-call(f32[4,1024]{1,0:T(4,128)} %copy-done.4, f32[1024,1]{1,0:T(8,128)} %copy.36.y_ref, f32[32,1024]{1,0:T(8,128)} %bitcast.55), custom_call_target="tpu_custom_call" | custom-call | flops 251658240 | bytes 4194304 | tf_op jit(solution)/shard_map/sort_region/pallas_call | solution.py:113
  17.5 1.3 broadcast_select_fusion
  18.8 0.7 constant_dynamic-update-slice_fusion.4
  19.5 4.1 %collective-permute-start = (f32[1,4,1024]{2,1,0:T(4,128)S(1)}, f32[1,4,1024]{2,1,0:T(4,128)S(1)}, u32[]{:S(2)}, u32[]{:S(2)}) collective-permute-start(f32[1,4,1024]{2,1,0:T(4,128)S(1)} %get-tuple-element.31), channel_id=1, source_target_pairs={{0,16},{2,18},{4,20},{6,22},{8,24},{10,26},{12,28},{14,30},{16,0},... | collective-permute-start | bytes 49160 | tf_op jit(solution)/shard_map/ppermute | solution.py:49
  23.7 1.4 fusion.7
  25.1 0.8 constant_dynamic-update-slice_fusion.9
  26.1 0.7 fusion.4
  27.0 1.9 collective-permute-start.1
  29.0 2.1 collective-permute-done.1
  31.0 1.8 collective-permute-start.2
  32.9 0.9 pad_maximum_fusion.5
  33.8 1.6 collective-permute-start.5
  35.5 1.8 collective-permute-start.3
  37.2 1.6 collective-permute-done.5
  38.8 0.9 pad_maximum_fusion.2
  40.0 0.5 collective-permute-done.3
  42.1 0.7 sub.28.ids_ref
  42.8 3.3 %collective-permute-done.6 = bf16[4,32,1024]{2,1,0:T(8,128)(2,1)S(1)} collective-permute-done((bf16[4,32,1024]{2,1,0:T(8,128)(2,1)S(1)}, bf16[4,32,1024]{2,1,0:T(8,128)(2,1)S(1)}, u32[]{:S(2)}, u32[]{:S(2)}) %collective-permute-start.6) | collective-permute-done | bytes 262176 | tf_op jit(solution)/shard_map/ppermute | solution.py:49
  46.1 0.9 pad_maximum_fusion
  47.0 1.6 collective-permute-start.7
  48.7 0.6 pad_add_fusion.plan_ref
  49.3 13.6 %build_tiles.1.tiles_ref = bf16[416,64,512]{2,1,0:T(8,128)(2,1)} custom-call(s32[1664]{0:T(1024)} %sub.28.ids_ref, s32[32]{0:T(128)} %pad_add_fusion.plan_ref, f32[4,1024]{1,0:T(4,128)} %get-tuple-element.22.own_ref, f32[16,4,1024]{2,1,0:T(4,128)} %copy-done.3), custom_call_target="tpu_custom_call" | custom-call | flops 125829120 | bytes 8388608 | tf_op jit(solution)/shard_map/build_tiles/pallas_call | solution.py:241
  63.0 1.0 copy-done
  64.0 14.0 %apply_tiles.2 = (f32[32,1024]{1,0:T(8,128)}, bf16[32,1024]{1,0:T(8,128)(2,1)}) custom-call(s32[1664]{0:T(1024)} %sub.28.ids_ref, s32[32]{0:T(128)} %pad_add_fusion.plan_ref, bf16[416,64,512]{2,1,0:T(8,128)(2,1)} %build_tiles.1.tiles_ref, bf16[16,32,1024]{2,1,0:T(8,128)(2,1)} %copy-done, f32[32,1024]{1,0:T(8,128)} %get-tuple-element.24.block_ref, ...), custom_call_target="tpu_custom_call" | custom-call | flops 201326592 | bytes 8388608 | tf_op jit(solution)/shard_map/apply_tiles/pallas_call | solution.py:314
  78.0 9.5 %collective-permute-start.8 = (bf16[1,32,1024]{2,1,0:T(8,128)(2,1)}, bf16[1,32,1024]{2,1,0:T(8,128)(2,1)S(1)}, u32[]{:S(2)}, u32[]{:S(2)}) collective-permute-start(bf16[1,32,1024]{2,1,0:T(8,128)(2,1)} %bitcast.47), channel_id=1, source_target_pairs={{0,16},{2,18},{4,20},{6,22},{8,24},{10,26},{12,28},{14,30},{16,0},... | collective-permute-start | bytes 196616 | tf_op jit(solution)/shard_map/ppermute | solution.py:49
  87.5 3.2 %collective-permute-done.8 = bf16[1,32,1024]{2,1,0:T(8,128)(2,1)S(1)} collective-permute-done((bf16[1,32,1024]{2,1,0:T(8,128)(2,1)}, bf16[1,32,1024]{2,1,0:T(8,128)(2,1)S(1)}, u32[]{:S(2)}, u32[]{:S(2)}) %collective-permute-start.8) | collective-permute-done | bytes 65568 | tf_op jit(solution)/shard_map/ppermute | solution.py:49
  90.7 0.9 pad_maximum_fusion.6
  91.5 5.6 %collective-permute-start.9 = (bf16[2,32,1024]{2,1,0:T(8,128)(2,1)S(1)}, bf16[2,32,1024]{2,1,0:T(8,128)(2,1)S(1)}, u32[]{:S(2)}, u32[]{:S(2)}) collective-permute-start(bf16[2,32,1024]{2,1,0:T(8,128)(2,1)S(1)} %pad_maximum_fusion.6), channel_id=1, source_target_pairs={{0,8},{2,10},{4,12},{6,14},{8,0},{10,2},{12,4},{14,6},{16,24},{18,... | collective-permute-start | bytes 393224 | tf_op jit(solution)/shard_map/ppermute | solution.py:49
  97.1 2.9 %collective-permute-done.9 = bf16[2,32,1024]{2,1,0:T(8,128)(2,1)S(1)} collective-permute-done((bf16[2,32,1024]{2,1,0:T(8,128)(2,1)S(1)}, bf16[2,32,1024]{2,1,0:T(8,128)(2,1)S(1)}, u32[]{:S(2)}, u32[]{:S(2)}) %collective-permute-start.9) | collective-permute-done | bytes 131104 | tf_op jit(solution)/shard_map/ppermute | solution.py:49
  100.0 0.9 pad_maximum_fusion.3
  100.9 6.0 %collective-permute-start.10 = (bf16[4,32,1024]{2,1,0:T(8,128)(2,1)S(1)}, bf16[4,32,1024]{2,1,0:T(8,128)(2,1)S(1)}, u32[]{:S(2)}, u32[]{:S(2)}) collective-permute-start(bf16[4,32,1024]{2,1,0:T(8,128)(2,1)S(1)} %pad_maximum_fusion.3), channel_id=1, source_target_pairs={{0,4},{2,6},{4,0},{6,2},{8,12},{10,14},{12,8},{14,10},{16,20},{18,... | collective-permute-start | bytes 786440 | tf_op jit(solution)/shard_map/ppermute | solution.py:49
  106.9 3.5 %all_gather.10.left_ref = f32[64,1024]{1,0:T(8,128)} all-gather(f32[32,1024]{1,0:T(8,128)} %get-tuple-element.25.block_ref), channel_id=1, replica_groups=mesh['region'=16,'tile'=2] {'tile'}, dimensions={0}, use_global_device_ids=true | all-gather | bytes 393216 | tf_op jit(solution)/shard_map/all_gather | solution.py:489
  110.4 0.8 collective-permute-done.10
  111.2 0.9 pad_maximum_fusion.1
  112.2 0.8 constant_dynamic-update-slice_fusion.14
  113.1 12.4 %collective-permute-done.11 = bf16[8,32,1024]{2,1,0:T(8,128)(2,1)S(1)} collective-permute-done((bf16[8,32,1024]{2,1,0:T(8,128)(2,1)S(1)}, bf16[8,32,1024]{2,1,0:T(8,128)(2,1)S(1)}, u32[]{:S(2)}, u32[]{:S(2)}) %collective-permute-start.11) | collective-permute-done | bytes 524320 | tf_op jit(solution)/shard_map/ppermute | solution.py:49
  125.6 1.0 copy-done.1
  126.6 14.0 %apply_tiles.3 = (f32[32,1024]{1,0:T(8,128)}, bf16[32,1024]{1,0:T(8,128)(2,1)}) custom-call(s32[1664]{0:T(1024)} %sub.28.ids_ref, s32[32]{0:T(128)} %pad_add_fusion.plan_ref, bf16[416,64,512]{2,1,0:T(8,128)(2,1)} %build_tiles.1.tiles_ref, bf16[16,32,1024]{2,1,0:T(8,128)(2,1)} %copy-done.1, f32[32,1024]{1,0:T(8,128)} %get-tuple-element.25.block_ref, ...), custom_call_target="tpu_custom_call" | custom-call | flops 201326592 | bytes 8388608 | tf_op jit(solution)/shard_map/apply_tiles/pallas_call | solution.py:314
  140.6 2.0 cross_gram.1
  142.5 0.9 collective-permute-start.12
  143.5 3.2 %collective-permute-done.12 = f32[64,32]{1,0:T(8,128)S(1)} collective-permute-done((f32[64,32]{1,0:T(8,128)}, f32[64,32]{1,0:T(8,128)S(1)}, u32[]{:S(2)}, u32[]{:S(2)}) %collective-permute-start.12) | collective-permute-done | bytes 8224 | tf_op jit(solution)/shard_map/ppermute | solution.py:68
  146.6 0.8 add.62
  147.4 0.7 collective-permute-start.13
  148.1 3.2 %unsort.2 = f32[32,1024]{1,0:T(8,128)} custom-call(f32[1,1024]{1,0:T(1,128)} %get-tuple-element.21.rank_ref, f32[32,1024]{1,0:T(8,128)} %get-tuple-element.25.block_ref), custom_call_target="tpu_custom_call" | custom-call | flops 201326592 | bytes 4194304 | tf_op jit(solution)/shard_map/unsort/pallas_call | solution.py:140
  151.3 0.9 copy.58
  152.2 4.5 %all_to_all.57 = f32[32,2,512]{2,0,1:T(8,128)} all-to-all(f32[32,2,512]{2,0,1:T(8,128)S(1)} %bitcast.54), channel_id=1, replica_groups=mesh['region'=16,'tile'=2] {'tile'}, dimensions={1} | all-to-all | bytes 262144 | tf_op jit(solution)/shard_map/all_to_all | solution.py:457
  156.8 2.1 gram_matrices.1
  158.8 9.0 %collective-permute-start.14 = (f32[64,32]{1,0:T(8,128)S(1)}, f32[64,32]{1,0:T(8,128)S(1)}, u32[]{:S(2)}, u32[]{:S(2)}) collective-permute-start(f32[64,32]{1,0:T(8,128)S(1)} %add.63), channel_id=1, source_target_pairs={{0,8},{2,10},{4,12},{6,14},{8,0},{10,2},{12,4},{14,6},{16,24},{18,... | collective-permute-start | bytes 24584 | tf_op jit(solution)/shard_map/ppermute | solution.py:68
  167.8 38.9 %psum.7.grams_ref = f32[3,64,64]{2,1,0:T(8,128)} all-reduce(f32[3,64,64]{2,1,0:T(8,128)} %gram_matrices.1), channel_id=1, replica_groups=mesh['region'=16,'tile'=2] {'region','tile'}, use_global_device_ids=true, to_apply=%region_7.8 | all-reduce | flops 12288 | bytes 98304 | tf_op jit(solution)/shard_map/psum | solution.py:491
  206.7 17.5 %first_step.1.first_ref = f32[4,64,64]{2,1,0:T(8,128)} custom-call(f32[3,64,64]{2,1,0:T(8,128)} %psum.7.grams_ref), custom_call_target="tpu_custom_call" | custom-call | tf_op jit(solution)/shard_map/first_step/pallas_call | solution.py:417
  224.2 2.1 collective-permute-start.15
  226.3 3.2 %unsort.3 = f32[32,1024]{1,0:T(8,128)} custom-call(f32[1,1024]{1,0:T(1,128)} %get-tuple-element.21.rank_ref, f32[32,1024]{1,0:T(8,128)} %get-tuple-element.27.right_ref.block_ref), custom_call_target="tpu_custom_call" | custom-call | flops 201326592 | bytes 4194304 | tf_op jit(solution)/shard_map/unsort/pallas_call | solution.py:140
  229.5 1.6 copy.57
  231.1 3.4 %all-to-all-start.2 = ((f32[32,2,512]{2,0,1:T(8,128)}), f32[32,2,512]{2,0,1:T(8,128)S(1)}, u32[]{:S(2)}, u32[]{:S(2)}) async-start(f32[32,2,512]{2,0,1:T(8,128)} %bitcast.37), calls=%async_computation.2 | async-start | bytes 262144 | tf_op jit(solution)/shard_map/all_to_all | solution.py:457
  234.6 2.0 all_gather.11
  236.5 0.7 copy.45.cross_ref
  237.2 0.6 copy-done.2
  237.9 10.5 %last_step.1 = (f32[64,512]{1,0:T(8,128)}, f32[64,512]{1,0:T(8,128)}) custom-call(f32[4,64,64]{2,1,0:T(8,128)} %first_step.1.first_ref, f32[64,64]{1,0:T(8,128)} %copy.45.cross_ref, f32[64,512]{1,0:T(8,128)} %start_ref.1, f32[64,512]{1,0:T(8,128)} %bitcast.42, f32[64,512]{1,0:T(8,128)} %bitcast.52), custom_call_target="tpu_custom_call" | custom-call | tf_op jit(solution)/shard_map/last_step/pallas_call | solution.py:438
  (63 shorter events, 2.9 us)
Async XLA Ops:
  0.6 7.9 %all-to-all-start = ((f32[2,32,512]{2,1,0:T(8,128)}), f32[2,32,512]{2,1,0:T(8,128)S(1)}, u32[]{:S(2)}, u32[]{:S(2)}) async-start(f32[2,32,512]{2,1,0:T(8,128)} %bitcast.40), calls=%async_computation | async-start | bytes 262144 | tf_op jit(solution)/shard_map/all_to_all | solution.py:454
  7.4 1.7 copy-start.4
  19.5 7.5 %collective-permute-start = (f32[1,4,1024]{2,1,0:T(4,128)S(1)}, f32[1,4,1024]{2,1,0:T(4,128)S(1)}, u32[]{:S(2)}, u32[]{:S(2)}) collective-permute-start(f32[1,4,1024]{2,1,0:T(4,128)S(1)} %get-tuple-element.31), channel_id=1, source_target_pairs={{0,16},{2,18},{4,20},{6,22},{8,24},{10,26},{12,28},{14,30},{16,0},... | collective-permute-start | bytes 49160 | tf_op jit(solution)/shard_map/ppermute | solution.py:49
  23.6 9.3 %collective-permute-start.4 = (bf16[1,32,1024]{2,1,0:T(8,128)(2,1)}, bf16[1,32,1024]{2,1,0:T(8,128)(2,1)S(1)}, u32[]{:S(2)}, u32[]{:S(2)}) collective-permute-start(bf16[1,32,1024]{2,1,0:T(8,128)(2,1)} %bitcast.43), channel_id=1, source_target_pairs={{0,16},{2,18},{4,20},{6,22},{8,24},{10,26},{12,28},{14,30},{16,0},... | collective-permute-start | bytes 196616 | tf_op jit(solution)/shard_map/ppermute | solution.py:49
  27.0 4.0 %collective-permute-start.1 = (f32[2,4,1024]{2,1,0:T(4,128)S(1)}, f32[2,4,1024]{2,1,0:T(4,128)S(1)}, u32[]{:S(2)}, u32[]{:S(2)}) collective-permute-start(f32[2,4,1024]{2,1,0:T(4,128)S(1)} %pad_maximum_fusion.8), channel_id=1, source_target_pairs={{0,8},{2,10},{4,12},{6,14},{8,0},{10,2},{12,4},{14,6},{16,24},{18,... | collective-permute-start | bytes 98312 | tf_op jit(solution)/shard_map/ppermute | solution.py:49
  31.0 4.4 %collective-permute-start.2 = (f32[4,4,1024]{2,1,0:T(4,128)S(1)}, f32[4,4,1024]{2,1,0:T(4,128)S(1)}, u32[]{:S(2)}, u32[]{:S(2)}) collective-permute-start(f32[4,4,1024]{2,1,0:T(4,128)S(1)} %pad_maximum_fusion.7), channel_id=1, source_target_pairs={{0,4},{2,6},{4,0},{6,2},{8,12},{10,14},{12,8},{14,10},{16,20},{18,... | collective-permute-start | bytes 196616 | tf_op jit(solution)/shard_map/ppermute | solution.py:49
  33.8 5.0 %collective-permute-start.5 = (bf16[2,32,1024]{2,1,0:T(8,128)(2,1)S(1)}, bf16[2,32,1024]{2,1,0:T(8,128)(2,1)S(1)}, u32[]{:S(2)}, u32[]{:S(2)}) collective-permute-start(bf16[2,32,1024]{2,1,0:T(8,128)(2,1)S(1)} %pad_maximum_fusion.5), channel_id=1, source_target_pairs={{0,8},{2,10},{4,12},{6,14},{8,0},{10,2},{12,4},{14,6},{16,24},{18,... | collective-permute-start | bytes 393224 | tf_op jit(solution)/shard_map/ppermute | solution.py:49
  35.5 5.0 %collective-permute-start.3 = (f32[8,4,1024]{2,1,0:T(4,128)S(1)}, f32[8,4,1024]{2,1,0:T(4,128)S(1)}, u32[]{:S(2)}, u32[]{:S(2)}) collective-permute-start(f32[8,4,1024]{2,1,0:T(4,128)S(1)} %pad_maximum_fusion.4), channel_id=1, source_target_pairs={{0,2},{2,0},{4,6},{6,4},{8,10},{10,8},{12,14},{14,12},{16,18},{18,... | collective-permute-start | bytes 393224 | tf_op jit(solution)/shard_map/ppermute | solution.py:49
  39.7 6.4 %collective-permute-start.6 = (bf16[4,32,1024]{2,1,0:T(8,128)(2,1)S(1)}, bf16[4,32,1024]{2,1,0:T(8,128)(2,1)S(1)}, u32[]{:S(2)}, u32[]{:S(2)}) collective-permute-start(bf16[4,32,1024]{2,1,0:T(8,128)(2,1)S(1)} %pad_maximum_fusion.2), channel_id=1, source_target_pairs={{0,4},{2,6},{4,0},{6,2},{8,12},{10,14},{12,8},{14,10},{16,20},{18,... | collective-permute-start | bytes 786440 | tf_op jit(solution)/shard_map/ppermute | solution.py:49
  40.5 8.8 %copy-start.3 = (f32[16,4,1024]{2,1,0:T(4,128)}, f32[16,4,1024]{2,1,0:T(4,128)S(1)}, u32[]{:S(2)}) copy-start(f32[16,4,1024]{2,1,0:T(4,128)S(1)} %constant_dynamic-update-slice_fusion.all_ref) | copy-start | bytes 786436
  47.0 16.0 %collective-permute-start.7 = (bf16[8,32,1024]{2,1,0:T(8,128)(2,1)S(1)}, bf16[8,32,1024]{2,1,0:T(8,128)(2,1)S(1)}, u32[]{:S(2)}, u32[]{:S(2)}) collective-permute-start(bf16[8,32,1024]{2,1,0:T(8,128)(2,1)S(1)} %pad_maximum_fusion), channel_id=1, source_target_pairs={{0,2},{2,0},{4,6},{6,4},{8,10},{10,8},{12,14},{14,12},{16,18},{18,... | collective-permute-start | bytes 1572872 | tf_op jit(solution)/shard_map/ppermute | solution.py:49
  63.0 1.0 copy-start
  78.0 12.7 %collective-permute-start.8 = (bf16[1,32,1024]{2,1,0:T(8,128)(2,1)}, bf16[1,32,1024]{2,1,0:T(8,128)(2,1)S(1)}, u32[]{:S(2)}, u32[]{:S(2)}) collective-permute-start(bf16[1,32,1024]{2,1,0:T(8,128)(2,1)} %bitcast.47), channel_id=1, source_target_pairs={{0,16},{2,18},{4,20},{6,22},{8,24},{10,26},{12,28},{14,30},{16,0},... | collective-permute-start | bytes 196616 | tf_op jit(solution)/shard_map/ppermute | solution.py:49
  91.5 8.5 %collective-permute-start.9 = (bf16[2,32,1024]{2,1,0:T(8,128)(2,1)S(1)}, bf16[2,32,1024]{2,1,0:T(8,128)(2,1)S(1)}, u32[]{:S(2)}, u32[]{:S(2)}) collective-permute-start(bf16[2,32,1024]{2,1,0:T(8,128)(2,1)S(1)} %pad_maximum_fusion.6), channel_id=1, source_target_pairs={{0,8},{2,10},{4,12},{6,14},{8,0},{10,2},{12,4},{14,6},{16,24},{18,... | collective-permute-start | bytes 393224 | tf_op jit(solution)/shard_map/ppermute | solution.py:49
  100.9 10.3 %collective-permute-start.10 = (bf16[4,32,1024]{2,1,0:T(8,128)(2,1)S(1)}, bf16[4,32,1024]{2,1,0:T(8,128)(2,1)S(1)}, u32[]{:S(2)}, u32[]{:S(2)}) collective-permute-start(bf16[4,32,1024]{2,1,0:T(8,128)(2,1)S(1)} %pad_maximum_fusion.3), channel_id=1, source_target_pairs={{0,4},{2,6},{4,0},{6,2},{8,12},{10,14},{12,8},{14,10},{16,20},{18,... | collective-permute-start | bytes 786440 | tf_op jit(solution)/shard_map/ppermute | solution.py:49
  112.1 13.4 %collective-permute-start.11 = (bf16[8,32,1024]{2,1,0:T(8,128)(2,1)S(1)}, bf16[8,32,1024]{2,1,0:T(8,128)(2,1)S(1)}, u32[]{:S(2)}, u32[]{:S(2)}) collective-permute-start(bf16[8,32,1024]{2,1,0:T(8,128)(2,1)S(1)} %pad_maximum_fusion.1), channel_id=1, source_target_pairs={{0,2},{2,0},{4,6},{6,4},{8,10},{10,8},{12,14},{14,12},{16,18},{18,... | collective-permute-start | bytes 1572872 | tf_op jit(solution)/shard_map/ppermute | solution.py:49
  125.6 1.0 copy-start.1
  142.5 4.1 %collective-permute-start.12 = (f32[64,32]{1,0:T(8,128)}, f32[64,32]{1,0:T(8,128)S(1)}, u32[]{:S(2)}, u32[]{:S(2)}) collective-permute-start(f32[64,32]{1,0:T(8,128)} %cross_gram.1), channel_id=1, source_target_pairs={{0,2},{2,0},{4,6},{6,4},{8,10},{10,8},{12,14},{14,12},{16,18},{18,... | collective-permute-start | bytes 24584 | tf_op jit(solution)/shard_map/ppermute | solution.py:68
  147.4 11.4 %collective-permute-start.13 = (f32[64,32]{1,0:T(8,128)S(1)}, f32[64,32]{1,0:T(8,128)S(1)}, u32[]{:S(2)}, u32[]{:S(2)}) collective-permute-start(f32[64,32]{1,0:T(8,128)S(1)} %add.62), channel_id=1, source_target_pairs={{0,4},{2,6},{4,0},{6,2},{8,12},{10,14},{12,8},{14,10},{16,20},{18,... | collective-permute-start | bytes 24584 | tf_op jit(solution)/shard_map/ppermute | solution.py:68
  158.8 65.4 %collective-permute-start.14 = (f32[64,32]{1,0:T(8,128)S(1)}, f32[64,32]{1,0:T(8,128)S(1)}, u32[]{:S(2)}, u32[]{:S(2)}) collective-permute-start(f32[64,32]{1,0:T(8,128)S(1)} %add.63), channel_id=1, source_target_pairs={{0,8},{2,10},{4,12},{6,14},{8,0},{10,2},{12,4},{14,6},{16,24},{18,... | collective-permute-start | bytes 24584 | tf_op jit(solution)/shard_map/ppermute | solution.py:68
  224.2 10.3 %collective-permute-start.15 = (f32[64,32]{1,0:T(8,128)S(1)}, f32[64,32]{1,0:T(8,128)S(1)}, u32[]{:S(2)}, u32[]{:S(2)}) collective-permute-start(f32[64,32]{1,0:T(8,128)S(1)} %add.64), channel_id=1, source_target_pairs={{0,16},{2,18},{4,20},{6,22},{8,24},{10,26},{12,28},{14,30},{16,0},... | collective-permute-start | bytes 24584 | tf_op jit(solution)/shard_map/ppermute | solution.py:68
  231.1 6.1 %all-to-all-start.2 = ((f32[32,2,512]{2,0,1:T(8,128)}), f32[32,2,512]{2,0,1:T(8,128)S(1)}, u32[]{:S(2)}, u32[]{:S(2)}) async-start(f32[32,2,512]{2,0,1:T(8,128)} %bitcast.37), calls=%async_computation.2 | async-start | bytes 262144 | tf_op jit(solution)/shard_map/all_to_all | solution.py:457
  237.2 0.6 copy-start.2

commit v2 on v1

v2 whole, which is shorter than its diff:
```python
import functools

import jax
import jax.numpy as jnp
from jax import lax
from jax.experimental import pallas as pl
from jax.experimental.pallas import tpu as pltpu
from jax.sharding import PartitionSpec as P

CUTOFF = 1.001
LANES = 128
PLANE = 4
ROWS = 64
BATCH = 4
GROUP = 4
UNROLL = 4
RING = 4
VMEM = 60 * 1024 * 1024
HIGHEST = lax.Precision.HIGHEST


def whole_vmem(count):
    return [pl.BlockSpec(memory_space=pltpu.VMEM)] * count


def dot_nt(left, right, precision=None):
    return lax.dot_general(
        left, right, (((1,), (1,)), ((), ())), precision=precision, preferred_element_type=jnp.float32
    )


def dot_nn(left, right, precision=None):
    return lax.dot_general(
        left, right, (((1,), (0,)), ((), ())), precision=precision, preferred_element_type=jnp.float32
    )


def three_parts(value):
    high = value.astype(jnp.bfloat16)
    rest = value - high.astype(jnp.float32)
    middle = rest.astype(jnp.bfloat16)
    low = (rest - middle.astype(jnp.float32)).astype(jnp.bfloat16)
    return high, middle, low


def partners(axis, bit):
    return [(i, i ^ bit) for i in range(lax.axis_size(axis))]


def swap_all(block, axis, join):
    bit = 1
    while bit < lax.axis_size(axis):
        block = jnp.concatenate([block, lax.ppermute(block, axis, partners(axis, bit))], axis=join)
        bit *= 2
    return block


def from_ahead(block, distance):
    count = lax.axis_size("region")
    route = [(i + distance, i) for i in range(count) if 0 <= i + distance < count]
    return lax.ppermute(block, "region", route)


def window_regions(reach):
    here = lax.axis_index("region")
    place, base = here % PLANE, here // PLANE * PLANE
    within = jnp.arange(PLANE, dtype=jnp.int32)
    pieces = [base + (place ^ within)]
    for step in range(1, (reach - 2) // PLANE + 2):
        keep = min(PLANE, reach - 1 - (step - 1) * PLANE)
        for sign in (1, -1):
            first = jnp.where(sign > 0, 0, PLANE - keep)
            order = within if keep == PLANE else (within[:keep] ^ (place & (keep - 1)))
            found = (place ^ within) if keep == PLANE else first + order
            pieces.append(base + sign * step * PLANE + found)
    return jnp.concatenate(pieces)


def window(block, reach):
    place = lax.axis_index("region") % PLANE
    block = block[None]
    bit = 1
    while bit < PLANE:
        block = jnp.concatenate([block, lax.ppermute(block, "region", partners("region", bit))], axis=0)
        bit *= 2
    pieces = [block]
    for step in range(1, (reach - 2) // PLANE + 2):
        keep = min(PLANE, reach - 1 - (step - 1) * PLANE)
        for sign in (1, -1):
            sent = block
            if keep < PLANE:
                first = 0 if sign > 0 else PLANE - keep
                sent = lax.dynamic_slice_in_dim(block, (place ^ first) // keep * keep, keep, axis=0)
            pieces.append(from_ahead(sent, sign * step * PLANE))
    return pieces


def sum_over(block, axis):
    count = lax.axis_size(axis)
    bit = 1
    while bit < count:
        block = block + lax.ppermute(block, axis, [(i, i ^ bit) for i in range(count)])
        bit *= 2
    return block


def stacked_parts(value):
    return jnp.concatenate([part.astype(jnp.float32) for part in three_parts(value)], axis=0).astype(
        jnp.bfloat16
    )


def add_parts(value):
    rows = value.shape[0] // 3
    return (value[2 * rows :] + value[rows : 2 * rows]) + value[:rows]


def fill_order(first, rank, order_ref, row, count):
    step = 64

    def fill(block, carry):
        start = pl.multiple_of(block * step, step)
        place = first + start + lax.broadcasted_iota(jnp.int32, (step, rank.shape[1]), 0)
        order_ref[pl.ds(pl.multiple_of(row + start, step), step), :] = jnp.where(
            place == rank, 1.0, 0.0
        ).astype(jnp.bfloat16)
        return carry

    lax.fori_loop(0, count // step, fill, 0)


def sort_kernel(first_ref, places_ref, column_ref, block_ref, places_out, block_out, rounded_out, rank_out, order_ref):
    n = places_ref.shape[1]
    local = block_out.shape[1]
    step = 64
    y_row, index_row = places_ref[1:2, :], places_ref[4:5, :]

    def count(block, total):
        start = pl.multiple_of(block * step, step)
        y_column = jnp.broadcast_to(column_ref[pl.ds(start, step), 0:1], (step, n))
        index_column = jnp.broadcast_to(column_ref[pl.ds(start, step), 1:2], (step, n))
        before = (y_column < y_row) | ((y_column == y_row) & (index_column < index_row))
        return total + jnp.sum(jnp.where(before, 1.0, 0.0).reshape(step // 8, 8, n), axis=0)

    total = lax.fori_loop(0, n // step, count, jnp.zeros((8, n), jnp.float32))
    rank = jnp.sum(total, axis=0, keepdims=True).astype(jnp.int32)
    rank_out[...] = rank[:, :local]
    fill_order(first_ref[0], rank, order_ref, 0, local)
    order = order_ref[...]
    places_out[...] = add_parts(dot_nt(stacked_parts(places_ref[...]), order))
    sorted_block = add_parts(dot_nt(stacked_parts(block_ref[...]), order))
    block_out[...] = sorted_block
    rounded_out[...] = sorted_block.astype(jnp.bfloat16)


def sort_region(first, places, block, local):
    n = places.shape[1]
    columns = block.shape[0]
    return pl.pallas_call(
        sort_kernel,
        out_shape=(
            jax.ShapeDtypeStruct((places.shape[0], local), jnp.float32),
            jax.ShapeDtypeStruct((columns, local), jnp.float32),
            jax.ShapeDtypeStruct((columns, local), jnp.bfloat16),
            jax.ShapeDtypeStruct((1, local), jnp.int32),
        ),
        in_specs=[pl.BlockSpec(memory_space=pltpu.SMEM)] + whole_vmem(3),
        out_specs=tuple(whole_vmem(4)),
        scratch_shapes=[pltpu.VMEM((local, n), jnp.bfloat16)],
        compiler_params=pltpu.CompilerParams(vmem_limit_bytes=VMEM),
        cost_estimate=pl.CostEstimate(
            flops=6 * n * local * (columns + 8), bytes_accessed=4 * n * local, transcendentals=0
        ),
        name="sort_region",
    )(first[:1], places, jnp.stack([places[1], places[4]], axis=1), block)


def unsort_kernel(first_ref, rank_ref, block_ref, block_out, order_ref):
    n, local = order_ref.shape
    for slot in range(n // local):
        fill_order(first_ref[slot], rank_ref[...], order_ref, slot * local, local)
    block_out[...] = add_parts(dot_nn(stacked_parts(block_ref[...]), order_ref[...]))


def unsort(first, rank, block):
    n = block.shape[1]
    local = rank.shape[1]
    return pl.pallas_call(
        unsort_kernel,
        out_shape=jax.ShapeDtypeStruct((block.shape[0], local), jnp.float32),
        in_specs=[pl.BlockSpec(memory_space=pltpu.SMEM)] + whole_vmem(2),
        out_specs=whole_vmem(1)[0],
        scratch_shapes=[pltpu.VMEM((n, local), jnp.bfloat16)],
        compiler_params=pltpu.CompilerParams(vmem_limit_bytes=VMEM),
        cost_estimate=pl.CostEstimate(
            flops=6 * n * local * block.shape[0], bytes_accessed=4 * n * local, transcendentals=0
        ),
        name="unsort",
    )(first, rank, block)


def plan_blocks(own, everyone, listed, length):
    n = own.shape[1]
    slots = everyone.shape[0]
    chunks = everyone.shape[2] // LANES
    y = everyone[:, 1, :].reshape(slots * chunks, LANES)
    y_own = own[1].reshape(n // ROWS, ROWS)
    near = (y[None, :, 0] <= y_own[:, -1:] + CUTOFF) & (y[None, :, -1] >= y_own[:, :1] - CUTOFF)
    active = near & jnp.broadcast_to(listed[:, None], (slots, chunks)).reshape(1, slots * chunks)
    total = slots * chunks
    index = jnp.arange(total, dtype=jnp.int32)
    counted = active.astype(jnp.int32)
    place = jnp.sum(
        jnp.where(index[None, :, None] < index[None, None, :], counted[:, :, None], 0), axis=1
    )
    spot = jnp.arange(length, dtype=jnp.int32)
    hit = active[:, :, None] & (place[:, :, None] == spot[None, None, :])
    ids = jnp.sum(jnp.where(hit, index[None, :, None] + 1, 0), axis=1) - 1
    batches = (jnp.sum(counted, axis=1) + BATCH - 1) // BATCH
    blocks = jnp.arange(n // ROWS, dtype=jnp.int32)
    base = jnp.sum(jnp.where(blocks[None, :] < blocks[:, None], batches[None, :], 0), axis=1)
    return ids.reshape(-1), jnp.concatenate([batches, base])


def gaspari_cohn(squared):
    squared = jnp.maximum(squared, 1e-12)
    inverse = lax.rsqrt(squared)
    scaled = squared * inverse
    near = (((-0.25 * scaled + 0.5) * scaled + 0.625) * scaled - 5.0 / 3.0) * squared + 1.0
    left = jnp.maximum(2.0 - scaled, 0.0)
    left = left * left
    far = (left * left) * ((scaled + 2.0) * scaled - 0.5) * (inverse * (1.0 / 12.0))
    return jnp.where(scaled <= 1.0, near, far)


def build_kernel(length, ids_ref, plan_ref, own_ref, all_ref, tiles_ref, wide_ref, ring_ref, sems):
    n = own_ref.shape[1]
    blocks = n // ROWS
    chunks = all_ref.shape[2] // LANES
    column = jnp.transpose(own_ref[...])
    for row in range(3):
        scale = 2.0 if row < 2 else 1.0
        wide_ref[row] = jnp.broadcast_to(scale * column[:, row : row + 1], (n, LANES))

    def copy_out(slot, batch):
        return pltpu.make_async_copy(ring_ref.at[slot], tiles_ref.at[batch], sems.at[slot])

    def build_block(block, carry):
        start = pl.multiple_of(block * ROWS, ROWS)
        base = plan_ref[blocks + block]

        def build_batch(step, inner):
            batch = base + step
            slot = lax.rem(batch, RING)

            @pl.when(batch >= RING)
            def _():
                copy_out(slot, batch).wait()

            for part in range(BATCH):
                entry = ids_ref[block * length + step * BATCH + part]
                chunk = jnp.maximum(entry, 0)
                place = chunk // chunks
                lane = pl.multiple_of((chunk - place * chunks) * LANES, LANES)
                far = all_ref[place, :, pl.ds(lane, LANES)]
                across_x = wide_ref[0, pl.ds(start, ROWS), :] - 2.0 * far[0:1, :]
                across_y = wide_ref[1, pl.ds(start, ROWS), :] - 2.0 * far[1:2, :]
                value = gaspari_cohn(across_x * across_x + across_y * across_y)
                spread = jnp.where(entry >= 0, far[2:3, :], 0.0)
                value = wide_ref[2, pl.ds(start, ROWS), :] * spread * value
                ring_ref[slot, :, part * LANES : (part + 1) * LANES] = value.astype(jnp.bfloat16)
            copy_out(slot, batch).start()
            return inner

        return lax.fori_loop(0, plan_ref[block], build_batch, carry)

    lax.fori_loop(0, blocks, build_block, 0)
    total = plan_ref[blocks - 1] + plan_ref[2 * blocks - 1]
    for slot in range(RING):

        @pl.when(slot < total)
        def _():
            copy_out(slot, slot).wait()


def build_tiles(ids, plan, own, everyone, length, capacity):
    n = own.shape[1]
    smem = pl.BlockSpec(memory_space=pltpu.SMEM)
    return pl.pallas_call(
        functools.partial(build_kernel, length),
        out_shape=jax.ShapeDtypeStruct((capacity, ROWS, BATCH * LANES), jnp.bfloat16),
        in_specs=[smem, smem] + whole_vmem(2),
        out_specs=pl.BlockSpec(memory_space=pl.ANY),
        scratch_shapes=[
            pltpu.VMEM((3, n, LANES), jnp.float32),
            pltpu.VMEM((RING, ROWS, BATCH * LANES), jnp.bfloat16),
            pltpu.SemaphoreType.DMA((RING,)),
        ],
        compiler_params=pltpu.CompilerParams(vmem_limit_bytes=VMEM),
        cost_estimate=pl.CostEstimate(
            flops=40 * 3 * n * n, bytes_accessed=8 * n * n, transcendentals=3 * n * n
        ),
        name="build_tiles",
    )(ids, plan, own, everyone)


def apply_kernel(length, wanted, ids_ref, plan_ref, tiles_ref, *refs):
    *piece_refs, block_ref, scale_ref, out_ref, rounded_ref, gram_ref = refs[:-5]
    held_ref, all_ref, total_ref, sems, piece_sems = refs[-5:]
    columns, n = block_ref.shape
    blocks = n // ROWS
    chunks = n // LANES
    slots = all_ref.shape[1]

    def pieces():
        half = all_ref.shape[0] // 2
        slot = 0
        for index in range(0, len(piece_refs), 2):
            count = piece_refs[index].shape[1]
            for part in range(2):
                yield pltpu.make_async_copy(
                    piece_refs[index + part],
                    all_ref.at[pl.ds(part * half, half), pl.ds(slot, count)],
                    piece_sems.at[index + part],
                )
            slot += count

    for copy in pieces():
        copy.start()
    total = plan_ref[blocks - 1] + plan_ref[2 * blocks - 1]
    groups = (total + GROUP - 1) // GROUP

    def copy_in(group):
        start = group * GROUP
        return pltpu.make_async_copy(
            tiles_ref.at[pl.ds(start, GROUP)], held_ref.at[pl.ds(start, GROUP)], sems.at[group]
        )

    def start_copy(group, carry):
        copy_in(group).start()
        return carry

    lax.fori_loop(0, groups, start_copy, 0)
    for copy in pieces():
        copy.wait()

    def apply_block(block, carry):
        base = plan_ref[blocks + block]

        batches = plan_ref[block]

        def apply_batches(turn, value):
            for inner in range(UNROLL):
                step = turn * UNROLL + inner
                batch = base + jnp.minimum(step, batches - 1)

                @pl.when((lax.rem(batch, GROUP) == 0) & (step < batches))
                def _(batch=batch):
                    copy_in(batch // GROUP).wait()

            sides, tiles = [], []
            for inner in range(UNROLL):
                step = turn * UNROLL + inner
                tiles.append(held_ref[base + jnp.minimum(step, batches - 1)])
                for part in range(BATCH):
                    entry = ids_ref[block * length + jnp.minimum(step, batches - 1) * BATCH + part]
                    chunk = jnp.maximum(entry, 0)
                    place = chunk // chunks
                    lane = pl.multiple_of((chunk - place * chunks) * LANES, LANES)
                    tile = place // slots
                    side = all_ref[tile, place - tile * slots, :, pl.ds(lane, LANES)]
                    sides.append(jnp.where(step < batches, side, jnp.zeros_like(side)))
            return value + dot_nt(jnp.concatenate(tiles, axis=1), jnp.concatenate(sides, axis=1))

        value = lax.fori_loop(
            0,
            (batches + UNROLL - 1) // UNROLL,
            apply_batches,
            jnp.zeros((ROWS, columns), jnp.float32),
        )
        total_ref[pl.ds(pl.multiple_of(block * ROWS, ROWS), ROWS), :] = value
        return carry

    lax.fori_loop(0, blocks, apply_block, 0)
    block = block_ref[...]
    result = jnp.transpose(total_ref[...]) + scale_ref[...] * block
    out_ref[...] = result
    rounded_ref[...] = result.astype(jnp.bfloat16)
    pairs = {"squares": (block, block), "mixed": (block, result), "images": (result, result)}
    for index, name in enumerate(wanted):
        gram_ref[index] = dot_nt(*pairs[name], HIGHEST)


def apply_tiles(ids, plan, tiles, pieces, block, scale, length, wanted):
    columns, n = block.shape
    smem = pl.BlockSpec(memory_space=pltpu.SMEM)
    anywhere = pl.BlockSpec(memory_space=pl.ANY)
    tile_slots = 2 * pieces[0].shape[0]
    slots = sum(piece.shape[1] for piece in pieces) // 2
    return pl.pallas_call(
        functools.partial(apply_kernel, length, wanted),
        out_shape=(
            jax.ShapeDtypeStruct(block.shape, jnp.float32),
            jax.ShapeDtypeStruct(block.shape, jnp.bfloat16),
            jax.ShapeDtypeStruct((len(wanted), columns, columns), jnp.float32),
        ),
        in_specs=[smem, smem, anywhere] + [anywhere] * len(pieces) + whole_vmem(2),
        out_specs=tuple(whole_vmem(3)),
        scratch_shapes=[
            pltpu.VMEM(tiles.shape, jnp.bfloat16),
            pltpu.VMEM((tile_slots, slots, columns, n), jnp.bfloat16),
            pltpu.VMEM((n, columns), jnp.float32),
            pltpu.SemaphoreType.DMA((tiles.shape[0] // GROUP,)),
            pltpu.SemaphoreType.DMA((len(pieces),)),
        ],
        compiler_params=pltpu.CompilerParams(vmem_limit_bytes=VMEM),
        cost_estimate=pl.CostEstimate(
            flops=6 * n * n * columns, bytes_accessed=8 * n * n, transcendentals=0
        ),
        name="apply_tiles",
    )(ids, plan, tiles, *pieces, block, scale)


def reciprocal(value):
    inverse = lax.rsqrt(value)
    inverse = inverse * inverse
    return inverse * (2.0 - value * inverse)


def small_product(left, right):
    return [[sum(l * r[j] for l, r in zip(row, right)) for j in range(len(right[0]))] for row in left]


def small_difference(left, right):
    return [[l - r for l, r in zip(*rows)] for rows in zip(left, right)]


def small_inverse(matrix):
    (a, b), (c, d) = matrix
    scale = reciprocal(a * d - b * c)
    return [[d * scale, -b * scale], [-c * scale, a * scale]]


def solve_positive(matrix, target):
    n = matrix.shape[0]
    table = jnp.concatenate([0.5 * (matrix + jnp.transpose(matrix)), target], axis=1)
    bands = [table[k : k + 8, :] for k in range(0, n, 8)]
    row_index = lax.broadcasted_iota(jnp.int32, bands[0].shape, 0)
    for k in range(0, n, 4):
        own, row = k // 8, k % 8
        columns = [
            [jnp.broadcast_to(band[:, k + j : k + j + 1], band.shape) for band in bands] for j in range(4)
        ]
        pivot = [[columns[j][own][row + i : row + i + 1] for j in range(4)] for i in range(4)]
        upper, lower = pivot[:2], pivot[2:]
        top = small_inverse([r[:2] for r in upper])
        factor = small_product([r[:2] for r in lower], top)
        right = [r[2:] for r in upper]
        rest = small_inverse(small_difference([r[2:] for r in lower], small_product(factor, right)))
        rows = [[bands[own][row + i : row + i + 1]] for i in range(4)]
        last = small_product(rest, small_difference(rows[2:], small_product(factor, rows[:2])))
        first = small_product(top, small_difference(rows[:2], small_product(right, last)))
        new = [r[0] for r in first + last]
        bands = [
            band - ((columns[0][i] * new[0] + columns[1][i] * new[1]) + (columns[2][i] * new[2] + columns[3][i] * new[3]))
            for i, band in enumerate(bands)
        ]
        for i in range(4):
            bands[own] = jnp.where(row_index == row + i, new[i], bands[own])
    return jnp.concatenate([band[:, n:] for band in bands], axis=0)


def first_kernel(grams_ref, out_ref):
    squares, mixed, images = grams_ref[0], grams_ref[1], grams_ref[2]
    n = squares.shape[0]
    step = solve_positive(mixed, squares)
    step_t = jnp.transpose(step)
    cross = dot_nn(mixed, step, HIGHEST)
    after = squares - cross - jnp.transpose(cross) + dot_nn(step_t, dot_nn(images, step, HIGHEST), HIGHEST)
    turn = solve_positive(squares, after)
    eye = (
        lax.broadcasted_iota(jnp.int32, (n, n), 0) == lax.broadcasted_iota(jnp.int32, (n, n), 1)
    ).astype(jnp.float32)
    lead = eye + jnp.transpose(turn)
    part = dot_nn(lead, dot_nn(images, step, HIGHEST), HIGHEST)
    known = dot_nt(dot_nn(lead, mixed, HIGHEST), lead, HIGHEST) - part - jnp.transpose(part)
    out_ref[0] = step_t
    out_ref[1] = lead
    out_ref[2] = after
    out_ref[3] = known


def first_step(grams):
    n = grams.shape[1]
    return pl.pallas_call(
        first_kernel,
        out_shape=jax.ShapeDtypeStruct((4, n, n), jnp.float32),
        in_specs=whole_vmem(1),
        out_specs=whole_vmem(1)[0],
        name="first_step",
    )(grams)


def last_kernel(first_ref, cross_ref, start_ref, images_ref, weights_ref, residual_ref):
    step_t, lead, after, known = first_ref[0], first_ref[1], first_ref[2], first_ref[3]
    n = step_t.shape[0]
    curvature = known + dot_nt(dot_nn(step_t, cross_ref[...], HIGHEST), step_t, HIGHEST)
    last_t = jnp.transpose(solve_positive(curvature, after))
    outer = step_t + dot_nn(last_t, lead, HIGHEST)
    inner = dot_nn(last_t, step_t, HIGHEST)
    start, image = start_ref[...], images_ref[:n, :]
    weights_ref[...] = dot_nn(outer, start, HIGHEST) - dot_nn(inner, image, HIGHEST)
    residual_ref[...] = start - dot_nn(outer, image, HIGHEST) + dot_nn(inner, images_ref[n:, :], HIGHEST)


def last_step(first, cross, start, images):
    return pl.pallas_call(
        last_kernel,
        out_shape=(jax.ShapeDtypeStruct(start.shape, jnp.float32),) * 2,
        in_specs=whole_vmem(4),
        out_specs=tuple(whole_vmem(2)),
        name="last_step",
    )(first, cross, start, images)


def shards(innovations, obs_geometry, obs_error, tile_owner):
    tiles_axis = lax.axis_size("tile")
    reach = tile_owner.shape[1]
    here, tile = lax.axis_index("region"), lax.axis_index("tile")
    columns, local = innovations.shape
    first = (tile ^ jnp.arange(tiles_axis, dtype=jnp.int32)) * local

    index = (first[0] + jnp.arange(local, dtype=jnp.int32)).astype(jnp.float32)
    places = jnp.concatenate([obs_geometry, obs_error[None, :], index[None, :]], axis=0)
    places = swap_all(places, "tile", 1)
    own, start, rounded, rank = sort_region(first, places, swap_all(innovations, "tile", 1), local)
    scale = own[3:4]

    flags = jnp.where(tile_owner[0] >= 0, 1.0, 0.0).astype(jnp.float32)
    flag_row = jnp.concatenate([flags, jnp.zeros((local - reach,), jnp.float32)])[None, :]
    message = swap_all(jnp.concatenate([own[:3], flag_row], axis=0)[None], "tile", 0)
    everyone = jnp.concatenate(window(message, reach), axis=0)
    slots = everyone.shape[0]
    region = window_regions(reach)
    distance = region - here
    ahead = jnp.arange(reach, dtype=jnp.int32)
    own_flag = jnp.sum(jnp.where(distance[:, None] == ahead[None, :], flags[None, :], 0.0), axis=1)
    far_flag = jnp.sum(
        jnp.where(-distance[:, None] == ahead[None, :], everyone[:, 0, 3, :reach], 0.0), axis=1
    )
    inside = (region >= 0) & (region < lax.axis_size("region"))
    listed = jnp.tile(inside & ((own_flag + far_flag) > 0.5), tiles_axis)
    everyone = jnp.swapaxes(everyone, 0, 1).reshape(tiles_axis * slots, 4, local)

    most = min(lax.axis_size("region"), 2 * reach - 1) * tiles_axis * (local // LANES)
    length = -(-most // BATCH) * BATCH
    capacity = (local // ROWS) * (length // BATCH)
    capacity = -(-capacity // GROUP) * GROUP
    ids, plan = plan_blocks(own, everyone, listed, length)
    tiles = build_tiles(ids, plan, own, everyone, length, capacity)

    def apply(rounded, block, wanted):
        pieces = []
        for piece in window(rounded, reach):
            piece = piece[None]
            bit = 1
            while 2 * bit < tiles_axis:
                piece = jnp.concatenate([piece, lax.ppermute(piece, "tile", partners("tile", bit))], axis=0)
                bit *= 2
            pieces += [piece, lax.ppermute(piece, "tile", partners("tile", bit))]
        return apply_tiles(ids, plan, tiles, pieces, block, scale, length, wanted)

    image, image_rounded, grams = apply(rounded, start, ("squares", "mixed", "images"))
    grams = sum_over(sum_over(grams, "tile"), "region")
    second, _, cross = apply(image_rounded, image, ("mixed",))
    cross = sum_over(sum_over(cross[0], "tile"), "region")
    images = swap_all(jnp.concatenate([image, second], axis=0), "tile", 1)
    images = unsort(first, rank, images)
    return last_step(first_step(grams), cross, innovations, images)


def solution(mesh):
    return jax.shard_map(
        shards,
        mesh=mesh,
        in_specs=(
            P(None, ("region", "tile")),
            P(None, ("region", "tile")),
            P(("region", "tile")),
            P("region", None),
        ),
        out_specs=(P(None, ("region", "tile")), P(None, ("region", "tile"))),
        check_vma=False,
    )
```

time: 250 us -> 174 us (0.70)
  blocking collectives: 50.9 us -> 0 us
  Pallas kernels: 88.3 us -> 44.8 us
  starting transfers between devices: 53.8 us -> 74.4 us
  local copies, waits for them, and re-layouts: 12.3 us -> 9.12 us
    psum x1 -> x0, blocking collectives: 38.9 us -> none  [shards(): grams = lax.psum(gram_matrices(innovations, image_rows), ('region', 'tile'))]
    ppermute x12 -> x32, starting transfers between devices: 34.3 us -> 58.1 us  [the longest x12 41.6 us: from_ahead(): return lax.ppermute(block, 'region', route)]
    pallas_call x7 -> x4, Pallas kernels: 46.6 us -> 23 us  [the longest x2 14.6 us: apply_tiles(): pl.pallas_call(functools.partial(apply_kernel, length, wanted), out_shape...]
    pallas_call x1, Pallas kernels: 17.5 us -> 8.18 us  [first_step(): pl.pallas_call(first_kernel, out_shape=jax.ShapeDtypeStruct((4, n, n), jn...]
    ppermute x4 -> x10, waiting for transfers between devices: 3.18 us -> 12.3 us  [sum_over(): lax.ppermute(block, axis, [(i, i ^ bit) for i in range(count)])]
    ppermute x12 -> x32, waiting for transfers between devices: 26.9 us -> 18.9 us  [the longest x6 14.4 us: window(): lax.ppermute(block, 'region', partners('region', bit))]
    all_gather x3 -> x0, blocking collectives: 7.46 us -> none  [the longest x1 3.52 us: shards(): image_all = lax.all_gather(image, 'tile', axis=0, tiled=True)]
    all_to_all x2 -> x0, starting transfers between devices: 6.77 us -> none  [the longest x1 3.39 us: to_columns(): return lax.all_to_all(block, 'tile', 0, 1, tiled=True)]
  transfers between devices with their start and end apart: 18 -> 42, of which waited for: 9 -> 12; matrix products, arithmetic and copies ran while one was open for 6% -> 7% of each run, Pallas kernels for 16% -> 13%
where the time goes in v2:
time: 174 us
  starting transfers between devices  74.4 us (43%)
  Pallas kernels  44.8 us (26%)
  waiting for transfers between devices  31.2 us (18%)
  other arithmetic  12.8 us (7%)
  local copies, waits for them, and re-layouts  9.12 us (5%)
    ppermute x12, starting transfers between devices, from_ahead(): return lax.ppermute(block, 'region', route)  41.6 us
    ppermute x10, starting transfers between devices, sum_over(): lax.ppermute(block, axis, [(i, i ^ bit) for i in range(count)])  16.3 us
    pallas_call x2, Pallas kernels, apply_tiles(): pl.pallas_call(functools.partial(apply_kernel, length, wanted), out_shape...  14.6 us
    ppermute x6, waiting for transfers between devices, window(): lax.ppermute(block, 'region', partners('region', bit))  14.4 us
    ppermute x6, starting transfers between devices, window(): lax.ppermute(block, 'region', partners('region', bit))  12.8 us
    ppermute x10, waiting for transfers between devices, sum_over(): lax.ppermute(block, axis, [(i, i ^ bit) for i in range(count)])  12.3 us
    pallas_call x1, Pallas kernels, first_step(): pl.pallas_call(first_kernel, out_shape=jax.ShapeDtypeStruct((4, n, n), jn...  8.18 us
    pallas_call x1, Pallas kernels, build_tiles(): pl.pallas_call(functools.partial(build_kernel, length), out_shape=jax.Sha...  7.77 us
  transfers between devices with their start and end apart: 42, of which 12 were waited for; matrix products, arithmetic and copies ran while one was open for 7% of the time, Pallas kernels for 13%

profile of v2, /device:TPU:0, one launch (start us, length us, event | category | flops | bytes accessed | tf_op | source)
XLA Modules:
  0.0 173.7 jit_solution(8854303923641616286)
XLA Ops:
  0.7 0.7 pad_maximum_fusion.9
  2.1 0.7 fusion.2
  3.0 0.7 pad_maximum_fusion.7.places_ref
  3.8 1.0 copy.27.column_ref
  4.8 1.6 pad_maximum_fusion.1.block_ref
  6.4 5.8 %sort_region.1 = (f32[5,512]{1,0:T(8,128)}, f32[64,512]{1,0:T(8,128)}, bf16[64,512]{1,0:T(8,128)(2,1)}, s32[1,512]{1,0:T(1,128)}) custom-call(s32[1]{0:T(128)} %bitcast.78, f32[5,1024]{1,0:T(8,128)} %copy-done.21, f32[1024,2]{1,0:T(8,128)} %copy.27.column_ref, f32[64,1024]{1,0:T(8,128)} %pad_maximum_fusion.1.block_ref), custom_call_target="tpu_custom_call" | custom-call | flops 226492416 | bytes 2097152 | tf_op jit(solution)/shard_map/sort_region/pallas_call | solution.py:159
  12.2 0.7 slice.44
  12.9 1.4 fusion.10
  15.2 2.6 %collective-permute-start.9 = (bf16[1,64,512]{2,1,0:T(8,128)(2,1)}, bf16[1,64,512]{2,1,0:T(8,128)(2,1)S(1)}, u32[]{:S(2)}, u32[]{:S(2)}) collective-permute-start(bf16[1,64,512]{2,1,0:T(8,128)(2,1)} %bitcast.55), channel_id=1, source_target_pairs={{0,2},{2,0},{4,6},{6,4},{8,10},{10,8},{12,14},{14,12},{16,18},{18,... | collective-permute-start | bytes 196616 | tf_op jit(solution)/shard_map/ppermute | solution.py:84
  17.7 0.8 collective-permute-start.3
  18.5 3.0 %collective-permute-done.3 = f32[1,2,4,512]{3,2,1,0:T(4,128)S(1)} collective-permute-done((f32[1,2,4,512]{3,2,1,0:T(4,128)S(1)}, f32[1,2,4,512]{3,2,1,0:T(4,128)S(1)}, u32[]{:S(2)}, u32[]{:S(2)}) %collective-permute-start.3) | collective-permute-done | bytes 16416 | tf_op jit(solution)/shard_map/ppermute | solution.py:84
  21.6 1.6 collective-permute-start.4
  23.1 2.4 %collective-permute-done.4 = f32[2,2,4,512]{3,2,1,0:T(4,128)S(1)} collective-permute-done((f32[2,2,4,512]{3,2,1,0:T(4,128)S(1)}, f32[2,2,4,512]{3,2,1,0:T(4,128)S(1)}, u32[]{:S(2)}, u32[]{:S(2)}) %collective-permute-start.4) | collective-permute-done | bytes 32800 | tf_op jit(solution)/shard_map/ppermute | solution.py:84
  25.6 1.3 collective-permute-start.5
  26.9 4.5 %collective-permute-start.6 = (f32[4,2,4,512]{3,2,1,0:T(4,128)S(1)}, f32[4,2,4,512]{3,2,1,0:T(4,128)S(1)}, u32[]{:S(2)}, u32[]{:S(2)}) collective-permute-start(f32[4,2,4,512]{3,2,1,0:T(4,128)S(1)} %pad_maximum_fusion.6), channel_id=1, source_target_pairs={{0,8},{2,10},{4,12},{6,14},{8,16},{10,18},{12,20},{14,22},{16,24},... | collective-permute-start | bytes 196616 | tf_op jit(solution)/shard_map/ppermute | solution.py:61
  31.4 1.3 collective-permute-start.7
  32.7 5.4 %collective-permute-start.8 = (f32[2,2,4,512]{3,2,1,0:T(4,128)S(1)}, f32[2,2,4,512]{3,2,1,0:T(4,128)S(1)}, u32[]{:S(2)}, u32[]{:S(2)}) collective-permute-start(f32[2,2,4,512]{3,2,1,0:T(4,128)S(1)} %get-tuple-element.34), channel_id=1, source_target_pairs={{0,16},{2,18},{4,20},{6,22},{8,24},{10,26},{12,28},{14,30},{1,17},... | collective-permute-start | bytes 98312 | tf_op jit(solution)/shard_map/ppermute | solution.py:61
  38.2 0.9 pad_maximum_fusion.4
  39.1 1.6 collective-permute-start.10
  42.2 1.9 %collective-permute-done.10 = bf16[2,64,512]{2,1,0:T(8,128)(2,1)S(1)} collective-permute-done((bf16[2,64,512]{2,1,0:T(8,128)(2,1)S(1)}, bf16[2,64,512]{2,1,0:T(8,128)(2,1)S(1)}, u32[]{:S(2)}, u32[]{:S(2)}) %collective-permute-start.10) | collective-permute-done | bytes 131104 | tf_op jit(solution)/shard_map/ppermute | solution.py:84
  44.1 0.9 pad_maximum_fusion.2
  45.0 1.3 collective-permute-start.12
  46.3 4.6 %collective-permute-start.14 = (bf16[4,64,512]{2,1,0:T(8,128)(2,1)S(1)}, bf16[4,64,512]{2,1,0:T(8,128)(2,1)S(1)}, u32[]{:S(2)}, u32[]{:S(2)}) collective-permute-start(bf16[4,64,512]{2,1,0:T(8,128)(2,1)S(1)} %get-tuple-element.30), channel_id=1, source_target_pairs={{0,8},{2,10},{4,12},{6,14},{8,16},{10,18},{12,20},{14,22},{16,24},... | collective-permute-start | bytes 786440 | tf_op jit(solution)/shard_map/ppermute | solution.py:61
  50.9 1.3 collective-permute-start.16
  52.2 5.5 %collective-permute-start.18 = (bf16[2,64,512]{2,1,0:T(8,128)(2,1)S(1)}, bf16[2,64,512]{2,1,0:T(8,128)(2,1)S(1)}, u32[]{:S(2)}, u32[]{:S(2)}) collective-permute-start(bf16[2,64,512]{2,1,0:T(8,128)(2,1)S(1)} %get-tuple-element.28), channel_id=1, source_target_pairs={{0,16},{2,18},{4,20},{6,22},{8,24},{10,26},{12,28},{14,30},{1,17},... | collective-permute-start | bytes 393224 | tf_op jit(solution)/shard_map/ppermute | solution.py:61
  58.4 1.7 collective-permute-done.16
  60.7 0.7 sub.55.ids_ref
  61.4 0.6 pad_add_fusion.plan_ref
  62.0 7.8 %build_tiles.1.tiles_ref = bf16[208,64,512]{2,1,0:T(8,128)(2,1)} custom-call(s32[832]{0:T(1024)} %sub.55.ids_ref, s32[16]{0:T(128)} %pad_add_fusion.plan_ref, f32[5,512]{1,0:T(8,128)} %get-tuple-element.11.own_ref, f32[32,4,512]{2,1,0:T(4,128)} %bitcast.44), custom_call_target="tpu_custom_call" | custom-call | flops 31457280 | bytes 2097152 | tf_op jit(solution)/shard_map/build_tiles/pallas_call | solution.py:289
  70.8 7.4 %apply_tiles.2 = (f32[64,512]{1,0:T(8,128)}, bf16[64,512]{1,0:T(8,128)(2,1)}, f32[3,64,64]{2,1,0:T(8,128)}) custom-call(s32[832]{0:T(1024)} %sub.55.ids_ref, s32[16]{0:T(128)} %pad_add_fusion.plan_ref, bf16[208,64,512]{2,1,0:T(8,128)(2,1)} %build_tiles.1.tiles_ref, bf16[1,4,64,512]{3,2,1,0:T(8,128)(2,1)} %copy-done.2, bf16[1,4,64,512]{3,2,1,0:T(8,128)(2,1)} %copy-done.7, ...), custom_call_target="tpu_custom_call" | custom-call | flops 100663296 | bytes 2097152 | tf_op jit(solution)/shard_map/apply_tiles/pallas_call | solution.py:400
  78.2 1.3 collective-permute-start.25
  79.4 3.3 %collective-permute-done.25 = bf16[1,64,512]{2,1,0:T(8,128)(2,1)S(1)} collective-permute-done((bf16[1,64,512]{2,1,0:T(8,128)(2,1)}, bf16[1,64,512]{2,1,0:T(8,128)(2,1)S(1)}, u32[]{:S(2)}, u32[]{:S(2)}) %collective-permute-start.25) | collective-permute-done | bytes 65568 | tf_op jit(solution)/shard_map/ppermute | solution.py:84
  82.7 0.9 pad_maximum_fusion.5
  83.6 5.1 %collective-permute-start.26 = (bf16[2,64,512]{2,1,0:T(8,128)(2,1)S(1)}, bf16[2,64,512]{2,1,0:T(8,128)(2,1)S(1)}, u32[]{:S(2)}, u32[]{:S(2)}) collective-permute-start(bf16[2,64,512]{2,1,0:T(8,128)(2,1)S(1)} %pad_maximum_fusion.5), channel_id=1, source_target_pairs={{0,4},{2,6},{4,0},{6,2},{8,12},{10,14},{12,8},{14,10},{16,20},{18,... | collective-permute-start | bytes 393224 | tf_op jit(solution)/shard_map/ppermute | solution.py:84
  88.6 3.8 %collective-permute-done.26 = bf16[2,64,512]{2,1,0:T(8,128)(2,1)S(1)} collective-permute-done((bf16[2,64,512]{2,1,0:T(8,128)(2,1)S(1)}, bf16[2,64,512]{2,1,0:T(8,128)(2,1)S(1)}, u32[]{:S(2)}, u32[]{:S(2)}) %collective-permute-start.26) | collective-permute-done | bytes 131104 | tf_op jit(solution)/shard_map/ppermute | solution.py:84
  92.4 0.9 pad_maximum_fusion.3
  93.3 1.3 collective-permute-start.28
  94.6 8.3 %collective-permute-start.30 = (bf16[4,64,512]{2,1,0:T(8,128)(2,1)S(1)}, bf16[4,64,512]{2,1,0:T(8,128)(2,1)S(1)}, u32[]{:S(2)}, u32[]{:S(2)}) collective-permute-start(bf16[4,64,512]{2,1,0:T(8,128)(2,1)S(1)} %get-tuple-element.26), channel_id=1, source_target_pairs={{0,8},{2,10},{4,12},{6,14},{8,16},{10,18},{12,20},{14,22},{16,24},... | collective-permute-start | bytes 786440 | tf_op jit(solution)/shard_map/ppermute | solution.py:61
  103.0 1.5 collective-permute-done.20
  104.5 0.9 add.199
  105.4 0.8 collective-permute-start.21
  106.2 4.1 %collective-permute-done.21 = f32[3,64,64]{2,1,0:T(8,128)S(1)} collective-permute-done((f32[3,64,64]{2,1,0:T(8,128)S(1)}, f32[3,64,64]{2,1,0:T(8,128)S(1)}, u32[]{:S(2)}, u32[]{:S(2)}) %collective-permute-start.21) | collective-permute-done | bytes 49184 | tf_op jit(solution)/shard_map/ppermute | solution.py:102
  110.4 1.8 %collective-permute-start.22 = (f32[3,64,64]{2,1,0:T(8,128)S(1)}, f32[3,64,64]{2,1,0:T(8,128)S(1)}, u32[]{:S(2)}, u32[]{:S(2)}) collective-permute-start(f32[3,64,64]{2,1,0:T(8,128)S(1)} %add.200), channel_id=1, source_target_pairs={{0,4},{2,6},{4,0},{6,2},{8,12},{10,14},{12,8},{14,10},{16,20},{18,... | collective-permute-start | bytes 147464 | tf_op jit(solution)/shard_map/ppermute | solution.py:102
  112.2 1.3 collective-permute-start.32
  113.5 5.5 %collective-permute-start.34 = (bf16[2,64,512]{2,1,0:T(8,128)(2,1)S(1)}, bf16[2,64,512]{2,1,0:T(8,128)(2,1)S(1)}, u32[]{:S(2)}, u32[]{:S(2)}) collective-permute-start(bf16[2,64,512]{2,1,0:T(8,128)(2,1)S(1)} %get-tuple-element.24), channel_id=1, source_target_pairs={{0,16},{2,18},{4,20},{6,22},{8,24},{10,26},{12,28},{14,30},{1,17},... | collective-permute-start | bytes 393224 | tf_op jit(solution)/shard_map/ppermute | solution.py:61
  119.6 2.6 %collective-permute-done.32 = bf16[2,64,512]{2,1,0:T(8,128)(2,1)S(1)} collective-permute-done((bf16[2,64,512]{2,1,0:T(8,128)(2,1)S(1)}, bf16[2,64,512]{2,1,0:T(8,128)(2,1)S(1)}, u32[]{:S(2)}, u32[]{:S(2)}) %collective-permute-start.32) | collective-permute-done | bytes 131104 | tf_op jit(solution)/shard_map/ppermute | solution.py:61
  122.8 0.9 constant_dynamic-update-slice_fusion.8
  123.7 2.2 %collective-permute-start.23 = (f32[3,64,64]{2,1,0:T(8,128)S(1)}, f32[3,64,64]{2,1,0:T(8,128)S(1)}, u32[]{:S(2)}, u32[]{:S(2)}) collective-permute-start(f32[3,64,64]{2,1,0:T(8,128)S(1)} %add.201), channel_id=1, source_target_pairs={{0,8},{2,10},{4,12},{6,14},{8,0},{10,2},{12,4},{14,6},{16,24},{18,... | collective-permute-start | bytes 147464 | tf_op jit(solution)/shard_map/ppermute | solution.py:102
  126.8 0.7 copy-done.12
  127.5 7.3 %apply_tiles.3 = (f32[64,512]{1,0:T(8,128)}, bf16[64,512]{1,0:T(8,128)(2,1)}, f32[1,64,64]{2,1,0:T(8,128)}) custom-call(s32[832]{0:T(1024)} %sub.55.ids_ref, s32[16]{0:T(128)} %pad_add_fusion.plan_ref, bf16[208,64,512]{2,1,0:T(8,128)(2,1)} %build_tiles.1.tiles_ref, bf16[1,4,64,512]{3,2,1,0:T(8,128)(2,1)} %copy-done.1, bf16[1,4,64,512]{3,2,1,0:T(8,128)(2,1)} %copy-done.8, ...), custom_call_target="tpu_custom_call" | custom-call | flops 100663296 | bytes 2097152 | tf_op jit(solution)/shard_map/apply_tiles/pallas_call | solution.py:400
  135.0 0.9 constant_dynamic-update-slice_fusion.7
  136.3 0.8 bitcast_add_fusion
  137.1 0.7 collective-permute-start.37
  137.9 3.2 %collective-permute-done.37 = f32[64,64]{1,0:T(8,128)S(1)} collective-permute-done((f32[64,64]{1,0:T(8,128)S(1)}, f32[64,64]{1,0:T(8,128)S(1)}, u32[]{:S(2)}, u32[]{:S(2)}) %collective-permute-start.37) | collective-permute-done | bytes 16416 | tf_op jit(solution)/shard_map/ppermute | solution.py:102
  141.0 1.6 collective-permute-start.38
  142.6 4.8 %collective-permute-start.24 = (f32[3,64,64]{2,1,0:T(8,128)S(1)}, f32[3,64,64]{2,1,0:T(8,128)S(1)}, u32[]{:S(2)}, u32[]{:S(2)}) collective-permute-start(f32[3,64,64]{2,1,0:T(8,128)S(1)} %add.202), channel_id=1, source_target_pairs={{0,16},{2,18},{4,20},{6,22},{8,24},{10,26},{12,28},{14,30},{16,0},... | collective-permute-start | bytes 147464 | tf_op jit(solution)/shard_map/ppermute | solution.py:102
  147.9 3.5 %collective-permute-done.39 = f32[64,64]{1,0:T(8,128)S(1)} collective-permute-done((f32[64,64]{1,0:T(8,128)S(1)}, f32[64,64]{1,0:T(8,128)S(1)}, u32[]{:S(2)}, u32[]{:S(2)}) %collective-permute-start.39) | collective-permute-done | bytes 16416 | tf_op jit(solution)/shard_map/ppermute | solution.py:102
  151.4 3.5 %collective-permute-start.40 = (f32[64,64]{1,0:T(8,128)S(1)}, f32[64,64]{1,0:T(8,128)S(1)}, u32[]{:S(2)}, u32[]{:S(2)}) collective-permute-start(f32[64,64]{1,0:T(8,128)S(1)} %add.207), channel_id=1, source_target_pairs={{0,16},{2,18},{4,20},{6,22},{8,24},{10,26},{12,28},{14,30},{16,0},... | collective-permute-start | bytes 49160 | tf_op jit(solution)/shard_map/ppermute | solution.py:102
  155.0 0.7 add.203.grams_ref
  155.6 8.2 %first_step.1.first_ref = f32[4,64,64]{2,1,0:T(8,128)} custom-call(f32[3,64,64]{2,1,0:T(8,128)} %add.203.grams_ref), custom_call_target="tpu_custom_call" | custom-call | tf_op jit(solution)/shard_map/first_step/pallas_call | solution.py:495
  163.8 0.6 add.208.cross_ref
  164.4 0.9 pad_maximum_fusion.block_ref
  165.3 2.6 %unsort.1.images_ref = f32[128,512]{1,0:T(8,128)} custom-call(s32[2]{0:T(128)} %copy-done.22, s32[1,512]{1,0:T(1,128)} %get-tuple-element.18.rank_ref, f32[128,1024]{1,0:T(8,128)} %pad_maximum_fusion.block_ref), custom_call_target="tpu_custom_call" | custom-call | flops 402653184 | bytes 2097152 | tf_op jit(solution)/shard_map/unsort/pallas_call | solution.py:188
  167.9 5.8 %last_step.1 = (f32[64,512]{1,0:T(8,128)}, f32[64,512]{1,0:T(8,128)}) custom-call(f32[4,64,64]{2,1,0:T(8,128)} %first_step.1.first_ref, f32[64,64]{1,0:T(8,128)} %add.208.cross_ref, f32[64,512]{1,0:T(8,128)} %start_ref.1, f32[128,512]{1,0:T(8,128)} %unsort.1.images_ref), custom_call_target="tpu_custom_call" | custom-call | tf_op jit(solution)/shard_map/last_step/pallas_call | solution.py:517
  (151 shorter events, 8.6 us)
Async XLA Ops:
  0.6 5.8 %copy-start.22 = (s32[2]{0:T(128)}, s32[2]{0:T(128)S(1)}, u32[]{:S(2)}) copy-start(s32[2]{0:T(128)S(1)} %xor_multiply_fusion.first_ref) | copy-start | bytes 28
  1.4 1.5 collective-permute-start
  1.9 2.9 %collective-permute-start.1 = (f32[64,512]{1,0:T(8,128)}, f32[64,512]{1,0:T(8,128)S(1)}, u32[]{:S(2)}, u32[]{:S(2)}) collective-permute-start(f32[64,512]{1,0:T(8,128)} %start_ref.1), channel_id=1, source_target_pairs={{0,1},{1,0},{2,3},{3,2},{4,5},{5,4},{6,7},{7,6},{8,9},{9,8},{10,11... | collective-permute-start | bytes 393224 | tf_op jit(solution)/shard_map/ppermute | solution.py:53
  3.7 2.7 %copy-start.21 = (f32[5,1024]{1,0:T(8,128)}, f32[5,1024]{1,0:T(8,128)S(1)}, u32[]{:S(2)}) copy-start(f32[5,1024]{1,0:T(8,128)S(1)} %pad_maximum_fusion.7.places_ref) | copy-start | bytes 61444
  14.3 3.4 %collective-permute-start.2 = (f32[1,4,512]{2,1,0:T(4,128)S(1)}, f32[1,4,512]{2,1,0:T(4,128)S(1)}, u32[]{:S(2)}, u32[]{:S(2)}) collective-permute-start(f32[1,4,512]{2,1,0:T(4,128)S(1)} %maximum_bitcast_fusion.1), channel_id=1, source_target_pairs={{0,1},{1,0},{2,3},{3,2},{4,5},{5,4},{6,7},{7,6},{8,9},{9,8},{10,11... | collective-permute-start | bytes 24584 | tf_op jit(solution)/shard_map/ppermute | solution.py:53
  15.2 23.0 %collective-permute-start.9 = (bf16[1,64,512]{2,1,0:T(8,128)(2,1)}, bf16[1,64,512]{2,1,0:T(8,128)(2,1)S(1)}, u32[]{:S(2)}, u32[]{:S(2)}) collective-permute-start(bf16[1,64,512]{2,1,0:T(8,128)(2,1)} %bitcast.55), channel_id=1, source_target_pairs={{0,2},{2,0},{4,6},{6,4},{8,10},{10,8},{12,14},{14,12},{16,18},{18,... | collective-permute-start | bytes 196616 | tf_op jit(solution)/shard_map/ppermute | solution.py:84
  17.7 3.8 %collective-permute-start.3 = (f32[1,2,4,512]{3,2,1,0:T(4,128)S(1)}, f32[1,2,4,512]{3,2,1,0:T(4,128)S(1)}, u32[]{:S(2)}, u32[]{:S(2)}) collective-permute-start(f32[1,2,4,512]{3,2,1,0:T(4,128)S(1)} %maximum_bitcast_fusion), channel_id=1, source_target_pairs={{0,2},{2,0},{4,6},{6,4},{8,10},{10,8},{12,14},{14,12},{16,18},{18,... | collective-permute-start | bytes 49160 | tf_op jit(solution)/shard_map/ppermute | solution.py:84
  21.6 4.0 %collective-permute-start.4 = (f32[2,2,4,512]{3,2,1,0:T(4,128)S(1)}, f32[2,2,4,512]{3,2,1,0:T(4,128)S(1)}, u32[]{:S(2)}, u32[]{:S(2)}) collective-permute-start(f32[2,2,4,512]{3,2,1,0:T(4,128)S(1)} %pad_maximum_fusion.8), channel_id=1, source_target_pairs={{0,4},{2,6},{4,0},{6,2},{8,12},{10,14},{12,8},{14,10},{16,20},{18,... | collective-permute-start | bytes 98312 | tf_op jit(solution)/shard_map/ppermute | solution.py:84
  25.6 15.1 %collective-permute-start.5 = (f32[4,2,4,512]{3,2,1,0:T(4,128)S(1)}, f32[4,2,4,512]{3,2,1,0:T(4,128)S(1)}, u32[]{:S(2)}, u32[]{:S(2)}) collective-permute-start(f32[4,2,4,512]{3,2,1,0:T(4,128)S(1)} %pad_maximum_fusion.6), channel_id=1, source_target_pairs={{8,0},{10,2},{12,4},{14,6},{16,8},{18,10},{20,12},{22,14},{24,16},... | collective-permute-start | bytes 196616 | tf_op jit(solution)/shard_map/ppermute | solution.py:61
  26.9 13.8 %collective-permute-start.6 = (f32[4,2,4,512]{3,2,1,0:T(4,128)S(1)}, f32[4,2,4,512]{3,2,1,0:T(4,128)S(1)}, u32[]{:S(2)}, u32[]{:S(2)}) collective-permute-start(f32[4,2,4,512]{3,2,1,0:T(4,128)S(1)} %pad_maximum_fusion.6), channel_id=1, source_target_pairs={{0,8},{2,10},{4,12},{6,14},{8,16},{10,18},{12,20},{14,22},{16,24},... | collective-permute-start | bytes 196616 | tf_op jit(solution)/shard_map/ppermute | solution.py:61
  31.4 9.3 %collective-permute-start.7 = (f32[2,2,4,512]{3,2,1,0:T(4,128)S(1)}, f32[2,2,4,512]{3,2,1,0:T(4,128)S(1)}, u32[]{:S(2)}, u32[]{:S(2)}) collective-permute-start(f32[2,2,4,512]{3,2,1,0:T(4,128)S(1)} %get-tuple-element.35), channel_id=1, source_target_pairs={{16,0},{18,2},{20,4},{22,6},{24,8},{26,10},{28,12},{30,14},{17,1},... | collective-permute-start | bytes 98312 | tf_op jit(solution)/shard_map/ppermute | solution.py:61
  32.7 8.0 %collective-permute-start.8 = (f32[2,2,4,512]{3,2,1,0:T(4,128)S(1)}, f32[2,2,4,512]{3,2,1,0:T(4,128)S(1)}, u32[]{:S(2)}, u32[]{:S(2)}) collective-permute-start(f32[2,2,4,512]{3,2,1,0:T(4,128)S(1)} %get-tuple-element.34), channel_id=1, source_target_pairs={{0,16},{2,18},{4,20},{6,22},{8,24},{10,26},{12,28},{14,30},{1,17},... | collective-permute-start | bytes 98312 | tf_op jit(solution)/shard_map/ppermute | solution.py:61
  39.1 5.0 %collective-permute-start.10 = (bf16[2,64,512]{2,1,0:T(8,128)(2,1)S(1)}, bf16[2,64,512]{2,1,0:T(8,128)(2,1)S(1)}, u32[]{:S(2)}, u32[]{:S(2)}) collective-permute-start(bf16[2,64,512]{2,1,0:T(8,128)(2,1)S(1)} %pad_maximum_fusion.4), channel_id=1, source_target_pairs={{0,4},{2,6},{4,0},{6,2},{8,12},{10,14},{12,8},{14,10},{16,20},{18,... | collective-permute-start | bytes 393224 | tf_op jit(solution)/shard_map/ppermute | solution.py:84
  40.8 21.2 %copy-start = (f32[2,16,4,512]{3,2,1,0:T(4,128)}, f32[2,16,4,512]{3,2,1,0:T(4,128)S(1)}, u32[]{:S(2)}) copy-start(f32[2,16,4,512]{3,2,1,0:T(4,128)S(1)} %copy.28) | copy-start | bytes 786436
  45.0 24.9 %copy-start.2 = (bf16[1,4,64,512]{3,2,1,0:T(8,128)(2,1)}, bf16[1,4,64,512]{3,2,1,0:T(8,128)(2,1)S(1)}, u32[]{:S(2)}) copy-start(bf16[1,4,64,512]{3,2,1,0:T(8,128)(2,1)S(1)} %get-tuple-element.31.refs_0_) | copy-start | bytes 786436
  45.0 12.8 %collective-permute-start.12 = (bf16[4,64,512]{2,1,0:T(8,128)(2,1)S(1)}, bf16[4,64,512]{2,1,0:T(8,128)(2,1)S(1)}, u32[]{:S(2)}, u32[]{:S(2)}) collective-permute-start(bf16[4,64,512]{2,1,0:T(8,128)(2,1)S(1)} %get-tuple-element.30), channel_id=1, source_target_pairs={{8,0},{10,2},{12,4},{14,6},{16,8},{18,10},{20,12},{22,14},{24,16},... | collective-permute-start | bytes 786440 | tf_op jit(solution)/shard_map/ppermute | solution.py:61
  46.3 12.0 %collective-permute-start.14 = (bf16[4,64,512]{2,1,0:T(8,128)(2,1)S(1)}, bf16[4,64,512]{2,1,0:T(8,128)(2,1)S(1)}, u32[]{:S(2)}, u32[]{:S(2)}) collective-permute-start(bf16[4,64,512]{2,1,0:T(8,128)(2,1)S(1)} %get-tuple-element.30), channel_id=1, source_target_pairs={{0,8},{2,10},{4,12},{6,14},{8,16},{10,18},{12,20},{14,22},{16,24},... | collective-permute-start | bytes 786440 | tf_op jit(solution)/shard_map/ppermute | solution.py:61
  50.9 9.2 %collective-permute-start.16 = (bf16[2,64,512]{2,1,0:T(8,128)(2,1)S(1)}, bf16[2,64,512]{2,1,0:T(8,128)(2,1)S(1)}, u32[]{:S(2)}, u32[]{:S(2)}) collective-permute-start(bf16[2,64,512]{2,1,0:T(8,128)(2,1)S(1)} %get-tuple-element.29), channel_id=1, source_target_pairs={{16,0},{18,2},{20,4},{22,6},{24,8},{26,10},{28,12},{30,14},{17,1},... | collective-permute-start | bytes 393224 | tf_op jit(solution)/shard_map/ppermute | solution.py:61
  52.2 8.0 %collective-permute-start.18 = (bf16[2,64,512]{2,1,0:T(8,128)(2,1)S(1)}, bf16[2,64,512]{2,1,0:T(8,128)(2,1)S(1)}, u32[]{:S(2)}, u32[]{:S(2)}) collective-permute-start(bf16[2,64,512]{2,1,0:T(8,128)(2,1)S(1)} %get-tuple-element.28), channel_id=1, source_target_pairs={{0,16},{2,18},{4,20},{6,22},{8,24},{10,26},{12,28},{14,30},{1,17},... | collective-permute-start | bytes 393224 | tf_op jit(solution)/shard_map/ppermute | solution.py:61
  57.7 12.1 %collective-permute-start.11 = (bf16[1,4,64,512]{3,2,1,0:T(8,128)(2,1)S(1)}, bf16[1,4,64,512]{3,2,1,0:T(8,128)(2,1)S(1)}, u32[]{:S(2)}, u32[]{:S(2)}) collective-permute-start(bf16[1,4,64,512]{3,2,1,0:T(8,128)(2,1)S(1)} %get-tuple-element.31.refs_0_), channel_id=1, source_target_pairs={{0,1},{1,0},{2,3},{3,2},{4,5},{5,4},{6,7},{7,6},{8,9},{9,8},{10,11... | collective-permute-start | bytes 786440 | tf_op jit(solution)/shard_map/ppermute | solution.py:570
  57.8 12.1 %copy-start.5 = (bf16[4,64,512]{2,1,0:T(8,128)(2,1)}, bf16[4,64,512]{2,1,0:T(8,128)(2,1)S(1)}, u32[]{:S(2)}) copy-start(bf16[4,64,512]{2,1,0:T(8,128)(2,1)S(1)} %collective-permute-done.12) | copy-start | bytes 786436
  57.8 12.1 %collective-permute-start.13 = (bf16[1,4,64,512]{3,2,1,0:T(8,128)(2,1)S(1)}, bf16[1,4,64,512]{3,2,1,0:T(8,128)(2,1)S(1)}, u32[]{:S(2)}, u32[]{:S(2)}) collective-permute-start(bf16[1,4,64,512]{3,2,1,0:T(8,128)(2,1)S(1)} %bitcast.51), channel_id=1, source_target_pairs={{0,1},{1,0},{2,3},{3,2},{4,5},{5,4},{6,7},{7,6},{8,9},{9,8},{10,11... | collective-permute-start | bytes 786440 | tf_op jit(solution)/shard_map/ppermute | solution.py:570
  58.3 11.7 %copy-start.6 = (bf16[4,64,512]{2,1,0:T(8,128)(2,1)}, bf16[4,64,512]{2,1,0:T(8,128)(2,1)S(1)}, u32[]{:S(2)}) copy-start(bf16[4,64,512]{2,1,0:T(8,128)(2,1)S(1)} %collective-permute-done.14) | copy-start | bytes 786436
  58.3 11.6 %collective-permute-start.15 = (bf16[1,4,64,512]{3,2,1,0:T(8,128)(2,1)S(1)}, bf16[1,4,64,512]{3,2,1,0:T(8,128)(2,1)S(1)}, u32[]{:S(2)}, u32[]{:S(2)}) collective-permute-start(bf16[1,4,64,512]{3,2,1,0:T(8,128)(2,1)S(1)} %bitcast.53), channel_id=1, source_target_pairs={{0,1},{1,0},{2,3},{3,2},{4,5},{5,4},{6,7},{7,6},{8,9},{9,8},{10,11... | collective-permute-start | bytes 786440 | tf_op jit(solution)/shard_map/ppermute | solution.py:570
  60.1 9.9 %copy-start.14 = (bf16[2,64,512]{2,1,0:T(8,128)(2,1)}, bf16[2,64,512]{2,1,0:T(8,128)(2,1)S(1)}, u32[]{:S(2)}) copy-start(bf16[2,64,512]{2,1,0:T(8,128)(2,1)S(1)} %collective-permute-done.16) | copy-start | bytes 393220
  60.1 9.7 %collective-permute-start.17 = (bf16[1,2,64,512]{3,2,1,0:T(8,128)(2,1)S(1)}, bf16[1,2,64,512]{3,2,1,0:T(8,128)(2,1)S(1)}, u32[]{:S(2)}, u32[]{:S(2)}) collective-permute-start(bf16[1,2,64,512]{3,2,1,0:T(8,128)(2,1)S(1)} %bitcast.63), channel_id=1, source_target_pairs={{0,1},{1,0},{2,3},{3,2},{4,5},{5,4},{6,7},{7,6},{8,9},{9,8},{10,11... | collective-permute-start | bytes 393224 | tf_op jit(solution)/shard_map/ppermute | solution.py:570
  60.2 9.8 %copy-start.16 = (bf16[2,64,512]{2,1,0:T(8,128)(2,1)}, bf16[2,64,512]{2,1,0:T(8,128)(2,1)S(1)}, u32[]{:S(2)}) copy-start(bf16[2,64,512]{2,1,0:T(8,128)(2,1)S(1)} %collective-permute-done.18) | copy-start | bytes 393220
  60.2 9.7 %collective-permute-start.19 = (bf16[1,2,64,512]{3,2,1,0:T(8,128)(2,1)S(1)}, bf16[1,2,64,512]{3,2,1,0:T(8,128)(2,1)S(1)}, u32[]{:S(2)}, u32[]{:S(2)}) collective-permute-start(bf16[1,2,64,512]{3,2,1,0:T(8,128)(2,1)S(1)} %bitcast.67), channel_id=1, source_target_pairs={{0,1},{1,0},{2,3},{3,2},{4,5},{5,4},{6,7},{7,6},{8,9},{9,8},{10,11... | collective-permute-start | bytes 393224 | tf_op jit(solution)/shard_map/ppermute | solution.py:570
  69.8 0.7 copy-start.7
  69.8 0.7 copy-start.18
  69.8 0.7 copy-start.20
  69.9 0.8 copy-start.9
  69.9 0.9 copy-start.11
  78.2 4.5 %collective-permute-start.25 = (bf16[1,64,512]{2,1,0:T(8,128)(2,1)}, bf16[1,64,512]{2,1,0:T(8,128)(2,1)S(1)}, u32[]{:S(2)}, u32[]{:S(2)}) collective-permute-start(bf16[1,64,512]{2,1,0:T(8,128)(2,1)} %bitcast.58), channel_id=1, source_target_pairs={{0,2},{2,0},{4,6},{6,4},{8,10},{10,8},{12,14},{14,12},{16,18},{18,... | collective-permute-start | bytes 196616 | tf_op jit(solution)/shard_map/ppermute | solution.py:84
  83.6 8.8 %collective-permute-start.26 = (bf16[2,64,512]{2,1,0:T(8,128)(2,1)S(1)}, bf16[2,64,512]{2,1,0:T(8,128)(2,1)S(1)}, u32[]{:S(2)}, u32[]{:S(2)}) collective-permute-start(bf16[2,64,512]{2,1,0:T(8,128)(2,1)S(1)} %pad_maximum_fusion.5), channel_id=1, source_target_pairs={{0,4},{2,6},{4,0},{6,2},{8,12},{10,14},{12,8},{14,10},{16,20},{18,... | collective-permute-start | bytes 393224 | tf_op jit(solution)/shard_map/ppermute | solution.py:84
  93.3 32.7 %copy-start.1 = (bf16[1,4,64,512]{3,2,1,0:T(8,128)(2,1)}, bf16[1,4,64,512]{3,2,1,0:T(8,128)(2,1)S(1)}, u32[]{:S(2)}) copy-start(bf16[1,4,64,512]{3,2,1,0:T(8,128)(2,1)S(1)} %get-tuple-element.27.refs_0_) | copy-start | bytes 786436
  93.3 25.7 %collective-permute-start.28 = (bf16[4,64,512]{2,1,0:T(8,128)(2,1)S(1)}, bf16[4,64,512]{2,1,0:T(8,128)(2,1)S(1)}, u32[]{:S(2)}, u32[]{:S(2)}) collective-permute-start(bf16[4,64,512]{2,1,0:T(8,128)(2,1)S(1)} %get-tuple-element.26), channel_id=1, source_target_pairs={{8,0},{10,2},{12,4},{14,6},{16,8},{18,10},{20,12},{22,14},{24,16},... | collective-permute-start | bytes 786440 | tf_op jit(solution)/shard_map/ppermute | solution.py:61
  94.6 24.9 %collective-permute-start.30 = (bf16[4,64,512]{2,1,0:T(8,128)(2,1)S(1)}, bf16[4,64,512]{2,1,0:T(8,128)(2,1)S(1)}, u32[]{:S(2)}, u32[]{:S(2)}) collective-permute-start(bf16[4,64,512]{2,1,0:T(8,128)(2,1)S(1)} %get-tuple-element.26), channel_id=1, source_target_pairs={{0,8},{2,10},{4,12},{6,14},{8,16},{10,18},{12,20},{14,22},{16,24},... | collective-permute-start | bytes 786440 | tf_op jit(solution)/shard_map/ppermute | solution.py:61
  102.9 1.6 collective-permute-start.20
  105.4 4.9 %collective-permute-start.21 = (f32[3,64,64]{2,1,0:T(8,128)S(1)}, f32[3,64,64]{2,1,0:T(8,128)S(1)}, u32[]{:S(2)}, u32[]{:S(2)}) collective-permute-start(f32[3,64,64]{2,1,0:T(8,128)S(1)} %add.199), channel_id=1, source_target_pairs={{0,2},{2,0},{4,6},{6,4},{8,10},{10,8},{12,14},{14,12},{16,18},{18,... | collective-permute-start | bytes 147464 | tf_op jit(solution)/shard_map/ppermute | solution.py:102
  110.4 8.6 %collective-permute-start.22 = (f32[3,64,64]{2,1,0:T(8,128)S(1)}, f32[3,64,64]{2,1,0:T(8,128)S(1)}, u32[]{:S(2)}, u32[]{:S(2)}) collective-permute-start(f32[3,64,64]{2,1,0:T(8,128)S(1)} %add.200), channel_id=1, source_target_pairs={{0,4},{2,6},{4,0},{6,2},{8,12},{10,14},{12,8},{14,10},{16,20},{18,... | collective-permute-start | bytes 147464 | tf_op jit(solution)/shard_map/ppermute | solution.py:102
  112.2 10.1 %collective-permute-start.32 = (bf16[2,64,512]{2,1,0:T(8,128)(2,1)S(1)}, bf16[2,64,512]{2,1,0:T(8,128)(2,1)S(1)}, u32[]{:S(2)}, u32[]{:S(2)}) collective-permute-start(bf16[2,64,512]{2,1,0:T(8,128)(2,1)S(1)} %get-tuple-element.25), channel_id=1, source_target_pairs={{16,0},{18,2},{20,4},{22,6},{24,8},{26,10},{28,12},{30,14},{17,1},... | collective-permute-start | bytes 393224 | tf_op jit(solution)/shard_map/ppermute | solution.py:61
  113.5 8.8 %collective-permute-start.34 = (bf16[2,64,512]{2,1,0:T(8,128)(2,1)S(1)}, bf16[2,64,512]{2,1,0:T(8,128)(2,1)S(1)}, u32[]{:S(2)}, u32[]{:S(2)}) collective-permute-start(bf16[2,64,512]{2,1,0:T(8,128)(2,1)S(1)} %get-tuple-element.24), channel_id=1, source_target_pairs={{0,16},{2,18},{4,20},{6,22},{8,24},{10,26},{12,28},{14,30},{1,17},... | collective-permute-start | bytes 393224 | tf_op jit(solution)/shard_map/ppermute | solution.py:61
  119.0 7.0 %collective-permute-start.27 = (bf16[1,4,64,512]{3,2,1,0:T(8,128)(2,1)S(1)}, bf16[1,4,64,512]{3,2,1,0:T(8,128)(2,1)S(1)}, u32[]{:S(2)}, u32[]{:S(2)}) collective-permute-start(bf16[1,4,64,512]{3,2,1,0:T(8,128)(2,1)S(1)} %get-tuple-element.27.refs_0_), channel_id=1, source_target_pairs={{0,1},{1,0},{2,3},{3,2},{4,5},{5,4},{6,7},{7,6},{8,9},{9,8},{10,11... | collective-permute-start | bytes 786440 | tf_op jit(solution)/shard_map/ppermute | solution.py:570
  119.0 7.0 %copy-start.3 = (bf16[4,64,512]{2,1,0:T(8,128)(2,1)}, bf16[4,64,512]{2,1,0:T(8,128)(2,1)S(1)}, u32[]{:S(2)}) copy-start(bf16[4,64,512]{2,1,0:T(8,128)(2,1)S(1)} %collective-permute-done.28) | copy-start | bytes 786436
  119.1 6.9 %collective-permute-start.29 = (bf16[1,4,64,512]{3,2,1,0:T(8,128)(2,1)S(1)}, bf16[1,4,64,512]{3,2,1,0:T(8,128)(2,1)S(1)}, u32[]{:S(2)}, u32[]{:S(2)}) collective-permute-start(bf16[1,4,64,512]{3,2,1,0:T(8,128)(2,1)S(1)} %bitcast.47), channel_id=1, source_target_pairs={{0,1},{1,0},{2,3},{3,2},{4,5},{5,4},{6,7},{7,6},{8,9},{9,8},{10,11... | collective-permute-start | bytes 786440 | tf_op jit(solution)/shard_map/ppermute | solution.py:570
  119.5 6.5 %copy-start.4 = (bf16[4,64,512]{2,1,0:T(8,128)(2,1)}, bf16[4,64,512]{2,1,0:T(8,128)(2,1)S(1)}, u32[]{:S(2)}) copy-start(bf16[4,64,512]{2,1,0:T(8,128)(2,1)S(1)} %collective-permute-done.30) | copy-start | bytes 786436
  119.5 6.5 %collective-permute-start.31 = (bf16[1,4,64,512]{3,2,1,0:T(8,128)(2,1)S(1)}, bf16[1,4,64,512]{3,2,1,0:T(8,128)(2,1)S(1)}, u32[]{:S(2)}, u32[]{:S(2)}) collective-permute-start(bf16[1,4,64,512]{3,2,1,0:T(8,128)(2,1)S(1)} %bitcast.49), channel_id=1, source_target_pairs={{0,1},{1,0},{2,3},{3,2},{4,5},{5,4},{6,7},{7,6},{8,9},{9,8},{10,11... | collective-permute-start | bytes 786440 | tf_op jit(solution)/shard_map/ppermute | solution.py:570
  122.3 3.8 %copy-start.13 = (bf16[2,64,512]{2,1,0:T(8,128)(2,1)}, bf16[2,64,512]{2,1,0:T(8,128)(2,1)S(1)}, u32[]{:S(2)}) copy-start(bf16[2,64,512]{2,1,0:T(8,128)(2,1)S(1)} %collective-permute-done.32) | copy-start | bytes 393220
  122.3 1.5 collective-permute-start.33
  122.3 3.8 %copy-start.15 = (bf16[2,64,512]{2,1,0:T(8,128)(2,1)}, bf16[2,64,512]{2,1,0:T(8,128)(2,1)S(1)}, u32[]{:S(2)}) copy-start(bf16[2,64,512]{2,1,0:T(8,128)(2,1)S(1)} %collective-permute-done.34) | copy-start | bytes 393220
  122.3 3.7 %collective-permute-start.35 = (bf16[1,2,64,512]{3,2,1,0:T(8,128)(2,1)S(1)}, bf16[1,2,64,512]{3,2,1,0:T(8,128)(2,1)S(1)}, u32[]{:S(2)}, u32[]{:S(2)}) collective-permute-start(bf16[1,2,64,512]{3,2,1,0:T(8,128)(2,1)S(1)} %bitcast.65), channel_id=1, source_target_pairs={{0,1},{1,0},{2,3},{3,2},{4,5},{5,4},{6,7},{7,6},{8,9},{9,8},{10,11... | collective-permute-start | bytes 393224 | tf_op jit(solution)/shard_map/ppermute | solution.py:570
  123.7 2.3 %copy-start.17 = (bf16[1,2,64,512]{3,2,1,0:T(8,128)(2,1)}, bf16[1,2,64,512]{3,2,1,0:T(8,128)(2,1)S(1)}, u32[]{:S(2)}) copy-start(bf16[1,2,64,512]{3,2,1,0:T(8,128)(2,1)S(1)} %collective-permute-done.33.refs_7_) | copy-start | bytes 393220
  123.7 14.1 %collective-permute-start.23 = (f32[3,64,64]{2,1,0:T(8,128)S(1)}, f32[3,64,64]{2,1,0:T(8,128)S(1)}, u32[]{:S(2)}, u32[]{:S(2)}) collective-permute-start(f32[3,64,64]{2,1,0:T(8,128)S(1)} %add.201), channel_id=1, source_target_pairs={{0,8},{2,10},{4,12},{6,14},{8,0},{10,2},{12,4},{14,6},{16,24},{18,... | collective-permute-start | bytes 147464 | tf_op jit(solution)/shard_map/ppermute | solution.py:102
  126.0 0.8 copy-start.8
  126.0 0.8 copy-start.10
  126.8 0.7 copy-start.12
  134.8 1.6 collective-permute-start.36
  135.9 28.5 %collective-permute-start.41 = (f32[128,512]{1,0:T(8,128)S(1)}, f32[128,512]{1,0:T(8,128)S(1)}, u32[]{:S(2)}, u32[]{:S(2)}) collective-permute-start(f32[128,512]{1,0:T(8,128)S(1)} %constant_dynamic-update-slice_fusion.7), channel_id=1, source_target_pairs={{0,1},{1,0},{2,3},{3,2},{4,5},{5,4},{6,7},{7,6},{8,9},{9,8},{10,11... | collective-permute-start | bytes 786440 | tf_op jit(solution)/shard_map/ppermute | solution.py:53
  137.1 3.9 %collective-permute-start.37 = (f32[64,64]{1,0:T(8,128)S(1)}, f32[64,64]{1,0:T(8,128)S(1)}, u32[]{:S(2)}, u32[]{:S(2)}) collective-permute-start(f32[64,64]{1,0:T(8,128)S(1)} %bitcast_add_fusion), channel_id=1, source_target_pairs={{0,2},{2,0},{4,6},{6,4},{8,10},{10,8},{12,14},{14,12},{16,18},{18,... | collective-permute-start | bytes 49160 | tf_op jit(solution)/shard_map/ppermute | solution.py:102
  141.0 6.4 %collective-permute-start.38 = (f32[64,64]{1,0:T(8,128)S(1)}, f32[64,64]{1,0:T(8,128)S(1)}, u32[]{:S(2)}, u32[]{:S(2)}) collective-permute-start(f32[64,64]{1,0:T(8,128)S(1)} %add.205), channel_id=1, source_target_pairs={{0,4},{2,6},{4,0},{6,2},{8,12},{10,14},{12,8},{14,10},{16,20},{18,... | collective-permute-start | bytes 49160 | tf_op jit(solution)/shard_map/ppermute | solution.py:102
  142.6 12.4 %collective-permute-start.24 = (f32[3,64,64]{2,1,0:T(8,128)S(1)}, f32[3,64,64]{2,1,0:T(8,128)S(1)}, u32[]{:S(2)}, u32[]{:S(2)}) collective-permute-start(f32[3,64,64]{2,1,0:T(8,128)S(1)} %add.202), channel_id=1, source_target_pairs={{0,16},{2,18},{4,20},{6,22},{8,24},{10,26},{12,28},{14,30},{16,0},... | collective-permute-start | bytes 147464 | tf_op jit(solution)/shard_map/ppermute | solution.py:102
  147.4 4.0 %collective-permute-start.39 = (f32[64,64]{1,0:T(8,128)S(1)}, f32[64,64]{1,0:T(8,128)S(1)}, u32[]{:S(2)}, u32[]{:S(2)}) collective-permute-start(f32[64,64]{1,0:T(8,128)S(1)} %add.206), channel_id=1, source_target_pairs={{0,8},{2,10},{4,12},{6,14},{8,0},{10,2},{12,4},{14,6},{16,24},{18,... | collective-permute-start | bytes 49160 | tf_op jit(solution)/shard_map/ppermute | solution.py:102
  151.4 12.4 %collective-permute-start.40 = (f32[64,64]{1,0:T(8,128)S(1)}, f32[64,64]{1,0:T(8,128)S(1)}, u32[]{:S(2)}, u32[]{:S(2)}) collective-permute-start(f32[64,64]{1,0:T(8,128)S(1)} %add.207), channel_id=1, source_target_pairs={{0,16},{2,18},{4,20},{6,22},{8,24},{10,26},{12,28},{14,30},{16,0},... | collective-permute-start | bytes 49160 | tf_op jit(solution)/shard_map/ppermute | solution.py:102
  (1 other events, 0.6 us)

commit v3 on v0

v3 whole, which is shorter than its diff:
```python
import functools

import jax
import jax.numpy as jnp
from jax import lax
from jax.experimental import pallas as pl
from jax.experimental.pallas import tpu as pltpu
from jax.sharding import PartitionSpec as P

CUTOFF = 1.001
LANES = 128
ROWS = 64
BATCH = 4
UNROLL = 4
RING = 8
VMEM = 48 * 1024 * 1024
EXTRA = 16
HIGHEST = lax.Precision.HIGHEST


def whole_vmem(count):
    return [pl.BlockSpec(memory_space=pltpu.VMEM)] * count


def dot_nt(left, right, precision=None):
    return lax.dot_general(
        left, right, (((1,), (1,)), ((), ())), precision=precision, preferred_element_type=jnp.float32
    )


def dot_nn(left, right, precision=None):
    return lax.dot_general(
        left, right, (((1,), (0,)), ((), ())), precision=precision, preferred_element_type=jnp.float32
    )


def three_parts(value):
    high = value.astype(jnp.bfloat16)
    rest = value - high.astype(jnp.float32)
    middle = rest.astype(jnp.bfloat16)
    low = (rest - middle.astype(jnp.float32)).astype(jnp.bfloat16)
    return high, middle, low


def halves(block, axis):
    count = lax.axis_size(axis)
    block = block[None]
    bit = 1
    while 2 * bit < count:
        block = jnp.concatenate([block, swapped(block, axis, bit)], axis=0)
        bit *= 2
    return block, swapped(block, axis, bit)


def swapped(block, axis, bit):
    return lax.ppermute(block, axis, [(i, i ^ bit) for i in range(lax.axis_size(axis))])


def sum_over(block, axis):
    bit = 1
    while bit < lax.axis_size(axis):
        block = block + swapped(block, axis, bit)
        bit *= 2
    return block


def region_orders(count):
    bits = []
    bit = count // 2
    while bit:
        bits.append(bit)
        bit //= 2
    return bits, bits[:1] + bits[-1:] + bits[1:-1] if len(bits) > 2 else bits[::-1]


def slot_offsets(count):
    table = []
    for bits in region_orders(count):
        offsets = [0]
        for bit in bits:
            offsets = offsets + [offset ^ bit for offset in offsets]
        table.append(offsets)
    return jnp.array(table, jnp.int32)


def exchange(block):
    regions, tiles = lax.axis_size("region"), lax.axis_size("tile")
    block = block[None]
    for even, odd in zip(*region_orders(regions)):
        route = [
            (region * tiles + tile, (region ^ (odd if tile % 2 else even)) * tiles + tile)
            for region in range(regions)
            for tile in range(tiles)
        ]
        other = lax.ppermute(block, ("region", "tile"), route)
        if 2 * block.shape[0] == regions:
            return block, other
        block = jnp.concatenate([block, other], axis=0)


def stacked_parts(value):
    return jnp.concatenate([part.astype(jnp.float32) for part in three_parts(value)], axis=0).astype(
        jnp.bfloat16
    )


def add_parts(value):
    rows = value.shape[0] // 3
    return (value[2 * rows :] + value[rows : 2 * rows]) + value[:rows]


def fill_order(first, rank, order_ref, row, count):
    step = 64

    def fill(block, carry):
        start = pl.multiple_of(block * step, step)
        place = first + start + lax.broadcasted_iota(jnp.int32, (step, rank.shape[1]), 0)
        order_ref[pl.ds(pl.multiple_of(row + start, step), step), :] = jnp.where(
            place == rank, 1.0, 0.0
        ).astype(jnp.bfloat16)
        return carry

    lax.fori_loop(0, count // step, fill, 0)


def sort_kernel(
    first_ref, owner_ref, near_ref, far_ref, block_ref, other_ref,
    message_out, own_out, block_out, rank_out, order_ref, column_ref,
):
    columns, local = block_out.shape
    stacks = [near_ref[i] for i in range(near_ref.shape[0])] + [far_ref[i] for i in range(far_ref.shape[0])]
    places = jnp.concatenate(stacks, axis=1)
    n = places.shape[1]
    step = 64
    index = jnp.concatenate(
        [
            (first_ref[i] + lax.broadcasted_iota(jnp.int32, (1, local), 1)).astype(jnp.float32)
            for i in range(n // local)
        ],
        axis=1,
    )
    y_row = places[1:2, :]
    column_ref[...] = jnp.transpose(
        jnp.concatenate([y_row, index, jnp.zeros((6, n), jnp.float32)], axis=0)
    )

    def count(block, total):
        start = pl.multiple_of(block * step, step)
        y_column = jnp.broadcast_to(column_ref[pl.ds(start, step), 0:1], (step, n))
        index_column = jnp.broadcast_to(column_ref[pl.ds(start, step), 1:2], (step, n))
        before = (y_column < y_row) | ((y_column == y_row) & (index_column < index))
        return total + jnp.sum(jnp.where(before, 1.0, 0.0).reshape(step // 8, 8, n), axis=0)

    total = lax.fori_loop(0, n // step, count, jnp.zeros((8, n), jnp.float32))
    rank = jnp.sum(total, axis=0, keepdims=True).astype(jnp.int32)
    rank_out[...] = rank[:, :local]
    fill_order(first_ref[0], rank, order_ref, 0, local)
    blocks = [block_ref[i] for i in range(block_ref.shape[0])]
    blocks += [other_ref[i] for i in range(other_ref.shape[0])]
    everything = jnp.concatenate([jnp.concatenate(blocks, axis=1), places, jnp.zeros((4, n), jnp.float32)], axis=0)
    rows = everything.shape[0]
    parts = dot_nt(stacked_parts(everything), order_ref[...])
    whole = add_parts(parts)
    block_out[...] = whole[:columns]
    own_out[...] = whole[columns:]
    message_out[:columns, :] = whole[:columns].astype(jnp.bfloat16)
    lane = lax.broadcasted_iota(jnp.int32, (1, local), 1)
    flags = jnp.zeros((1, local), jnp.float32)
    for offset in range(owner_ref.shape[1]):
        flags = jnp.where((lane == offset) & (owner_ref[0, offset] >= 0), 1.0, flags)
    pieces = [parts[part * rows + columns : part * rows + columns + 3] for part in range(3)]
    pieces += [flags, jnp.zeros((EXTRA - 10, local), jnp.float32)]
    message_out[columns:, :] = jnp.concatenate(pieces, axis=0).astype(jnp.bfloat16)


def sort_region(first, tile_owner, near, far, block, other):
    local = near.shape[2]
    n = local * 2 * near.shape[0]
    columns = block.shape[1]
    smem = pl.BlockSpec(memory_space=pltpu.SMEM)
    return pl.pallas_call(
        sort_kernel,
        out_shape=(
            jax.ShapeDtypeStruct((columns + EXTRA, local), jnp.bfloat16),
            jax.ShapeDtypeStruct((8, local), jnp.float32),
            jax.ShapeDtypeStruct((columns, local), jnp.float32),
            jax.ShapeDtypeStruct((1, local), jnp.int32),
        ),
        in_specs=[smem, smem] + whole_vmem(4),
        out_specs=tuple(whole_vmem(4)),
        scratch_shapes=[pltpu.VMEM((local, n), jnp.bfloat16), pltpu.VMEM((n, 8), jnp.float32)],
        compiler_params=pltpu.CompilerParams(vmem_limit_bytes=VMEM),
        cost_estimate=pl.CostEstimate(
            flops=6 * n * local * (columns + 8), bytes_accessed=4 * n * local, transcendentals=0
        ),
        name="sort_region",
    )(first, tile_owner, near, far, block, other)


def unsort_kernel(first_ref, rank_ref, block_ref, block_out, order_ref):
    n, local = order_ref.shape
    for slot in range(n // local):
        fill_order(first_ref[slot], rank_ref[...], order_ref, slot * local, local)
    block_out[...] = add_parts(dot_nn(stacked_parts(block_ref[...]), order_ref[...]))


def unsort(first, rank, block):
    n = block.shape[1]
    local = rank.shape[1]
    return pl.pallas_call(
        unsort_kernel,
        out_shape=jax.ShapeDtypeStruct((block.shape[0], local), jnp.float32),
        in_specs=[pl.BlockSpec(memory_space=pltpu.SMEM)] + whole_vmem(2),
        out_specs=whole_vmem(1)[0],
        scratch_shapes=[pltpu.VMEM((n, local), jnp.bfloat16)],
        compiler_params=pltpu.CompilerParams(vmem_limit_bytes=VMEM),
        cost_estimate=pl.CostEstimate(
            flops=6 * n * local * block.shape[0], bytes_accessed=4 * n * local, transcendentals=0
        ),
        name="unsort",
    )(first, rank, block)


def plan_blocks(own_y, near, far, regions, here, flags, columns, capacity):
    reach = flags.shape[0]
    rows = own_y.shape[0] // ROWS
    stack = jnp.concatenate([near, far], axis=0)[:, :, columns:, :].astype(jnp.float32)
    chunks = stack.shape[3] // LANES
    y = (stack[:, :, 1] + stack[:, :, 4]) + stack[:, :, 7]
    y = y.reshape(-1, LANES)
    distance = regions - here
    ahead = jnp.arange(reach, dtype=jnp.int32)
    own_flag = jnp.sum(jnp.where(distance[..., None] == ahead, flags, 0.0), axis=-1)
    far_flag = jnp.sum(jnp.where(-distance[..., None] == ahead, stack[:, :, 9, :reach], 0.0), axis=-1)
    listed = jnp.broadcast_to(((own_flag + far_flag) > 0.5)[..., None], regions.shape + (chunks,))
    y_own = own_y.reshape(rows, ROWS)
    near_enough = (y[None, :, 0] <= y_own[:, -1:] + CUTOFF) & (y[None, :, -1] >= y_own[:, :1] - CUTOFF)
    active = near_enough & listed.reshape(1, -1)
    total = y.shape[0]
    index = jnp.arange(total, dtype=jnp.int32)
    counted = active.astype(jnp.int32)
    batches = (jnp.sum(counted, axis=1) + BATCH - 1) // BATCH
    row = jnp.arange(rows, dtype=jnp.int32)
    base = jnp.sum(jnp.where(row[:, None] < row[None, :], batches[:, None], 0), axis=0)
    place = base[:, None] * BATCH + jnp.sum(
        jnp.where(index[None, :, None] < index[None, None, :], counted[:, :, None], 0), axis=1
    )
    spot = jnp.arange(capacity * BATCH, dtype=jnp.int32)
    hit = active[:, :, None] & (place[:, :, None] == spot)
    ids = jnp.sum(jnp.where(hit, index[None, :, None] + 1, 0), axis=(0, 1)) - 1
    step = jnp.arange(capacity, dtype=jnp.int32)
    owner = jnp.sum((base + batches)[:, None] <= step[None, :], axis=0, dtype=jnp.int32)
    return ids, jnp.concatenate([jnp.minimum(owner, rows - 1), jnp.sum(batches, keepdims=True)])


def gaspari_cohn(squared):
    squared = jnp.maximum(squared, 1e-12)
    inverse = lax.rsqrt(squared)
    scaled = squared * inverse
    near = (((-0.25 * scaled + 0.5) * scaled + 0.625) * scaled - 5.0 / 3.0) * squared + 1.0
    left = jnp.maximum(2.0 - scaled, 0.0)
    left = left * left
    far = (left * left) * ((scaled + 2.0) * scaled - 0.5) * (inverse * (1.0 / 12.0))
    return jnp.where(scaled <= 1.0, near, far)


def tiles_kernel(build, wanted, ids_ref, plan_ref, own_ref, near_ref, far_ref, *refs):
    refs = list(refs)
    tiles_in = None if build else refs.pop(0)
    start_ref = None
    block_ref = scale_ref = out_ref = rounded_ref = gram_ref = None
    if wanted:
        start_ref, block_ref, scale_ref = refs[:3]
        refs = refs[3:]
    tiles_out = refs.pop(0) if build else None
    if wanted:
        out_ref, rounded_ref, gram_ref = refs[:3]
        refs = refs[3:]
        wide_ref, held_ref, all_ref, total_ref, sems, piece_sems = refs
    else:
        total_ref, wide_ref, held_ref, all_ref, sems, piece_sems = refs
    half, slots, height, local = near_ref.shape
    columns = total_ref.shape[1]
    capacity = held_ref.shape[0]
    chunks = local // LANES
    total = plan_ref[capacity]

    copies = [
        pltpu.make_async_copy(ref, all_ref.at[pl.ds(part * half, half)], piece_sems.at[part])
        for part, ref in enumerate((near_ref, far_ref))
    ]
    for copy in copies:
        copy.start()

    def copy_out(batch):
        return pltpu.make_async_copy(
            held_ref.at[batch], tiles_out.at[batch], sems.at[lax.rem(batch, RING)]
        )

    def copy_in(group):
        first = group * UNROLL
        return pltpu.make_async_copy(
            tiles_in.at[pl.ds(first, UNROLL)], held_ref.at[pl.ds(first, UNROLL)], sems.at[group]
        )

    groups = (total + UNROLL - 1) // UNROLL
    if not build:

        def start_copy(group, carry):
            copy_in(group).start()
            return carry

        lax.fori_loop(0, groups, start_copy, 0)
    if start_ref is None:
        total_ref[...] = jnp.zeros(total_ref.shape, jnp.float32)
    else:
        total_ref[...] = start_ref[...]
    if build:
        column = jnp.transpose(own_ref[...])
        for row in range(3):
            scale = 2.0 if row < 2 else 1.0
            wide_ref[row] = jnp.broadcast_to(scale * column[:, row : row + 1], (local, LANES))
    for copy in copies:
        copy.wait()

    def locate(batch, part):
        entry = ids_ref[batch * BATCH + part]
        chunk = jnp.maximum(entry, 0)
        place = chunk // chunks
        tile = place // slots
        lane = pl.multiple_of((chunk - place * chunks) * LANES, LANES)
        return entry, tile, place - tile * slots, lane

    def build_batch(batch):
        start = pl.multiple_of(plan_ref[batch] * ROWS, ROWS)
        for part in range(BATCH):
            entry, tile, place, lane = locate(batch, part)
            rows = all_ref[tile, place, columns:, pl.ds(lane, LANES)].astype(jnp.float32)
            far = (rows[0:3] + rows[3:6]) + rows[6:9]
            across_x = wide_ref[0, pl.ds(start, ROWS), :] - 2.0 * far[0:1, :]
            across_y = wide_ref[1, pl.ds(start, ROWS), :] - 2.0 * far[1:2, :]
            value = gaspari_cohn(across_x * across_x + across_y * across_y)
            spread = jnp.where(entry >= 0, far[2:3, :], 0.0)
            value = wide_ref[2, pl.ds(start, ROWS), :] * spread * value
            held_ref[batch, :, part * LANES : (part + 1) * LANES] = value.astype(jnp.bfloat16)

    def product(batch, valid=None):
        sides = []
        for part in range(BATCH):
            _, tile, place, lane = locate(batch, part)
            sides.append(all_ref[tile, place, :columns, pl.ds(lane, LANES)])
        side = jnp.concatenate(sides, axis=1)
        if valid is not None:
            side = jnp.where(valid, side, jnp.zeros_like(side))
        return dot_nt(held_ref[batch], side)

    def add_product(batch, value):
        start = pl.multiple_of(plan_ref[batch] * ROWS, ROWS)
        total_ref[pl.ds(start, ROWS), :] += value

    if build:

        @pl.when(total > 0)
        def _():
            build_batch(0)
            copy_out(0).start()

            def turn(batch, carry):
                @pl.when(batch >= RING)
                def _():
                    copy_out(batch - RING).wait()

                value = product(batch - 1)
                build_batch(batch)
                add_product(batch - 1, value)
                copy_out(batch).start()
                return carry

            lax.fori_loop(1, total, turn, 0)
            add_product(total - 1, product(total - 1))

            def finish(batch, carry):
                copy_out(batch).wait()
                return carry

            lax.fori_loop(jnp.maximum(total - RING, 0), total, finish, 0)

    else:

        def turn(group, carry):
            copy_in(group).wait()
            batches = [jnp.minimum(group * UNROLL + i, total - 1) for i in range(UNROLL)]
            values = [
                product(batch, group * UNROLL + i < total if i else None)
                for i, batch in enumerate(batches)
            ]
            for batch, value in zip(batches, values):
                add_product(batch, value)
            return carry

        lax.fori_loop(0, groups, turn, 0)

    if wanted:
        block = block_ref[...]
        result = jnp.transpose(total_ref[...]) + scale_ref[...] * block
        out_ref[...] = result
        rounded_ref[...] = result.astype(jnp.bfloat16)
        pairs = {"squares": (block, block), "mixed": (block, result), "images": (result, result)}
        for index, name in enumerate(wanted):
            gram_ref[index] = dot_nt(*pairs[name], HIGHEST)


def run_tiles(plan, own, near, far, tiles, capacity, columns, finish=None):
    build = tiles is None
    half, slots, height, local = near.shape
    smem = pl.BlockSpec(memory_space=pltpu.SMEM)
    anywhere = pl.BlockSpec(memory_space=pl.ANY)
    operands = [*plan, own, near, far]
    in_specs = [smem, smem] + whole_vmem(1) + [anywhere] * 2
    out_shape, out_specs = [], []
    if not build:
        operands.append(tiles)
        in_specs.append(anywhere)
    wanted = ()
    if finish is not None:
        total, block, scale, wanted = finish
        operands += [total, block, scale]
        in_specs += whole_vmem(3)
    if build:
        out_shape.append(jax.ShapeDtypeStruct((capacity, ROWS, BATCH * LANES), jnp.bfloat16))
        out_specs.append(anywhere)
    total_shape = (local, columns)
    scratch = []
    if wanted:
        out_shape += [
            jax.ShapeDtypeStruct((columns, local), jnp.float32),
            jax.ShapeDtypeStruct((columns, local), jnp.bfloat16),
            jax.ShapeDtypeStruct((len(wanted), columns, columns), jnp.float32),
        ]
        out_specs += whole_vmem(3)
    else:
        out_shape.append(jax.ShapeDtypeStruct(total_shape, jnp.float32))
        out_specs += whole_vmem(1)
    scratch += [
        pltpu.VMEM((3, local, LANES), jnp.float32),
        pltpu.VMEM((capacity, ROWS, BATCH * LANES), jnp.bfloat16),
        pltpu.VMEM((2 * half, slots, height, local), jnp.bfloat16),
    ]
    if wanted:
        scratch.append(pltpu.VMEM(total_shape, jnp.float32))
    scratch += [
        pltpu.SemaphoreType.DMA((RING if build else capacity // UNROLL,)),
        pltpu.SemaphoreType.DMA((2,)),
    ]
    work = 2 * local * local
    return pl.pallas_call(
        functools.partial(tiles_kernel, build, wanted),
        out_shape=tuple(out_shape),
        in_specs=in_specs,
        out_specs=tuple(out_specs),
        scratch_shapes=scratch,
        compiler_params=pltpu.CompilerParams(vmem_limit_bytes=VMEM),
        cost_estimate=pl.CostEstimate(
            flops=work * (120 if build else 60), bytes_accessed=8 * work, transcendentals=0
        ),
        name=("build" if build else "apply") + ("_last" if wanted else "_first"),
    )(*operands)


def reciprocal(value):
    inverse = lax.rsqrt(value)
    inverse = inverse * inverse
    return inverse * (2.0 - value * inverse)


def small_product(left, right):
    return [[sum(l * r[j] for l, r in zip(row, right)) for j in range(len(right[0]))] for row in left]


def small_difference(left, right):
    return [[l - r for l, r in zip(*rows)] for rows in zip(left, right)]


def small_inverse(matrix):
    (a, b), (c, d) = matrix
    scale = reciprocal(a * d - b * c)
    return [[d * scale, -b * scale], [-c * scale, a * scale]]


def solve_positive(matrix, target):
    n = matrix.shape[0]
    table = jnp.concatenate([0.5 * (matrix + jnp.transpose(matrix)), target], axis=1)
    bands = [table[k : k + 8, :] for k in range(0, n, 8)]
    row_index = lax.broadcasted_iota(jnp.int32, bands[0].shape, 0)
    for k in range(0, n, 4):
        own, row = k // 8, k % 8
        columns = [
            [jnp.broadcast_to(band[:, k + j : k + j + 1], band.shape) for band in bands] for j in range(4)
        ]
        pivot = [[columns[j][own][row + i : row + i + 1] for j in range(4)] for i in range(4)]
        upper, lower = pivot[:2], pivot[2:]
        top = small_inverse([r[:2] for r in upper])
        factor = small_product([r[:2] for r in lower], top)
        right = [r[2:] for r in upper]
        rest = small_inverse(small_difference([r[2:] for r in lower], small_product(factor, right)))
        rows = [[bands[own][row + i : row + i + 1]] for i in range(4)]
        last = small_product(rest, small_difference(rows[2:], small_product(factor, rows[:2])))
        first = small_product(top, small_difference(rows[:2], small_product(right, last)))
        new = [r[0] for r in first + last]
        bands = [
            band - ((columns[0][i] * new[0] + columns[1][i] * new[1]) + (columns[2][i] * new[2] + columns[3][i] * new[3]))
            for i, band in enumerate(bands)
        ]
        for i in range(4):
            bands[own] = jnp.where(row_index == row + i, new[i], bands[own])
    return jnp.concatenate([band[:, n:] for band in bands], axis=0)


def last_kernel(grams_ref, start_ref, images_ref, weights_ref, residual_ref):
    squares, mixed, images, cross = grams_ref[0], grams_ref[1], grams_ref[2], grams_ref[3]
    n = squares.shape[0]
    solved = solve_positive(mixed, jnp.concatenate([squares, images], axis=1))
    step, carried = solved[:, :n], solved[:, n:]
    product = dot_nn(images, solved, HIGHEST)
    second = solve_positive(cross - product[:, n:], jnp.transpose(mixed) - product[:, :n])
    first = jnp.transpose(step - dot_nn(carried, second, HIGHEST))
    second = jnp.transpose(second)
    start, image = start_ref[...], images_ref[:n, :]
    weights_ref[...] = dot_nn(first, start, HIGHEST) + dot_nn(second, image, HIGHEST)
    residual_ref[...] = start - dot_nn(first, image, HIGHEST) - dot_nn(second, images_ref[n:, :], HIGHEST)


def last_step(grams, start, images):
    return pl.pallas_call(
        last_kernel,
        out_shape=(jax.ShapeDtypeStruct(start.shape, jnp.float32),) * 2,
        in_specs=whole_vmem(3),
        out_specs=tuple(whole_vmem(2)),
        compiler_params=pltpu.CompilerParams(vmem_limit_bytes=VMEM),
        name="last_step",
    )(grams, start, images)


def shards(innovations, obs_geometry, obs_error, tile_owner):
    tiles_axis, regions = lax.axis_size("tile"), lax.axis_size("region")
    reach = tile_owner.shape[1]
    here, tile = lax.axis_index("region"), lax.axis_index("tile")
    columns, local = innovations.shape
    slot_tile = tile ^ jnp.arange(tiles_axis, dtype=jnp.int32)
    first = slot_tile * local
    slot_region = here ^ slot_offsets(regions)[slot_tile % 2]

    places = jnp.concatenate([obs_geometry, obs_error[None, :]], axis=0)
    message, own, start, rank = sort_region(
        first, tile_owner, *halves(places, "tile"), *halves(innovations, "tile")
    )
    scale = own[3:4]
    flags = jnp.where(tile_owner[0] >= 0, 1.0, 0.0).astype(jnp.float32)

    half_regions = regions // 2
    most = min(half_regions, 2 * reach - 1) * tiles_axis * (local // LANES)
    capacity = (local // ROWS) * -(-most // BATCH)
    capacity = -(-capacity // UNROLL) * UNROLL
    run = functools.partial(run_tiles, own=own, capacity=capacity, columns=columns)

    plans, tiles = [], []
    total = None
    for part, block in enumerate(exchange(message)):
        near, far = halves(block, "tile")
        inside = slot_region[:, part * half_regions : (part + 1) * half_regions]
        plans.append(plan_blocks(own[1], near, far, inside, here, flags, columns, capacity))
        finish = None if part == 0 else (total, start, scale, ("squares", "mixed", "images"))
        built, total, *others = run(plans[part], near=near, far=far, tiles=None, finish=finish)
        tiles.append(built)
    image = total
    image_rounded, grams = others

    for part, block in enumerate(exchange(image_rounded)):
        near, far = halves(block, "tile")
        finish = None if part == 0 else (total, image, scale, ("mixed",))
        total, *others = run(plans[part], near=near, far=far, tiles=tiles[part], finish=finish)
    second, cross = total, others[1]

    grams = jnp.concatenate([grams, cross], axis=0)
    grams = sum_over(sum_over(grams, "tile"), "region")
    near, far = halves(jnp.concatenate([image, second], axis=0), "tile")
    images = unsort(first, rank, jnp.concatenate([*near, *far], axis=1))
    return last_step(grams, innovations, images)


def solution(mesh):
    return jax.shard_map(
        shards,
        mesh=mesh,
        in_specs=(
            P(None, ("region", "tile")),
            P(None, ("region", "tile")),
            P(("region", "tile")),
            P("region", None),
        ),
        out_specs=(P(None, ("region", "tile")), P(None, ("region", "tile"))),
        check_vma=False,
    )
```

time: 413 us -> 132 us (0.32); the launches traced: 405 us -> 132 us
  blocking collectives: 89.3 us -> 0 us
  other arithmetic: 66.4 us -> 9.69 us
  waiting for transfers between devices: 109 us -> 56 us
  starting transfers between devices: 70.1 us -> 32.3 us
  matrix products: 32.3 us -> 0 us
  Pallas kernels: 0 us -> 29 us
  between operations: 19.5 us -> 0.92 us
  local copies, waits for them, and re-layouts: 17.4 us -> 4.05 us
    psum x2 -> x0, blocking collectives: 82.3 us -> none  [the longest x1 41.6 us: shards(): squares = lax.psum(gram_matrix(residual, residual), ('region', 'tile'))]
    reduce_scatter x2 -> x0, waiting for transfers between devices: 39 us -> none  [shards(): lax.psum_scatter(total_block, 'tile', scatter_dimension=1, tiled=True)]
    ppermute x30 -> x20, starting transfers between devices: 69.8 us -> 32.3 us  [the longest x8 19.5 us: exchange(): other = lax.ppermute(block, ('region', 'tile'), route)]
    another operation x15 -> x0, other arithmetic: 36.2 us -> none  [the longest x9 19.6 us: gram_solve(): factor = jnp.linalg.cholesky(symmetric)]
    dot_general x24 -> x0, matrix products: 31.1 us -> none  [the longest x6 17.6 us: both_terms(): jnp.dot(home_block, tile_block, preferred_element_type=jnp.float32)]
    pallas_call x0 -> x6, Pallas kernels: none -> 29 us  [the longest x3 16.1 us: run_tiles(): pl.pallas_call(functools.partial(tiles_kernel, build, wanted), out_shape=...]
    convert_element_type x3 -> x4, other arithmetic: 23.6 us -> 0.07 us  [the longest x2 0.07 us: plan_blocks(): jnp.concatenate([near, far], axis=0)[:, :, columns:, :].astype(jnp.float32)]
    ppermute x30 -> x20, waiting for transfers between devices: 70.2 us -> 56 us  [the longest x8 41.3 us: exchange(): other = lax.ppermute(block, ('region', 'tile'), route)]
  transfers between devices with their start and end apart: 32 -> 20, of which waited for: 17 -> 15; matrix products, arithmetic and copies ran while one was open for 15% -> 3% of each run, Pallas kernels for 0% -> 4%
where the time goes in v3:
time: 132 us
  waiting for transfers between devices  56 us (42%)
  starting transfers between devices  32.3 us (24%)
  Pallas kernels  29 us (22%)
  other arithmetic  9.69 us (7%)
  local copies, waits for them, and re-layouts  4.05 us (3%)
    ppermute x8, waiting for transfers between devices, exchange(): other = lax.ppermute(block, ('region', 'tile'), route)  41.3 us
    ppermute x8, starting transfers between devices, exchange(): other = lax.ppermute(block, ('region', 'tile'), route)  19.5 us
    pallas_call x3, Pallas kernels, run_tiles(): pl.pallas_call(functools.partial(tiles_kernel, build, wanted), out_shape=...  16.1 us
    ppermute x12, waiting for transfers between devices, swapped(): lax.ppermute(block, axis, [(i, i ^ bit) for i in range(lax.axis_size(axis...  14.7 us
    ppermute x12, starting transfers between devices, swapped(): lax.ppermute(block, axis, [(i, i ^ bit) for i in range(lax.axis_size(axis...  12.8 us
    pallas_call x1, Pallas kernels, last_step(): pl.pallas_call(last_kernel, out_shape=(jax.ShapeDtypeStruct(start.shape,...  7.63 us
    pallas_call x1, Pallas kernels, sort_region(): pl.pallas_call(sort_kernel, out_shape=(jax.ShapeDtypeStruct((columns + EX...  3.85 us
    pallas_call x1, other arithmetic, run_tiles(): pl.pallas_call(functools.partial(tiles_kernel, build, wanted), out_shape=...  3.25 us
  transfers between devices with their start and end apart: 20, of which 15 were waited for; matrix products, arithmetic and copies ran while one was open for 3% of the time, Pallas kernels for 4%

profile of v3, /device:TPU:0, one launch (start us, length us, event | category | flops | bytes accessed | tf_op | source)
XLA Modules:
  0.0 132.0 jit_solution(15321742241812103273)
XLA Ops:
  0.6 0.5 collective-permute-start.1
  1.1 0.7 maximum_bitcast_fusion.near_ref
  1.9 0.1 collective-permute-start
  2.0 1.1 collective-permute-done.far_ref
  3.1 0.9 copy-done
  4.0 0.7 copy-done.2
  4.7 3.9 %sort_region.1 = (bf16[80,512]{1,0:T(8,128)(2,1)S(1)}, f32[8,512]{1,0:T(8,128)S(1)}, f32[64,512]{1,0:T(8,128)S(1)}, s32[1,512]{1,0:T(1,128)S(1)}) custom-call(s32[2]{0:T(128)S(1)} %xor_multiply_fusion.first_ref, s32[1,7]{1,0:T(1,128)S(1)} %copy-done.2, f32[1,4,512]{2,1,0:T(4,128)S(1)} %maximum_bitcast_fusion.near_ref, ...), custom_call_target="tpu_custom_call" | custom-call | flops 226492416 | bytes 2097152 | tf_op jit(solution)/shard_map/sort_region/pallas_call | solution.py:181
  8.5 3.8 %collective-permute-start.2 = (bf16[1,80,512]{2,1,0:T(8,128)(2,1)S(1)}, bf16[1,80,512]{2,1,0:T(8,128)(2,1)S(1)}, u32[]{:S(2)}, u32[]{:S(2)}) collective-permute-start(bf16[1,80,512]{2,1,0:T(8,128)(2,1)S(1)} %bitcast.37), channel_id=1, source_target_pairs={{0,16},{1,17},{2,18},{3,19},{4,20},{5,21},{6,22},{7,23},{8,24},{9,... | collective-permute-start | bytes 245768 | tf_op jit(solution)/shard_map/ppermute | solution.py:95
  12.3 1.2 gather_fusion
  13.6 3.5 %collective-permute-done.2 = bf16[1,80,512]{2,1,0:T(8,128)(2,1)S(1)} collective-permute-done((bf16[1,80,512]{2,1,0:T(8,128)(2,1)S(1)}, bf16[1,80,512]{2,1,0:T(8,128)(2,1)S(1)}, u32[]{:S(2)}, u32[]{:S(2)}) %collective-permute-start.2) | collective-permute-done | bytes 81952 | tf_op jit(solution)/shard_map/ppermute | solution.py:95
  17.1 0.8 collective-permute-start.3
  17.9 4.6 %collective-permute-done.3 = bf16[2,80,512]{2,1,0:T(8,128)(2,1)S(1)} collective-permute-done((bf16[2,80,512]{2,1,0:T(8,128)(2,1)S(1)}, bf16[2,80,512]{2,1,0:T(8,128)(2,1)S(1)}, u32[]{:S(2)}, u32[]{:S(2)}) %collective-permute-start.3) | collective-permute-done | bytes 163872 | tf_op jit(solution)/shard_map/ppermute | solution.py:95
  22.5 1.6 %collective-permute-start.4 = (bf16[4,80,512]{2,1,0:T(8,128)(2,1)S(1)}, bf16[4,80,512]{2,1,0:T(8,128)(2,1)S(1)}, u32[]{:S(2)}, u32[]{:S(2)}) collective-permute-start(bf16[4,80,512]{2,1,0:T(8,128)(2,1)S(1)} %pad_maximum_fusion.3), channel_id=1, source_target_pairs={{0,4},{1,9},{2,6},{3,11},{4,0},{5,13},{6,2},{7,15},{8,12},{9,1},{1... | collective-permute-start | bytes 983048 | tf_op jit(solution)/shard_map/ppermute | solution.py:95
  24.2 5.4 %collective-permute-done.4 = bf16[4,80,512]{2,1,0:T(8,128)(2,1)S(1)} collective-permute-done((bf16[4,80,512]{2,1,0:T(8,128)(2,1)S(1)}, bf16[4,80,512]{2,1,0:T(8,128)(2,1)S(1)}, u32[]{:S(2)}, u32[]{:S(2)}) %collective-permute-start.4) | collective-permute-done | bytes 327712 | tf_op jit(solution)/shard_map/ppermute | solution.py:95
  29.6 0.1 pad_maximum_fusion
  29.7 1.6 %collective-permute-start.5 = (bf16[8,80,512]{2,1,0:T(8,128)(2,1)S(1)}, bf16[8,80,512]{2,1,0:T(8,128)(2,1)S(1)}, u32[]{:S(2)}, u32[]{:S(2)}) collective-permute-start(bf16[8,80,512]{2,1,0:T(8,128)(2,1)S(1)} %get-tuple-element.51), channel_id=1, source_target_pairs={{0,2},{1,5},{2,0},{3,7},{4,6},{5,1},{6,4},{7,3},{8,10},{9,13},{10,... | collective-permute-start | bytes 1966088 | tf_op jit(solution)/shard_map/ppermute | solution.py:95
  31.3 0.7 fusion.8
  32.0 0.1 fusion.6
  32.2 8.2 %collective-permute-done.5 = bf16[8,80,512]{2,1,0:T(8,128)(2,1)S(1)} collective-permute-done((bf16[8,80,512]{2,1,0:T(8,128)(2,1)S(1)}, bf16[8,80,512]{2,1,0:T(8,128)(2,1)S(1)}, u32[]{:S(2)}, u32[]{:S(2)}) %collective-permute-start.5) | collective-permute-done | bytes 655392 | tf_op jit(solution)/shard_map/ppermute | solution.py:95
  40.5 0.1 copy.37
  40.5 0.1 copy.38
  40.6 0.1 convert_add_fusion
  41.0 0.1 copy.30
  41.0 1.4 %collective-permute-done.6.far_ref = bf16[1,8,80,512]{3,2,1,0:T(8,128)(2,1)S(1)} collective-permute-done((bf16[1,8,80,512]{3,2,1,0:T(8,128)(2,1)S(1)}, bf16[1,8,80,512]{3,2,1,0:T(8,128)(2,1)S(1)}, u32[]{:S(2)}, u32[]{:S(2)}) %collective-permute-start.6) | collective-permute-done | bytes 655392 | tf_op jit(solution)/shard_map/ppermute | solution.py:56
  42.5 0.1 convert_add_fusion.2
  42.8 0.1 copy.27
  43.0 0.1 and.136
  43.2 0.1 and.129
  43.3 0.2 convert_reduce_fusion.3
  43.5 0.7 fusion.17
  44.2 0.1 select_reduce_fusion.4
  44.3 0.1 convert_reduce_fusion
  44.4 0.6 fusion.18
  45.0 0.1 select_reduce_fusion.5
  45.1 0.2 select_reduce_fusion.2
  45.5 0.6 select_reduce_fusion
  46.1 0.1 convert_reduce_fusion.1
  46.2 0.7 pad_add_fusion.1.plan_ref
  46.8 0.7 pad_add_fusion.plan_ref
  47.5 6.3 %build_first.1 = (bf16[128,64,512]{2,1,0:T(8,128)(2,1)}, f32[512,64]{1,0:T(8,128)S(1)}) custom-call(s32[512]{0:T(512)S(1)} %broadcast_add_fusion.2.ids_ref, s32[129]{0:T(256)S(1)} %pad_add_fusion.1.plan_ref, f32[8,512]{1,0:T(8,128)S(1)} %get-tuple-element.15.own_ref, bf16[1,8,80,512]{3,2,1,0:T(8,128)(2,1)S(1)} %get-tuple-element.52.near_ref, ...), custom_call_target="tpu_custom_call" | custom-call | flops 62914560 | bytes 4194304 | tf_op jit(solution)/shard_map/build_first/pallas_call | solution.py:456
  53.8 6.5 %build_last.1 = (bf16[128,64,512]{2,1,0:T(8,128)(2,1)}, f32[64,512]{1,0:T(8,128)S(1)}, bf16[64,512]{1,0:T(8,128)(2,1)S(1)}, f32[3,64,64]{2,1,0:T(8,128)S(1)}) custom-call(s32[512]{0:T(512)S(1)} %broadcast_add_fusion.3.ids_ref, s32[129]{0:T(256)S(1)} %pad_add_fusion.plan_ref, f32[8,512]{1,0:T(8,128)S(1)} %get-tuple-element.15.own_ref, ...), custom_call_target="tpu_custom_call" | custom-call | flops 62914560 | bytes 4194304 | tf_op jit(solution)/shard_map/build_last/pallas_call | solution.py:456
  60.3 8.1 %collective-permute-start.8 = (bf16[1,64,512]{2,1,0:T(8,128)(2,1)S(1)}, bf16[1,64,512]{2,1,0:T(8,128)(2,1)S(1)}, u32[]{:S(2)}, u32[]{:S(2)}) collective-permute-start(bf16[1,64,512]{2,1,0:T(8,128)(2,1)S(1)} %bitcast.41), channel_id=1, source_target_pairs={{0,16},{1,17},{2,18},{3,19},{4,20},{5,21},{6,22},{7,23},{8,24},{9,... | collective-permute-start | bytes 196616 | tf_op jit(solution)/shard_map/ppermute | solution.py:95
  68.4 2.2 %collective-permute-done.8 = bf16[1,64,512]{2,1,0:T(8,128)(2,1)S(1)} collective-permute-done((bf16[1,64,512]{2,1,0:T(8,128)(2,1)S(1)}, bf16[1,64,512]{2,1,0:T(8,128)(2,1)S(1)}, u32[]{:S(2)}, u32[]{:S(2)}) %collective-permute-start.8) | collective-permute-done | bytes 65568 | tf_op jit(solution)/shard_map/ppermute | solution.py:95
  70.8 5.0 %collective-permute-done.9 = bf16[2,64,512]{2,1,0:T(8,128)(2,1)S(1)} collective-permute-done((bf16[2,64,512]{2,1,0:T(8,128)(2,1)S(1)}, bf16[2,64,512]{2,1,0:T(8,128)(2,1)S(1)}, u32[]{:S(2)}, u32[]{:S(2)}) %collective-permute-start.9) | collective-permute-done | bytes 131104 | tf_op jit(solution)/shard_map/ppermute | solution.py:95
  75.7 1.1 collective-permute-start.10
  76.9 5.3 %collective-permute-done.10 = bf16[4,64,512]{2,1,0:T(8,128)(2,1)S(1)} collective-permute-done((bf16[4,64,512]{2,1,0:T(8,128)(2,1)S(1)}, bf16[4,64,512]{2,1,0:T(8,128)(2,1)S(1)}, u32[]{:S(2)}, u32[]{:S(2)}) %collective-permute-start.10) | collective-permute-done | bytes 262176 | tf_op jit(solution)/shard_map/ppermute | solution.py:95
  82.2 0.1 fusion.11
  82.3 2.3 %collective-permute-start.11 = (bf16[8,64,512]{2,1,0:T(8,128)(2,1)S(1)}, bf16[8,64,512]{2,1,0:T(8,128)(2,1)S(1)}, u32[]{:S(2)}, u32[]{:S(2)}) collective-permute-start(bf16[8,64,512]{2,1,0:T(8,128)(2,1)S(1)} %get-tuple-element.54), channel_id=1, source_target_pairs={{0,2},{1,5},{2,0},{3,7},{4,6},{5,1},{6,4},{7,3},{8,10},{9,13},{10,... | collective-permute-start | bytes 1572872 | tf_op jit(solution)/shard_map/ppermute | solution.py:95
  84.6 7.2 %collective-permute-done.11 = bf16[8,64,512]{2,1,0:T(8,128)(2,1)S(1)} collective-permute-done((bf16[8,64,512]{2,1,0:T(8,128)(2,1)S(1)}, bf16[8,64,512]{2,1,0:T(8,128)(2,1)S(1)}, u32[]{:S(2)}, u32[]{:S(2)}) %collective-permute-start.11) | collective-permute-done | bytes 524320 | tf_op jit(solution)/shard_map/ppermute | solution.py:95
  91.8 3.3 %apply_first.1 = f32[512,64]{1,0:T(8,128)S(1)} custom-call(s32[512]{0:T(512)S(1)} %broadcast_add_fusion.2.ids_ref, s32[129]{0:T(256)S(1)} %pad_add_fusion.1.plan_ref, f32[8,512]{1,0:T(8,128)S(1)} %get-tuple-element.15.own_ref, bf16[1,8,64,512]{3,2,1,0:T(8,128)(2,1)S(1)} %get-tuple-element.53.near_ref, ...), custom_call_target="tpu_custom_call" | custom-call | flops 31457280 | bytes 4194304 | tf_op jit(solution)/shard_map/apply_first/pallas_call | solution.py:456
  95.1 3.3 %apply_last.1 = (f32[4,64,64]{2,1,0:T(8,128)S(1)}, f32[64,512]{1,0:T(8,128)S(1)}, bf16[64,512]{1,0:T(8,128)(2,1)}) fusion(f32[4,64,64]{2,1,0:T(8,128)S(1)} %constant_dynamic-update-slice_fusion.1, s32[512]{0:T(512)S(1)} %broadcast_add_fusion.3.ids_ref, s32[129]{0:T(256)S(1)} %pad_add_fusion.plan_ref, f32[8,512]{1,0:T(8,128)S(1)} %get-tuple-element.15.own_ref, ...), kind=kCustom, calls=%fused_computation.30 | custom fusion | flops 31457280 | bytes 10081280 | tf_op jit(solution)/shard_map/apply_last/pallas_call | solution.py:456
  98.4 0.6 collective-permute-start.14
  99.0 0.1 collective-permute-start.19
  99.1 0.9 collective-permute-done.14
  100.0 2.3 %collective-permute-start.15 = (f32[4,64,64]{2,1,0:T(8,128)S(1)}, f32[4,64,64]{2,1,0:T(8,128)S(1)}, u32[]{:S(2)}, u32[]{:S(2)}) collective-permute-start(f32[4,64,64]{2,1,0:T(8,128)S(1)} %add.199), channel_id=1, source_target_pairs={{0,2},{2,0},{4,6},{6,4},{8,10},{10,8},{12,14},{14,12},{16,18},{18,... | collective-permute-start | bytes 196616 | tf_op jit(solution)/shard_map/ppermute | solution.py:56
  102.3 3.8 %collective-permute-done.15 = f32[4,64,64]{2,1,0:T(8,128)S(1)} collective-permute-done((f32[4,64,64]{2,1,0:T(8,128)S(1)}, f32[4,64,64]{2,1,0:T(8,128)S(1)}, u32[]{:S(2)}, u32[]{:S(2)}) %collective-permute-start.15) | collective-permute-done | bytes 65568 | tf_op jit(solution)/shard_map/ppermute | solution.py:56
  106.1 3.0 %collective-permute-start.16 = (f32[4,64,64]{2,1,0:T(8,128)S(1)}, f32[4,64,64]{2,1,0:T(8,128)S(1)}, u32[]{:S(2)}, u32[]{:S(2)}) collective-permute-start(f32[4,64,64]{2,1,0:T(8,128)S(1)} %add.200), channel_id=1, source_target_pairs={{0,4},{2,6},{4,0},{6,2},{8,12},{10,14},{12,8},{14,10},{16,20},{18,... | collective-permute-start | bytes 196616 | tf_op jit(solution)/shard_map/ppermute | solution.py:56
  109.1 3.0 %collective-permute-done.16 = f32[4,64,64]{2,1,0:T(8,128)S(1)} collective-permute-done((f32[4,64,64]{2,1,0:T(8,128)S(1)}, f32[4,64,64]{2,1,0:T(8,128)S(1)}, u32[]{:S(2)}, u32[]{:S(2)}) %collective-permute-start.16) | collective-permute-done | bytes 65568 | tf_op jit(solution)/shard_map/ppermute | solution.py:56
  112.2 3.1 %collective-permute-start.17 = (f32[4,64,64]{2,1,0:T(8,128)S(1)}, f32[4,64,64]{2,1,0:T(8,128)S(1)}, u32[]{:S(2)}, u32[]{:S(2)}) collective-permute-start(f32[4,64,64]{2,1,0:T(8,128)S(1)} %add.201), channel_id=1, source_target_pairs={{0,8},{2,10},{4,12},{6,14},{8,0},{10,2},{12,4},{14,6},{16,24},{18,... | collective-permute-start | bytes 196616 | tf_op jit(solution)/shard_map/ppermute | solution.py:56
  115.3 2.9 %collective-permute-done.17 = f32[4,64,64]{2,1,0:T(8,128)S(1)} collective-permute-done((f32[4,64,64]{2,1,0:T(8,128)S(1)}, f32[4,64,64]{2,1,0:T(8,128)S(1)}, u32[]{:S(2)}, u32[]{:S(2)}) %collective-permute-start.17) | collective-permute-done | bytes 65568 | tf_op jit(solution)/shard_map/ppermute | solution.py:56
  118.3 3.1 %collective-permute-start.18 = (f32[4,64,64]{2,1,0:T(8,128)S(1)}, f32[4,64,64]{2,1,0:T(8,128)S(1)}, u32[]{:S(2)}, u32[]{:S(2)}) collective-permute-start(f32[4,64,64]{2,1,0:T(8,128)S(1)} %add.202), channel_id=1, source_target_pairs={{0,16},{2,18},{4,20},{6,22},{8,24},{10,26},{12,28},{14,30},{16,0},... | collective-permute-start | bytes 196616 | tf_op jit(solution)/shard_map/ppermute | solution.py:56
  121.4 1.4 %unsort.1.images_ref = f32[128,512]{1,0:T(8,128)S(1)} custom-call(s32[2]{0:T(128)S(1)} %xor_multiply_fusion.first_ref, s32[1,512]{1,0:T(1,128)S(1)} %get-tuple-element.24.rank_ref, f32[128,1024]{1,0:T(8,128)S(1)} %pad_maximum_fusion.2.block_ref), custom_call_target="tpu_custom_call" | custom-call | flops 402653184 | bytes 2097152 | tf_op jit(solution)/shard_map/unsort/pallas_call | solution.py:210
  122.8 1.5 %collective-permute-done.18 = f32[4,64,64]{2,1,0:T(8,128)S(1)} collective-permute-done((f32[4,64,64]{2,1,0:T(8,128)S(1)}, f32[4,64,64]{2,1,0:T(8,128)S(1)}, u32[]{:S(2)}, u32[]{:S(2)}) %collective-permute-start.18) | collective-permute-done | bytes 65568 | tf_op jit(solution)/shard_map/ppermute | solution.py:56
  124.3 7.6 %last_step.1 = (f32[64,512]{1,0:T(8,128)}, f32[64,512]{1,0:T(8,128)}) custom-call(f32[4,64,64]{2,1,0:T(8,128)S(1)} %add.203.grams_ref, f32[64,512]{1,0:T(8,128)S(1)} %copy-done.1, f32[128,512]{1,0:T(8,128)S(1)} %unsort.1.images_ref), custom_call_target="tpu_custom_call" | custom-call | tf_op jit(solution)/shard_map/last_step/pallas_call | solution.py:534
  (62 shorter events, 1.5 us)
Async XLA Ops:
  0.6 2.5 %collective-permute-start.1 = (f32[1,64,512]{2,1,0:T(8,128)}, f32[1,64,512]{2,1,0:T(8,128)S(1)}, u32[]{:S(2)}, u32[]{:S(2)}) collective-permute-start(f32[1,64,512]{2,1,0:T(8,128)} %bitcast.45), channel_id=1, source_target_pairs={{0,1},{1,0},{2,3},{3,2},{4,5},{5,4},{6,7},{7,6},{8,9},{9,8},{10,11... | collective-permute-start | bytes 393224 | tf_op jit(solution)/shard_map/ppermute | solution.py:56
  1.9 1.2 collective-permute-start
  3.1 0.9 copy-start
  4.0 0.7 copy-start.2
  8.5 8.5 %collective-permute-start.2 = (bf16[1,80,512]{2,1,0:T(8,128)(2,1)S(1)}, bf16[1,80,512]{2,1,0:T(8,128)(2,1)S(1)}, u32[]{:S(2)}, u32[]{:S(2)}) collective-permute-start(bf16[1,80,512]{2,1,0:T(8,128)(2,1)S(1)} %bitcast.37), channel_id=1, source_target_pairs={{0,16},{1,17},{2,18},{3,19},{4,20},{5,21},{6,22},{7,23},{8,24},{9,... | collective-permute-start | bytes 245768 | tf_op jit(solution)/shard_map/ppermute | solution.py:95
  17.1 5.4 %collective-permute-start.3 = (bf16[2,80,512]{2,1,0:T(8,128)(2,1)S(1)}, bf16[2,80,512]{2,1,0:T(8,128)(2,1)S(1)}, u32[]{:S(2)}, u32[]{:S(2)}) collective-permute-start(bf16[2,80,512]{2,1,0:T(8,128)(2,1)S(1)} %pad_maximum_fusion.5), channel_id=1, source_target_pairs={{0,8},{1,3},{2,10},{3,1},{4,12},{5,7},{6,14},{7,5},{8,0},{9,11},{1... | collective-permute-start | bytes 491528 | tf_op jit(solution)/shard_map/ppermute | solution.py:95
  22.5 7.1 %collective-permute-start.4 = (bf16[4,80,512]{2,1,0:T(8,128)(2,1)S(1)}, bf16[4,80,512]{2,1,0:T(8,128)(2,1)S(1)}, u32[]{:S(2)}, u32[]{:S(2)}) collective-permute-start(bf16[4,80,512]{2,1,0:T(8,128)(2,1)S(1)} %pad_maximum_fusion.3), channel_id=1, source_target_pairs={{0,4},{1,9},{2,6},{3,11},{4,0},{5,13},{6,2},{7,15},{8,12},{9,1},{1... | collective-permute-start | bytes 983048 | tf_op jit(solution)/shard_map/ppermute | solution.py:95
  29.7 10.7 %collective-permute-start.5 = (bf16[8,80,512]{2,1,0:T(8,128)(2,1)S(1)}, bf16[8,80,512]{2,1,0:T(8,128)(2,1)S(1)}, u32[]{:S(2)}, u32[]{:S(2)}) collective-permute-start(bf16[8,80,512]{2,1,0:T(8,128)(2,1)S(1)} %get-tuple-element.51), channel_id=1, source_target_pairs={{0,2},{1,5},{2,0},{3,7},{4,6},{5,1},{6,4},{7,3},{8,10},{9,13},{10,... | collective-permute-start | bytes 1966088 | tf_op jit(solution)/shard_map/ppermute | solution.py:95
  32.0 8.6 %collective-permute-start.7 = (bf16[1,8,80,512]{3,2,1,0:T(8,128)(2,1)S(1)}, bf16[1,8,80,512]{3,2,1,0:T(8,128)(2,1)S(1)}, u32[]{:S(2)}, u32[]{:S(2)}) collective-permute-start(bf16[1,8,80,512]{3,2,1,0:T(8,128)(2,1)S(1)} %get-tuple-element.52.near_ref), channel_id=1, source_target_pairs={{0,1},{1,0},{2,3},{3,2},{4,5},{5,4},{6,7},{7,6},{8,9},{9,8},{10,11... | collective-permute-start | bytes 1966088 | tf_op jit(solution)/shard_map/ppermute | solution.py:56
  40.4 2.1 %collective-permute-start.6 = (bf16[1,8,80,512]{3,2,1,0:T(8,128)(2,1)S(1)}, bf16[1,8,80,512]{3,2,1,0:T(8,128)(2,1)S(1)}, u32[]{:S(2)}, u32[]{:S(2)}) collective-permute-start(bf16[1,8,80,512]{3,2,1,0:T(8,128)(2,1)S(1)} %bitcast.33), channel_id=1, source_target_pairs={{0,1},{1,0},{2,3},{3,2},{4,5},{5,4},{6,7},{7,6},{8,9},{9,8},{10,11... | collective-permute-start | bytes 1966088 | tf_op jit(solution)/shard_map/ppermute | solution.py:56
  60.3 34.8 %copy-start.3 = (bf16[128,64,512]{2,1,0:T(8,128)(2,1)S(1)}, bf16[128,64,512]{2,1,0:T(8,128)(2,1)}, u32[]{:S(2)}) copy-start(bf16[128,64,512]{2,1,0:T(8,128)(2,1)} %get-tuple-element.20) | copy-start | bytes 25165828
  60.3 10.3 %collective-permute-start.8 = (bf16[1,64,512]{2,1,0:T(8,128)(2,1)S(1)}, bf16[1,64,512]{2,1,0:T(8,128)(2,1)S(1)}, u32[]{:S(2)}, u32[]{:S(2)}) collective-permute-start(bf16[1,64,512]{2,1,0:T(8,128)(2,1)S(1)} %bitcast.41), channel_id=1, source_target_pairs={{0,16},{1,17},{2,18},{3,19},{4,20},{5,21},{6,22},{7,23},{8,24},{9,... | collective-permute-start | bytes 196616 | tf_op jit(solution)/shard_map/ppermute | solution.py:95
  70.7 5.0 %collective-permute-start.9 = (bf16[2,64,512]{2,1,0:T(8,128)(2,1)S(1)}, bf16[2,64,512]{2,1,0:T(8,128)(2,1)S(1)}, u32[]{:S(2)}, u32[]{:S(2)}) collective-permute-start(bf16[2,64,512]{2,1,0:T(8,128)(2,1)S(1)} %pad_maximum_fusion.6), channel_id=1, source_target_pairs={{0,8},{1,3},{2,10},{3,1},{4,12},{5,7},{6,14},{7,5},{8,0},{9,11},{1... | collective-permute-start | bytes 393224 | tf_op jit(solution)/shard_map/ppermute | solution.py:95
  75.7 6.4 %collective-permute-start.10 = (bf16[4,64,512]{2,1,0:T(8,128)(2,1)S(1)}, bf16[4,64,512]{2,1,0:T(8,128)(2,1)S(1)}, u32[]{:S(2)}, u32[]{:S(2)}) collective-permute-start(bf16[4,64,512]{2,1,0:T(8,128)(2,1)S(1)} %pad_maximum_fusion.4), channel_id=1, source_target_pairs={{0,4},{1,9},{2,6},{3,11},{4,0},{5,13},{6,2},{7,15},{8,12},{9,1},{1... | collective-permute-start | bytes 786440 | tf_op jit(solution)/shard_map/ppermute | solution.py:95
  82.3 9.5 %collective-permute-start.11 = (bf16[8,64,512]{2,1,0:T(8,128)(2,1)S(1)}, bf16[8,64,512]{2,1,0:T(8,128)(2,1)S(1)}, u32[]{:S(2)}, u32[]{:S(2)}) collective-permute-start(bf16[8,64,512]{2,1,0:T(8,128)(2,1)S(1)} %get-tuple-element.54), channel_id=1, source_target_pairs={{0,2},{1,5},{2,0},{3,7},{4,6},{5,1},{6,4},{7,3},{8,10},{9,13},{10,... | collective-permute-start | bytes 1572872 | tf_op jit(solution)/shard_map/ppermute | solution.py:95
  84.6 7.2 %collective-permute-start.13 = (bf16[1,8,64,512]{3,2,1,0:T(8,128)(2,1)S(1)}, bf16[1,8,64,512]{3,2,1,0:T(8,128)(2,1)S(1)}, u32[]{:S(2)}, u32[]{:S(2)}) collective-permute-start(bf16[1,8,64,512]{3,2,1,0:T(8,128)(2,1)S(1)} %get-tuple-element.53.near_ref), channel_id=1, source_target_pairs={{0,1},{1,0},{2,3},{3,2},{4,5},{5,4},{6,7},{7,6},{8,9},{9,8},{10,11... | collective-permute-start | bytes 1572872 | tf_op jit(solution)/shard_map/ppermute | solution.py:56
  91.8 3.4 %collective-permute-start.12 = (bf16[1,8,64,512]{3,2,1,0:T(8,128)(2,1)S(1)}, bf16[1,8,64,512]{3,2,1,0:T(8,128)(2,1)S(1)}, u32[]{:S(2)}, u32[]{:S(2)}) collective-permute-start(bf16[1,8,64,512]{3,2,1,0:T(8,128)(2,1)S(1)} %bitcast.48), channel_id=1, source_target_pairs={{0,1},{1,0},{2,3},{3,2},{4,5},{5,4},{6,7},{7,6},{8,9},{9,8},{10,11... | collective-permute-start | bytes 1572872 | tf_op jit(solution)/shard_map/ppermute | solution.py:56
  95.1 29.2 %copy-start.1 = (f32[64,512]{1,0:T(8,128)S(1)}, f32[64,512]{1,0:T(8,128)}, u32[]{:S(2)}) copy-start(f32[64,512]{1,0:T(8,128)} %start_ref.1) | copy-start | bytes 393220
  98.4 1.6 %collective-permute-start.14 = (f32[4,64,64]{2,1,0:T(8,128)S(1)}, f32[4,64,64]{2,1,0:T(8,128)S(1)}, u32[]{:S(2)}, u32[]{:S(2)}) collective-permute-start(f32[4,64,64]{2,1,0:T(8,128)S(1)} %get-tuple-element.29), channel_id=1, source_target_pairs={{0,1},{1,0},{2,3},{3,2},{4,5},{5,4},{6,7},{7,6},{8,9},{9,8},{10,11... | collective-permute-start | bytes 196616 | tf_op jit(solution)/shard_map/ppermute | solution.py:56
  99.0 22.4 %collective-permute-start.19 = (f32[1,128,512]{2,1,0:T(8,128)S(1)}, f32[1,128,512]{2,1,0:T(8,128)S(1)}, u32[]{:S(2)}, u32[]{:S(2)}) collective-permute-start(f32[1,128,512]{2,1,0:T(8,128)S(1)} %bitcast.47), channel_id=1, source_target_pairs={{0,1},{1,0},{2,3},{3,2},{4,5},{5,4},{6,7},{7,6},{8,9},{9,8},{10,11... | collective-permute-start | bytes 786440 | tf_op jit(solution)/shard_map/ppermute | solution.py:56
  100.0 6.1 %collective-permute-start.15 = (f32[4,64,64]{2,1,0:T(8,128)S(1)}, f32[4,64,64]{2,1,0:T(8,128)S(1)}, u32[]{:S(2)}, u32[]{:S(2)}) collective-permute-start(f32[4,64,64]{2,1,0:T(8,128)S(1)} %add.199), channel_id=1, source_target_pairs={{0,2},{2,0},{4,6},{6,4},{8,10},{10,8},{12,14},{14,12},{16,18},{18,... | collective-permute-start | bytes 196616 | tf_op jit(solution)/shard_map/ppermute | solution.py:56
  106.1 6.0 %collective-permute-start.16 = (f32[4,64,64]{2,1,0:T(8,128)S(1)}, f32[4,64,64]{2,1,0:T(8,128)S(1)}, u32[]{:S(2)}, u32[]{:S(2)}) collective-permute-start(f32[4,64,64]{2,1,0:T(8,128)S(1)} %add.200), channel_id=1, source_target_pairs={{0,4},{2,6},{4,0},{6,2},{8,12},{10,14},{12,8},{14,10},{16,20},{18,... | collective-permute-start | bytes 196616 | tf_op jit(solution)/shard_map/ppermute | solution.py:56
  112.2 6.1 %collective-permute-start.17 = (f32[4,64,64]{2,1,0:T(8,128)S(1)}, f32[4,64,64]{2,1,0:T(8,128)S(1)}, u32[]{:S(2)}, u32[]{:S(2)}) collective-permute-start(f32[4,64,64]{2,1,0:T(8,128)S(1)} %add.201), channel_id=1, source_target_pairs={{0,8},{2,10},{4,12},{6,14},{8,0},{10,2},{12,4},{14,6},{16,24},{18,... | collective-permute-start | bytes 196616 | tf_op jit(solution)/shard_map/ppermute | solution.py:56
  118.3 6.0 %collective-permute-start.18 = (f32[4,64,64]{2,1,0:T(8,128)S(1)}, f32[4,64,64]{2,1,0:T(8,128)S(1)}, u32[]{:S(2)}, u32[]{:S(2)}) collective-permute-start(f32[4,64,64]{2,1,0:T(8,128)S(1)} %add.202), channel_id=1, source_target_pairs={{0,16},{2,18},{4,20},{6,22},{8,24},{10,26},{12,28},{14,30},{16,0},... | collective-permute-start | bytes 196616 | tf_op jit(solution)/shard_map/ppermute | solution.py:56

commit v4 on v3

--- a/solution.py
+++ b/solution.py
@@ -56,11 +56,29 @@
     return lax.ppermute(block, axis, [(i, i ^ bit) for i in range(lax.axis_size(axis))])
 
 
-def sum_over(block, axis):
+def sum_tiles(block):
     bit = 1
-    while bit < lax.axis_size(axis):
-        block = block + swapped(block, axis, bit)
+    while bit < lax.axis_size("tile"):
+        block = block + swapped(block, "tile", bit)
         bit *= 2
+    return block
+
+
+def swap_regions(block, even, odd):
+    tiles = lax.axis_size("tile")
+    route = [
+        (region * tiles + tile, (region ^ (odd if tile % 2 else even)) * tiles + tile)
+        for region in range(lax.axis_size("region"))
+        for tile in range(tiles)
+    ]
+    return lax.ppermute(block, ("region", "tile"), route)
+
+
+def sum_regions(block):
+    bits, _ = region_orders(lax.axis_size("region"))
+    middle = len(bits) // 2
+    for even, odd in zip(bits, bits[middle:] + bits[:middle]):
+        block = block + swap_regions(block, even, odd)
     return block
 
 
@@ -84,15 +102,10 @@
 
 
 def exchange(block):
-    regions, tiles = lax.axis_size("region"), lax.axis_size("tile")
+    regions = lax.axis_size("region")
     block = block[None]
     for even, odd in zip(*region_orders(regions)):
-        route = [
-            (region * tiles + tile, (region ^ (odd if tile % 2 else even)) * tiles + tile)
-            for region in range(regions)
-            for tile in range(tiles)
-        ]
-        other = lax.ppermute(block, ("region", "tile"), route)
+        other = swap_regions(block, even, odd)
         if 2 * block.shape[0] == regions:
             return block, other
         block = jnp.concatenate([block, other], axis=0)
@@ -461,7 +474,7 @@
         scratch_shapes=scratch,
         compiler_params=pltpu.CompilerParams(vmem_limit_bytes=VMEM),
         cost_estimate=pl.CostEstimate(
-            flops=work * (120 if build else 60), bytes_accessed=8 * work, transcendentals=0
+            flops=work * (18000 if build else 9000), bytes_accessed=8 * work, transcendentals=0
         ),
         name=("build" if build else "apply") + ("_last" if wanted else "_first"),
     )(*operands)
@@ -566,6 +579,8 @@
     plans, tiles = [], []
     total = None
     for part, block in enumerate(exchange(message)):
+        if part:
+            block, total = lax.optimization_barrier((block, total))
         near, far = halves(block, "tile")
         inside = slot_region[:, part * half_regions : (part + 1) * half_regions]
         plans.append(plan_blocks(own[1], near, far, inside, here, flags, columns, capacity))
@@ -576,13 +591,15 @@
     image_rounded, grams = others
 
     for part, block in enumerate(exchange(image_rounded)):
+        if part:
+            block, total = lax.optimization_barrier((block, total))
         near, far = halves(block, "tile")
         finish = None if part == 0 else (total, image, scale, ("mixed",))
         total, *others = run(plans[part], near=near, far=far, tiles=tiles[part], finish=finish)
     second, cross = total, others[1]
 
     grams = jnp.concatenate([grams, cross], axis=0)
-    grams = sum_over(sum_over(grams, "tile"), "region")
+    grams = sum_regions(sum_tiles(grams))
     near, far = halves(jnp.concatenate([image, second], axis=0), "tile")
     images = unsort(first, rank, jnp.concatenate([*near, *far], axis=1))
     return last_step(grams, innovations, images)

time: 132 us -> 122 us (0.924)
  waiting for transfers between devices: 56 us -> 50.1 us
  starting transfers between devices: 32.3 us -> 27.4 us
    ppermute x12 -> x8, starting transfers between devices: 12.8 us -> 1.93 us  [swapped(): lax.ppermute(block, axis, [(i, i ^ bit) for i in range(lax.axis_size(axis...]
    ppermute x12 -> x8, waiting for transfers between devices: 14.7 us -> 4.94 us  [swapped(): lax.ppermute(block, axis, [(i, i ^ bit) for i in range(lax.axis_size(axis...]
    ppermute x8 -> x12, starting transfers between devices: 19.5 us -> 25.4 us  [swap_regions(): return lax.ppermute(block, ('region', 'tile'), route)]
    ppermute x8 -> x12, waiting for transfers between devices: 41.3 us -> 45.2 us  [swap_regions(): return lax.ppermute(block, ('region', 'tile'), route)]
  transfers between devices with their start and end apart: 20 -> 20, of which waited for: 15 -> 15; matrix products, arithmetic and copies ran while one was open for 3% -> 5% of each run, Pallas kernels for 4% -> 9%
where the time goes in v4:
time: 122 us; the launch traced here: 121 us
  waiting for transfers between devices  50.1 us (41%)
  Pallas kernels  29 us (24%)
  starting transfers between devices  27.4 us (22%)
  other arithmetic  9.3 us (8%)
  local copies, waits for them, and re-layouts  4.06 us (3%)
    ppermute x12, waiting for transfers between devices, swap_regions(): return lax.ppermute(block, ('region', 'tile'), route)  45.2 us
    ppermute x12, starting transfers between devices, swap_regions(): return lax.ppermute(block, ('region', 'tile'), route)  25.4 us
    pallas_call x3, Pallas kernels, run_tiles(): pl.pallas_call(functools.partial(tiles_kernel, build, wanted), out_shape=...  16.1 us
    pallas_call x1, Pallas kernels, last_step(): pl.pallas_call(last_kernel, out_shape=(jax.ShapeDtypeStruct(start.shape,...  7.64 us
    ppermute x8, waiting for transfers between devices, swapped(): lax.ppermute(block, axis, [(i, i ^ bit) for i in range(lax.axis_size(axis...  4.94 us
    pallas_call x1, Pallas kernels, sort_region(): pl.pallas_call(sort_kernel, out_shape=(jax.ShapeDtypeStruct((columns + EX...  3.86 us
    pallas_call x1, other arithmetic, run_tiles(): pl.pallas_call(functools.partial(tiles_kernel, build, wanted), out_shape=...  3.25 us
  transfers between devices with their start and end apart: 20, of which 15 were waited for; matrix products, arithmetic and copies ran while one was open for 5% of the time, Pallas kernels for 9%

profile of v4, /device:TPU:0, one launch (start us, length us, event | category | flops | bytes accessed | tf_op | source)
XLA Modules:
  0.0 120.8 jit_solution(2691656846373059667)
XLA Ops:
  0.6 0.5 collective-permute-start.1
  1.1 0.7 maximum_bitcast_fusion.near_ref
  1.9 0.1 collective-permute-start
  2.0 1.2 %gather_fusion = s32[2,16]{1,0:T(2,128)S(1)} fusion(s32[2,16]{1,0:T(2,128)} %constant.77.clone, s32[1024]{0:T(1024)S(1)} %pad_clamp_fusion), kind=kCustom, calls=%fused_computation | custom fusion | bytes 264 | tf_op jit(solution)/shard_map/gather | solution.py:564
  3.3 0.9 copy-done
  4.2 0.7 copy-done.2
  4.8 3.9 %sort_region.1 = (bf16[80,512]{1,0:T(8,128)(2,1)S(1)}, f32[8,512]{1,0:T(8,128)S(1)}, f32[64,512]{1,0:T(8,128)S(1)}, s32[1,512]{1,0:T(1,128)S(1)}) custom-call(s32[2]{0:T(128)S(1)} %xor_multiply_fusion.first_ref, s32[1,7]{1,0:T(1,128)S(1)} %copy-done.2, f32[1,4,512]{2,1,0:T(4,128)S(1)} %maximum_bitcast_fusion.near_ref, ...), custom_call_target="tpu_custom_call" | custom-call | flops 226492416 | bytes 2097152 | tf_op jit(solution)/shard_map/sort_region/pallas_call | solution.py:194
  8.7 4.1 %collective-permute-start.2 = (bf16[1,80,512]{2,1,0:T(8,128)(2,1)S(1)}, bf16[1,80,512]{2,1,0:T(8,128)(2,1)S(1)}, u32[]{:S(2)}, u32[]{:S(2)}) collective-permute-start(bf16[1,80,512]{2,1,0:T(8,128)(2,1)S(1)} %bitcast.37), channel_id=1, source_target_pairs={{0,16},{1,17},{2,18},{3,19},{4,20},{5,21},{6,22},{7,23},{8,24},{9,... | collective-permute-start | bytes 245768 | tf_op jit(solution)/shard_map/ppermute | solution.py:74
  12.8 4.4 %collective-permute-done.2 = bf16[1,80,512]{2,1,0:T(8,128)(2,1)S(1)} collective-permute-done((bf16[1,80,512]{2,1,0:T(8,128)(2,1)S(1)}, bf16[1,80,512]{2,1,0:T(8,128)(2,1)S(1)}, u32[]{:S(2)}, u32[]{:S(2)}) %collective-permute-start.2) | collective-permute-done | bytes 81952 | tf_op jit(solution)/shard_map/ppermute | solution.py:74
  17.2 0.8 collective-permute-start.3
  18.0 4.6 %collective-permute-done.3 = bf16[2,80,512]{2,1,0:T(8,128)(2,1)S(1)} collective-permute-done((bf16[2,80,512]{2,1,0:T(8,128)(2,1)S(1)}, bf16[2,80,512]{2,1,0:T(8,128)(2,1)S(1)}, u32[]{:S(2)}, u32[]{:S(2)}) %collective-permute-start.3) | collective-permute-done | bytes 163872 | tf_op jit(solution)/shard_map/ppermute | solution.py:74
  22.6 1.7 %collective-permute-start.4 = (bf16[4,80,512]{2,1,0:T(8,128)(2,1)S(1)}, bf16[4,80,512]{2,1,0:T(8,128)(2,1)S(1)}, u32[]{:S(2)}, u32[]{:S(2)}) collective-permute-start(bf16[4,80,512]{2,1,0:T(8,128)(2,1)S(1)} %pad_maximum_fusion.3), channel_id=1, source_target_pairs={{0,4},{1,9},{2,6},{3,11},{4,0},{5,13},{6,2},{7,15},{8,12},{9,1},{1... | collective-permute-start | bytes 983048 | tf_op jit(solution)/shard_map/ppermute | solution.py:74
  24.4 5.3 %collective-permute-done.4 = bf16[4,80,512]{2,1,0:T(8,128)(2,1)S(1)} collective-permute-done((bf16[4,80,512]{2,1,0:T(8,128)(2,1)S(1)}, bf16[4,80,512]{2,1,0:T(8,128)(2,1)S(1)}, u32[]{:S(2)}, u32[]{:S(2)}) %collective-permute-start.4) | collective-permute-done | bytes 327712 | tf_op jit(solution)/shard_map/ppermute | solution.py:74
  29.8 0.1 fusion.12
  30.0 0.1 fusion.6
  30.2 0.1 copy.37
  30.3 0.1 copy.38
  30.4 1.6 %collective-permute-start.5 = (bf16[8,80,512]{2,1,0:T(8,128)(2,1)S(1)}, bf16[8,80,512]{2,1,0:T(8,128)(2,1)S(1)}, u32[]{:S(2)}, u32[]{:S(2)}) collective-permute-start(bf16[8,80,512]{2,1,0:T(8,128)(2,1)S(1)} %get-tuple-element.56), channel_id=1, source_target_pairs={{0,2},{1,5},{2,0},{3,7},{4,6},{5,1},{6,4},{7,3},{8,10},{9,13},{10,... | collective-permute-start | bytes 1966088 | tf_op jit(solution)/shard_map/ppermute | solution.py:74
  32.0 0.1 convert_add_fusion.2
  32.4 0.1 copy.27
  32.6 0.1 and.129
  32.7 0.2 convert_reduce_fusion.3
  32.9 0.6 fusion.19
  33.5 0.1 select_reduce_fusion.5
  33.6 0.1 convert_reduce_fusion.1
  33.7 0.1 select_reduce_fusion.3
  33.9 0.3 select_reduce_fusion.1
  34.2 0.7 pad_add_fusion.plan_ref
  34.9 6.0 %build_first.1 = (bf16[128,64,512]{2,1,0:T(8,128)(2,1)}, f32[512,64]{1,0:T(8,128)S(1)}) custom-call(s32[512]{0:T(512)S(1)} %broadcast_add_fusion.3.ids_ref, s32[129]{0:T(256)S(1)} %pad_add_fusion.plan_ref, f32[8,512]{1,0:T(8,128)S(1)} %get-tuple-element.19.own_ref, bf16[1,8,80,512]{3,2,1,0:T(8,128)(2,1)S(1)} %get-tuple-element.55.near_ref, ...), custom_call_target="tpu_custom_call" | custom-call | flops 9437184000 | bytes 4194304 | tf_op jit(solution)/shard_map/build_first/pallas_call | solution.py:469
  41.0 0.5 collective-permute-start.7
  41.5 1.7 %collective-permute-done.7.far_ref = bf16[1,8,80,512]{3,2,1,0:T(8,128)(2,1)S(1)} collective-permute-done((bf16[1,8,80,512]{3,2,1,0:T(8,128)(2,1)S(1)}, bf16[1,8,80,512]{3,2,1,0:T(8,128)(2,1)S(1)}, u32[]{:S(2)}, u32[]{:S(2)}) %collective-permute-start.7) | collective-permute-done | bytes 655392 | tf_op jit(solution)/shard_map/ppermute | solution.py:56
  43.6 0.1 copy.30
  43.8 0.1 and.136
  43.9 0.2 convert_reduce_fusion.2
  44.1 0.6 fusion.17
  44.7 0.1 select_reduce_fusion.4
  44.8 0.1 convert_reduce_fusion
  44.9 0.1 select_reduce_fusion.2
  45.1 0.3 select_reduce_fusion
  45.4 0.7 pad_add_fusion.1.plan_ref
  46.1 6.5 %build_last.1 = (bf16[128,64,512]{2,1,0:T(8,128)(2,1)}, f32[64,512]{1,0:T(8,128)S(1)}, bf16[64,512]{1,0:T(8,128)(2,1)S(1)}, f32[3,64,64]{2,1,0:T(8,128)S(1)}) custom-call(s32[512]{0:T(512)S(1)} %broadcast_add_fusion.2.ids_ref, s32[129]{0:T(256)S(1)} %pad_add_fusion.1.plan_ref, f32[8,512]{1,0:T(8,128)S(1)} %get-tuple-element.19.own_ref, ...), custom_call_target="tpu_custom_call" | custom-call | flops 9437184000 | bytes 4194304 | tf_op jit(solution)/shard_map/build_last/pallas_call | solution.py:469
  52.6 6.4 %collective-permute-start.8 = (bf16[1,64,512]{2,1,0:T(8,128)(2,1)S(1)}, bf16[1,64,512]{2,1,0:T(8,128)(2,1)S(1)}, u32[]{:S(2)}, u32[]{:S(2)}) collective-permute-start(bf16[1,64,512]{2,1,0:T(8,128)(2,1)S(1)} %bitcast.41), channel_id=1, source_target_pairs={{0,16},{1,17},{2,18},{3,19},{4,20},{5,21},{6,22},{7,23},{8,24},{9,... | collective-permute-start | bytes 196616 | tf_op jit(solution)/shard_map/ppermute | solution.py:74
  59.0 2.7 %collective-permute-done.8 = bf16[1,64,512]{2,1,0:T(8,128)(2,1)S(1)} collective-permute-done((bf16[1,64,512]{2,1,0:T(8,128)(2,1)S(1)}, bf16[1,64,512]{2,1,0:T(8,128)(2,1)S(1)}, u32[]{:S(2)}, u32[]{:S(2)}) %collective-permute-start.8) | collective-permute-done | bytes 65568 | tf_op jit(solution)/shard_map/ppermute | solution.py:74
  61.8 5.0 %collective-permute-done.9 = bf16[2,64,512]{2,1,0:T(8,128)(2,1)S(1)} collective-permute-done((bf16[2,64,512]{2,1,0:T(8,128)(2,1)S(1)}, bf16[2,64,512]{2,1,0:T(8,128)(2,1)S(1)}, u32[]{:S(2)}, u32[]{:S(2)}) %collective-permute-start.9) | collective-permute-done | bytes 131104 | tf_op jit(solution)/shard_map/ppermute | solution.py:74
  66.8 2.6 %collective-permute-start.10 = (bf16[4,64,512]{2,1,0:T(8,128)(2,1)S(1)}, bf16[4,64,512]{2,1,0:T(8,128)(2,1)S(1)}, u32[]{:S(2)}, u32[]{:S(2)}) collective-permute-start(bf16[4,64,512]{2,1,0:T(8,128)(2,1)S(1)} %pad_maximum_fusion.4), channel_id=1, source_target_pairs={{0,4},{1,9},{2,6},{3,11},{4,0},{5,13},{6,2},{7,15},{8,12},{9,1},{1... | collective-permute-start | bytes 786440 | tf_op jit(solution)/shard_map/ppermute | solution.py:74
  69.4 4.4 %collective-permute-done.10 = bf16[4,64,512]{2,1,0:T(8,128)(2,1)S(1)} collective-permute-done((bf16[4,64,512]{2,1,0:T(8,128)(2,1)S(1)}, bf16[4,64,512]{2,1,0:T(8,128)(2,1)S(1)}, u32[]{:S(2)}, u32[]{:S(2)}) %collective-permute-start.10) | collective-permute-done | bytes 262176 | tf_op jit(solution)/shard_map/ppermute | solution.py:74
  73.9 1.4 %collective-permute-start.11 = (bf16[8,64,512]{2,1,0:T(8,128)(2,1)S(1)}, bf16[8,64,512]{2,1,0:T(8,128)(2,1)S(1)}, u32[]{:S(2)}, u32[]{:S(2)}) collective-permute-start(bf16[8,64,512]{2,1,0:T(8,128)(2,1)S(1)} %get-tuple-element.58), channel_id=1, source_target_pairs={{0,2},{1,5},{2,0},{3,7},{4,6},{5,1},{6,4},{7,3},{8,10},{9,13},{10,... | collective-permute-start | bytes 1572872 | tf_op jit(solution)/shard_map/ppermute | solution.py:74
  75.3 0.5 collective-permute-done.12.far_ref
  75.8 3.6 %apply_first.1 = f32[512,64]{1,0:T(8,128)S(1)} custom-call(s32[512]{0:T(512)S(1)} %broadcast_add_fusion.3.ids_ref, s32[129]{0:T(256)S(1)} %pad_add_fusion.plan_ref, f32[8,512]{1,0:T(8,128)S(1)} %get-tuple-element.19.own_ref, bf16[1,8,64,512]{3,2,1,0:T(8,128)(2,1)S(1)} %get-tuple-element.57.near_ref, ...), custom_call_target="tpu_custom_call" | custom-call | flops 4718592000 | bytes 4194304 | tf_op jit(solution)/shard_map/apply_first/pallas_call | solution.py:469
  79.4 3.8 %collective-permute-done.11 = bf16[8,64,512]{2,1,0:T(8,128)(2,1)S(1)} collective-permute-done((bf16[8,64,512]{2,1,0:T(8,128)(2,1)S(1)}, bf16[8,64,512]{2,1,0:T(8,128)(2,1)S(1)}, u32[]{:S(2)}, u32[]{:S(2)}) %collective-permute-start.11) | collective-permute-done | bytes 524320 | tf_op jit(solution)/shard_map/ppermute | solution.py:74
  83.2 1.9 %collective-permute-done.13 = bf16[1,8,64,512]{3,2,1,0:T(8,128)(2,1)S(1)} collective-permute-done((bf16[1,8,64,512]{3,2,1,0:T(8,128)(2,1)S(1)}, bf16[1,8,64,512]{3,2,1,0:T(8,128)(2,1)S(1)}, u32[]{:S(2)}, u32[]{:S(2)}) %collective-permute-start.13) | collective-permute-done | bytes 524320 | tf_op jit(solution)/shard_map/ppermute | solution.py:56
  85.1 3.3 %apply_last.1 = (f32[4,64,64]{2,1,0:T(8,128)S(1)}, f32[64,512]{1,0:T(8,128)S(1)}, bf16[64,512]{1,0:T(8,128)(2,1)}) fusion(f32[4,64,64]{2,1,0:T(8,128)S(1)} %constant_dynamic-update-slice_fusion.1, s32[512]{0:T(512)S(1)} %broadcast_add_fusion.2.ids_ref, s32[129]{0:T(256)S(1)} %pad_add_fusion.1.plan_ref, f32[8,512]{1,0:T(8,128)S(1)} %get-tuple-element.19.own_ref, ...), kind=kCustom, calls=%fused_computation.30 | custom fusion | flops 4718592000 | bytes 10081280 | tf_op jit(solution)/shard_map/apply_last/pallas_call | solution.py:469
  88.4 0.2 collective-permute-start.14
  88.6 0.4 collective-permute-start.19
  89.0 0.8 collective-permute-done.14
  89.8 2.9 %collective-permute-start.15 = (f32[4,64,64]{2,1,0:T(8,128)S(1)}, f32[4,64,64]{2,1,0:T(8,128)S(1)}, u32[]{:S(2)}, u32[]{:S(2)}) collective-permute-start(f32[4,64,64]{2,1,0:T(8,128)S(1)} %add.199), channel_id=1, source_target_pairs={{0,16},{1,5},{2,18},{3,7},{4,20},{5,1},{6,22},{7,3},{8,24},{9,13},... | collective-permute-start | bytes 196616 | tf_op jit(solution)/shard_map/ppermute | solution.py:74
  92.7 4.5 %collective-permute-done.15 = f32[4,64,64]{2,1,0:T(8,128)S(1)} collective-permute-done((f32[4,64,64]{2,1,0:T(8,128)S(1)}, f32[4,64,64]{2,1,0:T(8,128)S(1)}, u32[]{:S(2)}, u32[]{:S(2)}) %collective-permute-start.15) | collective-permute-done | bytes 65568 | tf_op jit(solution)/shard_map/ppermute | solution.py:74
  97.2 5.8 %collective-permute-done.16 = f32[4,64,64]{2,1,0:T(8,128)S(1)} collective-permute-done((f32[4,64,64]{2,1,0:T(8,128)S(1)}, f32[4,64,64]{2,1,0:T(8,128)S(1)}, u32[]{:S(2)}, u32[]{:S(2)}) %collective-permute-start.16) | collective-permute-done | bytes 65568 | tf_op jit(solution)/shard_map/ppermute | solution.py:74
  103.0 1.7 %collective-permute-start.17 = (f32[4,64,64]{2,1,0:T(8,128)S(1)}, f32[4,64,64]{2,1,0:T(8,128)S(1)}, u32[]{:S(2)}, u32[]{:S(2)}) collective-permute-start(f32[4,64,64]{2,1,0:T(8,128)S(1)} %add.201), channel_id=1, source_target_pairs={{0,4},{1,17},{2,6},{3,19},{4,0},{5,21},{6,2},{7,23},{8,12},{9,25},... | collective-permute-start | bytes 196616 | tf_op jit(solution)/shard_map/ppermute | solution.py:74
  104.7 3.3 %collective-permute-done.17 = f32[4,64,64]{2,1,0:T(8,128)S(1)} collective-permute-done((f32[4,64,64]{2,1,0:T(8,128)S(1)}, f32[4,64,64]{2,1,0:T(8,128)S(1)}, u32[]{:S(2)}, u32[]{:S(2)}) %collective-permute-start.17) | collective-permute-done | bytes 65568 | tf_op jit(solution)/shard_map/ppermute | solution.py:74
  108.0 2.1 %collective-permute-start.18 = (f32[4,64,64]{2,1,0:T(8,128)S(1)}, f32[4,64,64]{2,1,0:T(8,128)S(1)}, u32[]{:S(2)}, u32[]{:S(2)}) collective-permute-start(f32[4,64,64]{2,1,0:T(8,128)S(1)} %add.202), channel_id=1, source_target_pairs={{0,2},{1,9},{2,0},{3,11},{4,6},{5,13},{6,4},{7,15},{8,10},{9,1},{1... | collective-permute-start | bytes 196616 | tf_op jit(solution)/shard_map/ppermute | solution.py:74
  110.2 1.4 %unsort.1.images_ref = f32[128,512]{1,0:T(8,128)S(1)} custom-call(s32[2]{0:T(128)S(1)} %xor_multiply_fusion.first_ref, s32[1,512]{1,0:T(1,128)S(1)} %get-tuple-element.32.rank_ref, f32[128,1024]{1,0:T(8,128)S(1)} %pad_maximum_fusion.2.block_ref), custom_call_target="tpu_custom_call" | custom-call | flops 402653184 | bytes 2097152 | tf_op jit(solution)/shard_map/unsort/pallas_call | solution.py:223
  111.6 1.5 %collective-permute-done.18 = f32[4,64,64]{2,1,0:T(8,128)S(1)} collective-permute-done((f32[4,64,64]{2,1,0:T(8,128)S(1)}, f32[4,64,64]{2,1,0:T(8,128)S(1)}, u32[]{:S(2)}, u32[]{:S(2)}) %collective-permute-start.18) | collective-permute-done | bytes 65568 | tf_op jit(solution)/shard_map/ppermute | solution.py:74
  113.2 7.6 %last_step.1 = (f32[64,512]{1,0:T(8,128)}, f32[64,512]{1,0:T(8,128)}) custom-call(f32[4,64,64]{2,1,0:T(8,128)S(1)} %add.203.grams_ref, f32[64,512]{1,0:T(8,128)S(1)} %copy-done.1, f32[128,512]{1,0:T(8,128)S(1)} %unsort.1.images_ref), custom_call_target="tpu_custom_call" | custom-call | tf_op jit(solution)/shard_map/last_step/pallas_call | solution.py:547
  (69 shorter events, 2.0 us)
Async XLA Ops:
  0.6 2.6 %collective-permute-start.1 = (f32[1,64,512]{2,1,0:T(8,128)}, f32[1,64,512]{2,1,0:T(8,128)S(1)}, u32[]{:S(2)}, u32[]{:S(2)}) collective-permute-start(f32[1,64,512]{2,1,0:T(8,128)} %bitcast.45), channel_id=1, source_target_pairs={{0,1},{1,0},{2,3},{3,2},{4,5},{5,4},{6,7},{7,6},{8,9},{9,8},{10,11... | collective-permute-start | bytes 393224 | tf_op jit(solution)/shard_map/ppermute | solution.py:56
  1.9 1.4 %collective-permute-start = (f32[1,4,512]{2,1,0:T(4,128)S(1)}, f32[1,4,512]{2,1,0:T(4,128)S(1)}, u32[]{:S(2)}, u32[]{:S(2)}) collective-permute-start(f32[1,4,512]{2,1,0:T(4,128)S(1)} %maximum_bitcast_fusion.near_ref), channel_id=1, source_target_pairs={{0,1},{1,0},{2,3},{3,2},{4,5},{5,4},{6,7},{7,6},{8,9},{9,8},{10,11... | collective-permute-start | bytes 24584 | tf_op jit(solution)/shard_map/ppermute | solution.py:56
  3.3 0.9 copy-start
  4.2 0.7 copy-start.2
  8.7 8.5 %collective-permute-start.2 = (bf16[1,80,512]{2,1,0:T(8,128)(2,1)S(1)}, bf16[1,80,512]{2,1,0:T(8,128)(2,1)S(1)}, u32[]{:S(2)}, u32[]{:S(2)}) collective-permute-start(bf16[1,80,512]{2,1,0:T(8,128)(2,1)S(1)} %bitcast.37), channel_id=1, source_target_pairs={{0,16},{1,17},{2,18},{3,19},{4,20},{5,21},{6,22},{7,23},{8,24},{9,... | collective-permute-start | bytes 245768 | tf_op jit(solution)/shard_map/ppermute | solution.py:74
  17.2 5.4 %collective-permute-start.3 = (bf16[2,80,512]{2,1,0:T(8,128)(2,1)S(1)}, bf16[2,80,512]{2,1,0:T(8,128)(2,1)S(1)}, u32[]{:S(2)}, u32[]{:S(2)}) collective-permute-start(bf16[2,80,512]{2,1,0:T(8,128)(2,1)S(1)} %pad_maximum_fusion.5), channel_id=1, source_target_pairs={{0,8},{1,3},{2,10},{3,1},{4,12},{5,7},{6,14},{7,5},{8,0},{9,11},{1... | collective-permute-start | bytes 491528 | tf_op jit(solution)/shard_map/ppermute | solution.py:74
  22.6 7.1 %collective-permute-start.4 = (bf16[4,80,512]{2,1,0:T(8,128)(2,1)S(1)}, bf16[4,80,512]{2,1,0:T(8,128)(2,1)S(1)}, u32[]{:S(2)}, u32[]{:S(2)}) collective-permute-start(bf16[4,80,512]{2,1,0:T(8,128)(2,1)S(1)} %pad_maximum_fusion.3), channel_id=1, source_target_pairs={{0,4},{1,9},{2,6},{3,11},{4,0},{5,13},{6,2},{7,15},{8,12},{9,1},{1... | collective-permute-start | bytes 983048 | tf_op jit(solution)/shard_map/ppermute | solution.py:74
  29.9 2.2 %collective-permute-start.6 = (bf16[1,8,80,512]{3,2,1,0:T(8,128)(2,1)S(1)}, bf16[1,8,80,512]{3,2,1,0:T(8,128)(2,1)S(1)}, u32[]{:S(2)}, u32[]{:S(2)}) collective-permute-start(bf16[1,8,80,512]{3,2,1,0:T(8,128)(2,1)S(1)} %get-tuple-element.55.near_ref), channel_id=1, source_target_pairs={{0,1},{1,0},{2,3},{3,2},{4,5},{5,4},{6,7},{7,6},{8,9},{9,8},{10,11... | collective-permute-start | bytes 1966088 | tf_op jit(solution)/shard_map/ppermute | solution.py:56
  30.4 10.6 %collective-permute-start.5 = (bf16[8,80,512]{2,1,0:T(8,128)(2,1)S(1)}, bf16[8,80,512]{2,1,0:T(8,128)(2,1)S(1)}, u32[]{:S(2)}, u32[]{:S(2)}) collective-permute-start(bf16[8,80,512]{2,1,0:T(8,128)(2,1)S(1)} %get-tuple-element.56), channel_id=1, source_target_pairs={{0,2},{1,5},{2,0},{3,7},{4,6},{5,1},{6,4},{7,3},{8,10},{9,13},{10,... | collective-permute-start | bytes 1966088 | tf_op jit(solution)/shard_map/ppermute | solution.py:74
  41.0 2.3 %collective-permute-start.7 = (bf16[1,8,80,512]{3,2,1,0:T(8,128)(2,1)S(1)}, bf16[1,8,80,512]{3,2,1,0:T(8,128)(2,1)S(1)}, u32[]{:S(2)}, u32[]{:S(2)}) collective-permute-start(bf16[1,8,80,512]{3,2,1,0:T(8,128)(2,1)S(1)} %bitcast.33), channel_id=1, source_target_pairs={{0,1},{1,0},{2,3},{3,2},{4,5},{5,4},{6,7},{7,6},{8,9},{9,8},{10,11... | collective-permute-start | bytes 1966088 | tf_op jit(solution)/shard_map/ppermute | solution.py:56
  52.6 9.1 %collective-permute-start.8 = (bf16[1,64,512]{2,1,0:T(8,128)(2,1)S(1)}, bf16[1,64,512]{2,1,0:T(8,128)(2,1)S(1)}, u32[]{:S(2)}, u32[]{:S(2)}) collective-permute-start(bf16[1,64,512]{2,1,0:T(8,128)(2,1)S(1)} %bitcast.41), channel_id=1, source_target_pairs={{0,16},{1,17},{2,18},{3,19},{4,20},{5,21},{6,22},{7,23},{8,24},{9,... | collective-permute-start | bytes 196616 | tf_op jit(solution)/shard_map/ppermute | solution.py:74
  61.7 5.0 %collective-permute-start.9 = (bf16[2,64,512]{2,1,0:T(8,128)(2,1)S(1)}, bf16[2,64,512]{2,1,0:T(8,128)(2,1)S(1)}, u32[]{:S(2)}, u32[]{:S(2)}) collective-permute-start(bf16[2,64,512]{2,1,0:T(8,128)(2,1)S(1)} %pad_maximum_fusion.6), channel_id=1, source_target_pairs={{0,8},{1,3},{2,10},{3,1},{4,12},{5,7},{6,14},{7,5},{8,0},{9,11},{1... | collective-permute-start | bytes 393224 | tf_op jit(solution)/shard_map/ppermute | solution.py:74
  66.8 7.0 %collective-permute-start.10 = (bf16[4,64,512]{2,1,0:T(8,128)(2,1)S(1)}, bf16[4,64,512]{2,1,0:T(8,128)(2,1)S(1)}, u32[]{:S(2)}, u32[]{:S(2)}) collective-permute-start(bf16[4,64,512]{2,1,0:T(8,128)(2,1)S(1)} %pad_maximum_fusion.4), channel_id=1, source_target_pairs={{0,4},{1,9},{2,6},{3,11},{4,0},{5,13},{6,2},{7,15},{8,12},{9,1},{1... | collective-permute-start | bytes 786440 | tf_op jit(solution)/shard_map/ppermute | solution.py:74
  73.8 11.3 %slice-start = ((s8[8388608]{0:T(1024)(128)(4,1)}), s8[4194304]{0:T(1024)(128)(4,1)S(1)}, s32[]{:S(2)}) async-start(s8[8388608]{0:T(1024)(128)(4,1)} %bitcast.62), calls=%async_computation | async-start | bytes 8388608
  73.8 2.0 %collective-permute-start.12 = (bf16[1,8,64,512]{3,2,1,0:T(8,128)(2,1)S(1)}, bf16[1,8,64,512]{3,2,1,0:T(8,128)(2,1)S(1)}, u32[]{:S(2)}, u32[]{:S(2)}) collective-permute-start(bf16[1,8,64,512]{3,2,1,0:T(8,128)(2,1)S(1)} %get-tuple-element.57.near_ref), channel_id=1, source_target_pairs={{0,1},{1,0},{2,3},{3,2},{4,5},{5,4},{6,7},{7,6},{8,9},{9,8},{10,11... | collective-permute-start | bytes 1572872 | tf_op jit(solution)/shard_map/ppermute | solution.py:56
  73.9 9.2 %collective-permute-start.11 = (bf16[8,64,512]{2,1,0:T(8,128)(2,1)S(1)}, bf16[8,64,512]{2,1,0:T(8,128)(2,1)S(1)}, u32[]{:S(2)}, u32[]{:S(2)}) collective-permute-start(bf16[8,64,512]{2,1,0:T(8,128)(2,1)S(1)} %get-tuple-element.58), channel_id=1, source_target_pairs={{0,2},{1,5},{2,0},{3,7},{4,6},{5,1},{6,4},{7,3},{8,10},{9,13},{10,... | collective-permute-start | bytes 1572872 | tf_op jit(solution)/shard_map/ppermute | solution.py:74
  75.8 9.3 %slice-start.1 = ((s8[8388608]{0:T(1024)(128)(4,1)}), s8[4194304]{0:T(1024)(128)(4,1)S(1)}, s32[]{:S(2)}) async-start(s8[8388608]{0:T(1024)(128)(4,1)} %bitcast.62), calls=%async_computation.1 | async-start | bytes 8388608
  83.2 1.9 %collective-permute-start.13 = (bf16[1,8,64,512]{3,2,1,0:T(8,128)(2,1)S(1)}, bf16[1,8,64,512]{3,2,1,0:T(8,128)(2,1)S(1)}, u32[]{:S(2)}, u32[]{:S(2)}) collective-permute-start(bf16[1,8,64,512]{3,2,1,0:T(8,128)(2,1)S(1)} %bitcast.60), channel_id=1, source_target_pairs={{0,1},{1,0},{2,3},{3,2},{4,5},{5,4},{6,7},{7,6},{8,9},{9,8},{10,11... | collective-permute-start | bytes 1572872 | tf_op jit(solution)/shard_map/ppermute | solution.py:56
  85.1 28.1 %copy-start.1 = (f32[64,512]{1,0:T(8,128)S(1)}, f32[64,512]{1,0:T(8,128)}, u32[]{:S(2)}) copy-start(f32[64,512]{1,0:T(8,128)} %start_ref.1) | copy-start | bytes 393220
  88.4 1.4 %collective-permute-start.14 = (f32[4,64,64]{2,1,0:T(8,128)S(1)}, f32[4,64,64]{2,1,0:T(8,128)S(1)}, u32[]{:S(2)}, u32[]{:S(2)}) collective-permute-start(f32[4,64,64]{2,1,0:T(8,128)S(1)} %get-tuple-element.37), channel_id=1, source_target_pairs={{0,1},{1,0},{2,3},{3,2},{4,5},{5,4},{6,7},{7,6},{8,9},{9,8},{10,11... | collective-permute-start | bytes 196616 | tf_op jit(solution)/shard_map/ppermute | solution.py:56
  88.6 21.6 %collective-permute-start.19 = (f32[1,128,512]{2,1,0:T(8,128)S(1)}, f32[1,128,512]{2,1,0:T(8,128)S(1)}, u32[]{:S(2)}, u32[]{:S(2)}) collective-permute-start(f32[1,128,512]{2,1,0:T(8,128)S(1)} %bitcast.47), channel_id=1, source_target_pairs={{0,1},{1,0},{2,3},{3,2},{4,5},{5,4},{6,7},{7,6},{8,9},{9,8},{10,11... | collective-permute-start | bytes 786440 | tf_op jit(solution)/shard_map/ppermute | solution.py:56
  89.8 7.3 %collective-permute-start.15 = (f32[4,64,64]{2,1,0:T(8,128)S(1)}, f32[4,64,64]{2,1,0:T(8,128)S(1)}, u32[]{:S(2)}, u32[]{:S(2)}) collective-permute-start(f32[4,64,64]{2,1,0:T(8,128)S(1)} %add.199), channel_id=1, source_target_pairs={{0,16},{1,5},{2,18},{3,7},{4,20},{5,1},{6,22},{7,3},{8,24},{9,13},... | collective-permute-start | bytes 196616 | tf_op jit(solution)/shard_map/ppermute | solution.py:74
  97.1 5.8 %collective-permute-start.16 = (f32[4,64,64]{2,1,0:T(8,128)S(1)}, f32[4,64,64]{2,1,0:T(8,128)S(1)}, u32[]{:S(2)}, u32[]{:S(2)}) collective-permute-start(f32[4,64,64]{2,1,0:T(8,128)S(1)} %add.200), channel_id=1, source_target_pairs={{0,8},{1,3},{2,10},{3,1},{4,12},{5,7},{6,14},{7,5},{8,0},{9,11},{1... | collective-permute-start | bytes 196616 | tf_op jit(solution)/shard_map/ppermute | solution.py:74
  103.0 5.0 %collective-permute-start.17 = (f32[4,64,64]{2,1,0:T(8,128)S(1)}, f32[4,64,64]{2,1,0:T(8,128)S(1)}, u32[]{:S(2)}, u32[]{:S(2)}) collective-permute-start(f32[4,64,64]{2,1,0:T(8,128)S(1)} %add.201), channel_id=1, source_target_pairs={{0,4},{1,17},{2,6},{3,19},{4,0},{5,21},{6,2},{7,23},{8,12},{9,25},... | collective-permute-start | bytes 196616 | tf_op jit(solution)/shard_map/ppermute | solution.py:74
  108.0 5.1 %collective-permute-start.18 = (f32[4,64,64]{2,1,0:T(8,128)S(1)}, f32[4,64,64]{2,1,0:T(8,128)S(1)}, u32[]{:S(2)}, u32[]{:S(2)}) collective-permute-start(f32[4,64,64]{2,1,0:T(8,128)S(1)} %add.202), channel_id=1, source_target_pairs={{0,2},{1,9},{2,0},{3,11},{4,6},{5,13},{6,4},{7,15},{8,10},{9,1},{1... | collective-permute-start | bytes 196616 | tf_op jit(solution)/shard_map/ppermute | solution.py:74

commit v5 on v4

--- a/solution.py
+++ b/solution.py
@@ -98,7 +98,7 @@
         for bit in bits:
             offsets = offsets + [offset ^ bit for offset in offsets]
         table.append(offsets)
-    return jnp.array(table, jnp.int32)
+    return [jnp.array(offsets, jnp.int32) for offsets in table]
 
 
 def exchange(block):
@@ -277,7 +277,7 @@
     return jnp.where(scaled <= 1.0, near, far)
 
 
-def tiles_kernel(build, wanted, ids_ref, plan_ref, own_ref, near_ref, far_ref, *refs):
+def tiles_kernel(build, wanted, ids_ref, plan_ref, own_ref, near_ref, other_ref, *refs):
     refs = list(refs)
     tiles_in = None if build else refs.pop(0)
     start_ref = None
@@ -289,18 +289,18 @@
     if wanted:
         out_ref, rounded_ref, gram_ref = refs[:3]
         refs = refs[3:]
-        wide_ref, held_ref, all_ref, total_ref, sems, piece_sems = refs
+        wide_ref, far_ref, held_ref, all_ref, total_ref, sems, piece_sems = refs
     else:
-        total_ref, wide_ref, held_ref, all_ref, sems, piece_sems = refs
-    half, slots, height, local = near_ref.shape
+        total_ref, wide_ref, far_ref, held_ref, all_ref, sems, piece_sems = refs
+    half, height, local = near_ref.shape
     columns = total_ref.shape[1]
     capacity = held_ref.shape[0]
-    chunks = local // LANES
+    chunk_bits = (local // LANES).bit_length() - 1
     total = plan_ref[capacity]
 
     copies = [
         pltpu.make_async_copy(ref, all_ref.at[pl.ds(part * half, half)], piece_sems.at[part])
-        for part, ref in enumerate((near_ref, far_ref))
+        for part, ref in enumerate((near_ref, other_ref))
     ]
     for copy in copies:
         copy.start()
@@ -335,23 +335,25 @@
             wide_ref[row] = jnp.broadcast_to(scale * column[:, row : row + 1], (local, LANES))
     for copy in copies:
         copy.wait()
+    if build:
+        for place in range(2 * half):
+            rows = all_ref[place, columns:, :].astype(jnp.float32)
+            rows = (rows[0:3] + rows[3:6]) + rows[6:9]
+            far_ref[place, 0:3, :] = jnp.concatenate([2.0 * rows[0:2], rows[2:3]], axis=0)
 
     def locate(batch, part):
         entry = ids_ref[batch * BATCH + part]
         chunk = jnp.maximum(entry, 0)
-        place = chunk // chunks
-        tile = place // slots
-        lane = pl.multiple_of((chunk - place * chunks) * LANES, LANES)
-        return entry, tile, place - tile * slots, lane
+        lane = pl.multiple_of((chunk & ((1 << chunk_bits) - 1)) * LANES, LANES)
+        return entry, lax.shift_right_logical(chunk, chunk_bits), lane
 
     def build_batch(batch):
         start = pl.multiple_of(plan_ref[batch] * ROWS, ROWS)
         for part in range(BATCH):
-            entry, tile, place, lane = locate(batch, part)
-            rows = all_ref[tile, place, columns:, pl.ds(lane, LANES)].astype(jnp.float32)
-            far = (rows[0:3] + rows[3:6]) + rows[6:9]
-            across_x = wide_ref[0, pl.ds(start, ROWS), :] - 2.0 * far[0:1, :]
-            across_y = wide_ref[1, pl.ds(start, ROWS), :] - 2.0 * far[1:2, :]
+            entry, place, lane = locate(batch, part)
+            far = far_ref[place, :, pl.ds(lane, LANES)]
+            across_x = wide_ref[0, pl.ds(start, ROWS), :] - far[0:1, :]
+            across_y = wide_ref[1, pl.ds(start, ROWS), :] - far[1:2, :]
             value = gaspari_cohn(across_x * across_x + across_y * across_y)
             spread = jnp.where(entry >= 0, far[2:3, :], 0.0)
             value = wide_ref[2, pl.ds(start, ROWS), :] * spread * value
@@ -360,8 +362,8 @@
     def product(batch, valid=None):
         sides = []
         for part in range(BATCH):
-            _, tile, place, lane = locate(batch, part)
-            sides.append(all_ref[tile, place, :columns, pl.ds(lane, LANES)])
+            _, place, lane = locate(batch, part)
+            sides.append(all_ref[place, :columns, pl.ds(lane, LANES)])
         side = jnp.concatenate(sides, axis=1)
         if valid is not None:
             side = jnp.where(valid, side, jnp.zeros_like(side))
@@ -418,14 +420,13 @@
         result = jnp.transpose(total_ref[...]) + scale_ref[...] * block
         out_ref[...] = result
         rounded_ref[...] = result.astype(jnp.bfloat16)
-        pairs = {"squares": (block, block), "mixed": (block, result), "images": (result, result)}
-        for index, name in enumerate(wanted):
-            gram_ref[index] = dot_nt(*pairs[name], HIGHEST)
+        gram_ref[...] = dot_nt(block, jnp.concatenate([block, result], axis=0), HIGHEST)
 
 
 def run_tiles(plan, own, near, far, tiles, capacity, columns, finish=None):
     build = tiles is None
-    half, slots, height, local = near.shape
+    near, far = [piece.reshape((-1,) + piece.shape[2:]) for piece in (near, far)]
+    half, height, local = near.shape
     smem = pl.BlockSpec(memory_space=pltpu.SMEM)
     anywhere = pl.BlockSpec(memory_space=pl.ANY)
     operands = [*plan, own, near, far]
@@ -434,9 +435,10 @@
     if not build:
         operands.append(tiles)
         in_specs.append(anywhere)
-    wanted = ()
+    wanted = False
     if finish is not None:
-        total, block, scale, wanted = finish
+        wanted = True
+        total, block, scale = finish
         operands += [total, block, scale]
         in_specs += whole_vmem(3)
     if build:
@@ -448,7 +450,7 @@
         out_shape += [
             jax.ShapeDtypeStruct((columns, local), jnp.float32),
             jax.ShapeDtypeStruct((columns, local), jnp.bfloat16),
-            jax.ShapeDtypeStruct((len(wanted), columns, columns), jnp.float32),
+            jax.ShapeDtypeStruct((columns, 2 * columns), jnp.float32),
         ]
         out_specs += whole_vmem(3)
     else:
@@ -456,8 +458,9 @@
         out_specs += whole_vmem(1)
     scratch += [
         pltpu.VMEM((3, local, LANES), jnp.float32),
+        pltpu.VMEM((2 * half, 8, local), jnp.float32),
         pltpu.VMEM((capacity, ROWS, BATCH * LANES), jnp.bfloat16),
-        pltpu.VMEM((2 * half, slots, height, local), jnp.bfloat16),
+        pltpu.VMEM((2 * half, height, local), jnp.bfloat16),
     ]
     if wanted:
         scratch.append(pltpu.VMEM(total_shape, jnp.float32))
@@ -530,8 +533,9 @@
 
 
 def last_kernel(grams_ref, start_ref, images_ref, weights_ref, residual_ref):
-    squares, mixed, images, cross = grams_ref[0], grams_ref[1], grams_ref[2], grams_ref[3]
-    n = squares.shape[0]
+    n = grams_ref.shape[1]
+    squares, mixed = grams_ref[0, :, :n], grams_ref[0, :, n:]
+    images, cross = grams_ref[1, :, :n], grams_ref[1, :, n:]
     solved = solve_positive(mixed, jnp.concatenate([squares, images], axis=1))
     step, carried = solved[:, :n], solved[:, n:]
     product = dot_nn(images, solved, HIGHEST)
@@ -561,7 +565,8 @@
     columns, local = innovations.shape
     slot_tile = tile ^ jnp.arange(tiles_axis, dtype=jnp.int32)
     first = slot_tile * local
-    slot_region = here ^ slot_offsets(regions)[slot_tile % 2]
+    even, odd = slot_offsets(regions)
+    slot_region = here ^ jnp.where((slot_tile % 2 == 0)[:, None], even, odd)
 
     places = jnp.concatenate([obs_geometry, obs_error[None, :]], axis=0)
     message, own, start, rank = sort_region(
@@ -584,7 +589,7 @@
         near, far = halves(block, "tile")
         inside = slot_region[:, part * half_regions : (part + 1) * half_regions]
         plans.append(plan_blocks(own[1], near, far, inside, here, flags, columns, capacity))
-        finish = None if part == 0 else (total, start, scale, ("squares", "mixed", "images"))
+        finish = None if part == 0 else (total, start, scale)
         built, total, *others = run(plans[part], near=near, far=far, tiles=None, finish=finish)
         tiles.append(built)
     image = total
@@ -594,11 +599,11 @@
         if part:
             block, total = lax.optimization_barrier((block, total))
         near, far = halves(block, "tile")
-        finish = None if part == 0 else (total, image, scale, ("mixed",))
+        finish = None if part == 0 else (total, image, scale)
         total, *others = run(plans[part], near=near, far=far, tiles=tiles[part], finish=finish)
     second, cross = total, others[1]
 
-    grams = jnp.concatenate([grams, cross], axis=0)
+    grams = jnp.stack([grams, cross])
     grams = sum_regions(sum_tiles(grams))
     near, far = halves(jnp.concatenate([image, second], axis=0), "tile")
     images = unsort(first, rank, jnp.concatenate([*near, *far], axis=1))

time: 122 us -> 116 us (0.951)
  starting transfers between devices: 27.4 us -> 24.7 us
  other arithmetic: 9.3 us -> 6.75 us
  Pallas kernels: 29 us -> 31.4 us
  waiting for transfers between devices: 50.1 us -> 48.5 us
  local copies, waits for them, and re-layouts: 4.06 us -> 2.8 us
    ppermute x12, waiting for transfers between devices: 45.2 us -> 41.8 us  [swap_regions(): return lax.ppermute(block, ('region', 'tile'), route)]
    pallas_call x1 -> x0, other arithmetic: 3.25 us -> none  [run_tiles(): pl.pallas_call(functools.partial(tiles_kernel, build, wanted), out_shape=...]
    pallas_call x3 -> x4, Pallas kernels: 16.1 us -> 18.2 us  [run_tiles(): pl.pallas_call(functools.partial(tiles_kernel, build, wanted), out_shape=...]
    ppermute x12, starting transfers between devices: 25.4 us -> 23.7 us  [swap_regions(): return lax.ppermute(block, ('region', 'tile'), route)]
    ppermute x8, waiting for transfers between devices: 4.94 us -> 6.64 us  [swapped(): lax.ppermute(block, axis, [(i, i ^ bit) for i in range(lax.axis_size(axis...]
    gather x1 -> x0, local copies, waits for them, and re-layouts: 1.25 us -> none  [shards(): slot_region = here ^ slot_offsets(regions)[slot_tile % 2]]
  transfers between devices with their start and end apart: 20 -> 20, of which waited for: 15 -> 18; matrix products, arithmetic and copies ran while one was open for 5% -> 4% of each run, Pallas kernels for 9% -> 9%
where the time goes in v5:
time: 116 us; the launch traced here: 115 us
  waiting for transfers between devices  48.5 us (42%)
  Pallas kernels  31.4 us (27%)
  starting transfers between devices  24.7 us (21%)
  other arithmetic  6.75 us (6%)
  local copies, waits for them, and re-layouts  2.8 us (2%)
    ppermute x12, waiting for transfers between devices, swap_regions(): return lax.ppermute(block, ('region', 'tile'), route)  41.8 us
    ppermute x12, starting transfers between devices, swap_regions(): return lax.ppermute(block, ('region', 'tile'), route)  23.7 us
    pallas_call x4, Pallas kernels, run_tiles(): pl.pallas_call(functools.partial(tiles_kernel, build, wanted), out_shape=...  18.2 us
    pallas_call x1, Pallas kernels, last_step(): pl.pallas_call(last_kernel, out_shape=(jax.ShapeDtypeStruct(start.shape,...  8.03 us
    ppermute x8, waiting for transfers between devices, swapped(): lax.ppermute(block, axis, [(i, i ^ bit) for i in range(lax.axis_size(axis...  6.64 us
    pallas_call x1, Pallas kernels, sort_region(): pl.pallas_call(sort_kernel, out_shape=(jax.ShapeDtypeStruct((columns + EX...  3.86 us
  transfers between devices with their start and end apart: 20, of which 18 were waited for; matrix products, arithmetic and copies ran while one was open for 4% of the time, Pallas kernels for 9%

profile of v5, /device:TPU:0, one launch (start us, length us, event | category | flops | bytes accessed | tf_op | source)
XLA Modules:
  0.0 115.1 jit_solution(5235127879705543666)
XLA Ops:
  0.6 0.5 collective-permute-start.1
  1.1 0.7 maximum_bitcast_fusion.near_ref
  1.9 0.1 collective-permute-start
  2.0 1.1 collective-permute-done.far_ref
  3.1 0.9 copy-done
  4.0 0.7 copy-done.2
  4.7 3.9 %sort_region.1 = (bf16[80,512]{1,0:T(8,128)(2,1)S(1)}, f32[8,512]{1,0:T(8,128)S(1)}, f32[64,512]{1,0:T(8,128)S(1)}, s32[1,512]{1,0:T(1,128)S(1)}) custom-call(s32[2]{0:T(128)S(1)} %fusion.11.first_ref, s32[1,7]{1,0:T(1,128)S(1)} %copy-done.2, f32[1,4,512]{2,1,0:T(4,128)S(1)} %maximum_bitcast_fusion.near_ref, f32[1,4,512]{2,1,0:T(4,128)S(1)} %collective-permute-done.far_ref, ...), custom_call_target="tpu_custom_call" | custom-call | flops 226492416 | bytes 2097152 | tf_op jit(solution)/shard_map/sort_region/pallas_call | solution.py:194
  8.5 3.8 %collective-permute-start.2 = (bf16[1,80,512]{2,1,0:T(8,128)(2,1)S(1)}, bf16[1,80,512]{2,1,0:T(8,128)(2,1)S(1)}, u32[]{:S(2)}, u32[]{:S(2)}) collective-permute-start(bf16[1,80,512]{2,1,0:T(8,128)(2,1)S(1)} %bitcast.41), channel_id=1, source_target_pairs={{0,16},{1,17},{2,18},{3,19},{4,20},{5,21},{6,22},{7,23},{8,24},{9,... | collective-permute-start | bytes 245768 | tf_op jit(solution)/shard_map/ppermute | solution.py:74
  12.3 0.7 select_xor_fusion
  13.1 4.0 %collective-permute-done.2 = bf16[1,80,512]{2,1,0:T(8,128)(2,1)S(1)} collective-permute-done((bf16[1,80,512]{2,1,0:T(8,128)(2,1)S(1)}, bf16[1,80,512]{2,1,0:T(8,128)(2,1)S(1)}, u32[]{:S(2)}, u32[]{:S(2)}) %collective-permute-start.2) | collective-permute-done | bytes 81952 | tf_op jit(solution)/shard_map/ppermute | solution.py:74
  17.1 0.8 collective-permute-start.3
  17.9 4.6 %collective-permute-done.3 = bf16[2,80,512]{2,1,0:T(8,128)(2,1)S(1)} collective-permute-done((bf16[2,80,512]{2,1,0:T(8,128)(2,1)S(1)}, bf16[2,80,512]{2,1,0:T(8,128)(2,1)S(1)}, u32[]{:S(2)}, u32[]{:S(2)}) %collective-permute-start.3) | collective-permute-done | bytes 163872 | tf_op jit(solution)/shard_map/ppermute | solution.py:74
  22.5 1.6 %collective-permute-start.4 = (bf16[4,80,512]{2,1,0:T(8,128)(2,1)S(1)}, bf16[4,80,512]{2,1,0:T(8,128)(2,1)S(1)}, u32[]{:S(2)}, u32[]{:S(2)}) collective-permute-start(bf16[4,80,512]{2,1,0:T(8,128)(2,1)S(1)} %pad_maximum_fusion.3), channel_id=1, source_target_pairs={{0,4},{1,9},{2,6},{3,11},{4,0},{5,13},{6,2},{7,15},{8,12},{9,1},{1... | collective-permute-start | bytes 983048 | tf_op jit(solution)/shard_map/ppermute | solution.py:74
  24.2 5.4 %collective-permute-done.4 = bf16[4,80,512]{2,1,0:T(8,128)(2,1)S(1)} collective-permute-done((bf16[4,80,512]{2,1,0:T(8,128)(2,1)S(1)}, bf16[4,80,512]{2,1,0:T(8,128)(2,1)S(1)}, u32[]{:S(2)}, u32[]{:S(2)}) %collective-permute-start.4) | collective-permute-done | bytes 327712 | tf_op jit(solution)/shard_map/ppermute | solution.py:74
  29.6 0.1 fusion.14
  29.8 0.1 fusion.6
  30.1 0.1 copy.38
  30.2 1.5 %collective-permute-start.5 = (bf16[8,80,512]{2,1,0:T(8,128)(2,1)S(1)}, bf16[8,80,512]{2,1,0:T(8,128)(2,1)S(1)}, u32[]{:S(2)}, u32[]{:S(2)}) collective-permute-start(bf16[8,80,512]{2,1,0:T(8,128)(2,1)S(1)} %get-tuple-element.49.near_ref), channel_id=1, source_target_pairs={{0,2},{1,5},{2,0},{3,7},{4,6},{5,1},{6,4},{7,3},{8,10},{9,13},{10,... | collective-permute-start | bytes 1966088 | tf_op jit(solution)/shard_map/ppermute | solution.py:74
  31.8 0.1 collective-permute-done.6
  32.2 0.1 copy.28
  32.4 0.1 and.123
  32.5 0.2 convert_reduce_fusion.3
  32.7 0.6 fusion.17
  33.4 0.1 select_reduce_fusion.5
  33.5 0.1 convert_reduce_fusion.1
  33.5 0.1 select_reduce_fusion.3
  33.8 0.3 select_reduce_fusion.1
  34.1 0.7 pad_add_fusion.plan_ref
  34.7 5.7 %build_first.1 = (bf16[128,64,512]{2,1,0:T(8,128)(2,1)}, f32[512,64]{1,0:T(8,128)S(1)}) custom-call(s32[512]{0:T(512)S(1)} %broadcast_add_fusion.3.ids_ref, s32[129]{0:T(256)S(1)} %pad_add_fusion.plan_ref, f32[8,512]{1,0:T(8,128)S(1)} %get-tuple-element.19.own_ref, bf16[8,80,512]{2,1,0:T(8,128)(2,1)S(1)} %get-tuple-element.49.near_ref, ...), custom_call_target="tpu_custom_call" | custom-call | flops 9437184000 | bytes 4194304 | tf_op jit(solution)/shard_map/build_first/pallas_call | solution.py:472
  40.5 0.4 collective-permute-done.5.near_ref
  40.8 2.1 %collective-permute-done.7 = bf16[1,8,80,512]{3,2,1,0:T(8,128)(2,1)S(1)} collective-permute-done((bf16[1,8,80,512]{3,2,1,0:T(8,128)(2,1)S(1)}, bf16[1,8,80,512]{3,2,1,0:T(8,128)(2,1)S(1)}, u32[]{:S(2)}, u32[]{:S(2)}) %collective-permute-start.7) | collective-permute-done | bytes 655392 | tf_op jit(solution)/shard_map/ppermute | solution.py:56
  43.3 0.1 copy.31
  43.5 0.1 and.130
  43.6 0.2 convert_reduce_fusion.2
  43.8 0.6 fusion.15
  44.5 0.1 convert_reduce_fusion
  44.6 0.1 select_reduce_fusion.2
  44.8 0.3 select_reduce_fusion
  45.1 0.7 pad_add_fusion.1.plan_ref
  45.8 6.0 %build_last.1 = (bf16[128,64,512]{2,1,0:T(8,128)(2,1)}, f32[64,512]{1,0:T(8,128)S(1)}, bf16[64,512]{1,0:T(8,128)(2,1)S(1)}, f32[64,128]{1,0:T(8,128)S(1)}) custom-call(s32[512]{0:T(512)S(1)} %broadcast_add_fusion.2.ids_ref, s32[129]{0:T(256)S(1)} %pad_add_fusion.1.plan_ref, f32[8,512]{1,0:T(8,128)S(1)} %get-tuple-element.19.own_ref, ...), custom_call_target="tpu_custom_call" | custom-call | flops 9437184000 | bytes 4194304 | tf_op jit(solution)/shard_map/build_last/pallas_call | solution.py:472
  51.8 5.3 %collective-permute-start.8 = (bf16[1,64,512]{2,1,0:T(8,128)(2,1)S(1)}, bf16[1,64,512]{2,1,0:T(8,128)(2,1)S(1)}, u32[]{:S(2)}, u32[]{:S(2)}) collective-permute-start(bf16[1,64,512]{2,1,0:T(8,128)(2,1)S(1)} %bitcast.45), channel_id=1, source_target_pairs={{0,16},{1,17},{2,18},{3,19},{4,20},{5,21},{6,22},{7,23},{8,24},{9,... | collective-permute-start | bytes 196616 | tf_op jit(solution)/shard_map/ppermute | solution.py:74
  57.0 3.8 %collective-permute-done.8 = bf16[1,64,512]{2,1,0:T(8,128)(2,1)S(1)} collective-permute-done((bf16[1,64,512]{2,1,0:T(8,128)(2,1)S(1)}, bf16[1,64,512]{2,1,0:T(8,128)(2,1)S(1)}, u32[]{:S(2)}, u32[]{:S(2)}) %collective-permute-start.8) | collective-permute-done | bytes 65568 | tf_op jit(solution)/shard_map/ppermute | solution.py:74
  60.8 0.7 collective-permute-start.9
  61.6 4.3 %collective-permute-done.9 = bf16[2,64,512]{2,1,0:T(8,128)(2,1)S(1)} collective-permute-done((bf16[2,64,512]{2,1,0:T(8,128)(2,1)S(1)}, bf16[2,64,512]{2,1,0:T(8,128)(2,1)S(1)}, u32[]{:S(2)}, u32[]{:S(2)}) %collective-permute-start.9) | collective-permute-done | bytes 131104 | tf_op jit(solution)/shard_map/ppermute | solution.py:74
  65.9 0.8 collective-permute-start.10
  66.7 5.6 %collective-permute-done.10 = bf16[4,64,512]{2,1,0:T(8,128)(2,1)S(1)} collective-permute-done((bf16[4,64,512]{2,1,0:T(8,128)(2,1)S(1)}, bf16[4,64,512]{2,1,0:T(8,128)(2,1)S(1)}, u32[]{:S(2)}, u32[]{:S(2)}) %collective-permute-start.10) | collective-permute-done | bytes 262176 | tf_op jit(solution)/shard_map/ppermute | solution.py:74
  72.5 1.6 %collective-permute-start.11 = (bf16[8,64,512]{2,1,0:T(8,128)(2,1)S(1)}, bf16[8,64,512]{2,1,0:T(8,128)(2,1)S(1)}, u32[]{:S(2)}, u32[]{:S(2)}) collective-permute-start(bf16[8,64,512]{2,1,0:T(8,128)(2,1)S(1)} %get-tuple-element.51.near_ref), channel_id=1, source_target_pairs={{0,2},{1,5},{2,0},{3,7},{4,6},{5,1},{6,4},{7,3},{8,10},{9,13},{10,... | collective-permute-start | bytes 1572872 | tf_op jit(solution)/shard_map/ppermute | solution.py:74
  74.1 0.3 collective-permute-done.12
  74.4 2.9 %apply_first.1.refs_1_ = f32[512,64]{1,0:T(8,128)S(1)} custom-call(s32[512]{0:T(512)S(1)} %broadcast_add_fusion.3.ids_ref, s32[129]{0:T(256)S(1)} %pad_add_fusion.plan_ref, f32[8,512]{1,0:T(8,128)S(1)} %get-tuple-element.19.own_ref, bf16[8,64,512]{2,1,0:T(8,128)(2,1)S(1)} %get-tuple-element.51.near_ref, bf16[8,64,512]{2,1,0:T(8,128)(2,1)S(1)} %bitcast.58, ...), custom_call_target="tpu_custom_call" | custom-call | flops 4718592000 | bytes 4194304 | tf_op jit(solution)/shard_map/apply_first/pallas_call | solution.py:472
  77.3 4.5 %collective-permute-done.11.near_ref = bf16[8,64,512]{2,1,0:T(8,128)(2,1)S(1)} collective-permute-done((bf16[8,64,512]{2,1,0:T(8,128)(2,1)S(1)}, bf16[8,64,512]{2,1,0:T(8,128)(2,1)S(1)}, u32[]{:S(2)}, u32[]{:S(2)}) %collective-permute-start.11) | collective-permute-done | bytes 524320 | tf_op jit(solution)/shard_map/ppermute | solution.py:74
  81.7 1.9 %collective-permute-done.13 = bf16[1,8,64,512]{3,2,1,0:T(8,128)(2,1)S(1)} collective-permute-done((bf16[1,8,64,512]{3,2,1,0:T(8,128)(2,1)S(1)}, bf16[1,8,64,512]{3,2,1,0:T(8,128)(2,1)S(1)}, u32[]{:S(2)}, u32[]{:S(2)}) %collective-permute-start.13) | collective-permute-done | bytes 524320 | tf_op jit(solution)/shard_map/ppermute | solution.py:56
  83.7 3.6 %apply_last.1 = (f32[64,512]{1,0:T(8,128)S(1)}, bf16[64,512]{1,0:T(8,128)(2,1)}, f32[64,128]{1,0:T(8,128)S(1)}) custom-call(s32[512]{0:T(512)S(1)} %broadcast_add_fusion.2.ids_ref, s32[129]{0:T(256)S(1)} %pad_add_fusion.1.plan_ref, f32[8,512]{1,0:T(8,128)S(1)} %get-tuple-element.19.own_ref, bf16[8,64,512]{2,1,0:T(8,128)(2,1)S(1)} %collective-permute-done.11.near_ref, ...), custom_call_target="tpu_custom_call" | custom-call | flops 4718592000 | bytes 4194304 | tf_op jit(solution)/shard_map/apply_last/pallas_call | solution.py:472
  87.3 0.2 collective-permute-start.14
  87.5 1.1 collective-permute-done.14
  88.6 2.6 %collective-permute-start.15 = (f32[2,64,128]{2,1,0:T(8,128)S(1)}, f32[2,64,128]{2,1,0:T(8,128)S(1)}, u32[]{:S(2)}, u32[]{:S(2)}) collective-permute-start(f32[2,64,128]{2,1,0:T(8,128)S(1)} %fusion.12), channel_id=1, source_target_pairs={{0,16},{1,5},{2,18},{3,7},{4,20},{5,1},{6,22},{7,3},{8,24},{9,13},... | collective-permute-start | bytes 196616 | tf_op jit(solution)/shard_map/ppermute | solution.py:74
  91.3 2.6 %collective-permute-done.15 = f32[2,64,128]{2,1,0:T(8,128)S(1)} collective-permute-done((f32[2,64,128]{2,1,0:T(8,128)S(1)}, f32[2,64,128]{2,1,0:T(8,128)S(1)}, u32[]{:S(2)}, u32[]{:S(2)}) %collective-permute-start.15) | collective-permute-done | bytes 65568 | tf_op jit(solution)/shard_map/ppermute | solution.py:74
  93.9 1.5 %collective-permute-start.16 = (f32[2,64,128]{2,1,0:T(8,128)S(1)}, f32[2,64,128]{2,1,0:T(8,128)S(1)}, u32[]{:S(2)}, u32[]{:S(2)}) collective-permute-start(f32[2,64,128]{2,1,0:T(8,128)S(1)} %fusion.24), channel_id=1, source_target_pairs={{0,8},{1,3},{2,10},{3,1},{4,12},{5,7},{6,14},{7,5},{8,0},{9,11},{1... | collective-permute-start | bytes 196616 | tf_op jit(solution)/shard_map/ppermute | solution.py:74
  95.3 2.9 %collective-permute-done.16 = f32[2,64,128]{2,1,0:T(8,128)S(1)} collective-permute-done((f32[2,64,128]{2,1,0:T(8,128)S(1)}, f32[2,64,128]{2,1,0:T(8,128)S(1)}, u32[]{:S(2)}, u32[]{:S(2)}) %collective-permute-start.16) | collective-permute-done | bytes 65568 | tf_op jit(solution)/shard_map/ppermute | solution.py:74
  98.2 1.3 %collective-permute-start.17 = (f32[2,64,128]{2,1,0:T(8,128)S(1)}, f32[2,64,128]{2,1,0:T(8,128)S(1)}, u32[]{:S(2)}, u32[]{:S(2)}) collective-permute-start(f32[2,64,128]{2,1,0:T(8,128)S(1)} %add.187), channel_id=1, source_target_pairs={{0,4},{1,17},{2,6},{3,19},{4,0},{5,21},{6,2},{7,23},{8,12},{9,25},... | collective-permute-start | bytes 196616 | tf_op jit(solution)/shard_map/ppermute | solution.py:74
  99.5 3.0 %collective-permute-done.17 = f32[2,64,128]{2,1,0:T(8,128)S(1)} collective-permute-done((f32[2,64,128]{2,1,0:T(8,128)S(1)}, f32[2,64,128]{2,1,0:T(8,128)S(1)}, u32[]{:S(2)}, u32[]{:S(2)}) %collective-permute-start.17) | collective-permute-done | bytes 65568 | tf_op jit(solution)/shard_map/ppermute | solution.py:74
  102.6 2.2 %collective-permute-start.18 = (f32[2,64,128]{2,1,0:T(8,128)S(1)}, f32[2,64,128]{2,1,0:T(8,128)S(1)}, u32[]{:S(2)}, u32[]{:S(2)}) collective-permute-start(f32[2,64,128]{2,1,0:T(8,128)S(1)} %add.188), channel_id=1, source_target_pairs={{0,2},{1,9},{2,0},{3,11},{4,6},{5,13},{6,4},{7,15},{8,10},{9,1},{1... | collective-permute-start | bytes 196616 | tf_op jit(solution)/shard_map/ppermute | solution.py:74
  104.8 1.4 %unsort.1.images_ref = f32[128,512]{1,0:T(8,128)S(1)} custom-call(s32[2]{0:T(128)S(1)} %fusion.11.first_ref, s32[1,512]{1,0:T(1,128)S(1)} %get-tuple-element.32.rank_ref, f32[128,1024]{1,0:T(8,128)S(1)} %pad_maximum_fusion.2.block_ref), custom_call_target="tpu_custom_call" | custom-call | flops 402653184 | bytes 2097152 | tf_op jit(solution)/shard_map/unsort/pallas_call | solution.py:223
  106.2 0.8 collective-permute-done.18
  107.0 8.0 %last_step.1 = (f32[64,512]{1,0:T(8,128)}, f32[64,512]{1,0:T(8,128)}) custom-call(f32[2,64,128]{2,1,0:T(8,128)S(1)} %add.189.grams_ref, f32[64,512]{1,0:T(8,128)S(1)} %copy-done.1, f32[128,512]{1,0:T(8,128)S(1)} %unsort.1.images_ref), custom_call_target="tpu_custom_call" | custom-call | tf_op jit(solution)/shard_map/last_step/pallas_call | solution.py:551
  (62 shorter events, 2.0 us)
Async XLA Ops:
  0.6 2.5 %collective-permute-start.1 = (f32[1,64,512]{2,1,0:T(8,128)}, f32[1,64,512]{2,1,0:T(8,128)S(1)}, u32[]{:S(2)}, u32[]{:S(2)}) collective-permute-start(f32[1,64,512]{2,1,0:T(8,128)} %bitcast.55), channel_id=1, source_target_pairs={{0,1},{1,0},{2,3},{3,2},{4,5},{5,4},{6,7},{7,6},{8,9},{9,8},{10,11... | collective-permute-start | bytes 393224 | tf_op jit(solution)/shard_map/ppermute | solution.py:56
  1.9 1.2 %collective-permute-start = (f32[1,4,512]{2,1,0:T(4,128)S(1)}, f32[1,4,512]{2,1,0:T(4,128)S(1)}, u32[]{:S(2)}, u32[]{:S(2)}) collective-permute-start(f32[1,4,512]{2,1,0:T(4,128)S(1)} %maximum_bitcast_fusion.near_ref), channel_id=1, source_target_pairs={{0,1},{1,0},{2,3},{3,2},{4,5},{5,4},{6,7},{7,6},{8,9},{9,8},{10,11... | collective-permute-start | bytes 24584 | tf_op jit(solution)/shard_map/ppermute | solution.py:56
  3.1 0.9 copy-start
  4.0 0.7 copy-start.2
  8.5 8.5 %collective-permute-start.2 = (bf16[1,80,512]{2,1,0:T(8,128)(2,1)S(1)}, bf16[1,80,512]{2,1,0:T(8,128)(2,1)S(1)}, u32[]{:S(2)}, u32[]{:S(2)}) collective-permute-start(bf16[1,80,512]{2,1,0:T(8,128)(2,1)S(1)} %bitcast.41), channel_id=1, source_target_pairs={{0,16},{1,17},{2,18},{3,19},{4,20},{5,21},{6,22},{7,23},{8,24},{9,... | collective-permute-start | bytes 245768 | tf_op jit(solution)/shard_map/ppermute | solution.py:74
  17.1 5.4 %collective-permute-start.3 = (bf16[2,80,512]{2,1,0:T(8,128)(2,1)S(1)}, bf16[2,80,512]{2,1,0:T(8,128)(2,1)S(1)}, u32[]{:S(2)}, u32[]{:S(2)}) collective-permute-start(bf16[2,80,512]{2,1,0:T(8,128)(2,1)S(1)} %pad_maximum_fusion.5), channel_id=1, source_target_pairs={{0,8},{1,3},{2,10},{3,1},{4,12},{5,7},{6,14},{7,5},{8,0},{9,11},{1... | collective-permute-start | bytes 491528 | tf_op jit(solution)/shard_map/ppermute | solution.py:74
  22.5 7.1 %collective-permute-start.4 = (bf16[4,80,512]{2,1,0:T(8,128)(2,1)S(1)}, bf16[4,80,512]{2,1,0:T(8,128)(2,1)S(1)}, u32[]{:S(2)}, u32[]{:S(2)}) collective-permute-start(bf16[4,80,512]{2,1,0:T(8,128)(2,1)S(1)} %pad_maximum_fusion.3), channel_id=1, source_target_pairs={{0,4},{1,9},{2,6},{3,11},{4,0},{5,13},{6,2},{7,15},{8,12},{9,1},{1... | collective-permute-start | bytes 983048 | tf_op jit(solution)/shard_map/ppermute | solution.py:74
  29.7 2.2 %collective-permute-start.6 = (bf16[1,8,80,512]{3,2,1,0:T(8,128)(2,1)S(1)}, bf16[1,8,80,512]{3,2,1,0:T(8,128)(2,1)S(1)}, u32[]{:S(2)}, u32[]{:S(2)}) collective-permute-start(bf16[1,8,80,512]{3,2,1,0:T(8,128)(2,1)S(1)} %get-tuple-element.48), channel_id=1, source_target_pairs={{0,1},{1,0},{2,3},{3,2},{4,5},{5,4},{6,7},{7,6},{8,9},{9,8},{10,11... | collective-permute-start | bytes 1966088 | tf_op jit(solution)/shard_map/ppermute | solution.py:56
  30.2 10.6 %collective-permute-start.5 = (bf16[8,80,512]{2,1,0:T(8,128)(2,1)S(1)}, bf16[8,80,512]{2,1,0:T(8,128)(2,1)S(1)}, u32[]{:S(2)}, u32[]{:S(2)}) collective-permute-start(bf16[8,80,512]{2,1,0:T(8,128)(2,1)S(1)} %get-tuple-element.49.near_ref), channel_id=1, source_target_pairs={{0,2},{1,5},{2,0},{3,7},{4,6},{5,1},{6,4},{7,3},{8,10},{9,13},{10,... | collective-permute-start | bytes 1966088 | tf_op jit(solution)/shard_map/ppermute | solution.py:74
  40.8 2.1 %collective-permute-start.7 = (bf16[1,8,80,512]{3,2,1,0:T(8,128)(2,1)S(1)}, bf16[1,8,80,512]{3,2,1,0:T(8,128)(2,1)S(1)}, u32[]{:S(2)}, u32[]{:S(2)}) collective-permute-start(bf16[1,8,80,512]{3,2,1,0:T(8,128)(2,1)S(1)} %bitcast.36), channel_id=1, source_target_pairs={{0,1},{1,0},{2,3},{3,2},{4,5},{5,4},{6,7},{7,6},{8,9},{9,8},{10,11... | collective-permute-start | bytes 1966088 | tf_op jit(solution)/shard_map/ppermute | solution.py:56
  51.8 9.1 %collective-permute-start.8 = (bf16[1,64,512]{2,1,0:T(8,128)(2,1)S(1)}, bf16[1,64,512]{2,1,0:T(8,128)(2,1)S(1)}, u32[]{:S(2)}, u32[]{:S(2)}) collective-permute-start(bf16[1,64,512]{2,1,0:T(8,128)(2,1)S(1)} %bitcast.45), channel_id=1, source_target_pairs={{0,16},{1,17},{2,18},{3,19},{4,20},{5,21},{6,22},{7,23},{8,24},{9,... | collective-permute-start | bytes 196616 | tf_op jit(solution)/shard_map/ppermute | solution.py:74
  60.8 5.0 %collective-permute-start.9 = (bf16[2,64,512]{2,1,0:T(8,128)(2,1)S(1)}, bf16[2,64,512]{2,1,0:T(8,128)(2,1)S(1)}, u32[]{:S(2)}, u32[]{:S(2)}) collective-permute-start(bf16[2,64,512]{2,1,0:T(8,128)(2,1)S(1)} %pad_maximum_fusion.6), channel_id=1, source_target_pairs={{0,8},{1,3},{2,10},{3,1},{4,12},{5,7},{6,14},{7,5},{8,0},{9,11},{1... | collective-permute-start | bytes 393224 | tf_op jit(solution)/shard_map/ppermute | solution.py:74
  65.9 6.4 %collective-permute-start.10 = (bf16[4,64,512]{2,1,0:T(8,128)(2,1)S(1)}, bf16[4,64,512]{2,1,0:T(8,128)(2,1)S(1)}, u32[]{:S(2)}, u32[]{:S(2)}) collective-permute-start(bf16[4,64,512]{2,1,0:T(8,128)(2,1)S(1)} %pad_maximum_fusion.4), channel_id=1, source_target_pairs={{0,4},{1,9},{2,6},{3,11},{4,0},{5,13},{6,2},{7,15},{8,12},{9,1},{1... | collective-permute-start | bytes 786440 | tf_op jit(solution)/shard_map/ppermute | solution.py:74
  72.4 2.0 %collective-permute-start.12 = (bf16[1,8,64,512]{3,2,1,0:T(8,128)(2,1)S(1)}, bf16[1,8,64,512]{3,2,1,0:T(8,128)(2,1)S(1)}, u32[]{:S(2)}, u32[]{:S(2)}) collective-permute-start(bf16[1,8,64,512]{3,2,1,0:T(8,128)(2,1)S(1)} %get-tuple-element.50), channel_id=1, source_target_pairs={{0,1},{1,0},{2,3},{3,2},{4,5},{5,4},{6,7},{7,6},{8,9},{9,8},{10,11... | collective-permute-start | bytes 1572872 | tf_op jit(solution)/shard_map/ppermute | solution.py:56
  72.5 9.2 %collective-permute-start.11 = (bf16[8,64,512]{2,1,0:T(8,128)(2,1)S(1)}, bf16[8,64,512]{2,1,0:T(8,128)(2,1)S(1)}, u32[]{:S(2)}, u32[]{:S(2)}) collective-permute-start(bf16[8,64,512]{2,1,0:T(8,128)(2,1)S(1)} %get-tuple-element.51.near_ref), channel_id=1, source_target_pairs={{0,2},{1,5},{2,0},{3,7},{4,6},{5,1},{6,4},{7,3},{8,10},{9,13},{10,... | collective-permute-start | bytes 1572872 | tf_op jit(solution)/shard_map/ppermute | solution.py:74
  81.7 1.9 %collective-permute-start.13 = (bf16[1,8,64,512]{3,2,1,0:T(8,128)(2,1)S(1)}, bf16[1,8,64,512]{3,2,1,0:T(8,128)(2,1)S(1)}, u32[]{:S(2)}, u32[]{:S(2)}) collective-permute-start(bf16[1,8,64,512]{3,2,1,0:T(8,128)(2,1)S(1)} %bitcast.57), channel_id=1, source_target_pairs={{0,1},{1,0},{2,3},{3,2},{4,5},{5,4},{6,7},{7,6},{8,9},{9,8},{10,11... | collective-permute-start | bytes 1572872 | tf_op jit(solution)/shard_map/ppermute | solution.py:56
  83.7 23.4 %copy-start.1 = (f32[64,512]{1,0:T(8,128)S(1)}, f32[64,512]{1,0:T(8,128)}, u32[]{:S(2)}) copy-start(f32[64,512]{1,0:T(8,128)} %start_ref.1) | copy-start | bytes 393220
  87.3 1.3 %collective-permute-start.14 = (f32[2,64,128]{2,1,0:T(8,128)S(1)}, f32[2,64,128]{2,1,0:T(8,128)S(1)}, u32[]{:S(2)}, u32[]{:S(2)}) collective-permute-start(f32[2,64,128]{2,1,0:T(8,128)S(1)} %pad_maximum_fusion.7), channel_id=1, source_target_pairs={{0,1},{1,0},{2,3},{3,2},{4,5},{5,4},{6,7},{7,6},{8,9},{9,8},{10,11... | collective-permute-start | bytes 196616 | tf_op jit(solution)/shard_map/ppermute | solution.py:56
  88.6 5.2 %collective-permute-start.15 = (f32[2,64,128]{2,1,0:T(8,128)S(1)}, f32[2,64,128]{2,1,0:T(8,128)S(1)}, u32[]{:S(2)}, u32[]{:S(2)}) collective-permute-start(f32[2,64,128]{2,1,0:T(8,128)S(1)} %fusion.12), channel_id=1, source_target_pairs={{0,16},{1,5},{2,18},{3,7},{4,20},{5,1},{6,22},{7,3},{8,24},{9,13},... | collective-permute-start | bytes 196616 | tf_op jit(solution)/shard_map/ppermute | solution.py:74
  91.2 13.6 %collective-permute-start.19 = (f32[1,128,512]{2,1,0:T(8,128)S(1)}, f32[1,128,512]{2,1,0:T(8,128)S(1)}, u32[]{:S(2)}, u32[]{:S(2)}) collective-permute-start(f32[1,128,512]{2,1,0:T(8,128)S(1)} %bitcast.60), channel_id=1, source_target_pairs={{0,1},{1,0},{2,3},{3,2},{4,5},{5,4},{6,7},{7,6},{8,9},{9,8},{10,11... | collective-permute-start | bytes 786440 | tf_op jit(solution)/shard_map/ppermute | solution.py:56
  93.9 4.3 %collective-permute-start.16 = (f32[2,64,128]{2,1,0:T(8,128)S(1)}, f32[2,64,128]{2,1,0:T(8,128)S(1)}, u32[]{:S(2)}, u32[]{:S(2)}) collective-permute-start(f32[2,64,128]{2,1,0:T(8,128)S(1)} %fusion.24), channel_id=1, source_target_pairs={{0,8},{1,3},{2,10},{3,1},{4,12},{5,7},{6,14},{7,5},{8,0},{9,11},{1... | collective-permute-start | bytes 196616 | tf_op jit(solution)/shard_map/ppermute | solution.py:74
  98.2 4.3 %collective-permute-start.17 = (f32[2,64,128]{2,1,0:T(8,128)S(1)}, f32[2,64,128]{2,1,0:T(8,128)S(1)}, u32[]{:S(2)}, u32[]{:S(2)}) collective-permute-start(f32[2,64,128]{2,1,0:T(8,128)S(1)} %add.187), channel_id=1, source_target_pairs={{0,4},{1,17},{2,6},{3,19},{4,0},{5,21},{6,2},{7,23},{8,12},{9,25},... | collective-permute-start | bytes 196616 | tf_op jit(solution)/shard_map/ppermute | solution.py:74
  102.6 4.4 %collective-permute-start.18 = (f32[2,64,128]{2,1,0:T(8,128)S(1)}, f32[2,64,128]{2,1,0:T(8,128)S(1)}, u32[]{:S(2)}, u32[]{:S(2)}) collective-permute-start(f32[2,64,128]{2,1,0:T(8,128)S(1)} %add.188), channel_id=1, source_target_pairs={{0,2},{1,9},{2,0},{3,11},{4,6},{5,13},{6,4},{7,15},{8,10},{9,1},{1... | collective-permute-start | bytes 196616 | tf_op jit(solution)/shard_map/ppermute | solution.py:74

commit v6 on v5

--- a/solution.py
+++ b/solution.py
@@ -10,16 +10,21 @@
 CUTOFF = 1.001
 LANES = 128
 ROWS = 64
-BATCH = 4
+PAIR = 2
+BATCH = 2 * PAIR
+RING = 8
 UNROLL = 4
-RING = 8
-VMEM = 48 * 1024 * 1024
+VMEM = 16 * 1024 * 1024
 EXTRA = 16
 HIGHEST = lax.Precision.HIGHEST
 
 
 def whole_vmem(count):
     return [pl.BlockSpec(memory_space=pltpu.VMEM)] * count
+
+
+def in_hbm(value):
+    return pltpu.with_memory_space_constraint(value, pltpu.HBM)
 
 
 def dot_nt(left, right, precision=None):
@@ -137,12 +142,30 @@
 
 
 def sort_kernel(
-    first_ref, owner_ref, near_ref, far_ref, block_ref, other_ref,
-    message_out, own_out, block_out, rank_out, order_ref, column_ref,
+    first_ref, owner_ref, near_ref, far_ref, near_error_ref, far_error_ref, block_ref, other_ref,
+    message_out, own_out, block_out, rank_out,
+    order_ref, column_ref, owned_ref, places_ref, errors_ref, blocks_ref, sems,
 ):
     columns, local = block_out.shape
-    stacks = [near_ref[i] for i in range(near_ref.shape[0])] + [far_ref[i] for i in range(far_ref.shape[0])]
-    places = jnp.concatenate(stacks, axis=1)
+    half = block_ref.shape[0]
+    pairs = [(owner_ref, owned_ref)]
+    for sources, target in (
+        ((near_ref, far_ref), places_ref),
+        ((near_error_ref, far_error_ref), errors_ref),
+        ((block_ref, other_ref), blocks_ref),
+    ):
+        pairs += [(ref, target.at[pl.ds(part * half, half)]) for part, ref in enumerate(sources)]
+    copies = [
+        pltpu.make_async_copy(source, target, sems.at[index])
+        for index, (source, target) in enumerate(pairs)
+    ]
+    for copy in copies:
+        copy.start()
+    for copy in copies[:5]:
+        copy.wait()
+    places = jnp.concatenate(
+        [jnp.concatenate([places_ref[i], errors_ref[i]], axis=0) for i in range(2 * half)], axis=1
+    )
     n = places.shape[1]
     step = 64
     index = jnp.concatenate(
@@ -168,8 +191,9 @@
     rank = jnp.sum(total, axis=0, keepdims=True).astype(jnp.int32)
     rank_out[...] = rank[:, :local]
     fill_order(first_ref[0], rank, order_ref, 0, local)
-    blocks = [block_ref[i] for i in range(block_ref.shape[0])]
-    blocks += [other_ref[i] for i in range(other_ref.shape[0])]
+    for copy in copies[5:]:
+        copy.wait()
+    blocks = [blocks_ref[i] for i in range(2 * half)]
     everything = jnp.concatenate([jnp.concatenate(blocks, axis=1), places, jnp.zeros((4, n), jnp.float32)], axis=0)
     rows = everything.shape[0]
     parts = dot_nt(stacked_parts(everything), order_ref[...])
@@ -180,13 +204,13 @@
     lane = lax.broadcasted_iota(jnp.int32, (1, local), 1)
     flags = jnp.zeros((1, local), jnp.float32)
     for offset in range(owner_ref.shape[1]):
-        flags = jnp.where((lane == offset) & (owner_ref[0, offset] >= 0), 1.0, flags)
+        flags = jnp.where((lane == offset) & (owned_ref[0, offset] >= 0), 1.0, flags)
     pieces = [parts[part * rows + columns : part * rows + columns + 3] for part in range(3)]
     pieces += [flags, jnp.zeros((EXTRA - 10, local), jnp.float32)]
     message_out[columns:, :] = jnp.concatenate(pieces, axis=0).astype(jnp.bfloat16)
 
 
-def sort_region(first, tile_owner, near, far, block, other):
+def sort_region(first, tile_owner, near, far, near_error, far_error, block, other):
     local = near.shape[2]
     n = local * 2 * near.shape[0]
     columns = block.shape[1]
@@ -199,15 +223,23 @@
             jax.ShapeDtypeStruct((columns, local), jnp.float32),
             jax.ShapeDtypeStruct((1, local), jnp.int32),
         ),
-        in_specs=[smem, smem] + whole_vmem(4),
+        in_specs=[smem] + [pl.BlockSpec(memory_space=pl.ANY)] * 7,
         out_specs=tuple(whole_vmem(4)),
-        scratch_shapes=[pltpu.VMEM((local, n), jnp.bfloat16), pltpu.VMEM((n, 8), jnp.float32)],
+        scratch_shapes=[
+            pltpu.VMEM((local, n), jnp.bfloat16),
+            pltpu.VMEM((n, 8), jnp.float32),
+            pltpu.SMEM(tile_owner.shape, jnp.int32),
+            pltpu.VMEM((n // local, 3, local), jnp.float32),
+            pltpu.VMEM((n // local, 1, local), jnp.float32),
+            pltpu.VMEM((n // local, columns, local), jnp.float32),
+            pltpu.SemaphoreType.DMA((7,)),
+        ],
         compiler_params=pltpu.CompilerParams(vmem_limit_bytes=VMEM),
         cost_estimate=pl.CostEstimate(
             flops=6 * n * local * (columns + 8), bytes_accessed=4 * n * local, transcendentals=0
         ),
         name="sort_region",
-    )(first, tile_owner, near, far, block, other)
+    )(first, in_hbm(tile_owner), in_hbm(near), far, in_hbm(near_error), far_error, in_hbm(block), other)
 
 
 def unsort_kernel(first_ref, rank_ref, block_ref, block_out, order_ref):
@@ -237,66 +269,75 @@
 def plan_blocks(own_y, near, far, regions, here, flags, columns, capacity):
     reach = flags.shape[0]
     rows = own_y.shape[0] // ROWS
-    stack = jnp.concatenate([near, far], axis=0)[:, :, columns:, :].astype(jnp.float32)
-    chunks = stack.shape[3] // LANES
-    y = (stack[:, :, 1] + stack[:, :, 4]) + stack[:, :, 7]
-    y = y.reshape(-1, LANES)
+    y_own = own_y.reshape(rows, ROWS)
     distance = regions - here
     ahead = jnp.arange(reach, dtype=jnp.int32)
     own_flag = jnp.sum(jnp.where(distance[..., None] == ahead, flags, 0.0), axis=-1)
-    far_flag = jnp.sum(jnp.where(-distance[..., None] == ahead, stack[:, :, 9, :reach], 0.0), axis=-1)
-    listed = jnp.broadcast_to(((own_flag + far_flag) > 0.5)[..., None], regions.shape + (chunks,))
-    y_own = own_y.reshape(rows, ROWS)
-    near_enough = (y[None, :, 0] <= y_own[:, -1:] + CUTOFF) & (y[None, :, -1] >= y_own[:, :1] - CUTOFF)
-    active = near_enough & listed.reshape(1, -1)
-    total = y.shape[0]
-    index = jnp.arange(total, dtype=jnp.int32)
-    counted = active.astype(jnp.int32)
-    batches = (jnp.sum(counted, axis=1) + BATCH - 1) // BATCH
+    half = near.shape[0]
+    counted = []
+    for part, piece in enumerate((near, far)):
+        extra = piece[:, :, columns:, :]
+        y = [extra[:, :, k].astype(jnp.float32).reshape(half, -1, extra.shape[3] // LANES, LANES) for k in (1, 4, 7)]
+        lowest = (y[0][..., 0] + y[1][..., 0]) + y[2][..., 0]
+        highest = (y[0][..., -1] + y[1][..., -1]) + y[2][..., -1]
+        side = slice(part * half, (part + 1) * half)
+        far_flag = jnp.sum(
+            jnp.where(-distance[side, :, None] == ahead, extra[:, :, 9, :reach].astype(jnp.float32), 0.0), axis=-1
+        )
+        listed = ((own_flag[side] + far_flag) > 0.5)[..., None]
+        active = listed & (lowest <= y_own[:, -1, None, None, None] + CUTOFF)
+        active = active & (highest >= y_own[:, 0, None, None, None] - CUTOFF)
+        counted.append(active.astype(jnp.int32).reshape(rows, -1))
+    size = counted[0].shape[1]
+    totals = [jnp.sum(count, axis=1) for count in counted]
+    pairs = lax.shift_right_logical(totals[0] + totals[1] + PAIR - 1, PAIR.bit_length() - 1)
     row = jnp.arange(rows, dtype=jnp.int32)
-    base = jnp.sum(jnp.where(row[:, None] < row[None, :], batches[:, None], 0), axis=0)
-    place = base[:, None] * BATCH + jnp.sum(
-        jnp.where(index[None, :, None] < index[None, None, :], counted[:, :, None], 0), axis=1
-    )
+    base = jnp.sum(jnp.where(row[:, None] < row[None, :], pairs[:, None], 0), axis=0)
+    index = jnp.arange(size, dtype=jnp.int32)
     spot = jnp.arange(capacity * BATCH, dtype=jnp.int32)
-    hit = active[:, :, None] & (place[:, :, None] == spot)
-    ids = jnp.sum(jnp.where(hit, index[None, :, None] + 1, 0), axis=(0, 1)) - 1
-    step = jnp.arange(capacity, dtype=jnp.int32)
-    owner = jnp.sum((base + batches)[:, None] <= step[None, :], axis=0, dtype=jnp.int32)
-    return ids, jnp.concatenate([jnp.minimum(owner, rows - 1), jnp.sum(batches, keepdims=True)])
+    ids = jnp.full(spot.shape, -1, jnp.int32)
+    for part, count in enumerate(counted):
+        before = jnp.sum(jnp.where(index[None, :, None] < index[None, None, :], count[:, :, None], 0), axis=1)
+        place = (base * PAIR + (totals[0] if part else 0))[:, None] + before
+        hit = (count > 0)[:, :, None] & (place[:, :, None] == spot)
+        ids = ids + jnp.sum(jnp.where(hit, index[None, :, None] + (part * size + 1), 0), axis=(0, 1))
+    step = jnp.arange(capacity * BATCH // PAIR, dtype=jnp.int32)
+    owner = jnp.sum((base + pairs)[:, None] <= step[None, :], axis=0, dtype=jnp.int32)
+    return ids, jnp.minimum(owner, rows - 1), base + pairs
 
 
 def gaspari_cohn(squared):
     squared = jnp.maximum(squared, 1e-12)
     inverse = lax.rsqrt(squared)
     scaled = squared * inverse
-    near = (((-0.25 * scaled + 0.5) * scaled + 0.625) * scaled - 5.0 / 3.0) * squared + 1.0
+    near = (((-3.0 * scaled + 6.0) * scaled + 7.5) * scaled - 20.0) * squared + 12.0
     left = jnp.maximum(2.0 - scaled, 0.0)
     left = left * left
-    far = (left * left) * ((scaled + 2.0) * scaled - 0.5) * (inverse * (1.0 / 12.0))
+    far = (left * left) * (((scaled + 2.0) * scaled - 0.5) * inverse)
     return jnp.where(scaled <= 1.0, near, far)
 
 
-def tiles_kernel(build, wanted, ids_ref, plan_ref, own_ref, near_ref, other_ref, *refs):
+def tiles_kernel(build, started, wanted, ids_ref, owner_ref, count_ref, own_ref, near_ref, other_ref, *refs):
     refs = list(refs)
-    tiles_in = None if build else refs.pop(0)
-    start_ref = None
+    tiles_ref = None if build else refs.pop(0)
+    start_ref = refs.pop(0) if started else None
     block_ref = scale_ref = out_ref = rounded_ref = gram_ref = None
     if wanted:
-        start_ref, block_ref, scale_ref = refs[:3]
-        refs = refs[3:]
-    tiles_out = refs.pop(0) if build else None
+        block_ref, scale_ref = refs[:2]
+        refs = refs[2:]
+    tiles_ref = refs.pop(0) if build else tiles_ref
     if wanted:
         out_ref, rounded_ref, gram_ref = refs[:3]
         refs = refs[3:]
-        wide_ref, far_ref, held_ref, all_ref, total_ref, sems, piece_sems = refs
+        wide_ref, far_ref, all_ref, total_ref, piece_sems = refs
+        held_ref = tiles_ref
     else:
-        total_ref, wide_ref, far_ref, held_ref, all_ref, sems, piece_sems = refs
+        total_ref, wide_ref, far_ref, all_ref, piece_sems, held_ref, sems = refs
     half, height, local = near_ref.shape
     columns = total_ref.shape[1]
     capacity = held_ref.shape[0]
     chunk_bits = (local // LANES).bit_length() - 1
-    total = plan_ref[capacity]
+    total = lax.div(count_ref[local // ROWS - 1] * PAIR + BATCH - 1, BATCH)
 
     copies = [
         pltpu.make_async_copy(ref, all_ref.at[pl.ds(part * half, half)], piece_sems.at[part])
@@ -307,17 +348,17 @@
 
     def copy_out(batch):
         return pltpu.make_async_copy(
-            held_ref.at[batch], tiles_out.at[batch], sems.at[lax.rem(batch, RING)]
+            held_ref.at[batch], tiles_ref.at[batch], sems.at[lax.rem(batch, RING)]
         )
 
     def copy_in(group):
         first = group * UNROLL
         return pltpu.make_async_copy(
-            tiles_in.at[pl.ds(first, UNROLL)], held_ref.at[pl.ds(first, UNROLL)], sems.at[group]
+            tiles_ref.at[pl.ds(first, UNROLL)], held_ref.at[pl.ds(first, UNROLL)], sems.at[group]
         )
 
-    groups = (total + UNROLL - 1) // UNROLL
-    if not build:
+    groups = lax.div(total + UNROLL - 1, UNROLL)
+    if not build and not wanted:
 
         def start_copy(group, carry):
             copy_in(group).start()
@@ -339,7 +380,7 @@
         for place in range(2 * half):
             rows = all_ref[place, columns:, :].astype(jnp.float32)
             rows = (rows[0:3] + rows[3:6]) + rows[6:9]
-            far_ref[place, 0:3, :] = jnp.concatenate([2.0 * rows[0:2], rows[2:3]], axis=0)
+            far_ref[place, 0:3, :] = jnp.concatenate([2.0 * rows[0:2], (1.0 / 12.0) * rows[2:3]], axis=0)
 
     def locate(batch, part):
         entry = ids_ref[batch * BATCH + part]
@@ -347,63 +388,76 @@
         lane = pl.multiple_of((chunk & ((1 << chunk_bits) - 1)) * LANES, LANES)
         return entry, lax.shift_right_logical(chunk, chunk_bits), lane
 
+    def rows_of(batch, pair):
+        return pl.ds(pl.multiple_of(owner_ref[batch * (BATCH // PAIR) + pair] * ROWS, ROWS), ROWS)
+
     def build_batch(batch):
-        start = pl.multiple_of(plan_ref[batch] * ROWS, ROWS)
         for part in range(BATCH):
+            rows = rows_of(batch, part // PAIR)
             entry, place, lane = locate(batch, part)
             far = far_ref[place, :, pl.ds(lane, LANES)]
-            across_x = wide_ref[0, pl.ds(start, ROWS), :] - far[0:1, :]
-            across_y = wide_ref[1, pl.ds(start, ROWS), :] - far[1:2, :]
+            across_x = wide_ref[0, rows, :] - far[0:1, :]
+            across_y = wide_ref[1, rows, :] - far[1:2, :]
             value = gaspari_cohn(across_x * across_x + across_y * across_y)
             spread = jnp.where(entry >= 0, far[2:3, :], 0.0)
-            value = wide_ref[2, pl.ds(start, ROWS), :] * spread * value
+            value = wide_ref[2, rows, :] * spread * value
             held_ref[batch, :, part * LANES : (part + 1) * LANES] = value.astype(jnp.bfloat16)
 
     def product(batch, valid=None):
-        sides = []
-        for part in range(BATCH):
-            _, place, lane = locate(batch, part)
-            sides.append(all_ref[place, :columns, pl.ds(lane, LANES)])
-        side = jnp.concatenate(sides, axis=1)
-        if valid is not None:
-            side = jnp.where(valid, side, jnp.zeros_like(side))
-        return dot_nt(held_ref[batch], side)
-
-    def add_product(batch, value):
-        start = pl.multiple_of(plan_ref[batch] * ROWS, ROWS)
-        total_ref[pl.ds(start, ROWS), :] += value
+        values = []
+        for pair in range(BATCH // PAIR):
+            sides = []
+            for part in range(pair * PAIR, (pair + 1) * PAIR):
+                _, place, lane = locate(batch, part)
+                sides.append(all_ref[place, :columns, pl.ds(lane, LANES)])
+            side = jnp.concatenate(sides, axis=1)
+            if valid is not None:
+                side = jnp.where(valid, side, jnp.zeros_like(side))
+            lanes = slice(pair * PAIR * LANES, (pair + 1) * PAIR * LANES)
+            values.append(dot_nt(held_ref[batch, :, lanes], side))
+        return values
+
+    def add_product(batch, values):
+        for pair, value in enumerate(values):
+            total_ref[rows_of(batch, pair), :] += value
 
     if build:
 
         @pl.when(total > 0)
         def _():
             build_batch(0)
-            copy_out(0).start()
+            if not wanted:
+                copy_out(0).start()
 
             def turn(batch, carry):
-                @pl.when(batch >= RING)
-                def _():
-                    copy_out(batch - RING).wait()
+                if not wanted:
+
+                    @pl.when(batch >= RING)
+                    def _():
+                        copy_out(batch - RING).wait()
 
                 value = product(batch - 1)
                 build_batch(batch)
                 add_product(batch - 1, value)
-                copy_out(batch).start()
+                if not wanted:
+                    copy_out(batch).start()
                 return carry
 
             lax.fori_loop(1, total, turn, 0)
             add_product(total - 1, product(total - 1))
-
-            def finish(batch, carry):
-                copy_out(batch).wait()
-                return carry
-
-            lax.fori_loop(jnp.maximum(total - RING, 0), total, finish, 0)
+            if not wanted:
+
+                def finish(batch, carry):
+                    copy_out(batch).wait()
+                    return carry
+
+                lax.fori_loop(jnp.maximum(total - RING, 0), total, finish, 0)
 
     else:
 
         def turn(group, carry):
-            copy_in(group).wait()
+            if not wanted:
+                copy_in(group).wait()
             batches = [jnp.minimum(group * UNROLL + i, total - 1) for i in range(UNROLL)]
             values = [
                 product(batch, group * UNROLL + i < total if i else None)
@@ -423,27 +477,30 @@
         gram_ref[...] = dot_nt(block, jnp.concatenate([block, result], axis=0), HIGHEST)
 
 
-def run_tiles(plan, own, near, far, tiles, capacity, columns, finish=None):
+def run_tiles(plan, own, near, far, tiles, capacity, columns, start, finish):
     build = tiles is None
+    wanted = finish is not None
+    kept = pl.BlockSpec(memory_space=pltpu.VMEM if wanted else pltpu.HBM)
     near, far = [piece.reshape((-1,) + piece.shape[2:]) for piece in (near, far)]
     half, height, local = near.shape
     smem = pl.BlockSpec(memory_space=pltpu.SMEM)
     anywhere = pl.BlockSpec(memory_space=pl.ANY)
     operands = [*plan, own, near, far]
-    in_specs = [smem, smem] + whole_vmem(1) + [anywhere] * 2
+    in_specs = [smem, smem, smem] + whole_vmem(1) + [anywhere] * 2
     out_shape, out_specs = [], []
     if not build:
         operands.append(tiles)
-        in_specs.append(anywhere)
-    wanted = False
-    if finish is not None:
-        wanted = True
-        total, block, scale = finish
-        operands += [total, block, scale]
-        in_specs += whole_vmem(3)
+        in_specs.append(kept)
+    if start is not None:
+        operands.append(start)
+        in_specs += whole_vmem(1)
+    if wanted:
+        operands += finish
+        in_specs += whole_vmem(2)
     if build:
-        out_shape.append(jax.ShapeDtypeStruct((capacity, ROWS, BATCH * LANES), jnp.bfloat16))
-        out_specs.append(anywhere)
+        space = pltpu.VMEM if wanted else pltpu.HBM
+        out_shape.append(space((capacity, ROWS, BATCH * LANES), jnp.bfloat16))
+        out_specs.append(kept)
     total_shape = (local, columns)
     scratch = []
     if wanted:
@@ -459,18 +516,17 @@
     scratch += [
         pltpu.VMEM((3, local, LANES), jnp.float32),
         pltpu.VMEM((2 * half, 8, local), jnp.float32),
-        pltpu.VMEM((capacity, ROWS, BATCH * LANES), jnp.bfloat16),
         pltpu.VMEM((2 * half, height, local), jnp.bfloat16),
     ]
     if wanted:
         scratch.append(pltpu.VMEM(total_shape, jnp.float32))
-    scratch += [
-        pltpu.SemaphoreType.DMA((RING if build else capacity // UNROLL,)),
-        pltpu.SemaphoreType.DMA((2,)),
-    ]
+    scratch.append(pltpu.SemaphoreType.DMA((2,)))
+    if not wanted:
+        scratch.append(pltpu.VMEM((capacity, ROWS, BATCH * LANES), jnp.bfloat16))
+        scratch.append(pltpu.SemaphoreType.DMA((RING if build else capacity // UNROLL,)))
     work = 2 * local * local
     return pl.pallas_call(
-        functools.partial(tiles_kernel, build, wanted),
+        functools.partial(tiles_kernel, build, start is not None, wanted),
         out_shape=tuple(out_shape),
         in_specs=in_specs,
         out_specs=tuple(out_specs),
@@ -484,9 +540,8 @@
 
 
 def reciprocal(value):
-    inverse = lax.rsqrt(value)
-    inverse = inverse * inverse
-    return inverse * (2.0 - value * inverse)
+    root = lax.rsqrt(value)
+    return root * root
 
 
 def small_product(left, right):
@@ -542,9 +597,10 @@
     second = solve_positive(cross - product[:, n:], jnp.transpose(mixed) - product[:, :n])
     first = jnp.transpose(step - dot_nn(carried, second, HIGHEST))
     second = jnp.transpose(second)
-    start, image = start_ref[...], images_ref[:n, :]
-    weights_ref[...] = dot_nn(first, start, HIGHEST) + dot_nn(second, image, HIGHEST)
-    residual_ref[...] = start - dot_nn(first, image, HIGHEST) - dot_nn(second, images_ref[n:, :], HIGHEST)
+    both = jnp.concatenate([first, second], axis=1)
+    start, images = start_ref[...], images_ref[...]
+    weights_ref[...] = dot_nn(both, jnp.concatenate([start, images[:n]], axis=0), HIGHEST)
+    residual_ref[...] = start - dot_nn(both, images, HIGHEST)
 
 
 def last_step(grams, start, images):
@@ -568,41 +624,49 @@
     even, odd = slot_offsets(regions)
     slot_region = here ^ jnp.where((slot_tile % 2 == 0)[:, None], even, odd)
 
-    places = jnp.concatenate([obs_geometry, obs_error[None, :]], axis=0)
     message, own, start, rank = sort_region(
-        first, tile_owner, *halves(places, "tile"), *halves(innovations, "tile")
+        first,
+        tile_owner,
+        *halves(obs_geometry, "tile"),
+        *halves(obs_error[None, :], "tile"),
+        *halves(innovations, "tile"),
     )
     scale = own[3:4]
     flags = jnp.where(tile_owner[0] >= 0, 1.0, 0.0).astype(jnp.float32)
 
-    half_regions = regions // 2
-    most = min(half_regions, 2 * reach - 1) * tiles_axis * (local // LANES)
-    capacity = (local // ROWS) * -(-most // BATCH)
-    capacity = -(-capacity // UNROLL) * UNROLL
-    run = functools.partial(run_tiles, own=own, capacity=capacity, columns=columns)
-
-    plans, tiles = [], []
-    total = None
-    for part, block in enumerate(exchange(message)):
-        if part:
-            block, total = lax.optimization_barrier((block, total))
-        near, far = halves(block, "tile")
-        inside = slot_region[:, part * half_regions : (part + 1) * half_regions]
-        plans.append(plan_blocks(own[1], near, far, inside, here, flags, columns, capacity))
-        finish = None if part == 0 else (total, start, scale)
-        built, total, *others = run(plans[part], near=near, far=far, tiles=None, finish=finish)
-        tiles.append(built)
-    image = total
-    image_rounded, grams = others
-
-    for part, block in enumerate(exchange(image_rounded)):
-        if part:
-            block, total = lax.optimization_barrier((block, total))
-        near, far = halves(block, "tile")
-        finish = None if part == 0 else (total, image, scale)
-        total, *others = run(plans[part], near=near, far=far, tiles=tiles[part], finish=finish)
-    second, cross = total, others[1]
-
+    def capacity_of(count):
+        most = min(count, 2 * reach - 1) * tiles_axis * (local // LANES)
+        batches = -(-(local // ROWS) * -(-most // PAIR) * PAIR // BATCH)
+        return -(-batches // UNROLL) * UNROLL
+
+    def sweep(sent, block, plans, stored):
+        total, slot, results = None, 0, None
+        groups = exchange(sent)
+        for index, group in enumerate(groups):
+            if index:
+                group, total = lax.optimization_barrier((group, total))
+            count = group.shape[0]
+            capacity = capacity_of(count)
+            near, far = halves(group, "tile")
+            if stored is None:
+                inside = slot_region[:, slot : slot + count]
+                plan = plan_blocks(own[1], near, far, inside, here, flags, columns, capacity)
+                plans.append(plan)
+            slot += count
+            last = index + 1 == len(groups)
+            results = run_tiles(
+                plans[index], own, near, far, None if stored is None else stored[index], capacity,
+                columns, total, (block, scale) if last else None,
+            )
+            if stored is None:
+                made.append(results[0])
+                results = results[1:]
+            total = results[0]
+        return results
+
+    plans, made = [], []
+    image, image_rounded, grams = sweep(message, start, plans, None)
+    second, _, cross = sweep(image_rounded, image, plans, made)
     grams = jnp.stack([grams, cross])
     grams = sum_regions(sum_tiles(grams))
     near, far = halves(jnp.concatenate([image, second], axis=0), "tile")

time: 116 us -> 112 us (0.966); the launches traced: 115 us -> 112 us
  local copies, waits for them, and re-layouts: 2.8 us -> 9.39 us
  waiting for transfers between devices: 48.5 us -> 44.1 us
  Pallas kernels: 31.4 us -> 27.9 us
  other arithmetic: 6.75 us -> 4.73 us
    unnamed x13 -> x31, local copies, waits for them, and re-layouts: 2.02 us -> 6.74 us
    pallas_call x4, Pallas kernels: 18.2 us -> 14.2 us  [run_tiles(): pl.pallas_call(functools.partial(tiles_kernel, build, start is not None,...]
    ppermute x8 -> x9, waiting for transfers between devices: 6.64 us -> 3.74 us  [swapped(): lax.ppermute(block, axis, [(i, i ^ bit) for i in range(lax.axis_size(axis...]
    ppermute x12, waiting for transfers between devices: 41.8 us -> 40.4 us  [swap_regions(): return lax.ppermute(block, ('region', 'tile'), route)]
    concatenate x2 -> x0, other arithmetic: 1.31 us -> none  [plan_blocks(): jnp.concatenate([jnp.minimum(owner, rows - 1), jnp.sum(batches, keepdims=...]
    reduce_sum x14 -> x15, other arithmetic: 2.92 us -> 1.9 us  [the longest x4 0.74 us: plan_blocks(): jnp.sum(jnp.where(hit, index[None, :, None] + (part * size + 1), 0), axis...]
  transfers between devices with their start and end apart: 20 -> 21, of which waited for: 18 -> 15; matrix products, arithmetic and copies ran while one was open for 4% -> 7% of each run, Pallas kernels for 9% -> 8%
where the time goes in v6:
time: 112 us
  waiting for transfers between devices  44.1 us (39%)
  Pallas kernels  27.9 us (25%)
  starting transfers between devices  25.4 us (23%)
  local copies, waits for them, and re-layouts  9.39 us (8%)
  other arithmetic  4.73 us (4%)
    ppermute x12, waiting for transfers between devices, swap_regions(): return lax.ppermute(block, ('region', 'tile'), route)  40.4 us
    ppermute x12, starting transfers between devices, swap_regions(): return lax.ppermute(block, ('region', 'tile'), route)  23.9 us
    pallas_call x4, Pallas kernels, run_tiles(): pl.pallas_call(functools.partial(tiles_kernel, build, start is not None,...  14.2 us
    pallas_call x1, Pallas kernels, last_step(): pl.pallas_call(last_kernel, out_shape=(jax.ShapeDtypeStruct(start.shape,...  7.67 us
    unnamed x31, local copies, waits for them, and re-layouts  6.74 us
    pallas_call x1, Pallas kernels, sort_region(): pl.pallas_call(sort_kernel, out_shape=(jax.ShapeDtypeStruct((columns + EX...  4.62 us
    ppermute x9, waiting for transfers between devices, swapped(): lax.ppermute(block, axis, [(i, i ^ bit) for i in range(lax.axis_size(axis...  3.74 us
  transfers between devices with their start and end apart: 21, of which 15 were waited for; matrix products, arithmetic and copies ran while one was open for 7% of the time, Pallas kernels for 8%

profile of v6, /device:TPU:0, one launch (start us, length us, event | category | flops | bytes accessed | tf_op | source)
XLA Modules:
  0.0 112.5 jit_solution(6520048800009824421)
XLA Ops:
  0.6 0.5 collective-permute-start.2
  1.2 0.4 collective-permute-start.1
  1.7 0.7 select_xor_fusion
  2.5 0.7 fusion.19
  3.2 4.6 %sort_region.1 = (bf16[80,512]{1,0:T(8,128)(2,1)S(1)}, f32[8,512]{1,0:T(8,128)S(1)}, f32[64,512]{1,0:T(8,128)S(1)}, s32[1,512]{1,0:T(1,128)S(1)}) custom-call(s32[2]{0:T(128)S(1)} %fusion.21.first_ref, s32[1,7]{1,0:T(1,128)} %owner_ref.1, f32[1,3,512]{2,1,0:T(4,128)} %bitcast.162, f32[1,3,512]{2,1,0:T(4,128)S(1)} %collective-permute-done.far_ref, ...), custom_call_target="tpu_custom_call" | custom-call | flops 226492416 | bytes 2097152 | tf_op jit(solution)/shard_map/sort_region/pallas_call | solution.py:218
  7.8 3.7 %collective-permute-start.3 = (bf16[1,80,512]{2,1,0:T(8,128)(2,1)S(1)}, bf16[1,80,512]{2,1,0:T(8,128)(2,1)S(1)}, u32[]{:S(2)}, u32[]{:S(2)}) collective-permute-start(bf16[1,80,512]{2,1,0:T(8,128)(2,1)S(1)} %bitcast.115), channel_id=1, source_target_pairs={{0,16},{1,17},{2,18},{3,19},{4,20},{5,21},{6,22},{7,23},{8,24},{9,... | collective-permute-start | bytes 245768 | tf_op jit(solution)/shard_map/ppermute | solution.py:79
  11.6 4.8 %collective-permute-done.3 = bf16[1,80,512]{2,1,0:T(8,128)(2,1)S(1)} collective-permute-done((bf16[1,80,512]{2,1,0:T(8,128)(2,1)S(1)}, bf16[1,80,512]{2,1,0:T(8,128)(2,1)S(1)}, u32[]{:S(2)}, u32[]{:S(2)}) %collective-permute-start.3) | collective-permute-done | bytes 81952 | tf_op jit(solution)/shard_map/ppermute | solution.py:79
  16.4 0.8 collective-permute-start.4
  17.3 4.5 %collective-permute-done.4 = bf16[2,80,512]{2,1,0:T(8,128)(2,1)S(1)} collective-permute-done((bf16[2,80,512]{2,1,0:T(8,128)(2,1)S(1)}, bf16[2,80,512]{2,1,0:T(8,128)(2,1)S(1)}, u32[]{:S(2)}, u32[]{:S(2)}) %collective-permute-start.4) | collective-permute-done | bytes 163872 | tf_op jit(solution)/shard_map/ppermute | solution.py:79
  21.8 1.6 %collective-permute-start.5 = (bf16[4,80,512]{2,1,0:T(8,128)(2,1)S(1)}, bf16[4,80,512]{2,1,0:T(8,128)(2,1)S(1)}, u32[]{:S(2)}, u32[]{:S(2)}) collective-permute-start(bf16[4,80,512]{2,1,0:T(8,128)(2,1)S(1)} %pad_maximum_fusion.3), channel_id=1, source_target_pairs={{0,4},{1,9},{2,6},{3,11},{4,0},{5,13},{6,2},{7,15},{8,12},{9,1},{1... | collective-permute-start | bytes 983048 | tf_op jit(solution)/shard_map/ppermute | solution.py:79
  23.8 5.1 %collective-permute-done.5 = bf16[4,80,512]{2,1,0:T(8,128)(2,1)S(1)} collective-permute-done((bf16[4,80,512]{2,1,0:T(8,128)(2,1)S(1)}, bf16[4,80,512]{2,1,0:T(8,128)(2,1)S(1)}, u32[]{:S(2)}, u32[]{:S(2)}) %collective-permute-start.5) | collective-permute-done | bytes 327712 | tf_op jit(solution)/shard_map/ppermute | solution.py:79
  29.4 0.1 copy.128
  29.6 0.1 copy.129
  29.8 0.1 copy.130
  30.1 0.1 copy.133
  30.3 0.1 copy.134
  30.5 1.6 %collective-permute-start.6 = (bf16[8,80,512]{2,1,0:T(8,128)(2,1)S(1)}, bf16[8,80,512]{2,1,0:T(8,128)(2,1)S(1)}, u32[]{:S(2)}, u32[]{:S(2)}) collective-permute-start(bf16[8,80,512]{2,1,0:T(8,128)(2,1)S(1)} %get-tuple-element.57.near_ref), channel_id=1, source_target_pairs={{0,2},{1,5},{2,0},{3,7},{4,6},{5,1},{6,4},{7,3},{8,10},{9,13},{10,... | collective-permute-start | bytes 1966088 | tf_op jit(solution)/shard_map/ppermute | solution.py:79
  32.2 0.1 copy.136
  32.4 0.1 copy.137
  32.6 0.1 copy.138
  32.9 0.1 copy.140
  33.1 0.1 copy.141
  33.8 0.2 fusion.13
  34.3 0.1 select_reduce_fusion.7
  34.6 0.2 select_reduce_fusion.3
  34.8 0.2 select_reduce_fusion.2
  35.0 5.5 %build_first.1 = (bf16[128,64,512]{2,1,0:T(8,128)(2,1)}, f32[512,64]{1,0:T(8,128)S(1)}) custom-call(s32[512]{0:T(512)S(1)} %add_add_fusion.9.ids_ref, s32[256]{0:T(256)S(1)} %broadcast_minimum_fusion.1.owner_ref, s32[8]{0:T(128)S(1)} %get-tuple-element.113.count_ref, f32[8,512]{1,0:T(8,128)S(1)} %get-tuple-element.19.own_ref, ...), custom_call_target="tpu_custom_call" | custom-call | flops 9437184000 | bytes 4194304 | tf_op jit(solution)/shard_map/build_first/pallas_call | solution.py:528
  40.4 0.6 collective-permute-done.6.near_ref
  41.5 0.1 copy.142
  41.6 0.1 copy.143
  41.7 0.1 copy.144
  42.1 0.1 copy.146
  42.2 0.1 copy.147
  42.5 0.7 collective-permute-done.8
  43.3 0.1 copy.148
  43.9 0.1 copy.151
  44.1 0.1 copy.152
  44.9 0.2 fusion.17
  45.4 0.1 select_reduce_fusion.5
  45.6 0.2 select_reduce_fusion.1
  45.9 0.2 select_reduce_fusion
  46.1 4.4 %build_last.1 = (bf16[128,64,512]{2,1,0:T(8,128)(2,1)S(1)}, f32[64,512]{1,0:T(8,128)S(1)}, bf16[64,512]{1,0:T(8,128)(2,1)S(1)}, f32[64,128]{1,0:T(8,128)S(1)}) custom-call(s32[512]{0:T(512)S(1)} %add_add_fusion.8.ids_ref, s32[256]{0:T(256)S(1)} %broadcast_minimum_fusion.owner_ref, s32[8]{0:T(128)S(1)} %get-tuple-element.110.count_ref, ...), custom_call_target="tpu_custom_call" | custom-call | flops 9437184000 | bytes 4194304 | tf_op jit(solution)/shard_map/build_last/pallas_call | solution.py:528
  50.5 3.0 %collective-permute-start.9 = (bf16[1,64,512]{2,1,0:T(8,128)(2,1)S(1)}, bf16[1,64,512]{2,1,0:T(8,128)(2,1)S(1)}, u32[]{:S(2)}, u32[]{:S(2)}) collective-permute-start(bf16[1,64,512]{2,1,0:T(8,128)(2,1)S(1)} %bitcast.119), channel_id=1, source_target_pairs={{0,16},{1,17},{2,18},{3,19},{4,20},{5,21},{6,22},{7,23},{8,24},{9,... | collective-permute-start | bytes 196616 | tf_op jit(solution)/shard_map/ppermute | solution.py:79
  53.5 2.5 %collective-permute-done.9 = bf16[1,64,512]{2,1,0:T(8,128)(2,1)S(1)} collective-permute-done((bf16[1,64,512]{2,1,0:T(8,128)(2,1)S(1)}, bf16[1,64,512]{2,1,0:T(8,128)(2,1)S(1)}, u32[]{:S(2)}, u32[]{:S(2)}) %collective-permute-start.9) | collective-permute-done | bytes 65568 | tf_op jit(solution)/shard_map/ppermute | solution.py:79
  56.0 3.1 %collective-permute-start.10 = (bf16[2,64,512]{2,1,0:T(8,128)(2,1)S(1)}, bf16[2,64,512]{2,1,0:T(8,128)(2,1)S(1)}, u32[]{:S(2)}, u32[]{:S(2)}) collective-permute-start(bf16[2,64,512]{2,1,0:T(8,128)(2,1)S(1)} %pad_maximum_fusion.6), channel_id=1, source_target_pairs={{0,8},{1,3},{2,10},{3,1},{4,12},{5,7},{6,14},{7,5},{8,0},{9,11},{1... | collective-permute-start | bytes 393224 | tf_op jit(solution)/shard_map/ppermute | solution.py:79
  59.1 2.9 %collective-permute-done.10 = bf16[2,64,512]{2,1,0:T(8,128)(2,1)S(1)} collective-permute-done((bf16[2,64,512]{2,1,0:T(8,128)(2,1)S(1)}, bf16[2,64,512]{2,1,0:T(8,128)(2,1)S(1)}, u32[]{:S(2)}, u32[]{:S(2)}) %collective-permute-start.10) | collective-permute-done | bytes 131104 | tf_op jit(solution)/shard_map/ppermute | solution.py:79
  62.1 2.0 %collective-permute-start.11 = (bf16[4,64,512]{2,1,0:T(8,128)(2,1)S(1)}, bf16[4,64,512]{2,1,0:T(8,128)(2,1)S(1)}, u32[]{:S(2)}, u32[]{:S(2)}) collective-permute-start(bf16[4,64,512]{2,1,0:T(8,128)(2,1)S(1)} %pad_maximum_fusion.4), channel_id=1, source_target_pairs={{0,4},{1,9},{2,6},{3,11},{4,0},{5,13},{6,2},{7,15},{8,12},{9,1},{1... | collective-permute-start | bytes 786440 | tf_op jit(solution)/shard_map/ppermute | solution.py:79
  64.1 4.5 %collective-permute-done.11 = bf16[4,64,512]{2,1,0:T(8,128)(2,1)S(1)} collective-permute-done((bf16[4,64,512]{2,1,0:T(8,128)(2,1)S(1)}, bf16[4,64,512]{2,1,0:T(8,128)(2,1)S(1)}, u32[]{:S(2)}, u32[]{:S(2)}) %collective-permute-start.11) | collective-permute-done | bytes 262176 | tf_op jit(solution)/shard_map/ppermute | solution.py:79
  68.7 4.2 %collective-permute-start.12 = (bf16[8,64,512]{2,1,0:T(8,128)(2,1)S(1)}, bf16[8,64,512]{2,1,0:T(8,128)(2,1)S(1)}, u32[]{:S(2)}, u32[]{:S(2)}) collective-permute-start(bf16[8,64,512]{2,1,0:T(8,128)(2,1)S(1)} %get-tuple-element.59.near_ref), channel_id=1, source_target_pairs={{0,2},{1,5},{2,0},{3,7},{4,6},{5,1},{6,4},{7,3},{8,10},{9,13},{10,... | collective-permute-start | bytes 1572872 | tf_op jit(solution)/shard_map/ppermute | solution.py:79
  72.9 3.4 %copy-done.1 = bf16[128,64,512]{2,1,0:T(8,128)(2,1)S(1)} copy-done((bf16[128,64,512]{2,1,0:T(8,128)(2,1)S(1)}, bf16[128,64,512]{2,1,0:T(8,128)(2,1)}, u32[]{:S(2)}) %copy-start.1) | copy-done | bytes 8388632
  76.3 2.0 %apply_first.1.refs_1_ = f32[512,64]{1,0:T(8,128)S(1)} custom-call(s32[512]{0:T(512)S(1)} %add_add_fusion.9.ids_ref, s32[256]{0:T(256)S(1)} %broadcast_minimum_fusion.1.owner_ref, s32[8]{0:T(128)S(1)} %get-tuple-element.113.count_ref, f32[8,512]{1,0:T(8,128)S(1)} %get-tuple-element.19.own_ref, bf16[8,64,512]{2,1,0:T(8,128)(2,1)S(1)} %get-tuple-element.59.near_ref, ...), custom_call_target="tpu_custom_call" | custom-call | flops 4718592000 | bytes 4194304 | tf_op jit(solution)/shard_map/apply_first/pallas_call | solution.py:528
  78.3 1.7 %collective-permute-done.12.near_ref = bf16[8,64,512]{2,1,0:T(8,128)(2,1)S(1)} collective-permute-done((bf16[8,64,512]{2,1,0:T(8,128)(2,1)S(1)}, bf16[8,64,512]{2,1,0:T(8,128)(2,1)S(1)}, u32[]{:S(2)}, u32[]{:S(2)}) %collective-permute-start.12) | collective-permute-done | bytes 524320 | tf_op jit(solution)/shard_map/ppermute | solution.py:79
  80.1 1.9 %collective-permute-done.14 = bf16[1,8,64,512]{3,2,1,0:T(8,128)(2,1)S(1)} collective-permute-done((bf16[1,8,64,512]{3,2,1,0:T(8,128)(2,1)S(1)}, bf16[1,8,64,512]{3,2,1,0:T(8,128)(2,1)S(1)}, u32[]{:S(2)}, u32[]{:S(2)}) %collective-permute-start.14) | collective-permute-done | bytes 524320 | tf_op jit(solution)/shard_map/ppermute | solution.py:61
  82.0 2.3 %apply_last.1 = (f32[64,512]{1,0:T(8,128)S(1)}, bf16[64,512]{1,0:T(8,128)(2,1)}, f32[64,128]{1,0:T(8,128)S(1)}) custom-call(s32[512]{0:T(512)S(1)} %add_add_fusion.8.ids_ref, s32[256]{0:T(256)S(1)} %broadcast_minimum_fusion.owner_ref, s32[8]{0:T(128)S(1)} %get-tuple-element.110.count_ref, f32[8,512]{1,0:T(8,128)S(1)} %get-tuple-element.19.own_ref, ...), custom_call_target="tpu_custom_call" | custom-call | flops 4718592000 | bytes 4194304 | tf_op jit(solution)/shard_map/apply_last/pallas_call | solution.py:528
  84.3 0.2 collective-permute-start.15
  84.6 1.1 collective-permute-done.15
  85.7 1.4 %collective-permute-start.16 = (f32[2,64,128]{2,1,0:T(8,128)S(1)}, f32[2,64,128]{2,1,0:T(8,128)S(1)}, u32[]{:S(2)}, u32[]{:S(2)}) collective-permute-start(f32[2,64,128]{2,1,0:T(8,128)S(1)} %fusion.24), channel_id=1, source_target_pairs={{0,16},{1,5},{2,18},{3,7},{4,20},{5,1},{6,22},{7,3},{8,24},{9,13},... | collective-permute-start | bytes 196616 | tf_op jit(solution)/shard_map/ppermute | solution.py:79
  87.2 4.3 %collective-permute-done.16 = f32[2,64,128]{2,1,0:T(8,128)S(1)} collective-permute-done((f32[2,64,128]{2,1,0:T(8,128)S(1)}, f32[2,64,128]{2,1,0:T(8,128)S(1)}, u32[]{:S(2)}, u32[]{:S(2)}) %collective-permute-start.16) | collective-permute-done | bytes 65568 | tf_op jit(solution)/shard_map/ppermute | solution.py:79
  91.6 4.3 %collective-permute-done.17 = f32[2,64,128]{2,1,0:T(8,128)S(1)} collective-permute-done((f32[2,64,128]{2,1,0:T(8,128)S(1)}, f32[2,64,128]{2,1,0:T(8,128)S(1)}, u32[]{:S(2)}, u32[]{:S(2)}) %collective-permute-start.17) | collective-permute-done | bytes 65568 | tf_op jit(solution)/shard_map/ppermute | solution.py:79
  95.9 4.3 %collective-permute-done.18 = f32[2,64,128]{2,1,0:T(8,128)S(1)} collective-permute-done((f32[2,64,128]{2,1,0:T(8,128)S(1)}, f32[2,64,128]{2,1,0:T(8,128)S(1)}, u32[]{:S(2)}, u32[]{:S(2)}) %collective-permute-start.18) | collective-permute-done | bytes 65568 | tf_op jit(solution)/shard_map/ppermute | solution.py:79
  100.2 2.3 %collective-permute-start.19 = (f32[2,64,128]{2,1,0:T(8,128)S(1)}, f32[2,64,128]{2,1,0:T(8,128)S(1)}, u32[]{:S(2)}, u32[]{:S(2)}) collective-permute-start(f32[2,64,128]{2,1,0:T(8,128)S(1)} %add.434), channel_id=1, source_target_pairs={{0,2},{1,9},{2,0},{3,11},{4,6},{5,13},{6,4},{7,15},{8,10},{9,1},{1... | collective-permute-start | bytes 196616 | tf_op jit(solution)/shard_map/ppermute | solution.py:79
  102.6 1.4 %unsort.1.images_ref = f32[128,512]{1,0:T(8,128)S(1)} custom-call(s32[2]{0:T(128)S(1)} %fusion.21.first_ref, s32[1,512]{1,0:T(1,128)S(1)} %get-tuple-element.32.rank_ref, f32[128,1024]{1,0:T(8,128)S(1)} %pad_maximum_fusion.2.block_ref), custom_call_target="tpu_custom_call" | custom-call | flops 402653184 | bytes 2097152 | tf_op jit(solution)/shard_map/unsort/pallas_call | solution.py:255
  104.0 0.8 collective-permute-done.19
  104.8 7.7 %last_step.1 = (f32[64,512]{1,0:T(8,128)}, f32[64,512]{1,0:T(8,128)}) custom-call(f32[2,64,128]{2,1,0:T(8,128)S(1)} %add.435.grams_ref, f32[64,512]{1,0:T(8,128)S(1)} %copy-done, f32[128,512]{1,0:T(8,128)S(1)} %unsort.1.images_ref), custom_call_target="tpu_custom_call" | custom-call | tf_op jit(solution)/shard_map/last_step/pallas_call | solution.py:607
  (123 shorter events, 5.9 us)
Async XLA Ops:
  0.6 2.6 %collective-permute-start.2 = (f32[1,64,512]{2,1,0:T(8,128)}, f32[1,64,512]{2,1,0:T(8,128)S(1)}, u32[]{:S(2)}, u32[]{:S(2)}) collective-permute-start(f32[1,64,512]{2,1,0:T(8,128)} %bitcast.129), channel_id=1, source_target_pairs={{0,1},{1,0},{2,3},{3,2},{4,5},{5,4},{6,7},{7,6},{8,9},{9,8},{10,11... | collective-permute-start | bytes 393224 | tf_op jit(solution)/shard_map/ppermute | solution.py:61
  1.1 2.0 %collective-permute-start = (f32[1,3,512]{2,1,0:T(4,128)}, f32[1,3,512]{2,1,0:T(4,128)S(1)}, u32[]{:S(2)}, u32[]{:S(2)}) collective-permute-start(f32[1,3,512]{2,1,0:T(4,128)} %bitcast.161), channel_id=1, source_target_pairs={{0,1},{1,0},{2,3},{3,2},{4,5},{5,4},{6,7},{7,6},{8,9},{9,8},{10,11... | collective-permute-start | bytes 18440 | tf_op jit(solution)/shard_map/ppermute | solution.py:61
  1.2 2.0 %collective-permute-start.1 = (f32[1,1,512]{2,1,0:T(1,128)}, f32[1,1,512]{2,1,0:T(1,128)S(1)}, u32[]{:S(2)}, u32[]{:S(2)}) collective-permute-start(f32[1,1,512]{2,1,0:T(1,128)} %bitcast.163), channel_id=1, source_target_pairs={{0,1},{1,0},{2,3},{3,2},{4,5},{5,4},{6,7},{7,6},{8,9},{9,8},{10,11... | collective-permute-start | bytes 6152 | tf_op jit(solution)/shard_map/ppermute | solution.py:61
  7.8 8.5 %collective-permute-start.3 = (bf16[1,80,512]{2,1,0:T(8,128)(2,1)S(1)}, bf16[1,80,512]{2,1,0:T(8,128)(2,1)S(1)}, u32[]{:S(2)}, u32[]{:S(2)}) collective-permute-start(bf16[1,80,512]{2,1,0:T(8,128)(2,1)S(1)} %bitcast.115), channel_id=1, source_target_pairs={{0,16},{1,17},{2,18},{3,19},{4,20},{5,21},{6,22},{7,23},{8,24},{9,... | collective-permute-start | bytes 245768 | tf_op jit(solution)/shard_map/ppermute | solution.py:79
  16.4 5.4 %collective-permute-start.4 = (bf16[2,80,512]{2,1,0:T(8,128)(2,1)S(1)}, bf16[2,80,512]{2,1,0:T(8,128)(2,1)S(1)}, u32[]{:S(2)}, u32[]{:S(2)}) collective-permute-start(bf16[2,80,512]{2,1,0:T(8,128)(2,1)S(1)} %pad_maximum_fusion.5), channel_id=1, source_target_pairs={{0,8},{1,3},{2,10},{3,1},{4,12},{5,7},{6,14},{7,5},{8,0},{9,11},{1... | collective-permute-start | bytes 491528 | tf_op jit(solution)/shard_map/ppermute | solution.py:79
  21.8 7.1 %collective-permute-start.5 = (bf16[4,80,512]{2,1,0:T(8,128)(2,1)S(1)}, bf16[4,80,512]{2,1,0:T(8,128)(2,1)S(1)}, u32[]{:S(2)}, u32[]{:S(2)}) collective-permute-start(bf16[4,80,512]{2,1,0:T(8,128)(2,1)S(1)} %pad_maximum_fusion.3), channel_id=1, source_target_pairs={{0,4},{1,9},{2,6},{3,11},{4,0},{5,13},{6,2},{7,15},{8,12},{9,1},{1... | collective-permute-start | bytes 983048 | tf_op jit(solution)/shard_map/ppermute | solution.py:79
  29.1 3.0 %collective-permute-start.7 = (bf16[1,8,80,512]{3,2,1,0:T(8,128)(2,1)S(1)}, bf16[1,8,80,512]{3,2,1,0:T(8,128)(2,1)S(1)}, u32[]{:S(2)}, u32[]{:S(2)}) collective-permute-start(bf16[1,8,80,512]{3,2,1,0:T(8,128)(2,1)S(1)} %get-tuple-element.56), channel_id=1, source_target_pairs={{0,1},{1,0},{2,3},{3,2},{4,5},{5,4},{6,7},{7,6},{8,9},{9,8},{10,11... | collective-permute-start | bytes 1966088 | tf_op jit(solution)/shard_map/ppermute | solution.py:61
  30.5 10.6 %collective-permute-start.6 = (bf16[8,80,512]{2,1,0:T(8,128)(2,1)S(1)}, bf16[8,80,512]{2,1,0:T(8,128)(2,1)S(1)}, u32[]{:S(2)}, u32[]{:S(2)}) collective-permute-start(bf16[8,80,512]{2,1,0:T(8,128)(2,1)S(1)} %get-tuple-element.57.near_ref), channel_id=1, source_target_pairs={{0,2},{1,5},{2,0},{3,7},{4,6},{5,1},{6,4},{7,3},{8,10},{9,13},{10,... | collective-permute-start | bytes 1966088 | tf_op jit(solution)/shard_map/ppermute | solution.py:79
  41.1 2.1 %collective-permute-start.8 = (bf16[1,8,80,512]{3,2,1,0:T(8,128)(2,1)S(1)}, bf16[1,8,80,512]{3,2,1,0:T(8,128)(2,1)S(1)}, u32[]{:S(2)}, u32[]{:S(2)}) collective-permute-start(bf16[1,8,80,512]{3,2,1,0:T(8,128)(2,1)S(1)} %bitcast.131), channel_id=1, source_target_pairs={{0,1},{1,0},{2,3},{3,2},{4,5},{5,4},{6,7},{7,6},{8,9},{9,8},{10,11... | collective-permute-start | bytes 1966088 | tf_op jit(solution)/shard_map/ppermute | solution.py:61
  50.5 5.5 %collective-permute-start.9 = (bf16[1,64,512]{2,1,0:T(8,128)(2,1)S(1)}, bf16[1,64,512]{2,1,0:T(8,128)(2,1)S(1)}, u32[]{:S(2)}, u32[]{:S(2)}) collective-permute-start(bf16[1,64,512]{2,1,0:T(8,128)(2,1)S(1)} %bitcast.119), channel_id=1, source_target_pairs={{0,16},{1,17},{2,18},{3,19},{4,20},{5,21},{6,22},{7,23},{8,24},{9,... | collective-permute-start | bytes 196616 | tf_op jit(solution)/shard_map/ppermute | solution.py:79
  56.0 6.0 %collective-permute-start.10 = (bf16[2,64,512]{2,1,0:T(8,128)(2,1)S(1)}, bf16[2,64,512]{2,1,0:T(8,128)(2,1)S(1)}, u32[]{:S(2)}, u32[]{:S(2)}) collective-permute-start(bf16[2,64,512]{2,1,0:T(8,128)(2,1)S(1)} %pad_maximum_fusion.6), channel_id=1, source_target_pairs={{0,8},{1,3},{2,10},{3,1},{4,12},{5,7},{6,14},{7,5},{8,0},{9,11},{1... | collective-permute-start | bytes 393224 | tf_op jit(solution)/shard_map/ppermute | solution.py:79
  62.1 6.4 %collective-permute-start.11 = (bf16[4,64,512]{2,1,0:T(8,128)(2,1)S(1)}, bf16[4,64,512]{2,1,0:T(8,128)(2,1)S(1)}, u32[]{:S(2)}, u32[]{:S(2)}) collective-permute-start(bf16[4,64,512]{2,1,0:T(8,128)(2,1)S(1)} %pad_maximum_fusion.4), channel_id=1, source_target_pairs={{0,4},{1,9},{2,6},{3,11},{4,0},{5,13},{6,2},{7,15},{8,12},{9,1},{1... | collective-permute-start | bytes 786440 | tf_op jit(solution)/shard_map/ppermute | solution.py:79
  68.6 4.3 %collective-permute-start.13 = (bf16[1,8,64,512]{3,2,1,0:T(8,128)(2,1)S(1)}, bf16[1,8,64,512]{3,2,1,0:T(8,128)(2,1)S(1)}, u32[]{:S(2)}, u32[]{:S(2)}) collective-permute-start(bf16[1,8,64,512]{3,2,1,0:T(8,128)(2,1)S(1)} %get-tuple-element.58), channel_id=1, source_target_pairs={{0,1},{1,0},{2,3},{3,2},{4,5},{5,4},{6,7},{7,6},{8,9},{9,8},{10,11... | collective-permute-start | bytes 1572872 | tf_op jit(solution)/shard_map/ppermute | solution.py:61
  68.7 11.3 %collective-permute-start.12 = (bf16[8,64,512]{2,1,0:T(8,128)(2,1)S(1)}, bf16[8,64,512]{2,1,0:T(8,128)(2,1)S(1)}, u32[]{:S(2)}, u32[]{:S(2)}) collective-permute-start(bf16[8,64,512]{2,1,0:T(8,128)(2,1)S(1)} %get-tuple-element.59.near_ref), channel_id=1, source_target_pairs={{0,2},{1,5},{2,0},{3,7},{4,6},{5,1},{6,4},{7,3},{8,10},{9,13},{10,... | collective-permute-start | bytes 1572872 | tf_op jit(solution)/shard_map/ppermute | solution.py:79
  72.9 3.4 %copy-start.1 = (bf16[128,64,512]{2,1,0:T(8,128)(2,1)S(1)}, bf16[128,64,512]{2,1,0:T(8,128)(2,1)}, u32[]{:S(2)}) copy-start(bf16[128,64,512]{2,1,0:T(8,128)(2,1)} %get-tuple-element.26.refs_0_) | copy-start | bytes 25165828
  80.1 1.9 %collective-permute-start.14 = (bf16[1,8,64,512]{3,2,1,0:T(8,128)(2,1)S(1)}, bf16[1,8,64,512]{3,2,1,0:T(8,128)(2,1)S(1)}, u32[]{:S(2)}, u32[]{:S(2)}) collective-permute-start(bf16[1,8,64,512]{3,2,1,0:T(8,128)(2,1)S(1)} %bitcast.136), channel_id=1, source_target_pairs={{0,1},{1,0},{2,3},{3,2},{4,5},{5,4},{6,7},{7,6},{8,9},{9,8},{10,11... | collective-permute-start | bytes 1572872 | tf_op jit(solution)/shard_map/ppermute | solution.py:61
  82.0 22.8 %copy-start = (f32[64,512]{1,0:T(8,128)S(1)}, f32[64,512]{1,0:T(8,128)}, u32[]{:S(2)}) copy-start(f32[64,512]{1,0:T(8,128)} %start_ref.1) | copy-start | bytes 393220
  84.3 1.3 %collective-permute-start.15 = (f32[2,64,128]{2,1,0:T(8,128)S(1)}, f32[2,64,128]{2,1,0:T(8,128)S(1)}, u32[]{:S(2)}, u32[]{:S(2)}) collective-permute-start(f32[2,64,128]{2,1,0:T(8,128)S(1)} %pad_maximum_fusion.7), channel_id=1, source_target_pairs={{0,1},{1,0},{2,3},{3,2},{4,5},{5,4},{6,7},{7,6},{8,9},{9,8},{10,11... | collective-permute-start | bytes 196616 | tf_op jit(solution)/shard_map/ppermute | solution.py:61
  85.7 5.8 %collective-permute-start.16 = (f32[2,64,128]{2,1,0:T(8,128)S(1)}, f32[2,64,128]{2,1,0:T(8,128)S(1)}, u32[]{:S(2)}, u32[]{:S(2)}) collective-permute-start(f32[2,64,128]{2,1,0:T(8,128)S(1)} %fusion.24), channel_id=1, source_target_pairs={{0,16},{1,5},{2,18},{3,7},{4,20},{5,1},{6,22},{7,3},{8,24},{9,13},... | collective-permute-start | bytes 196616 | tf_op jit(solution)/shard_map/ppermute | solution.py:79
  87.1 15.4 %collective-permute-start.20 = (f32[1,128,512]{2,1,0:T(8,128)S(1)}, f32[1,128,512]{2,1,0:T(8,128)S(1)}, u32[]{:S(2)}, u32[]{:S(2)}) collective-permute-start(f32[1,128,512]{2,1,0:T(8,128)S(1)} %bitcast.139), channel_id=1, source_target_pairs={{0,1},{1,0},{2,3},{3,2},{4,5},{5,4},{6,7},{7,6},{8,9},{9,8},{10,11... | collective-permute-start | bytes 786440 | tf_op jit(solution)/shard_map/ppermute | solution.py:61
  91.5 4.3 %collective-permute-start.17 = (f32[2,64,128]{2,1,0:T(8,128)S(1)}, f32[2,64,128]{2,1,0:T(8,128)S(1)}, u32[]{:S(2)}, u32[]{:S(2)}) collective-permute-start(f32[2,64,128]{2,1,0:T(8,128)S(1)} %fusion.42), channel_id=1, source_target_pairs={{0,8},{1,3},{2,10},{3,1},{4,12},{5,7},{6,14},{7,5},{8,0},{9,11},{1... | collective-permute-start | bytes 196616 | tf_op jit(solution)/shard_map/ppermute | solution.py:79
  95.9 4.3 %collective-permute-start.18 = (f32[2,64,128]{2,1,0:T(8,128)S(1)}, f32[2,64,128]{2,1,0:T(8,128)S(1)}, u32[]{:S(2)}, u32[]{:S(2)}) collective-permute-start(f32[2,64,128]{2,1,0:T(8,128)S(1)} %add.433), channel_id=1, source_target_pairs={{0,4},{1,17},{2,6},{3,19},{4,0},{5,21},{6,2},{7,23},{8,12},{9,25},... | collective-permute-start | bytes 196616 | tf_op jit(solution)/shard_map/ppermute | solution.py:79
  100.2 4.6 %collective-permute-start.19 = (f32[2,64,128]{2,1,0:T(8,128)S(1)}, f32[2,64,128]{2,1,0:T(8,128)S(1)}, u32[]{:S(2)}, u32[]{:S(2)}) collective-permute-start(f32[2,64,128]{2,1,0:T(8,128)S(1)} %add.434), channel_id=1, source_target_pairs={{0,2},{1,9},{2,0},{3,11},{4,6},{5,13},{6,4},{7,15},{8,10},{9,1},{1... | collective-permute-start | bytes 196616 | tf_op jit(solution)/shard_map/ppermute | solution.py:79

commit v7 on v6

v7 whole, which is shorter than its diff:
```python
import functools

import jax
import jax.numpy as jnp
from jax import lax
from jax.experimental import pallas as pl
from jax.experimental.pallas import tpu as pltpu
from jax.sharding import PartitionSpec as P

CUTOFF = 1.001
ROW_SHIFT, SKIP = 20, 1 << 19
LANES = 128
ROWS = 64
PAIR = 2
BATCH = 2 * PAIR
RING = 8
UNROLL = 4
VMEM = 16 * 1024 * 1024
HIGHEST = lax.Precision.HIGHEST


def whole_vmem(count):
    return [pl.BlockSpec(memory_space=pltpu.VMEM)] * count


def in_hbm(value):
    return pltpu.with_memory_space_constraint(value, pltpu.HBM)


def dot_nt(left, right, precision=None):
    return lax.dot_general(
        left, right, (((1,), (1,)), ((), ())), precision=precision, preferred_element_type=jnp.float32
    )


def dot_nn(left, right, precision=None):
    return lax.dot_general(
        left, right, (((1,), (0,)), ((), ())), precision=precision, preferred_element_type=jnp.float32
    )


def three_parts(value):
    high = value.astype(jnp.bfloat16)
    rest = value - high.astype(jnp.float32)
    middle = rest.astype(jnp.bfloat16)
    low = (rest - middle.astype(jnp.float32)).astype(jnp.bfloat16)
    return high, middle, low


def halves(block, axis):
    count = lax.axis_size(axis)
    block = block[None]
    bit = 1
    while 2 * bit < count:
        block = jnp.concatenate([block, swapped(block, axis, bit)], axis=0)
        bit *= 2
    return block, swapped(block, axis, bit)


def swapped(block, axis, bit):
    return lax.ppermute(block, axis, [(i, i ^ bit) for i in range(lax.axis_size(axis))])


def sum_tiles(block):
    bit = 1
    while bit < lax.axis_size("tile"):
        block = block + swapped(block, "tile", bit)
        bit *= 2
    return block


def swap_regions(block, even, odd):
    tiles = lax.axis_size("tile")
    route = [
        (region * tiles + tile, (region ^ (odd if tile % 2 else even)) * tiles + tile)
        for region in range(lax.axis_size("region"))
        for tile in range(tiles)
    ]
    return lax.ppermute(block, ("region", "tile"), route)


def sum_regions(block):
    bits, _ = region_orders(lax.axis_size("region"))
    middle = len(bits) // 2
    for even, odd in zip(bits, bits[middle:] + bits[:middle]):
        block = block + swap_regions(block, even, odd)
    return block


def region_orders(count):
    bits = []
    bit = count // 2
    while bit:
        bits.append(bit)
        bit //= 2
    return bits, bits[:1] + bits[-1:] + bits[1:-1] if len(bits) > 2 else bits[::-1]


def slot_offsets(count):
    table = []
    for bits in region_orders(count):
        offsets = [0]
        for bit in bits:
            offsets = offsets + [offset ^ bit for offset in offsets]
        table.append(offsets)
    return [jnp.array(offsets, jnp.int32) for offsets in table]


def exchange(block):
    regions = lax.axis_size("region")
    block = block[None]
    for even, odd in zip(*region_orders(regions)):
        other = swap_regions(block, even, odd)
        if 2 * block.shape[0] == regions:
            return block, other
        block = jnp.concatenate([block, other], axis=0)


def stacked_parts(value):
    return jnp.concatenate([part.astype(jnp.float32) for part in three_parts(value)], axis=0).astype(
        jnp.bfloat16
    )


def add_parts(value):
    rows = value.shape[0] // 3
    return (value[2 * rows :] + value[rows : 2 * rows]) + value[:rows]


def fill_order(first, rank, order_ref, row, count):
    step = 64

    def fill(block, carry):
        start = pl.multiple_of(block * step, step)
        place = first + start + lax.broadcasted_iota(jnp.int32, (step, rank.shape[1]), 0)
        order_ref[pl.ds(pl.multiple_of(row + start, step), step), :] = jnp.where(
            place == rank, 1.0, 0.0
        ).astype(jnp.bfloat16)
        return carry

    lax.fori_loop(0, count // step, fill, 0)


def sort_kernel(
    first_ref, owner_ref, near_ref, far_ref, near_error_ref, far_error_ref, block_ref, other_ref,
    rounded_out, places_out, own_out, block_out, rank_out,
    order_ref, column_ref, owned_ref, places_ref, errors_ref, blocks_ref, sems,
):
    columns, local = block_out.shape
    half = block_ref.shape[0]
    pairs = [(owner_ref, owned_ref)]
    for sources, target in (
        ((near_ref, far_ref), places_ref),
        ((near_error_ref, far_error_ref), errors_ref),
        ((block_ref, other_ref), blocks_ref),
    ):
        pairs += [(ref, target.at[pl.ds(part * half, half)]) for part, ref in enumerate(sources)]
    copies = [
        pltpu.make_async_copy(source, target, sems.at[index])
        for index, (source, target) in enumerate(pairs)
    ]
    for copy in copies:
        copy.start()
    for copy in copies[:5]:
        copy.wait()
    places = jnp.concatenate(
        [jnp.concatenate([places_ref[i], errors_ref[i]], axis=0) for i in range(2 * half)], axis=1
    )
    n = places.shape[1]
    step = 64
    index = jnp.concatenate(
        [
            (first_ref[i] + lax.broadcasted_iota(jnp.int32, (1, local), 1)).astype(jnp.float32)
            for i in range(n // local)
        ],
        axis=1,
    )
    y_row = places[1:2, :]
    column_ref[...] = jnp.transpose(
        jnp.concatenate([y_row, index, jnp.zeros((6, n), jnp.float32)], axis=0)
    )

    def count(block, total):
        start = pl.multiple_of(block * step, step)
        y_column = jnp.broadcast_to(column_ref[pl.ds(start, step), 0:1], (step, n))
        index_column = jnp.broadcast_to(column_ref[pl.ds(start, step), 1:2], (step, n))
        before = (y_column < y_row) | ((y_column == y_row) & (index_column < index))
        return total + jnp.sum(jnp.where(before, 1.0, 0.0).reshape(step // 8, 8, n), axis=0)

    total = lax.fori_loop(0, n // step, count, jnp.zeros((8, n), jnp.float32))
    rank = jnp.sum(total, axis=0, keepdims=True).astype(jnp.int32)
    rank_out[...] = rank[:, :local]
    fill_order(first_ref[0], rank, order_ref, 0, local)
    for copy in copies[5:]:
        copy.wait()
    blocks = [blocks_ref[i] for i in range(2 * half)]
    everything = jnp.concatenate([jnp.concatenate(blocks, axis=1), places, jnp.zeros((4, n), jnp.float32)], axis=0)
    whole = add_parts(dot_nt(stacked_parts(everything), order_ref[...]))
    block_out[...] = whole[:columns]
    own_out[...] = whole[columns:]
    rounded_out[...] = whole[:columns].astype(jnp.bfloat16)
    lane = lax.broadcasted_iota(jnp.int32, (1, local), 1)
    flags = jnp.zeros((1, local), jnp.float32)
    for offset in range(owner_ref.shape[1]):
        flags = jnp.where((lane == offset) & (owned_ref[0, offset] >= 0), 1.0, flags)
    places_out[...] = jnp.concatenate([whole[columns : columns + 3], flags], axis=0)


def sort_region(first, tile_owner, near, far, near_error, far_error, block, other):
    local = near.shape[2]
    n = local * 2 * near.shape[0]
    columns = block.shape[1]
    smem = pl.BlockSpec(memory_space=pltpu.SMEM)
    return pl.pallas_call(
        sort_kernel,
        out_shape=(
            jax.ShapeDtypeStruct((columns, local), jnp.bfloat16),
            jax.ShapeDtypeStruct((4, local), jnp.float32),
            jax.ShapeDtypeStruct((8, local), jnp.float32),
            jax.ShapeDtypeStruct((columns, local), jnp.float32),
            jax.ShapeDtypeStruct((1, local), jnp.int32),
        ),
        in_specs=[smem] + [pl.BlockSpec(memory_space=pl.ANY)] * 7,
        out_specs=tuple(whole_vmem(5)),
        scratch_shapes=[
            pltpu.VMEM((local, n), jnp.bfloat16),
            pltpu.VMEM((n, 8), jnp.float32),
            pltpu.SMEM(tile_owner.shape, jnp.int32),
            pltpu.VMEM((n // local, 3, local), jnp.float32),
            pltpu.VMEM((n // local, 1, local), jnp.float32),
            pltpu.VMEM((n // local, columns, local), jnp.float32),
            pltpu.SemaphoreType.DMA((7,)),
        ],
        compiler_params=pltpu.CompilerParams(vmem_limit_bytes=VMEM),
        cost_estimate=pl.CostEstimate(
            flops=6 * n * local * (columns + 8), bytes_accessed=4 * n * local, transcendentals=0
        ),
        name="sort_region",
    )(first, in_hbm(tile_owner), in_hbm(near), far, in_hbm(near_error), far_error, in_hbm(block), other)


def unsort_kernel(first_ref, rank_ref, block_ref, block_out, order_ref):
    n, local = order_ref.shape
    for slot in range(n // local):
        fill_order(first_ref[slot], rank_ref[...], order_ref, slot * local, local)
    block_out[...] = add_parts(dot_nn(stacked_parts(block_ref[...]), order_ref[...]))


def unsort(first, rank, block):
    n = block.shape[1]
    local = rank.shape[1]
    return pl.pallas_call(
        unsort_kernel,
        out_shape=jax.ShapeDtypeStruct((block.shape[0], local), jnp.float32),
        in_specs=[pl.BlockSpec(memory_space=pltpu.SMEM)] + whole_vmem(2),
        out_specs=whole_vmem(1)[0],
        scratch_shapes=[pltpu.VMEM((n, local), jnp.bfloat16)],
        compiler_params=pltpu.CompilerParams(vmem_limit_bytes=VMEM),
        cost_estimate=pl.CostEstimate(
            flops=6 * n * local * block.shape[0], bytes_accessed=4 * n * local, transcendentals=0
        ),
        name="unsort",
    )(first, rank, block)


def plan_blocks(
    distance_ref, listed_ref, own_ref, far_ref, chunks, stage_ref, bounds_ref, ids_ref, count_ref, sem, prepare,
):
    places, local = far_ref.shape[0], own_ref.shape[1]
    reach = listed_ref.shape[1]
    blocks = local // ROWS
    lane = lax.broadcasted_iota(jnp.int32, (1, LANES), 1)

    lowest = jnp.zeros((1, LANES), jnp.float32)
    highest = lowest
    for block in range(blocks):
        here = (lane == block) | (lane == blocks + block)
        low = own_ref[1:2, block * ROWS : block * ROWS + 1]
        high = own_ref[1:2, (block + 1) * ROWS - 1 : (block + 1) * ROWS]
        lowest = jnp.where(here, 2.0 * (low - CUTOFF), lowest)
        highest = jnp.where(here, 2.0 * (high + CUTOFF), highest)
    y = far_ref[:, 1, :]
    first = jnp.zeros((places, LANES), jnp.int32)
    beyond = first
    for chunk in range(chunks):
        low = y[:, chunk * LANES : chunk * LANES + 1]
        high = y[:, (chunk + 1) * LANES - 1 : (chunk + 1) * LANES]
        first = first + (high < lowest).astype(jnp.int32)
        beyond = beyond + (low <= highest).astype(jnp.int32)
    distance = distance_ref[...]
    flags = jnp.where((lane == -distance) & (far_ref[:, 3, :LANES] > 0.0), 1.0, 0.0)
    for offset in range(reach):
        mine = jnp.where(listed_ref[0, offset] >= 0, 1.0, 0.0)
        flags = flags + jnp.where((lane == offset) & (distance == offset), mine, 0.0)
    listed = jnp.sum(flags, axis=1, keepdims=True) > 0.0
    found = jnp.where(listed, jnp.maximum(beyond - first, 0), 0)
    stage_ref[...] = jnp.where(lane < blocks, first, found)
    copy = pltpu.make_async_copy(stage_ref, bounds_ref, sem)
    copy.start()
    prepare()
    copy.wait()

    count = jnp.int32(0)
    for block in range(blocks):

        def add_place(place, count, block=block):
            entry = (block << ROW_SHIFT) + place * chunks + bounds_ref[place, block]
            for chunk in range(chunks):
                ids_ref[count + chunk] = entry + chunk
            return count + bounds_ref[place, blocks + block]

        count = lax.fori_loop(0, places, add_place, count, unroll=8)
        for extra in range(PAIR - 1):
            ids_ref[count + extra] = (block << ROW_SHIFT) + SKIP
        count = lax.div(count + PAIR - 1, PAIR) * PAIR
    for extra in range(BATCH - PAIR):
        ids_ref[count + extra] = SKIP
    count_ref[0] = lax.div(count + BATCH - 1, BATCH)


def gaspari_cohn(squared):
    squared = jnp.maximum(squared, 1e-12)
    inverse = lax.rsqrt(squared)
    scaled = squared * inverse
    near = (((-3.0 * scaled + 6.0) * scaled + 7.5) * scaled - 20.0) * squared + 12.0
    left = jnp.maximum(2.0 - scaled, 0.0)
    left = left * left
    far = (left * left) * (((scaled + 2.0) * scaled - 0.5) * inverse)
    return jnp.where(scaled <= 1.0, near, far)


def locate(ids_ref, batch, part, chunk_bits):
    entry = ids_ref[batch * BATCH + part]
    lane = pl.multiple_of((entry & ((1 << chunk_bits) - 1)) * LANES, LANES)
    start = pl.multiple_of(lax.shift_right_logical(entry, ROW_SHIFT) * ROWS, ROWS)
    place = lax.shift_right_logical(entry & (SKIP - 1), chunk_bits)
    return (entry & SKIP) == 0, place, pl.ds(lane, LANES), pl.ds(start, ROWS)


def build_kernel(
    kept, place_ref, distance_ref, listed_ref, own_ref, near_ref, other_ref,
    ids_ref, count_ref, tiles_ref,
    wide_ref, far_ref, stage_ref, bounds_ref, bounds_sem, *through,
):
    local = own_ref.shape[1]
    places = far_ref.shape[0]
    chunk_bits = (local // LANES).bit_length() - 1
    factor = jnp.where(lax.broadcasted_iota(jnp.int32, (4, 1), 0) < 2, 2.0, 1.0 / 12.0)
    for index in range(places):
        side_ref = near_ref if 2 * index < places else other_ref
        far_ref[index, 0:4, :] = factor * side_ref[place_ref[index]]

    def prepare():
        column = jnp.transpose(own_ref[...])
        for row in range(3):
            scale = 2.0 if row < 2 else 1.0
            wide_ref[row] = jnp.broadcast_to(scale * column[:, row : row + 1], (local, LANES))

    plan_blocks(
        distance_ref, listed_ref, own_ref, far_ref, 1 << chunk_bits,
        stage_ref, bounds_ref, ids_ref, count_ref, bounds_sem, prepare,
    )
    total = count_ref[0]
    held_ref, sems = (tiles_ref, None) if kept else through

    def copy_out(batch):
        return pltpu.make_async_copy(
            held_ref.at[batch], tiles_ref.at[batch], sems.at[lax.rem(batch, RING)]
        )

    def build_batch(batch, carry):
        if not kept:

            @pl.when(batch >= RING)
            def _():
                copy_out(batch - RING).wait()

        for part in range(BATCH):
            real, place, lanes, rows = locate(ids_ref, batch, part, chunk_bits)
            far = far_ref[place, :, lanes]
            across_x = wide_ref[0, rows, :] - far[0:1, :]
            across_y = wide_ref[1, rows, :] - far[1:2, :]
            value = gaspari_cohn(across_x * across_x + across_y * across_y)
            spread = jnp.where(real, far[2:3, :], 0.0)
            value = wide_ref[2, rows, :] * spread * value
            held_ref[batch, :, part * LANES : (part + 1) * LANES] = value.astype(jnp.bfloat16)
        if not kept:
            copy_out(batch).start()
        return carry

    lax.fori_loop(0, total, build_batch, 0)
    if not kept:

        def finish(batch, carry):
            copy_out(batch).wait()
            return carry

        lax.fori_loop(jnp.maximum(total - RING, 0), total, finish, 0)


def build_tiles(place, distance, tile_owner, own, near, far, capacity, kept):
    near, far = [piece.reshape((-1,) + piece.shape[2:]) for piece in (near, far)]
    places, local = place.shape[0], own.shape[1]
    smem = pl.BlockSpec(memory_space=pltpu.SMEM)
    sizes = (capacity * BATCH + local // LANES, 1)
    shape = (capacity, ROWS, BATCH * LANES)
    scratch = [
        pltpu.VMEM((3, local, LANES), jnp.float32),
        pltpu.VMEM((places, 8, local), jnp.float32),
        pltpu.VMEM((places, LANES), jnp.int32),
        pltpu.SMEM((places, LANES), jnp.int32),
        pltpu.SemaphoreType.DMA,
    ]
    if not kept:
        scratch += [pltpu.VMEM(shape, jnp.bfloat16), pltpu.SemaphoreType.DMA((RING,))]
    return pl.pallas_call(
        functools.partial(build_kernel, kept),
        out_shape=tuple(jax.ShapeDtypeStruct((size,), jnp.int32) for size in sizes)
        + ((pltpu.VMEM if kept else pltpu.HBM)(shape, jnp.bfloat16),),
        in_specs=[smem] + whole_vmem(1) + [smem] + whole_vmem(3),
        out_specs=(smem,) * 2 + (pl.BlockSpec(memory_space=pltpu.VMEM if kept else pltpu.HBM),),
        scratch_shapes=scratch,
        compiler_params=pltpu.CompilerParams(vmem_limit_bytes=VMEM),
        cost_estimate=pl.CostEstimate(
            flops=2 * local * local * 16000, bytes_accessed=16 * local * local, transcendentals=0
        ),
        name="build_kept" if kept else "build_passed",
    )(place, distance, tile_owner, own, near, far)


def apply_kernel(started, last, ids_ref, count_ref, near_ref, other_ref, tiles_ref, *refs):
    refs = list(refs)
    start_ref = refs.pop(0) if started else None
    if last:
        block_ref, scale_ref, out_ref, rounded_ref, gram_ref, all_ref, piece_sems, total_ref = refs
        held_ref = tiles_ref
    else:
        total_ref, all_ref, piece_sems, held_ref, sems = refs
    half, columns, local = near_ref.shape
    chunk_bits = (local // LANES).bit_length() - 1
    total = count_ref[0]
    groups = lax.div(total + UNROLL - 1, UNROLL)

    copies = [
        pltpu.make_async_copy(ref, all_ref.at[pl.ds(part * half, half)], piece_sems.at[part])
        for part, ref in enumerate((near_ref, other_ref))
    ]
    for copy in copies:
        copy.start()

    def copy_in(group):
        first = group * UNROLL
        return pltpu.make_async_copy(
            tiles_ref.at[pl.ds(first, UNROLL)], held_ref.at[pl.ds(first, UNROLL)], sems.at[group]
        )

    if not last:

        def start_copy(group, carry):
            copy_in(group).start()
            return carry

        lax.fori_loop(0, groups, start_copy, 0)
    if started:
        total_ref[...] = start_ref[...]
    else:
        total_ref[...] = jnp.zeros(total_ref.shape, jnp.float32)
    for copy in copies:
        copy.wait()

    def turn(group, carry):
        if not last:
            copy_in(group).wait()
        values = []
        for inner in range(UNROLL):
            batch = jnp.minimum(group * UNROLL + inner, total - 1)
            valid = group * UNROLL + inner < total
            for pair in range(BATCH // PAIR):
                sides = []
                for part in range(pair * PAIR, (pair + 1) * PAIR):
                    _, place, chunk, rows = locate(ids_ref, batch, part, chunk_bits)
                    sides.append(all_ref[place, :, chunk])
                side = jnp.concatenate(sides, axis=1)
                if inner:
                    side = jnp.where(valid, side, jnp.zeros_like(side))
                lanes = slice(pair * PAIR * LANES, (pair + 1) * PAIR * LANES)
                values.append((rows, dot_nt(held_ref[batch, :, lanes], side)))
        for rows, value in values:
            total_ref[rows, :] += value
        return carry

    lax.fori_loop(0, groups, turn, 0)
    if last:
        block = block_ref[...]
        result = jnp.transpose(total_ref[...]) + scale_ref[...] * block
        out_ref[...] = result
        rounded_ref[...] = result.astype(jnp.bfloat16)
        gram_ref[...] = dot_nt(block, jnp.concatenate([block, result], axis=0), HIGHEST)


def apply_tiles(plan, near, far, tiles, start, finish):
    near, far = [piece.reshape((-1,) + piece.shape[2:]) for piece in (near, far)]
    half, columns, local = near.shape
    last = finish is not None
    smem = pl.BlockSpec(memory_space=pltpu.SMEM)
    anywhere = pl.BlockSpec(memory_space=pl.ANY)
    operands = [*plan, near, far, tiles]
    in_specs = [smem] * 2 + [anywhere] * 2
    in_specs.append(pl.BlockSpec(memory_space=pltpu.VMEM if last else pltpu.HBM))
    if start is not None:
        operands.append(start)
        in_specs += whole_vmem(1)
    scratch = [
        pltpu.VMEM((2 * half, columns, local), jnp.bfloat16),
        pltpu.SemaphoreType.DMA((2,)),
    ]
    if last:
        operands += finish
        in_specs += whole_vmem(2)
        out_shape = (
            jax.ShapeDtypeStruct((columns, local), jnp.float32),
            jax.ShapeDtypeStruct((columns, local), jnp.bfloat16),
            jax.ShapeDtypeStruct((columns, 2 * columns), jnp.float32),
        )
        scratch.append(pltpu.VMEM((local, columns), jnp.float32))
    else:
        out_shape = (jax.ShapeDtypeStruct((local, columns), jnp.float32),)
        scratch.append(pltpu.VMEM(tiles.shape, jnp.bfloat16))
        scratch.append(pltpu.SemaphoreType.DMA((tiles.shape[0] // UNROLL,)))
    return pl.pallas_call(
        functools.partial(apply_kernel, start is not None, last),
        out_shape=out_shape,
        in_specs=in_specs,
        out_specs=tuple(whole_vmem(len(out_shape))),
        scratch_shapes=scratch,
        compiler_params=pltpu.CompilerParams(vmem_limit_bytes=VMEM),
        cost_estimate=pl.CostEstimate(
            flops=2 * local * local * 6000, bytes_accessed=16 * local * local, transcendentals=0
        ),
        name="apply_last" if last else "apply_first",
    )(*operands)


def reciprocal(value):
    root = lax.rsqrt(value)
    return root * root


def small_product(left, right):
    return [[sum(l * r[j] for l, r in zip(row, right)) for j in range(len(right[0]))] for row in left]


def small_difference(left, right):
    return [[l - r for l, r in zip(*rows)] for rows in zip(left, right)]


def small_inverse(matrix):
    (a, b), (c, d) = matrix
    scale = reciprocal(a * d - b * c)
    return [[d * scale, -b * scale], [-c * scale, a * scale]]


def solve_positive(matrix, target):
    n = matrix.shape[0]
    table = jnp.concatenate([0.5 * (matrix + jnp.transpose(matrix)), target], axis=1)
    bands = [table[k : k + 8, :] for k in range(0, n, 8)]
    row_index = lax.broadcasted_iota(jnp.int32, bands[0].shape, 0)
    for k in range(0, n, 4):
        own, row = k // 8, k % 8
        columns = [
            [jnp.broadcast_to(band[:, k + j : k + j + 1], band.shape) for band in bands] for j in range(4)
        ]
        pivot = [[columns[j][own][row + i : row + i + 1] for j in range(4)] for i in range(4)]
        upper, lower = pivot[:2], pivot[2:]
        top = small_inverse([r[:2] for r in upper])
        factor = small_product([r[:2] for r in lower], top)
        right = [r[2:] for r in upper]
        rest = small_inverse(small_difference([r[2:] for r in lower], small_product(factor, right)))
        rows = [[bands[own][row + i : row + i + 1]] for i in range(4)]
        last = small_product(rest, small_difference(rows[2:], small_product(factor, rows[:2])))
        first = small_product(top, small_difference(rows[:2], small_product(right, last)))
        new = [r[0] for r in first + last]
        bands = [
            band - ((columns[0][i] * new[0] + columns[1][i] * new[1]) + (columns[2][i] * new[2] + columns[3][i] * new[3]))
            for i, band in enumerate(bands)
        ]
        for i in range(4):
            bands[own] = jnp.where(row_index == row + i, new[i], bands[own])
    return jnp.concatenate([band[:, n:] for band in bands], axis=0)


def last_kernel(grams_ref, start_ref, images_ref, weights_ref, residual_ref):
    n = grams_ref.shape[1]
    squares, mixed = grams_ref[0, :, :n], grams_ref[0, :, n:]
    images, cross = grams_ref[1, :, :n], grams_ref[1, :, n:]
    solved = solve_positive(mixed, jnp.concatenate([squares, images], axis=1))
    step, carried = solved[:, :n], solved[:, n:]
    product = dot_nn(images, solved, HIGHEST)
    second = solve_positive(cross - product[:, n:], jnp.transpose(mixed) - product[:, :n])
    first = jnp.transpose(step - dot_nn(carried, second, HIGHEST))
    second = jnp.transpose(second)
    both = jnp.concatenate([first, second], axis=1)
    start, images = start_ref[...], images_ref[...]
    weights_ref[...] = dot_nn(both, jnp.concatenate([start, images[:n]], axis=0), HIGHEST)
    residual_ref[...] = start - dot_nn(both, images, HIGHEST)


def last_step(grams, start, images):
    return pl.pallas_call(
        last_kernel,
        out_shape=(jax.ShapeDtypeStruct(start.shape, jnp.float32),) * 2,
        in_specs=whole_vmem(3),
        out_specs=tuple(whole_vmem(2)),
        compiler_params=pltpu.CompilerParams(vmem_limit_bytes=VMEM),
        name="last_step",
    )(grams, start, images)


def shards(innovations, obs_geometry, obs_error, tile_owner):
    tiles_axis, regions = lax.axis_size("tile"), lax.axis_size("region")
    reach = tile_owner.shape[1]
    here, tile = lax.axis_index("region"), lax.axis_index("tile")
    columns, local = innovations.shape
    slot_tile = tile ^ jnp.arange(tiles_axis, dtype=jnp.int32)
    first = slot_tile * local
    even, odd = slot_offsets(regions)
    slot_region = here ^ jnp.where((slot_tile % 2 == 0)[:, None], even, odd)

    rounded, places, own, start, rank = sort_region(
        first,
        tile_owner,
        *halves(obs_geometry, "tile"),
        *halves(obs_error[None, :], "tile"),
        *halves(innovations, "tile"),
    )
    scale = own[3:4]
    everywhere = jnp.broadcast_to(places[None], (regions,) + places.shape)
    everywhere = lax.all_to_all(everywhere, "region", 0, 0)
    near_places, far_places = halves(everywhere, "tile")

    half_regions = regions // 2
    most = min(half_regions, 2 * reach - 1) * tiles_axis * (local // LANES)
    batches = -(-(local // ROWS) * -(-most // PAIR) * PAIR // BATCH) + 1
    capacity = -(-batches // UNROLL) * UNROLL
    stack = jnp.arange(tiles_axis, dtype=jnp.int32) % (tiles_axis // 2) * regions
    plans, tiles = [], []
    for part in range(2):
        inside = slot_region[:, part * half_regions : (part + 1) * half_regions]
        *plan, built = build_tiles(
            (stack[:, None] + inside).reshape(-1), (inside - here).reshape(-1, 1), tile_owner, own,
            near_places, far_places, capacity, part == 1,
        )
        plans.append(plan)
        tiles.append(built)

    def operate(sent, block, building):
        total = None
        for part, group in enumerate(exchange(sent)):
            if building:
                group, plans[part] = lax.optimization_barrier((group, plans[part]))
            elif part:
                group, total = lax.optimization_barrier((group, total))
            near, far = halves(group, "tile")
            results = apply_tiles(
                plans[part], near, far, tiles[part], total, (block, scale) if part else None
            )
            total = results[0]
        return results

    image, image_rounded, grams = operate(rounded, start, True)
    second, _, cross = operate(image_rounded, image, False)
    grams = jnp.stack([grams, cross])
    grams = sum_regions(sum_tiles(grams))
    near, far = halves(jnp.concatenate([image, second], axis=0), "tile")
    images = unsort(first, rank, jnp.concatenate([*near, *far], axis=1))
    return last_step(grams, innovations, images)


def solution(mesh):
    return jax.shard_map(
        shards,
        mesh=mesh,
        in_specs=(
            P(None, ("region", "tile")),
            P(None, ("region", "tile")),
            P(("region", "tile")),
            P("region", None),
        ),
        out_specs=(P(None, ("region", "tile")), P(None, ("region", "tile"))),
        check_vma=False,
    )
```

time: 112 us -> 109 us (0.973); the launches traced: 112 us -> 108 us
  local copies, waits for them, and re-layouts: 9.39 us -> 1.68 us
  Pallas kernels: 27.9 us -> 34.9 us
  other arithmetic: 4.73 us -> 1.15 us
  waiting for transfers between devices: 44.1 us -> 46.9 us
  starting transfers between devices: 25.4 us -> 22.9 us
    ppermute x12, starting transfers between devices: 23.9 us -> 16.6 us  [swap_regions(): return lax.ppermute(block, ('region', 'tile'), route)]
    pallas_call x5 -> x7, Pallas kernels: 18.9 us -> 25.8 us  [the longest x4 10.7 us: apply_tiles(): pl.pallas_call(functools.partial(apply_kernel, start is not None, last),...]
    unnamed x31 -> x11, local copies, waits for them, and re-layouts: 6.74 us -> 0.68 us
    all_to_all x0 -> x1, waiting for transfers between devices: none -> 5.05 us  [shards(): everywhere = lax.all_to_all(everywhere, 'region', 0, 0)]
    all_to_all x0 -> x1, starting transfers between devices: none -> 4.84 us  [shards(): everywhere = lax.all_to_all(everywhere, 'region', 0, 0)]
    ppermute x12, waiting for transfers between devices: 40.4 us -> 37.1 us  [swap_regions(): return lax.ppermute(block, ('region', 'tile'), route)]
    reduce_sum x16 -> x0, other arithmetic: 1.98 us -> none  [the longest x4 0.74 us: plan_blocks(): jnp.sum(jnp.where(hit, index[None, :, None] + (part * size + 1), 0), axis...]
    ppermute x9 -> x10, waiting for transfers between devices: 3.74 us -> 4.75 us  [swapped(): lax.ppermute(block, axis, [(i, i ^ bit) for i in range(lax.axis_size(axis...]
  transfers between devices with their start and end apart: 21 -> 23, of which waited for: 15 -> 15; matrix products, arithmetic and copies ran while one was open for 7% -> 2% of each run, Pallas kernels for 8% -> 16%
where the time goes in v7:
time: 109 us; the launch traced here: 108 us
  waiting for transfers between devices  46.9 us (43%)
  Pallas kernels  34.9 us (32%)
  starting transfers between devices  22.9 us (21%)
  local copies, waits for them, and re-layouts  1.68 us (2%)
  other arithmetic  1.15 us (1%)
    ppermute x12, waiting for transfers between devices, swap_regions(): return lax.ppermute(block, ('region', 'tile'), route)  37.1 us
    ppermute x12, starting transfers between devices, swap_regions(): return lax.ppermute(block, ('region', 'tile'), route)  16.6 us
    pallas_call x4, Pallas kernels, apply_tiles(): pl.pallas_call(functools.partial(apply_kernel, start is not None, last),...  10.7 us
    pallas_call x2, Pallas kernels, build_tiles(): pl.pallas_call(functools.partial(build_kernel, kept), out_shape=tuple((ja...  10.5 us
    pallas_call x1, Pallas kernels, last_step(): pl.pallas_call(last_kernel, out_shape=(jax.ShapeDtypeStruct(start.shape,...  7.67 us
    all_to_all x1, waiting for transfers between devices, shards(): everywhere = lax.all_to_all(everywhere, 'region', 0, 0)  5.05 us
    all_to_all x1, starting transfers between devices, shards(): everywhere = lax.all_to_all(everywhere, 'region', 0, 0)  4.84 us
    ppermute x10, waiting for transfers between devices, swapped(): lax.ppermute(block, axis, [(i, i ^ bit) for i in range(lax.axis_size(axis...  4.75 us
  transfers between devices with their start and end apart: 23, of which 15 were waited for; matrix products, arithmetic and copies ran while one was open for 2% of the time, Pallas kernels for 16%

profile of v7, /device:TPU:0, one launch (start us, length us, event | category | flops | bytes accessed | tf_op | source)
XLA Modules:
  0.0 108.4 jit_solution(7416710858161018089)
XLA Ops:
  0.6 0.5 collective-permute-start.2
  1.1 0.1 collective-permute-start
  1.2 0.4 collective-permute-start.1
  1.7 1.0 collective-permute-done.1.far_error_ref
  2.7 0.0 collective-permute-done.far_ref
  2.7 0.0 collective-permute-done.2.other_ref
  2.7 4.6 %sort_region.1 = (bf16[64,512]{1,0:T(8,128)(2,1)S(1)}, f32[4,512]{1,0:T(4,128)S(1)}, f32[8,512]{1,0:T(8,128)S(1)}, f32[64,512]{1,0:T(8,128)S(1)}, s32[1,512]{1,0:T(1,128)S(1)}) custom-call(s32[2]{0:T(128)S(1)} %fusion.2.first_ref, s32[1,7]{1,0:T(1,128)} %listed_ref.3, f32[1,3,512]{2,1,0:T(4,128)} %bitcast.51, f32[1,3,512]{2,1,0:T(4,128)S(1)} %collective-permute-done.far_ref, ...), custom_call_target="tpu_custom_call" | custom-call | flops 226492416 | bytes 2097152 | tf_op jit(solution)/shard_map/sort_region/pallas_call | solution.py:214
  7.3 4.0 %collective-permute-start.3 = (bf16[1,64,512]{2,1,0:T(8,128)(2,1)S(1)}, bf16[1,64,512]{2,1,0:T(8,128)(2,1)S(1)}, u32[]{:S(2)}, u32[]{:S(2)}) collective-permute-start(bf16[1,64,512]{2,1,0:T(8,128)(2,1)S(1)} %bitcast.20), channel_id=1, source_target_pairs={{0,16},{1,17},{2,18},{3,19},{4,20},{5,21},{6,22},{7,23},{8,24},{9,... | collective-permute-start | bytes 196616 | tf_op jit(solution)/shard_map/ppermute | solution.py:79
  11.3 0.7 broadcast_in_dim.61
  12.0 4.8 %all-to-all-start = ((f32[16,4,512]{2,1,0:T(4,128)}), f32[16,4,512]{2,1,0:T(4,128)S(1)}, u32[]{:S(2)}, u32[]{:S(2)}) async-start(f32[16,4,512]{2,1,0:T(4,128)} %broadcast_in_dim.61), calls=%async_computation | async-start | bytes 262144 | tf_op jit(solution)/shard_map/all_to_all | solution.py:638
  16.8 0.7 select_xor_fusion
  17.6 0.0 collective-permute-done.3
  17.6 2.0 %collective-permute-start.4 = (bf16[2,64,512]{2,1,0:T(8,128)(2,1)S(1)}, bf16[2,64,512]{2,1,0:T(8,128)(2,1)S(1)}, u32[]{:S(2)}, u32[]{:S(2)}) collective-permute-start(bf16[2,64,512]{2,1,0:T(8,128)(2,1)S(1)} %pad_maximum_fusion.5), channel_id=1, source_target_pairs={{0,8},{1,3},{2,10},{3,1},{4,12},{5,7},{6,14},{7,5},{8,0},{9,11},{1... | collective-permute-start | bytes 393224 | tf_op jit(solution)/shard_map/ppermute | solution.py:79
  19.6 5.0 %all-to-all-done.near_ref = f32[16,4,512]{2,1,0:T(4,128)S(1)} async-done(((f32[16,4,512]{2,1,0:T(4,128)}), f32[16,4,512]{2,1,0:T(4,128)S(1)}, u32[]{:S(2)}, u32[]{:S(2)}) %all-to-all-start) | async-done | bytes 131104 | tf_op jit(solution)/shard_map/all_to_all | solution.py:638
  24.6 0.1 broadcast_subtract_fusion
  24.7 0.1 reshape.59.distance_ref
  24.8 0.1 reshape.53.place_ref
  24.9 0.1 reshape.58.distance_ref
  24.9 0.1 reshape.49.place_ref
  25.0 0.0 collective-permute-done.4
  25.1 0.8 collective-permute-start.5
  25.9 0.1 collective-permute-done.7
  26.0 0.7 copy-done.1
  26.6 5.9 %build_passed.1 = (s32[532]{0:T(1024)S(1)}, s32[1]{0:T(128)}, bf16[132,64,512]{2,1,0:T(8,128)(2,1)}) custom-call(s32[16]{0:T(128)S(1)} %reshape.53.place_ref, s32[16,1]{1,0:T(8,128)S(1)} %reshape.59.distance_ref, s32[1,7]{1,0:T(1,128)S(1)} %copy-done.1, f32[8,512]{1,0:T(8,128)S(1)} %get-tuple-element.27.own_ref, f32[16,4,512]{2,1,0:T(4,128)S(1)} %all-to-all-done.near_ref, ...), custom_call_target="tpu_custom_call" | custom-call | flops 8388608000 | bytes 4194304 | tf_op jit(solution)/shard_map/build_passed/pallas_call | solution.py:416
  32.5 0.0 collective-permute-done.5
  32.5 0.1 pad_maximum_fusion.near_ref
  32.6 1.2 %collective-permute-start.6 = (bf16[8,64,512]{2,1,0:T(8,128)(2,1)S(1)}, bf16[8,64,512]{2,1,0:T(8,128)(2,1)S(1)}, u32[]{:S(2)}, u32[]{:S(2)}) collective-permute-start(bf16[8,64,512]{2,1,0:T(8,128)(2,1)S(1)} %pad_maximum_fusion.near_ref), channel_id=1, source_target_pairs={{0,2},{1,5},{2,0},{3,7},{4,6},{5,1},{6,4},{7,3},{8,10},{9,13},{10,... | collective-permute-start | bytes 1572872 | tf_op jit(solution)/shard_map/ppermute | solution.py:79
  33.7 0.0 collective-permute-start.9
  33.7 4.7 %build_kept.1 = (s32[532]{0:T(1024)S(1)}, s32[1]{0:T(128)}, bf16[132,64,512]{2,1,0:T(8,128)(2,1)S(1)}) custom-call(s32[16]{0:T(128)S(1)} %reshape.49.place_ref, s32[16,1]{1,0:T(8,128)S(1)} %reshape.58.distance_ref, s32[1,7]{1,0:T(1,128)S(1)} %copy-done.1, f32[8,512]{1,0:T(8,128)S(1)} %get-tuple-element.27.own_ref, f32[16,4,512]{2,1,0:T(4,128)S(1)} %all-to-all-done.near_ref, ...), custom_call_target="tpu_custom_call" | custom-call | flops 8388608000 | bytes 4194304 | tf_op jit(solution)/shard_map/build_kept/pallas_call | solution.py:416
  38.4 3.4 %collective-permute-done.6.near_ref = bf16[8,64,512]{2,1,0:T(8,128)(2,1)S(1)} collective-permute-done((bf16[8,64,512]{2,1,0:T(8,128)(2,1)S(1)}, bf16[8,64,512]{2,1,0:T(8,128)(2,1)S(1)}, u32[]{:S(2)}, u32[]{:S(2)}) %collective-permute-start.6) | collective-permute-done | bytes 524320 | tf_op jit(solution)/shard_map/ppermute | solution.py:79
  41.8 0.0 collective-permute-start.8
  41.8 0.0 collective-permute-done.9
  41.9 2.7 %apply_first.2.refs_0_ = f32[512,64]{1,0:T(8,128)S(1)} custom-call(s32[532]{0:T(1024)S(1)} %get-tuple-element.37.ids_ref, s32[1]{0:T(128)} %get-tuple-element.38.count_ref, bf16[8,64,512]{2,1,0:T(8,128)(2,1)S(1)} %pad_maximum_fusion.near_ref, bf16[8,64,512]{2,1,0:T(8,128)(2,1)S(1)} %bitcast.40, bf16[132,64,512]{2,1,0:T(8,128)(2,1)S(1)} %bitcast.47), custom_call_target="tpu_custom_call" | custom-call | flops 3145728000 | bytes 4194304 | tf_op jit(solution)/shard_map/apply_first/pallas_call | solution.py:530
  44.6 0.0 collective-permute-done.8
  44.6 2.5 %apply_last.2 = (f32[64,512]{1,0:T(8,128)S(1)}, bf16[64,512]{1,0:T(8,128)(2,1)S(1)}, f32[64,128]{1,0:T(8,128)S(1)}) custom-call(s32[532]{0:T(1024)S(1)} %get-tuple-element.31.ids_ref, s32[1]{0:T(128)} %get-tuple-element.32.count_ref, bf16[8,64,512]{2,1,0:T(8,128)(2,1)S(1)} %collective-permute-done.6.near_ref, bf16[8,64,512]{2,1,0:T(8,128)(2,1)S(1)} %bitcast.41, ...), custom_call_target="tpu_custom_call" | custom-call | flops 3145728000 | bytes 4194304 | tf_op jit(solution)/shard_map/apply_last/pallas_call | solution.py:530
  47.1 3.5 %collective-permute-start.10 = (bf16[1,64,512]{2,1,0:T(8,128)(2,1)S(1)}, bf16[1,64,512]{2,1,0:T(8,128)(2,1)S(1)}, u32[]{:S(2)}, u32[]{:S(2)}) collective-permute-start(bf16[1,64,512]{2,1,0:T(8,128)(2,1)S(1)} %bitcast.24), channel_id=1, source_target_pairs={{0,16},{1,17},{2,18},{3,19},{4,20},{5,21},{6,22},{7,23},{8,24},{9,... | collective-permute-start | bytes 196616 | tf_op jit(solution)/shard_map/ppermute | solution.py:79
  50.6 4.1 %collective-permute-done.10 = bf16[1,64,512]{2,1,0:T(8,128)(2,1)S(1)} collective-permute-done((bf16[1,64,512]{2,1,0:T(8,128)(2,1)S(1)}, bf16[1,64,512]{2,1,0:T(8,128)(2,1)S(1)}, u32[]{:S(2)}, u32[]{:S(2)}) %collective-permute-start.10) | collective-permute-done | bytes 65568 | tf_op jit(solution)/shard_map/ppermute | solution.py:79
  54.8 0.1 collective-permute-start.11
  54.9 5.0 %collective-permute-done.11 = bf16[2,64,512]{2,1,0:T(8,128)(2,1)S(1)} collective-permute-done((bf16[2,64,512]{2,1,0:T(8,128)(2,1)S(1)}, bf16[2,64,512]{2,1,0:T(8,128)(2,1)S(1)}, u32[]{:S(2)}, u32[]{:S(2)}) %collective-permute-start.11) | collective-permute-done | bytes 131104 | tf_op jit(solution)/shard_map/ppermute | solution.py:79
  59.9 0.1 collective-permute-start.12
  59.9 6.4 %collective-permute-done.12 = bf16[4,64,512]{2,1,0:T(8,128)(2,1)S(1)} collective-permute-done((bf16[4,64,512]{2,1,0:T(8,128)(2,1)S(1)}, bf16[4,64,512]{2,1,0:T(8,128)(2,1)S(1)}, u32[]{:S(2)}, u32[]{:S(2)}) %collective-permute-start.12) | collective-permute-done | bytes 262176 | tf_op jit(solution)/shard_map/ppermute | solution.py:79
  66.3 0.1 fusion.4
  66.4 0.1 collective-permute-start.14
  66.5 1.3 %collective-permute-start.13 = (bf16[8,64,512]{2,1,0:T(8,128)(2,1)S(1)}, bf16[8,64,512]{2,1,0:T(8,128)(2,1)S(1)}, u32[]{:S(2)}, u32[]{:S(2)}) collective-permute-start(bf16[8,64,512]{2,1,0:T(8,128)(2,1)S(1)} %get-tuple-element.51.near_ref), channel_id=1, source_target_pairs={{0,2},{1,5},{2,0},{3,7},{4,6},{5,1},{6,4},{7,3},{8,10},{9,13},{10,... | collective-permute-start | bytes 1572872 | tf_op jit(solution)/shard_map/ppermute | solution.py:79
  67.8 0.6 collective-permute-done.14
  68.4 2.7 %apply_first.3.refs_0_ = f32[512,64]{1,0:T(8,128)S(1)} custom-call(s32[532]{0:T(1024)S(1)} %get-tuple-element.37.ids_ref, s32[1]{0:T(128)} %get-tuple-element.38.count_ref, bf16[8,64,512]{2,1,0:T(8,128)(2,1)S(1)} %get-tuple-element.51.near_ref, bf16[8,64,512]{2,1,0:T(8,128)(2,1)S(1)} %bitcast.42, bf16[132,64,512]{2,1,0:T(8,128)(2,1)S(1)} %bitcast.47), custom_call_target="tpu_custom_call" | custom-call | flops 3145728000 | bytes 4194304 | tf_op jit(solution)/shard_map/apply_first/pallas_call | solution.py:530
  71.0 0.0 copy-start
  71.1 4.7 %collective-permute-done.13.near_ref = bf16[8,64,512]{2,1,0:T(8,128)(2,1)S(1)} collective-permute-done((bf16[8,64,512]{2,1,0:T(8,128)(2,1)S(1)}, bf16[8,64,512]{2,1,0:T(8,128)(2,1)S(1)}, u32[]{:S(2)}, u32[]{:S(2)}) %collective-permute-start.13) | collective-permute-done | bytes 524320 | tf_op jit(solution)/shard_map/ppermute | solution.py:79
  75.7 0.0 collective-permute-start.15
  75.7 1.9 %collective-permute-done.15 = bf16[1,8,64,512]{3,2,1,0:T(8,128)(2,1)S(1)} collective-permute-done((bf16[1,8,64,512]{3,2,1,0:T(8,128)(2,1)S(1)}, bf16[1,8,64,512]{3,2,1,0:T(8,128)(2,1)S(1)}, u32[]{:S(2)}, u32[]{:S(2)}) %collective-permute-start.15) | collective-permute-done | bytes 524320 | tf_op jit(solution)/shard_map/ppermute | solution.py:61
  77.6 2.8 %apply_last.3 = (f32[64,512]{1,0:T(8,128)S(1)}, bf16[64,512]{1,0:T(8,128)(2,1)}, f32[64,128]{1,0:T(8,128)S(1)}) custom-call(s32[532]{0:T(1024)S(1)} %get-tuple-element.31.ids_ref, s32[1]{0:T(128)} %get-tuple-element.32.count_ref, bf16[8,64,512]{2,1,0:T(8,128)(2,1)S(1)} %collective-permute-done.13.near_ref, bf16[8,64,512]{2,1,0:T(8,128)(2,1)S(1)} %bitcast.43, ...), custom_call_target="tpu_custom_call" | custom-call | flops 3145728000 | bytes 4194304 | tf_op jit(solution)/shard_map/apply_last/pallas_call | solution.py:530
  80.4 0.2 collective-permute-start.16
  80.6 1.1 %collective-permute-done.16 = f32[2,64,128]{2,1,0:T(8,128)S(1)} collective-permute-done((f32[2,64,128]{2,1,0:T(8,128)S(1)}, f32[2,64,128]{2,1,0:T(8,128)S(1)}, u32[]{:S(2)}, u32[]{:S(2)}) %collective-permute-start.16) | collective-permute-done | bytes 65568 | tf_op jit(solution)/shard_map/ppermute | solution.py:61
  81.8 2.0 %collective-permute-start.17 = (f32[2,64,128]{2,1,0:T(8,128)S(1)}, f32[2,64,128]{2,1,0:T(8,128)S(1)}, u32[]{:S(2)}, u32[]{:S(2)}) collective-permute-start(f32[2,64,128]{2,1,0:T(8,128)S(1)} %fusion.3), channel_id=1, source_target_pairs={{0,16},{1,5},{2,18},{3,7},{4,20},{5,1},{6,22},{7,3},{8,24},{9,13},... | collective-permute-start | bytes 196616 | tf_op jit(solution)/shard_map/ppermute | solution.py:79
  83.8 0.1 collective-permute-start.21
  83.9 3.7 %collective-permute-done.17 = f32[2,64,128]{2,1,0:T(8,128)S(1)} collective-permute-done((f32[2,64,128]{2,1,0:T(8,128)S(1)}, f32[2,64,128]{2,1,0:T(8,128)S(1)}, u32[]{:S(2)}, u32[]{:S(2)}) %collective-permute-start.17) | collective-permute-done | bytes 65568 | tf_op jit(solution)/shard_map/ppermute | solution.py:79
  87.6 0.1 collective-permute-start.18
  87.7 4.3 %collective-permute-done.18 = f32[2,64,128]{2,1,0:T(8,128)S(1)} collective-permute-done((f32[2,64,128]{2,1,0:T(8,128)S(1)}, f32[2,64,128]{2,1,0:T(8,128)S(1)}, u32[]{:S(2)}, u32[]{:S(2)}) %collective-permute-start.18) | collective-permute-done | bytes 65568 | tf_op jit(solution)/shard_map/ppermute | solution.py:79
  92.0 0.2 collective-permute-start.19
  92.2 4.1 %collective-permute-done.19 = f32[2,64,128]{2,1,0:T(8,128)S(1)} collective-permute-done((f32[2,64,128]{2,1,0:T(8,128)S(1)}, f32[2,64,128]{2,1,0:T(8,128)S(1)}, u32[]{:S(2)}, u32[]{:S(2)}) %collective-permute-start.19) | collective-permute-done | bytes 65568 | tf_op jit(solution)/shard_map/ppermute | solution.py:79
  96.3 1.5 %collective-permute-start.20 = (f32[2,64,128]{2,1,0:T(8,128)S(1)}, f32[2,64,128]{2,1,0:T(8,128)S(1)}, u32[]{:S(2)}, u32[]{:S(2)}) collective-permute-start(f32[2,64,128]{2,1,0:T(8,128)S(1)} %add.39), channel_id=1, source_target_pairs={{0,2},{1,9},{2,0},{3,11},{4,6},{5,13},{6,4},{7,15},{8,10},{9,1},{1... | collective-permute-start | bytes 196616 | tf_op jit(solution)/shard_map/ppermute | solution.py:79
  97.9 1.4 %unsort.1.images_ref = f32[128,512]{1,0:T(8,128)S(1)} custom-call(s32[2]{0:T(128)S(1)} %fusion.2.first_ref, s32[1,512]{1,0:T(1,128)S(1)} %get-tuple-element.48.rank_ref, f32[128,1024]{1,0:T(8,128)S(1)} %pad_maximum_fusion.2.block_ref), custom_call_target="tpu_custom_call" | custom-call | flops 402653184 | bytes 2097152 | tf_op jit(solution)/shard_map/unsort/pallas_call | solution.py:252
  99.3 1.4 %collective-permute-done.20 = f32[2,64,128]{2,1,0:T(8,128)S(1)} collective-permute-done((f32[2,64,128]{2,1,0:T(8,128)S(1)}, f32[2,64,128]{2,1,0:T(8,128)S(1)}, u32[]{:S(2)}, u32[]{:S(2)}) %collective-permute-start.20) | collective-permute-done | bytes 65568 | tf_op jit(solution)/shard_map/ppermute | solution.py:79
  100.7 7.7 %last_step.1 = (f32[64,512]{1,0:T(8,128)}, f32[64,512]{1,0:T(8,128)}) custom-call(f32[2,64,128]{2,1,0:T(8,128)S(1)} %add.40.grams_ref, f32[64,512]{1,0:T(8,128)S(1)} %copy-done, f32[128,512]{1,0:T(8,128)S(1)} %unsort.1.images_ref), custom_call_target="tpu_custom_call" | custom-call | tf_op jit(solution)/shard_map/last_step/pallas_call | solution.py:609
  (27 shorter events, 0.2 us)
Async XLA Ops:
  0.6 2.1 %collective-permute-start.2 = (f32[1,64,512]{2,1,0:T(8,128)}, f32[1,64,512]{2,1,0:T(8,128)S(1)}, u32[]{:S(2)}, u32[]{:S(2)}) collective-permute-start(f32[1,64,512]{2,1,0:T(8,128)} %bitcast.35), channel_id=1, source_target_pairs={{0,1},{1,0},{2,3},{3,2},{4,5},{5,4},{6,7},{7,6},{8,9},{9,8},{10,11... | collective-permute-start | bytes 393224 | tf_op jit(solution)/shard_map/ppermute | solution.py:61
  1.1 1.5 %collective-permute-start = (f32[1,3,512]{2,1,0:T(4,128)}, f32[1,3,512]{2,1,0:T(4,128)S(1)}, u32[]{:S(2)}, u32[]{:S(2)}) collective-permute-start(f32[1,3,512]{2,1,0:T(4,128)} %bitcast.50), channel_id=1, source_target_pairs={{0,1},{1,0},{2,3},{3,2},{4,5},{5,4},{6,7},{7,6},{8,9},{9,8},{10,11... | collective-permute-start | bytes 18440 | tf_op jit(solution)/shard_map/ppermute | solution.py:61
  1.2 1.5 %collective-permute-start.1 = (f32[1,1,512]{2,1,0:T(1,128)}, f32[1,1,512]{2,1,0:T(1,128)S(1)}, u32[]{:S(2)}, u32[]{:S(2)}) collective-permute-start(f32[1,1,512]{2,1,0:T(1,128)} %bitcast.52), channel_id=1, source_target_pairs={{0,1},{1,0},{2,3},{3,2},{4,5},{5,4},{6,7},{7,6},{8,9},{9,8},{10,11... | collective-permute-start | bytes 6152 | tf_op jit(solution)/shard_map/ppermute | solution.py:61
  7.3 10.3 %collective-permute-start.3 = (bf16[1,64,512]{2,1,0:T(8,128)(2,1)S(1)}, bf16[1,64,512]{2,1,0:T(8,128)(2,1)S(1)}, u32[]{:S(2)}, u32[]{:S(2)}) collective-permute-start(bf16[1,64,512]{2,1,0:T(8,128)(2,1)S(1)} %bitcast.20), channel_id=1, source_target_pairs={{0,16},{1,17},{2,18},{3,19},{4,20},{5,21},{6,22},{7,23},{8,24},{9,... | collective-permute-start | bytes 196616 | tf_op jit(solution)/shard_map/ppermute | solution.py:79
  12.0 12.7 %all-to-all-start = ((f32[16,4,512]{2,1,0:T(4,128)}), f32[16,4,512]{2,1,0:T(4,128)S(1)}, u32[]{:S(2)}, u32[]{:S(2)}) async-start(f32[16,4,512]{2,1,0:T(4,128)} %broadcast_in_dim.61), calls=%async_computation | async-start | bytes 262144 | tf_op jit(solution)/shard_map/all_to_all | solution.py:638
  17.6 7.4 %collective-permute-start.4 = (bf16[2,64,512]{2,1,0:T(8,128)(2,1)S(1)}, bf16[2,64,512]{2,1,0:T(8,128)(2,1)S(1)}, u32[]{:S(2)}, u32[]{:S(2)}) collective-permute-start(bf16[2,64,512]{2,1,0:T(8,128)(2,1)S(1)} %pad_maximum_fusion.5), channel_id=1, source_target_pairs={{0,8},{1,3},{2,10},{3,1},{4,12},{5,7},{6,14},{7,5},{8,0},{9,11},{1... | collective-permute-start | bytes 393224 | tf_op jit(solution)/shard_map/ppermute | solution.py:79
  24.6 1.3 %collective-permute-start.7 = (f32[1,16,4,512]{3,2,1,0:T(4,128)S(1)}, f32[1,16,4,512]{3,2,1,0:T(4,128)S(1)}, u32[]{:S(2)}, u32[]{:S(2)}) collective-permute-start(f32[1,16,4,512]{3,2,1,0:T(4,128)S(1)} %bitcast.37), channel_id=1, source_target_pairs={{0,1},{1,0},{2,3},{3,2},{4,5},{5,4},{6,7},{7,6},{8,9},{9,8},{10,11... | collective-permute-start | bytes 393224 | tf_op jit(solution)/shard_map/ppermute | solution.py:61
  25.1 7.4 %collective-permute-start.5 = (bf16[4,64,512]{2,1,0:T(8,128)(2,1)S(1)}, bf16[4,64,512]{2,1,0:T(8,128)(2,1)S(1)}, u32[]{:S(2)}, u32[]{:S(2)}) collective-permute-start(bf16[4,64,512]{2,1,0:T(8,128)(2,1)S(1)} %pad_maximum_fusion.3), channel_id=1, source_target_pairs={{0,4},{1,9},{2,6},{3,11},{4,0},{5,13},{6,2},{7,15},{8,12},{9,1},{1... | collective-permute-start | bytes 786440 | tf_op jit(solution)/shard_map/ppermute | solution.py:79
  26.0 0.7 copy-start.1
  32.6 9.2 %collective-permute-start.6 = (bf16[8,64,512]{2,1,0:T(8,128)(2,1)S(1)}, bf16[8,64,512]{2,1,0:T(8,128)(2,1)S(1)}, u32[]{:S(2)}, u32[]{:S(2)}) collective-permute-start(bf16[8,64,512]{2,1,0:T(8,128)(2,1)S(1)} %pad_maximum_fusion.near_ref), channel_id=1, source_target_pairs={{0,2},{1,5},{2,0},{3,7},{4,6},{5,1},{6,4},{7,3},{8,10},{9,13},{10,... | collective-permute-start | bytes 1572872 | tf_op jit(solution)/shard_map/ppermute | solution.py:79
  33.7 8.1 %slice-start = ((s8[8650752]{0:T(1024)(128)(4,1)}), s8[4194304]{0:T(1024)(128)(4,1)S(1)}, s32[]{:S(2)}) async-start(s8[8650752]{0:T(1024)(128)(4,1)} %bitcast.46), calls=%async_computation.1 | async-start | bytes 8388608
  33.7 8.1 %slice-start.1 = ((s8[8650752]{0:T(1024)(128)(4,1)}), s8[4194304]{0:T(1024)(128)(4,1)S(1)}, s32[]{:S(2)}) async-start(s8[8650752]{0:T(1024)(128)(4,1)} %bitcast.46), calls=%async_computation.2 | async-start | bytes 8388608
  33.7 8.1 %slice-start.2 = ((s8[8650752]{0:T(1024)(128)(4,1)}), s8[262144]{0:T(1024)(128)(4,1)S(1)}, s32[]{:S(2)}) async-start(s8[8650752]{0:T(1024)(128)(4,1)} %bitcast.46), calls=%async_computation.3 | async-start | bytes 524288
  33.7 8.1 %collective-permute-start.9 = (bf16[1,8,64,512]{3,2,1,0:T(8,128)(2,1)S(1)}, bf16[1,8,64,512]{3,2,1,0:T(8,128)(2,1)S(1)}, u32[]{:S(2)}, u32[]{:S(2)}) collective-permute-start(bf16[1,8,64,512]{3,2,1,0:T(8,128)(2,1)S(1)} %bitcast.28), channel_id=1, source_target_pairs={{0,1},{1,0},{2,3},{3,2},{4,5},{5,4},{6,7},{7,6},{8,9},{9,8},{10,11... | collective-permute-start | bytes 1572872 | tf_op jit(solution)/shard_map/ppermute | solution.py:61
  41.8 2.8 %collective-permute-start.8 = (bf16[1,8,64,512]{3,2,1,0:T(8,128)(2,1)S(1)}, bf16[1,8,64,512]{3,2,1,0:T(8,128)(2,1)S(1)}, u32[]{:S(2)}, u32[]{:S(2)}) collective-permute-start(bf16[1,8,64,512]{3,2,1,0:T(8,128)(2,1)S(1)} %bitcast.38), channel_id=1, source_target_pairs={{0,1},{1,0},{2,3},{3,2},{4,5},{5,4},{6,7},{7,6},{8,9},{9,8},{10,11... | collective-permute-start | bytes 1572872 | tf_op jit(solution)/shard_map/ppermute | solution.py:61
  47.1 7.7 %collective-permute-start.10 = (bf16[1,64,512]{2,1,0:T(8,128)(2,1)S(1)}, bf16[1,64,512]{2,1,0:T(8,128)(2,1)S(1)}, u32[]{:S(2)}, u32[]{:S(2)}) collective-permute-start(bf16[1,64,512]{2,1,0:T(8,128)(2,1)S(1)} %bitcast.24), channel_id=1, source_target_pairs={{0,16},{1,17},{2,18},{3,19},{4,20},{5,21},{6,22},{7,23},{8,24},{9,... | collective-permute-start | bytes 196616 | tf_op jit(solution)/shard_map/ppermute | solution.py:79
  54.8 5.0 %collective-permute-start.11 = (bf16[2,64,512]{2,1,0:T(8,128)(2,1)S(1)}, bf16[2,64,512]{2,1,0:T(8,128)(2,1)S(1)}, u32[]{:S(2)}, u32[]{:S(2)}) collective-permute-start(bf16[2,64,512]{2,1,0:T(8,128)(2,1)S(1)} %pad_maximum_fusion.6), channel_id=1, source_target_pairs={{0,8},{1,3},{2,10},{3,1},{4,12},{5,7},{6,14},{7,5},{8,0},{9,11},{1... | collective-permute-start | bytes 393224 | tf_op jit(solution)/shard_map/ppermute | solution.py:79
  59.9 6.4 %collective-permute-start.12 = (bf16[4,64,512]{2,1,0:T(8,128)(2,1)S(1)}, bf16[4,64,512]{2,1,0:T(8,128)(2,1)S(1)}, u32[]{:S(2)}, u32[]{:S(2)}) collective-permute-start(bf16[4,64,512]{2,1,0:T(8,128)(2,1)S(1)} %pad_maximum_fusion.4), channel_id=1, source_target_pairs={{0,4},{1,9},{2,6},{3,11},{4,0},{5,13},{6,2},{7,15},{8,12},{9,1},{1... | collective-permute-start | bytes 786440 | tf_op jit(solution)/shard_map/ppermute | solution.py:79
  66.4 2.0 %collective-permute-start.14 = (bf16[1,8,64,512]{3,2,1,0:T(8,128)(2,1)S(1)}, bf16[1,8,64,512]{3,2,1,0:T(8,128)(2,1)S(1)}, u32[]{:S(2)}, u32[]{:S(2)}) collective-permute-start(bf16[1,8,64,512]{3,2,1,0:T(8,128)(2,1)S(1)} %get-tuple-element.50), channel_id=1, source_target_pairs={{0,1},{1,0},{2,3},{3,2},{4,5},{5,4},{6,7},{7,6},{8,9},{9,8},{10,11... | collective-permute-start | bytes 1572872 | tf_op jit(solution)/shard_map/ppermute | solution.py:61
  66.5 9.2 %collective-permute-start.13 = (bf16[8,64,512]{2,1,0:T(8,128)(2,1)S(1)}, bf16[8,64,512]{2,1,0:T(8,128)(2,1)S(1)}, u32[]{:S(2)}, u32[]{:S(2)}) collective-permute-start(bf16[8,64,512]{2,1,0:T(8,128)(2,1)S(1)} %get-tuple-element.51.near_ref), channel_id=1, source_target_pairs={{0,2},{1,5},{2,0},{3,7},{4,6},{5,1},{6,4},{7,3},{8,10},{9,13},{10,... | collective-permute-start | bytes 1572872 | tf_op jit(solution)/shard_map/ppermute | solution.py:79
  71.0 29.6 %copy-start = (f32[64,512]{1,0:T(8,128)S(1)}, f32[64,512]{1,0:T(8,128)}, u32[]{:S(2)}) copy-start(f32[64,512]{1,0:T(8,128)} %start_ref.1) | copy-start | bytes 393220
  75.7 1.9 %collective-permute-start.15 = (bf16[1,8,64,512]{3,2,1,0:T(8,128)(2,1)S(1)}, bf16[1,8,64,512]{3,2,1,0:T(8,128)(2,1)S(1)}, u32[]{:S(2)}, u32[]{:S(2)}) collective-permute-start(bf16[1,8,64,512]{3,2,1,0:T(8,128)(2,1)S(1)} %bitcast.39), channel_id=1, source_target_pairs={{0,1},{1,0},{2,3},{3,2},{4,5},{5,4},{6,7},{7,6},{8,9},{9,8},{10,11... | collective-permute-start | bytes 1572872 | tf_op jit(solution)/shard_map/ppermute | solution.py:61
  80.4 1.3 %collective-permute-start.16 = (f32[2,64,128]{2,1,0:T(8,128)S(1)}, f32[2,64,128]{2,1,0:T(8,128)S(1)}, u32[]{:S(2)}, u32[]{:S(2)}) collective-permute-start(f32[2,64,128]{2,1,0:T(8,128)S(1)} %pad_maximum_fusion.7), channel_id=1, source_target_pairs={{0,1},{1,0},{2,3},{3,2},{4,5},{5,4},{6,7},{7,6},{8,9},{9,8},{10,11... | collective-permute-start | bytes 196616 | tf_op jit(solution)/shard_map/ppermute | solution.py:61
  81.8 5.8 %collective-permute-start.17 = (f32[2,64,128]{2,1,0:T(8,128)S(1)}, f32[2,64,128]{2,1,0:T(8,128)S(1)}, u32[]{:S(2)}, u32[]{:S(2)}) collective-permute-start(f32[2,64,128]{2,1,0:T(8,128)S(1)} %fusion.3), channel_id=1, source_target_pairs={{0,16},{1,5},{2,18},{3,7},{4,20},{5,1},{6,22},{7,3},{8,24},{9,13},... | collective-permute-start | bytes 196616 | tf_op jit(solution)/shard_map/ppermute | solution.py:79
  83.8 14.1 %collective-permute-start.21 = (f32[1,128,512]{2,1,0:T(8,128)S(1)}, f32[1,128,512]{2,1,0:T(8,128)S(1)}, u32[]{:S(2)}, u32[]{:S(2)}) collective-permute-start(f32[1,128,512]{2,1,0:T(8,128)S(1)} %bitcast.48), channel_id=1, source_target_pairs={{0,1},{1,0},{2,3},{3,2},{4,5},{5,4},{6,7},{7,6},{8,9},{9,8},{10,11... | collective-permute-start | bytes 786440 | tf_op jit(solution)/shard_map/ppermute | solution.py:61
  87.6 4.3 %collective-permute-start.18 = (f32[2,64,128]{2,1,0:T(8,128)S(1)}, f32[2,64,128]{2,1,0:T(8,128)S(1)}, u32[]{:S(2)}, u32[]{:S(2)}) collective-permute-start(f32[2,64,128]{2,1,0:T(8,128)S(1)} %fusion.5), channel_id=1, source_target_pairs={{0,8},{1,3},{2,10},{3,1},{4,12},{5,7},{6,14},{7,5},{8,0},{9,11},{1... | collective-permute-start | bytes 196616 | tf_op jit(solution)/shard_map/ppermute | solution.py:79
  92.0 4.3 %collective-permute-start.19 = (f32[2,64,128]{2,1,0:T(8,128)S(1)}, f32[2,64,128]{2,1,0:T(8,128)S(1)}, u32[]{:S(2)}, u32[]{:S(2)}) collective-permute-start(f32[2,64,128]{2,1,0:T(8,128)S(1)} %add.38), channel_id=1, source_target_pairs={{0,4},{1,17},{2,6},{3,19},{4,0},{5,21},{6,2},{7,23},{8,12},{9,25},... | collective-permute-start | bytes 196616 | tf_op jit(solution)/shard_map/ppermute | solution.py:79
  96.3 4.3 %collective-permute-start.20 = (f32[2,64,128]{2,1,0:T(8,128)S(1)}, f32[2,64,128]{2,1,0:T(8,128)S(1)}, u32[]{:S(2)}, u32[]{:S(2)}) collective-permute-start(f32[2,64,128]{2,1,0:T(8,128)S(1)} %add.39), channel_id=1, source_target_pairs={{0,2},{1,9},{2,0},{3,11},{4,6},{5,13},{6,4},{7,15},{8,10},{9,1},{1... | collective-permute-start | bytes 196616 | tf_op jit(solution)/shard_map/ppermute | solution.py:79

commit v8 on v7

--- a/solution.py
+++ b/solution.py
@@ -106,13 +106,14 @@
     return [jnp.array(offsets, jnp.int32) for offsets in table]
 
 
-def exchange(block):
+def exchange(block, *beside):
     regions = lax.axis_size("region")
     block = block[None]
     for even, odd in zip(*region_orders(regions)):
         other = swap_regions(block, even, odd)
         if 2 * block.shape[0] == regions:
             return block, other
+        other, *beside = lax.optimization_barrier((other, *beside))
         block = jnp.concatenate([block, other], axis=0)
 
 
@@ -144,7 +145,7 @@
 def sort_kernel(
     first_ref, owner_ref, near_ref, far_ref, near_error_ref, far_error_ref, block_ref, other_ref,
     rounded_out, places_out, own_out, block_out, rank_out,
-    order_ref, column_ref, owned_ref, places_ref, errors_ref, blocks_ref, sems,
+    order_ref, column_ref, rank_ref, owned_ref, places_ref, errors_ref, blocks_ref, sems,
 ):
     columns, local = block_out.shape
     half = block_ref.shape[0]
@@ -180,15 +181,27 @@
         jnp.concatenate([y_row, index, jnp.zeros((6, n), jnp.float32)], axis=0)
     )
 
-    def count(block, total):
+    def count(ties, block, total):
         start = pl.multiple_of(block * step, step)
         y_column = jnp.broadcast_to(column_ref[pl.ds(start, step), 0:1], (step, n))
-        index_column = jnp.broadcast_to(column_ref[pl.ds(start, step), 1:2], (step, n))
-        before = (y_column < y_row) | ((y_column == y_row) & (index_column < index))
+        before = y_column < y_row
+        if ties:
+            index_column = jnp.broadcast_to(column_ref[pl.ds(start, step), 1:2], (step, n))
+            before = before | ((y_column == y_row) & (index_column < index))
         return total + jnp.sum(jnp.where(before, 1.0, 0.0).reshape(step // 8, 8, n), axis=0)
 
-    total = lax.fori_loop(0, n // step, count, jnp.zeros((8, n), jnp.float32))
-    rank = jnp.sum(total, axis=0, keepdims=True).astype(jnp.int32)
+    def ranks(ties):
+        start = jnp.zeros((8, n), jnp.float32)
+        total = lax.fori_loop(0, n // step, functools.partial(count, ties), start)
+        rank_ref[...] = jnp.sum(total, axis=0, keepdims=True).astype(jnp.int32)
+
+    ranks(False)
+
+    @pl.when(jnp.sum(rank_ref[...]) != n * (n - 1) // 2)
+    def _():
+        ranks(True)
+
+    rank = rank_ref[...]
     rank_out[...] = rank[:, :local]
     fill_order(first_ref[0], rank, order_ref, 0, local)
     for copy in copies[5:]:
@@ -225,6 +238,7 @@
         scratch_shapes=[
             pltpu.VMEM((local, n), jnp.bfloat16),
             pltpu.VMEM((n, 8), jnp.float32),
+            pltpu.VMEM((1, n), jnp.int32),
             pltpu.SMEM(tile_owner.shape, jnp.int32),
             pltpu.VMEM((n // local, 3, local), jnp.float32),
             pltpu.VMEM((n // local, 1, local), jnp.float32),
@@ -428,11 +442,13 @@
     )(place, distance, tile_owner, own, near, far)
 
 
-def apply_kernel(started, last, ids_ref, count_ref, near_ref, other_ref, tiles_ref, *refs):
+def apply_kernel(started, last, grams, ids_ref, count_ref, near_ref, other_ref, tiles_ref, *refs):
     refs = list(refs)
     start_ref = refs.pop(0) if started else None
     if last:
-        block_ref, scale_ref, out_ref, rounded_ref, gram_ref, all_ref, piece_sems, total_ref = refs
+        first_ref = refs.pop(2) if grams else None
+        block_ref, scale_ref, out_ref, rounded_ref = refs[:4]
+        all_ref, piece_sems, total_ref = refs[-3:]
         held_ref = tiles_ref
     else:
         total_ref, all_ref, piece_sems, held_ref, sems = refs
@@ -495,13 +511,15 @@
         result = jnp.transpose(total_ref[...]) + scale_ref[...] * block
         out_ref[...] = result
         rounded_ref[...] = result.astype(jnp.bfloat16)
-        gram_ref[...] = dot_nt(block, jnp.concatenate([block, result], axis=0), HIGHEST)
+        if grams:
+            refs[4][...] = jnp.concatenate([first_ref[...], packed_grams(block, result)], axis=1)
 
 
 def apply_tiles(plan, near, far, tiles, start, finish):
     near, far = [piece.reshape((-1,) + piece.shape[2:]) for piece in (near, far)]
     half, columns, local = near.shape
     last = finish is not None
+    grams = last and len(finish) > 2
     smem = pl.BlockSpec(memory_space=pltpu.SMEM)
     anywhere = pl.BlockSpec(memory_space=pl.ANY)
     operands = [*plan, near, far, tiles]
@@ -516,19 +534,20 @@
     ]
     if last:
         operands += finish
-        in_specs += whole_vmem(2)
+        in_specs += whole_vmem(len(finish))
         out_shape = (
             jax.ShapeDtypeStruct((columns, local), jnp.float32),
             jax.ShapeDtypeStruct((columns, local), jnp.bfloat16),
-            jax.ShapeDtypeStruct((columns, 2 * columns), jnp.float32),
         )
+        if grams:
+            out_shape += (jax.ShapeDtypeStruct((columns + 8, 2 * columns), jnp.float32),)
         scratch.append(pltpu.VMEM((local, columns), jnp.float32))
     else:
         out_shape = (jax.ShapeDtypeStruct((local, columns), jnp.float32),)
         scratch.append(pltpu.VMEM(tiles.shape, jnp.bfloat16))
         scratch.append(pltpu.SemaphoreType.DMA((tiles.shape[0] // UNROLL,)))
     return pl.pallas_call(
-        functools.partial(apply_kernel, start is not None, last),
+        functools.partial(apply_kernel, start is not None, last, grams),
         out_shape=out_shape,
         in_specs=in_specs,
         out_specs=tuple(whole_vmem(len(out_shape))),
@@ -539,6 +558,46 @@
         ),
         name="apply_last" if last else "apply_first",
     )(*operands)
+
+
+def packed_grams(left, right):
+    n = left.shape[0]
+    both = dot_nt(left, jnp.concatenate([left, right], axis=0), HIGHEST)
+    square, mixed = both[:, :n], both[:, n:]
+    mixed = 0.5 * (mixed + jnp.transpose(mixed))
+    row, column = [lax.broadcasted_iota(jnp.int32, (n, n), axis) for axis in range(2)]
+    diagonals = [
+        jnp.sum(jnp.where(row == column, matrix, 0.0), axis=0, keepdims=True) for matrix in (square, mixed)
+    ]
+    rest = jnp.zeros((6, n), jnp.float32)
+    return jnp.concatenate([jnp.where(row < column, square, mixed), *diagonals, rest], axis=0)
+
+
+def unpacked_grams(packed):
+    n = packed.shape[1]
+    matrix = packed[:n]
+    row, column = [lax.broadcasted_iota(jnp.int32, (n, n), axis) for axis in range(2)]
+    upper = jnp.where(row < column, matrix, 0.0)
+    lower = jnp.where(row > column, matrix, 0.0)
+    diagonals = [jnp.where(row == column, packed[n + k : n + k + 1], 0.0) for k in range(2)]
+    return upper + jnp.transpose(upper) + diagonals[0], lower + jnp.transpose(lower) + diagonals[1]
+
+
+def grams_kernel(left_ref, right_ref, out_ref):
+    out_ref[...] = packed_grams(left_ref[...], right_ref[...])
+
+
+def first_grams(left, right):
+    n = left.shape[0]
+    return pl.pallas_call(
+        grams_kernel,
+        out_shape=jax.ShapeDtypeStruct((n + 8, n), jnp.float32),
+        in_specs=whole_vmem(2),
+        out_specs=whole_vmem(1)[0],
+        compiler_params=pltpu.CompilerParams(vmem_limit_bytes=VMEM),
+        cost_estimate=pl.CostEstimate(flops=2 * 10**9, bytes_accessed=8 * left.size, transcendentals=0),
+        name="first_grams",
+    )(left, right)
 
 
 def reciprocal(value):
@@ -590,13 +649,13 @@
 
 
 def last_kernel(grams_ref, start_ref, images_ref, weights_ref, residual_ref):
-    n = grams_ref.shape[1]
-    squares, mixed = grams_ref[0, :, :n], grams_ref[0, :, n:]
-    images, cross = grams_ref[1, :, :n], grams_ref[1, :, n:]
+    n = grams_ref.shape[1] // 2
+    squares, mixed = unpacked_grams(grams_ref[:, :n])
+    images, cross = unpacked_grams(grams_ref[:, n:])
     solved = solve_positive(mixed, jnp.concatenate([squares, images], axis=1))
     step, carried = solved[:, :n], solved[:, n:]
     product = dot_nn(images, solved, HIGHEST)
-    second = solve_positive(cross - product[:, n:], jnp.transpose(mixed) - product[:, :n])
+    second = solve_positive(cross - product[:, n:], mixed - product[:, :n])
     first = jnp.transpose(step - dot_nn(carried, second, HIGHEST))
     second = jnp.transpose(second)
     both = jnp.concatenate([first, second], axis=1)
@@ -653,23 +712,23 @@
         plans.append(plan)
         tiles.append(built)
 
-    def operate(sent, block, building):
+    def operate(sent, block, *grams):
+        building = not grams
         total = None
-        for part, group in enumerate(exchange(sent)):
+        for part, group in enumerate(exchange(sent, *grams)):
             if building:
                 group, plans[part] = lax.optimization_barrier((group, plans[part]))
             elif part:
                 group, total = lax.optimization_barrier((group, total))
             near, far = halves(group, "tile")
             results = apply_tiles(
-                plans[part], near, far, tiles[part], total, (block, scale) if part else None
+                plans[part], near, far, tiles[part], total, (block, scale, *grams) if part else None
             )
             total = results[0]
         return results
 
-    image, image_rounded, grams = operate(rounded, start, True)
-    second, _, cross = operate(image_rounded, image, False)
-    grams = jnp.stack([grams, cross])
+    image, image_rounded = operate(rounded, start)
+    second, _, grams = operate(image_rounded, image, first_grams(start, image))
     grams = sum_regions(sum_tiles(grams))
     near, far = halves(jnp.concatenate([image, second], axis=0), "tile")
     images = unsort(first, rank, jnp.concatenate([*near, *far], axis=1))

time: 109 us -> 108 us (level); the launches traced: 108 us -> 109 us
  starting transfers between devices: 22.9 us -> 33 us
  waiting for transfers between devices: 46.9 us -> 37.5 us
    ppermute x12, waiting for transfers between devices: 37.1 us -> 27 us  [swap_regions(): return lax.ppermute(block, ('region', 'tile'), route)]
    ppermute x12, starting transfers between devices: 16.6 us -> 24.3 us  [swap_regions(): return lax.ppermute(block, ('region', 'tile'), route)]
    all_to_all x1, starting transfers between devices: 4.84 us -> 6.98 us  [shards(): everywhere = lax.all_to_all(everywhere, 'region', 0, 0)]
    pallas_call x4 -> x5, Pallas kernels: 10.7 us -> 11.1 us  [the longest x4 10.4 us: apply_tiles(): pl.pallas_call(functools.partial(apply_kernel, start is not None, last, g...]
  transfers between devices with their start and end apart: 23 -> 23, of which waited for: 15 -> 15; matrix products, arithmetic and copies ran while one was open for 2% -> 2% of each run, Pallas kernels for 16% -> 15%
where the time goes in v8:
time: 108 us; the launch traced here: 109 us
  waiting for transfers between devices  37.5 us (35%)
  Pallas kernels  34.4 us (32%)
  starting transfers between devices  33 us (31%)
  local copies, waits for them, and re-layouts  1.69 us (2%)
  other arithmetic  1.13 us (1%)
    ppermute x12, waiting for transfers between devices, swap_regions(): return lax.ppermute(block, ('region', 'tile'), route)  27 us
    ppermute x12, starting transfers between devices, swap_regions(): return lax.ppermute(block, ('region', 'tile'), route)  24.3 us
    pallas_call x2, Pallas kernels, build_tiles(): pl.pallas_call(functools.partial(build_kernel, kept), out_shape=tuple((ja...  10.5 us
    pallas_call x4, Pallas kernels, apply_tiles(): pl.pallas_call(functools.partial(apply_kernel, start is not None, last, g...  10.4 us
    pallas_call x1, Pallas kernels, last_step(): pl.pallas_call(last_kernel, out_shape=(jax.ShapeDtypeStruct(start.shape,...  7.52 us
    all_to_all x1, starting transfers between devices, shards(): everywhere = lax.all_to_all(everywhere, 'region', 0, 0)  6.98 us
    ppermute x10, waiting for transfers between devices, swapped(): lax.ppermute(block, axis, [(i, i ^ bit) for i in range(lax.axis_size(axis...  5.44 us
    all_to_all x1, waiting for transfers between devices, shards(): everywhere = lax.all_to_all(everywhere, 'region', 0, 0)  5.05 us
  transfers between devices with their start and end apart: 23, of which 15 were waited for; matrix products, arithmetic and copies ran while one was open for 2% of the time, Pallas kernels for 15%

profile of v8, /device:TPU:0, one launch (start us, length us, event | category | flops | bytes accessed | tf_op | source)
XLA Modules:
  0.0 108.6 jit_solution(15667080307270548439)
XLA Ops:
  0.6 0.5 collective-permute-start.2
  1.1 0.1 collective-permute-start
  1.2 0.4 collective-permute-start.1
  1.7 1.0 collective-permute-done.1.far_error_ref
  2.7 0.0 collective-permute-done.far_ref
  2.7 0.0 collective-permute-done.2.other_ref
  2.7 3.9 %sort_region.1 = (bf16[64,512]{1,0:T(8,128)(2,1)S(1)}, f32[4,512]{1,0:T(4,128)S(1)}, f32[8,512]{1,0:T(8,128)S(1)}, f32[64,512]{1,0:T(8,128)S(1)}, s32[1,512]{1,0:T(1,128)S(1)}) custom-call(s32[2]{0:T(128)S(1)} %fusion.2.first_ref, s32[1,7]{1,0:T(1,128)} %listed_ref.3, f32[1,3,512]{2,1,0:T(4,128)} %bitcast.43, f32[1,3,512]{2,1,0:T(4,128)S(1)} %collective-permute-done.far_ref, ...), custom_call_target="tpu_custom_call" | custom-call | flops 226492416 | bytes 2097152 | tf_op jit(solution)/shard_map/sort_region/pallas_call | solution.py:227
  6.6 4.0 %collective-permute-start.3 = (bf16[1,64,512]{2,1,0:T(8,128)(2,1)S(1)}, bf16[1,64,512]{2,1,0:T(8,128)(2,1)S(1)}, u32[]{:S(2)}, u32[]{:S(2)}) collective-permute-start(bf16[1,64,512]{2,1,0:T(8,128)(2,1)S(1)} %bitcast.18), channel_id=1, source_target_pairs={{0,16},{1,17},{2,18},{3,19},{4,20},{5,21},{6,22},{7,23},{8,24},{9,... | collective-permute-start | bytes 196616 | tf_op jit(solution)/shard_map/ppermute | solution.py:79
  10.6 0.7 broadcast_in_dim.61
  11.3 7.0 %all-to-all-start = ((f32[16,4,512]{2,1,0:T(4,128)}), f32[16,4,512]{2,1,0:T(4,128)S(1)}, u32[]{:S(2)}, u32[]{:S(2)}) async-start(f32[16,4,512]{2,1,0:T(4,128)} %broadcast_in_dim.61), calls=%async_computation | async-start | bytes 262144 | tf_op jit(solution)/shard_map/all_to_all | solution.py:697
  18.3 0.7 select_xor_fusion
  19.0 0.0 collective-permute-done.3
  19.1 2.0 %collective-permute-start.4 = (bf16[2,64,512]{2,1,0:T(8,128)(2,1)S(1)}, bf16[2,64,512]{2,1,0:T(8,128)(2,1)S(1)}, u32[]{:S(2)}, u32[]{:S(2)}) collective-permute-start(bf16[2,64,512]{2,1,0:T(8,128)(2,1)S(1)} %pad_maximum_fusion.5), channel_id=1, source_target_pairs={{0,8},{1,3},{2,10},{3,1},{4,12},{5,7},{6,14},{7,5},{8,0},{9,11},{1... | collective-permute-start | bytes 393224 | tf_op jit(solution)/shard_map/ppermute | solution.py:79
  21.1 5.0 %all-to-all-done.near_ref = f32[16,4,512]{2,1,0:T(4,128)S(1)} async-done(((f32[16,4,512]{2,1,0:T(4,128)}), f32[16,4,512]{2,1,0:T(4,128)S(1)}, u32[]{:S(2)}, u32[]{:S(2)}) %all-to-all-start) | async-done | bytes 131104 | tf_op jit(solution)/shard_map/all_to_all | solution.py:697
  26.1 0.0 collective-permute-start.7
  26.1 0.1 broadcast_subtract_fusion
  26.2 0.1 reshape.59.distance_ref
  26.3 0.1 reshape.53.place_ref
  26.3 0.1 reshape.58.distance_ref
  26.4 0.1 reshape.49.place_ref
  26.5 0.0 collective-permute-done.4
  26.5 0.8 collective-permute-start.5
  27.4 0.1 collective-permute-done.7
  27.5 0.7 copy-done.1
  28.1 5.9 %build_passed.1 = (s32[532]{0:T(1024)S(1)}, s32[1]{0:T(128)}, bf16[132,64,512]{2,1,0:T(8,128)(2,1)}) custom-call(s32[16]{0:T(128)S(1)} %reshape.53.place_ref, s32[16,1]{1,0:T(8,128)S(1)} %reshape.59.distance_ref, s32[1,7]{1,0:T(1,128)S(1)} %copy-done.1, f32[8,512]{1,0:T(8,128)S(1)} %get-tuple-element.27.own_ref, f32[16,4,512]{2,1,0:T(4,128)S(1)} %all-to-all-done.near_ref, ...), custom_call_target="tpu_custom_call" | custom-call | flops 8388608000 | bytes 4194304 | tf_op jit(solution)/shard_map/build_passed/pallas_call | solution.py:430
  34.0 0.0 collective-permute-done.5
  34.0 0.1 pad_maximum_fusion.near_ref
  34.0 1.2 %collective-permute-start.6 = (bf16[8,64,512]{2,1,0:T(8,128)(2,1)S(1)}, bf16[8,64,512]{2,1,0:T(8,128)(2,1)S(1)}, u32[]{:S(2)}, u32[]{:S(2)}) collective-permute-start(bf16[8,64,512]{2,1,0:T(8,128)(2,1)S(1)} %pad_maximum_fusion.near_ref), channel_id=1, source_target_pairs={{0,2},{1,5},{2,0},{3,7},{4,6},{5,1},{6,4},{7,3},{8,10},{9,13},{10,... | collective-permute-start | bytes 1572872 | tf_op jit(solution)/shard_map/ppermute | solution.py:79
  35.2 4.7 %build_kept.1 = (s32[532]{0:T(1024)S(1)}, s32[1]{0:T(128)}, bf16[132,64,512]{2,1,0:T(8,128)(2,1)S(1)}) custom-call(s32[16]{0:T(128)S(1)} %reshape.49.place_ref, s32[16,1]{1,0:T(8,128)S(1)} %reshape.58.distance_ref, s32[1,7]{1,0:T(1,128)S(1)} %copy-done.1, f32[8,512]{1,0:T(8,128)S(1)} %get-tuple-element.27.own_ref, f32[16,4,512]{2,1,0:T(4,128)S(1)} %all-to-all-done.near_ref, ...), custom_call_target="tpu_custom_call" | custom-call | flops 8388608000 | bytes 4194304 | tf_op jit(solution)/shard_map/build_kept/pallas_call | solution.py:430
  39.9 3.4 %collective-permute-done.6.near_ref = bf16[8,64,512]{2,1,0:T(8,128)(2,1)S(1)} collective-permute-done((bf16[8,64,512]{2,1,0:T(8,128)(2,1)S(1)}, bf16[8,64,512]{2,1,0:T(8,128)(2,1)S(1)}, u32[]{:S(2)}, u32[]{:S(2)}) %collective-permute-start.6) | collective-permute-done | bytes 524320 | tf_op jit(solution)/shard_map/ppermute | solution.py:79
  43.3 2.7 %apply_first.2.refs_0_ = f32[512,64]{1,0:T(8,128)S(1)} custom-call(s32[532]{0:T(1024)S(1)} %get-tuple-element.37.ids_ref, s32[1]{0:T(128)} %get-tuple-element.38.count_ref, bf16[8,64,512]{2,1,0:T(8,128)(2,1)S(1)} %pad_maximum_fusion.near_ref, bf16[8,64,512]{2,1,0:T(8,128)(2,1)S(1)} %bitcast.32, bf16[132,64,512]{2,1,0:T(8,128)(2,1)S(1)} %bitcast.39), custom_call_target="tpu_custom_call" | custom-call | flops 3145728000 | bytes 4194304 | tf_op jit(solution)/shard_map/apply_first/pallas_call | solution.py:549
  46.0 0.0 collective-permute-done.8
  46.1 2.2 %apply_last.2 = (f32[64,512]{1,0:T(8,128)S(1)}, bf16[64,512]{1,0:T(8,128)(2,1)S(1)}) custom-call(s32[532]{0:T(1024)S(1)} %get-tuple-element.31.ids_ref, s32[1]{0:T(128)} %get-tuple-element.32.count_ref, bf16[8,64,512]{2,1,0:T(8,128)(2,1)S(1)} %collective-permute-done.6.near_ref, bf16[8,64,512]{2,1,0:T(8,128)(2,1)S(1)} %bitcast.33, ...), custom_call_target="tpu_custom_call" | custom-call | flops 3145728000 | bytes 4194304 | tf_op jit(solution)/shard_map/apply_last/pallas_call | solution.py:549
  48.2 3.3 %collective-permute-start.10 = (bf16[1,64,512]{2,1,0:T(8,128)(2,1)S(1)}, bf16[1,64,512]{2,1,0:T(8,128)(2,1)S(1)}, u32[]{:S(2)}, u32[]{:S(2)}) collective-permute-start(bf16[1,64,512]{2,1,0:T(8,128)(2,1)S(1)} %bitcast.22), channel_id=1, source_target_pairs={{0,16},{1,17},{2,18},{3,19},{4,20},{5,21},{6,22},{7,23},{8,24},{9,... | collective-permute-start | bytes 196616 | tf_op jit(solution)/shard_map/ppermute | solution.py:79
  51.5 0.7 first_grams.1.refs_3_
  52.2 2.1 %collective-permute-done.10 = bf16[1,64,512]{2,1,0:T(8,128)(2,1)S(1)} collective-permute-done((bf16[1,64,512]{2,1,0:T(8,128)(2,1)S(1)}, bf16[1,64,512]{2,1,0:T(8,128)(2,1)S(1)}, u32[]{:S(2)}, u32[]{:S(2)}) %collective-permute-start.10) | collective-permute-done | bytes 65568 | tf_op jit(solution)/shard_map/ppermute | solution.py:79
  54.3 2.4 %collective-permute-start.11 = (bf16[2,64,512]{2,1,0:T(8,128)(2,1)S(1)}, bf16[2,64,512]{2,1,0:T(8,128)(2,1)S(1)}, u32[]{:S(2)}, u32[]{:S(2)}) collective-permute-start(bf16[2,64,512]{2,1,0:T(8,128)(2,1)S(1)} %pad_maximum_fusion.6), channel_id=1, source_target_pairs={{0,8},{1,3},{2,10},{3,1},{4,12},{5,7},{6,14},{7,5},{8,0},{9,11},{1... | collective-permute-start | bytes 393224 | tf_op jit(solution)/shard_map/ppermute | solution.py:79
  56.7 2.9 %collective-permute-done.11 = bf16[2,64,512]{2,1,0:T(8,128)(2,1)S(1)} collective-permute-done((bf16[2,64,512]{2,1,0:T(8,128)(2,1)S(1)}, bf16[2,64,512]{2,1,0:T(8,128)(2,1)S(1)}, u32[]{:S(2)}, u32[]{:S(2)}) %collective-permute-start.11) | collective-permute-done | bytes 131104 | tf_op jit(solution)/shard_map/ppermute | solution.py:79
  59.6 2.3 %collective-permute-start.12 = (bf16[4,64,512]{2,1,0:T(8,128)(2,1)S(1)}, bf16[4,64,512]{2,1,0:T(8,128)(2,1)S(1)}, u32[]{:S(2)}, u32[]{:S(2)}) collective-permute-start(bf16[4,64,512]{2,1,0:T(8,128)(2,1)S(1)} %pad_maximum_fusion.4), channel_id=1, source_target_pairs={{0,4},{1,9},{2,6},{3,11},{4,0},{5,13},{6,2},{7,15},{8,12},{9,1},{1... | collective-permute-start | bytes 786440 | tf_op jit(solution)/shard_map/ppermute | solution.py:79
  61.9 4.4 %collective-permute-done.12 = bf16[4,64,512]{2,1,0:T(8,128)(2,1)S(1)} collective-permute-done((bf16[4,64,512]{2,1,0:T(8,128)(2,1)S(1)}, bf16[4,64,512]{2,1,0:T(8,128)(2,1)S(1)}, u32[]{:S(2)}, u32[]{:S(2)}) %collective-permute-start.12) | collective-permute-done | bytes 262176 | tf_op jit(solution)/shard_map/ppermute | solution.py:79
  66.3 0.1 fusion.3
  66.4 0.1 collective-permute-start.14
  66.5 0.5 collective-permute-start.13
  67.0 1.4 %collective-permute-done.14 = bf16[1,8,64,512]{3,2,1,0:T(8,128)(2,1)S(1)} collective-permute-done((bf16[1,8,64,512]{3,2,1,0:T(8,128)(2,1)S(1)}, bf16[1,8,64,512]{3,2,1,0:T(8,128)(2,1)S(1)}, u32[]{:S(2)}, u32[]{:S(2)}) %collective-permute-start.14) | collective-permute-done | bytes 524320 | tf_op jit(solution)/shard_map/ppermute | solution.py:61
  68.4 2.7 %apply_first.3.refs_0_ = f32[512,64]{1,0:T(8,128)S(1)} custom-call(s32[532]{0:T(1024)S(1)} %get-tuple-element.37.ids_ref, s32[1]{0:T(128)} %get-tuple-element.38.count_ref, bf16[8,64,512]{2,1,0:T(8,128)(2,1)S(1)} %get-tuple-element.51.near_ref, bf16[8,64,512]{2,1,0:T(8,128)(2,1)S(1)} %bitcast.35, bf16[132,64,512]{2,1,0:T(8,128)(2,1)S(1)} %bitcast.39), custom_call_target="tpu_custom_call" | custom-call | flops 3145728000 | bytes 4194304 | tf_op jit(solution)/shard_map/apply_first/pallas_call | solution.py:549
  71.1 0.0 copy-start
  71.1 4.6 %collective-permute-done.13.near_ref = bf16[8,64,512]{2,1,0:T(8,128)(2,1)S(1)} collective-permute-done((bf16[8,64,512]{2,1,0:T(8,128)(2,1)S(1)}, bf16[8,64,512]{2,1,0:T(8,128)(2,1)S(1)}, u32[]{:S(2)}, u32[]{:S(2)}) %collective-permute-start.13) | collective-permute-done | bytes 524320 | tf_op jit(solution)/shard_map/ppermute | solution.py:79
  75.7 0.0 collective-permute-start.15
  75.7 1.9 %collective-permute-done.15 = bf16[1,8,64,512]{3,2,1,0:T(8,128)(2,1)S(1)} collective-permute-done((bf16[1,8,64,512]{3,2,1,0:T(8,128)(2,1)S(1)}, bf16[1,8,64,512]{3,2,1,0:T(8,128)(2,1)S(1)}, u32[]{:S(2)}, u32[]{:S(2)}) %collective-permute-start.15) | collective-permute-done | bytes 524320 | tf_op jit(solution)/shard_map/ppermute | solution.py:61
  77.6 2.9 %apply_last.3 = (f32[64,512]{1,0:T(8,128)S(1)}, bf16[64,512]{1,0:T(8,128)(2,1)}, f32[72,128]{1,0:T(8,128)S(1)}) custom-call(s32[532]{0:T(1024)S(1)} %get-tuple-element.31.ids_ref, s32[1]{0:T(128)} %get-tuple-element.32.count_ref, bf16[8,64,512]{2,1,0:T(8,128)(2,1)S(1)} %collective-permute-done.13.near_ref, bf16[8,64,512]{2,1,0:T(8,128)(2,1)S(1)} %bitcast.34, ...), custom_call_target="tpu_custom_call" | custom-call | flops 3145728000 | bytes 4194304 | tf_op jit(solution)/shard_map/apply_last/pallas_call | solution.py:549
  80.5 0.2 collective-permute-start.21
  80.7 0.4 collective-permute-start.16
  81.1 1.1 collective-permute-done.16
  82.2 2.7 %collective-permute-start.17 = (f32[72,128]{1,0:T(8,128)S(1)}, f32[72,128]{1,0:T(8,128)S(1)}, u32[]{:S(2)}, u32[]{:S(2)}) collective-permute-start(f32[72,128]{1,0:T(8,128)S(1)} %add.36), channel_id=1, source_target_pairs={{0,16},{1,5},{2,18},{3,7},{4,20},{5,1},{6,22},{7,3},{8,24},{9,13},... | collective-permute-start | bytes 110600 | tf_op jit(solution)/shard_map/ppermute | solution.py:79
  84.8 2.2 %collective-permute-done.17 = f32[72,128]{1,0:T(8,128)S(1)} collective-permute-done((f32[72,128]{1,0:T(8,128)S(1)}, f32[72,128]{1,0:T(8,128)S(1)}, u32[]{:S(2)}, u32[]{:S(2)}) %collective-permute-start.17) | collective-permute-done | bytes 36896 | tf_op jit(solution)/shard_map/ppermute | solution.py:79
  87.0 2.5 %collective-permute-start.18 = (f32[72,128]{1,0:T(8,128)S(1)}, f32[72,128]{1,0:T(8,128)S(1)}, u32[]{:S(2)}, u32[]{:S(2)}) collective-permute-start(f32[72,128]{1,0:T(8,128)S(1)} %add.37), channel_id=1, source_target_pairs={{0,8},{1,3},{2,10},{3,1},{4,12},{5,7},{6,14},{7,5},{8,0},{9,11},{1... | collective-permute-start | bytes 110600 | tf_op jit(solution)/shard_map/ppermute | solution.py:79
  89.5 1.9 %collective-permute-done.18 = f32[72,128]{1,0:T(8,128)S(1)} collective-permute-done((f32[72,128]{1,0:T(8,128)S(1)}, f32[72,128]{1,0:T(8,128)S(1)}, u32[]{:S(2)}, u32[]{:S(2)}) %collective-permute-start.18) | collective-permute-done | bytes 36896 | tf_op jit(solution)/shard_map/ppermute | solution.py:79
  91.5 2.3 %collective-permute-start.19 = (f32[72,128]{1,0:T(8,128)S(1)}, f32[72,128]{1,0:T(8,128)S(1)}, u32[]{:S(2)}, u32[]{:S(2)}) collective-permute-start(f32[72,128]{1,0:T(8,128)S(1)} %add.38), channel_id=1, source_target_pairs={{0,4},{1,17},{2,6},{3,19},{4,0},{5,21},{6,2},{7,23},{8,12},{9,25},... | collective-permute-start | bytes 110600 | tf_op jit(solution)/shard_map/ppermute | solution.py:79
  93.7 1.9 %collective-permute-done.19 = f32[72,128]{1,0:T(8,128)S(1)} collective-permute-done((f32[72,128]{1,0:T(8,128)S(1)}, f32[72,128]{1,0:T(8,128)S(1)}, u32[]{:S(2)}, u32[]{:S(2)}) %collective-permute-start.19) | collective-permute-done | bytes 36896 | tf_op jit(solution)/shard_map/ppermute | solution.py:79
  95.7 0.4 collective-permute-start.20
  96.1 3.5 %collective-permute-done.20 = f32[72,128]{1,0:T(8,128)S(1)} collective-permute-done((f32[72,128]{1,0:T(8,128)S(1)}, f32[72,128]{1,0:T(8,128)S(1)}, u32[]{:S(2)}, u32[]{:S(2)}) %collective-permute-start.20) | collective-permute-done | bytes 36896 | tf_op jit(solution)/shard_map/ppermute | solution.py:79
  99.6 0.0 collective-permute-done.21
  99.7 1.4 %unsort.1.images_ref = f32[128,512]{1,0:T(8,128)S(1)} custom-call(s32[2]{0:T(128)S(1)} %fusion.2.first_ref, s32[1,512]{1,0:T(1,128)S(1)} %get-tuple-element.48.rank_ref, f32[128,1024]{1,0:T(8,128)S(1)} %pad_maximum_fusion.2.block_ref), custom_call_target="tpu_custom_call" | custom-call | flops 402653184 | bytes 2097152 | tf_op jit(solution)/shard_map/unsort/pallas_call | solution.py:266
  101.1 7.5 %last_step.1 = (f32[64,512]{1,0:T(8,128)}, f32[64,512]{1,0:T(8,128)}) custom-call(f32[72,128]{1,0:T(8,128)S(1)} %add.40.grams_ref, f32[64,512]{1,0:T(8,128)S(1)} %copy-done, f32[128,512]{1,0:T(8,128)S(1)} %unsort.1.images_ref), custom_call_target="tpu_custom_call" | custom-call | tf_op jit(solution)/shard_map/last_step/pallas_call | solution.py:668
  (27 shorter events, 0.2 us)
Async XLA Ops:
  0.6 2.1 %collective-permute-start.2 = (f32[1,64,512]{2,1,0:T(8,128)}, f32[1,64,512]{2,1,0:T(8,128)S(1)}, u32[]{:S(2)}, u32[]{:S(2)}) collective-permute-start(f32[1,64,512]{2,1,0:T(8,128)} %bitcast.27), channel_id=1, source_target_pairs={{0,1},{1,0},{2,3},{3,2},{4,5},{5,4},{6,7},{7,6},{8,9},{9,8},{10,11... | collective-permute-start | bytes 393224 | tf_op jit(solution)/shard_map/ppermute | solution.py:61
  1.1 1.5 %collective-permute-start = (f32[1,3,512]{2,1,0:T(4,128)}, f32[1,3,512]{2,1,0:T(4,128)S(1)}, u32[]{:S(2)}, u32[]{:S(2)}) collective-permute-start(f32[1,3,512]{2,1,0:T(4,128)} %bitcast.42), channel_id=1, source_target_pairs={{0,1},{1,0},{2,3},{3,2},{4,5},{5,4},{6,7},{7,6},{8,9},{9,8},{10,11... | collective-permute-start | bytes 18440 | tf_op jit(solution)/shard_map/ppermute | solution.py:61
  1.2 1.5 %collective-permute-start.1 = (f32[1,1,512]{2,1,0:T(1,128)}, f32[1,1,512]{2,1,0:T(1,128)S(1)}, u32[]{:S(2)}, u32[]{:S(2)}) collective-permute-start(f32[1,1,512]{2,1,0:T(1,128)} %bitcast.44), channel_id=1, source_target_pairs={{0,1},{1,0},{2,3},{3,2},{4,5},{5,4},{6,7},{7,6},{8,9},{9,8},{10,11... | collective-permute-start | bytes 6152 | tf_op jit(solution)/shard_map/ppermute | solution.py:61
  6.6 12.4 %collective-permute-start.3 = (bf16[1,64,512]{2,1,0:T(8,128)(2,1)S(1)}, bf16[1,64,512]{2,1,0:T(8,128)(2,1)S(1)}, u32[]{:S(2)}, u32[]{:S(2)}) collective-permute-start(bf16[1,64,512]{2,1,0:T(8,128)(2,1)S(1)} %bitcast.18), channel_id=1, source_target_pairs={{0,16},{1,17},{2,18},{3,19},{4,20},{5,21},{6,22},{7,23},{8,24},{9,... | collective-permute-start | bytes 196616 | tf_op jit(solution)/shard_map/ppermute | solution.py:79
  11.3 14.8 %all-to-all-start = ((f32[16,4,512]{2,1,0:T(4,128)}), f32[16,4,512]{2,1,0:T(4,128)S(1)}, u32[]{:S(2)}, u32[]{:S(2)}) async-start(f32[16,4,512]{2,1,0:T(4,128)} %broadcast_in_dim.61), calls=%async_computation | async-start | bytes 262144 | tf_op jit(solution)/shard_map/all_to_all | solution.py:697
  19.1 7.4 %collective-permute-start.4 = (bf16[2,64,512]{2,1,0:T(8,128)(2,1)S(1)}, bf16[2,64,512]{2,1,0:T(8,128)(2,1)S(1)}, u32[]{:S(2)}, u32[]{:S(2)}) collective-permute-start(bf16[2,64,512]{2,1,0:T(8,128)(2,1)S(1)} %pad_maximum_fusion.5), channel_id=1, source_target_pairs={{0,8},{1,3},{2,10},{3,1},{4,12},{5,7},{6,14},{7,5},{8,0},{9,11},{1... | collective-permute-start | bytes 393224 | tf_op jit(solution)/shard_map/ppermute | solution.py:79
  26.1 1.3 %collective-permute-start.7 = (f32[1,16,4,512]{3,2,1,0:T(4,128)S(1)}, f32[1,16,4,512]{3,2,1,0:T(4,128)S(1)}, u32[]{:S(2)}, u32[]{:S(2)}) collective-permute-start(f32[1,16,4,512]{3,2,1,0:T(4,128)S(1)} %bitcast.29), channel_id=1, source_target_pairs={{0,1},{1,0},{2,3},{3,2},{4,5},{5,4},{6,7},{7,6},{8,9},{9,8},{10,11... | collective-permute-start | bytes 393224 | tf_op jit(solution)/shard_map/ppermute | solution.py:61
  26.5 7.4 %collective-permute-start.5 = (bf16[4,64,512]{2,1,0:T(8,128)(2,1)S(1)}, bf16[4,64,512]{2,1,0:T(8,128)(2,1)S(1)}, u32[]{:S(2)}, u32[]{:S(2)}) collective-permute-start(bf16[4,64,512]{2,1,0:T(8,128)(2,1)S(1)} %pad_maximum_fusion.3), channel_id=1, source_target_pairs={{0,4},{1,9},{2,6},{3,11},{4,0},{5,13},{6,2},{7,15},{8,12},{9,1},{1... | collective-permute-start | bytes 786440 | tf_op jit(solution)/shard_map/ppermute | solution.py:79
  27.5 0.7 copy-start.1
  34.0 9.2 %collective-permute-start.6 = (bf16[8,64,512]{2,1,0:T(8,128)(2,1)S(1)}, bf16[8,64,512]{2,1,0:T(8,128)(2,1)S(1)}, u32[]{:S(2)}, u32[]{:S(2)}) collective-permute-start(bf16[8,64,512]{2,1,0:T(8,128)(2,1)S(1)} %pad_maximum_fusion.near_ref), channel_id=1, source_target_pairs={{0,2},{1,5},{2,0},{3,7},{4,6},{5,1},{6,4},{7,3},{8,10},{9,13},{10,... | collective-permute-start | bytes 1572872 | tf_op jit(solution)/shard_map/ppermute | solution.py:79
  35.2 8.1 %slice-start = ((s8[8650752]{0:T(1024)(128)(4,1)}), s8[4194304]{0:T(1024)(128)(4,1)S(1)}, s32[]{:S(2)}) async-start(s8[8650752]{0:T(1024)(128)(4,1)} %bitcast.38), calls=%async_computation.1 | async-start | bytes 8388608
  35.2 8.1 %slice-start.1 = ((s8[8650752]{0:T(1024)(128)(4,1)}), s8[4194304]{0:T(1024)(128)(4,1)S(1)}, s32[]{:S(2)}) async-start(s8[8650752]{0:T(1024)(128)(4,1)} %bitcast.38), calls=%async_computation.2 | async-start | bytes 8388608
  35.2 8.1 %slice-start.2 = ((s8[8650752]{0:T(1024)(128)(4,1)}), s8[262144]{0:T(1024)(128)(4,1)S(1)}, s32[]{:S(2)}) async-start(s8[8650752]{0:T(1024)(128)(4,1)} %bitcast.38), calls=%async_computation.3 | async-start | bytes 524288
  35.2 8.1 %collective-permute-start.9 = (bf16[1,8,64,512]{3,2,1,0:T(8,128)(2,1)S(1)}, bf16[1,8,64,512]{3,2,1,0:T(8,128)(2,1)S(1)}, u32[]{:S(2)}, u32[]{:S(2)}) collective-permute-start(bf16[1,8,64,512]{3,2,1,0:T(8,128)(2,1)S(1)} %bitcast.26), channel_id=1, source_target_pairs={{0,1},{1,0},{2,3},{3,2},{4,5},{5,4},{6,7},{7,6},{8,9},{9,8},{10,11... | collective-permute-start | bytes 1572872 | tf_op jit(solution)/shard_map/ppermute | solution.py:61
  43.3 2.8 %collective-permute-start.8 = (bf16[1,8,64,512]{3,2,1,0:T(8,128)(2,1)S(1)}, bf16[1,8,64,512]{3,2,1,0:T(8,128)(2,1)S(1)}, u32[]{:S(2)}, u32[]{:S(2)}) collective-permute-start(bf16[1,8,64,512]{3,2,1,0:T(8,128)(2,1)S(1)} %bitcast.30), channel_id=1, source_target_pairs={{0,1},{1,0},{2,3},{3,2},{4,5},{5,4},{6,7},{7,6},{8,9},{9,8},{10,11... | collective-permute-start | bytes 1572872 | tf_op jit(solution)/shard_map/ppermute | solution.py:61
  48.2 6.0 %collective-permute-start.10 = (bf16[1,64,512]{2,1,0:T(8,128)(2,1)S(1)}, bf16[1,64,512]{2,1,0:T(8,128)(2,1)S(1)}, u32[]{:S(2)}, u32[]{:S(2)}) collective-permute-start(bf16[1,64,512]{2,1,0:T(8,128)(2,1)S(1)} %bitcast.22), channel_id=1, source_target_pairs={{0,16},{1,17},{2,18},{3,19},{4,20},{5,21},{6,22},{7,23},{8,24},{9,... | collective-permute-start | bytes 196616 | tf_op jit(solution)/shard_map/ppermute | solution.py:79
  54.3 5.3 %collective-permute-start.11 = (bf16[2,64,512]{2,1,0:T(8,128)(2,1)S(1)}, bf16[2,64,512]{2,1,0:T(8,128)(2,1)S(1)}, u32[]{:S(2)}, u32[]{:S(2)}) collective-permute-start(bf16[2,64,512]{2,1,0:T(8,128)(2,1)S(1)} %pad_maximum_fusion.6), channel_id=1, source_target_pairs={{0,8},{1,3},{2,10},{3,1},{4,12},{5,7},{6,14},{7,5},{8,0},{9,11},{1... | collective-permute-start | bytes 393224 | tf_op jit(solution)/shard_map/ppermute | solution.py:79
  59.6 6.7 %collective-permute-start.12 = (bf16[4,64,512]{2,1,0:T(8,128)(2,1)S(1)}, bf16[4,64,512]{2,1,0:T(8,128)(2,1)S(1)}, u32[]{:S(2)}, u32[]{:S(2)}) collective-permute-start(bf16[4,64,512]{2,1,0:T(8,128)(2,1)S(1)} %pad_maximum_fusion.4), channel_id=1, source_target_pairs={{0,4},{1,9},{2,6},{3,11},{4,0},{5,13},{6,2},{7,15},{8,12},{9,1},{1... | collective-permute-start | bytes 786440 | tf_op jit(solution)/shard_map/ppermute | solution.py:79
  66.4 2.0 %collective-permute-start.14 = (bf16[1,8,64,512]{3,2,1,0:T(8,128)(2,1)S(1)}, bf16[1,8,64,512]{3,2,1,0:T(8,128)(2,1)S(1)}, u32[]{:S(2)}, u32[]{:S(2)}) collective-permute-start(bf16[1,8,64,512]{3,2,1,0:T(8,128)(2,1)S(1)} %get-tuple-element.50), channel_id=1, source_target_pairs={{0,1},{1,0},{2,3},{3,2},{4,5},{5,4},{6,7},{7,6},{8,9},{9,8},{10,11... | collective-permute-start | bytes 1572872 | tf_op jit(solution)/shard_map/ppermute | solution.py:61
  66.5 9.2 %collective-permute-start.13 = (bf16[8,64,512]{2,1,0:T(8,128)(2,1)S(1)}, bf16[8,64,512]{2,1,0:T(8,128)(2,1)S(1)}, u32[]{:S(2)}, u32[]{:S(2)}) collective-permute-start(bf16[8,64,512]{2,1,0:T(8,128)(2,1)S(1)} %get-tuple-element.51.near_ref), channel_id=1, source_target_pairs={{0,2},{1,5},{2,0},{3,7},{4,6},{5,1},{6,4},{7,3},{8,10},{9,13},{10,... | collective-permute-start | bytes 1572872 | tf_op jit(solution)/shard_map/ppermute | solution.py:79
  71.1 30.0 %copy-start = (f32[64,512]{1,0:T(8,128)S(1)}, f32[64,512]{1,0:T(8,128)}, u32[]{:S(2)}) copy-start(f32[64,512]{1,0:T(8,128)} %start_ref.1) | copy-start | bytes 393220
  75.7 1.9 %collective-permute-start.15 = (bf16[1,8,64,512]{3,2,1,0:T(8,128)(2,1)S(1)}, bf16[1,8,64,512]{3,2,1,0:T(8,128)(2,1)S(1)}, u32[]{:S(2)}, u32[]{:S(2)}) collective-permute-start(bf16[1,8,64,512]{3,2,1,0:T(8,128)(2,1)S(1)} %bitcast.31), channel_id=1, source_target_pairs={{0,1},{1,0},{2,3},{3,2},{4,5},{5,4},{6,7},{7,6},{8,9},{9,8},{10,11... | collective-permute-start | bytes 1572872 | tf_op jit(solution)/shard_map/ppermute | solution.py:61
  80.5 19.1 %collective-permute-start.21 = (f32[1,128,512]{2,1,0:T(8,128)S(1)}, f32[1,128,512]{2,1,0:T(8,128)S(1)}, u32[]{:S(2)}, u32[]{:S(2)}) collective-permute-start(f32[1,128,512]{2,1,0:T(8,128)S(1)} %bitcast.40), channel_id=1, source_target_pairs={{0,1},{1,0},{2,3},{3,2},{4,5},{5,4},{6,7},{7,6},{8,9},{9,8},{10,11... | collective-permute-start | bytes 786440 | tf_op jit(solution)/shard_map/ppermute | solution.py:61
  80.7 1.4 %collective-permute-start.16 = (f32[72,128]{1,0:T(8,128)S(1)}, f32[72,128]{1,0:T(8,128)S(1)}, u32[]{:S(2)}, u32[]{:S(2)}) collective-permute-start(f32[72,128]{1,0:T(8,128)S(1)} %get-tuple-element.47), channel_id=1, source_target_pairs={{0,1},{1,0},{2,3},{3,2},{4,5},{5,4},{6,7},{7,6},{8,9},{9,8},{10,11... | collective-permute-start | bytes 110600 | tf_op jit(solution)/shard_map/ppermute | solution.py:61
  82.2 4.9 %collective-permute-start.17 = (f32[72,128]{1,0:T(8,128)S(1)}, f32[72,128]{1,0:T(8,128)S(1)}, u32[]{:S(2)}, u32[]{:S(2)}) collective-permute-start(f32[72,128]{1,0:T(8,128)S(1)} %add.36), channel_id=1, source_target_pairs={{0,16},{1,5},{2,18},{3,7},{4,20},{5,1},{6,22},{7,3},{8,24},{9,13},... | collective-permute-start | bytes 110600 | tf_op jit(solution)/shard_map/ppermute | solution.py:79
  87.0 4.4 %collective-permute-start.18 = (f32[72,128]{1,0:T(8,128)S(1)}, f32[72,128]{1,0:T(8,128)S(1)}, u32[]{:S(2)}, u32[]{:S(2)}) collective-permute-start(f32[72,128]{1,0:T(8,128)S(1)} %add.37), channel_id=1, source_target_pairs={{0,8},{1,3},{2,10},{3,1},{4,12},{5,7},{6,14},{7,5},{8,0},{9,11},{1... | collective-permute-start | bytes 110600 | tf_op jit(solution)/shard_map/ppermute | solution.py:79
  91.5 4.2 %collective-permute-start.19 = (f32[72,128]{1,0:T(8,128)S(1)}, f32[72,128]{1,0:T(8,128)S(1)}, u32[]{:S(2)}, u32[]{:S(2)}) collective-permute-start(f32[72,128]{1,0:T(8,128)S(1)} %add.38), channel_id=1, source_target_pairs={{0,4},{1,17},{2,6},{3,19},{4,0},{5,21},{6,2},{7,23},{8,12},{9,25},... | collective-permute-start | bytes 110600 | tf_op jit(solution)/shard_map/ppermute | solution.py:79
  95.7 4.0 %collective-permute-start.20 = (f32[72,128]{1,0:T(8,128)S(1)}, f32[72,128]{1,0:T(8,128)S(1)}, u32[]{:S(2)}, u32[]{:S(2)}) collective-permute-start(f32[72,128]{1,0:T(8,128)S(1)} %add.39), channel_id=1, source_target_pairs={{0,2},{1,9},{2,0},{3,11},{4,6},{5,13},{6,4},{7,15},{8,10},{9,1},{1... | collective-permute-start | bytes 110600 | tf_op jit(solution)/shard_map/ppermute | solution.py:79

commit v9 on v8

--- a/solution.py
+++ b/solution.py
@@ -13,7 +13,6 @@
 ROWS = 64
 PAIR = 2
 BATCH = 2 * PAIR
-RING = 8
 UNROLL = 4
 VMEM = 16 * 1024 * 1024
 HIGHEST = lax.Precision.HIGHEST
@@ -206,17 +205,28 @@
     fill_order(first_ref[0], rank, order_ref, 0, local)
     for copy in copies[5:]:
         copy.wait()
-    blocks = [blocks_ref[i] for i in range(2 * half)]
-    everything = jnp.concatenate([jnp.concatenate(blocks, axis=1), places, jnp.zeros((4, n), jnp.float32)], axis=0)
-    whole = add_parts(dot_nt(stacked_parts(everything), order_ref[...]))
-    block_out[...] = whole[:columns]
-    own_out[...] = whole[columns:]
-    rounded_out[...] = whole[:columns].astype(jnp.bfloat16)
+    block = jnp.concatenate([blocks_ref[i] for i in range(2 * half)], axis=1)
+    everything = jnp.concatenate(
+        [
+            *[part.astype(jnp.float32) for part in three_parts(block)[:2]],
+            *[part.astype(jnp.float32) for part in three_parts(places)],
+            jnp.zeros((4, n), jnp.float32),
+        ],
+        axis=0,
+    ).astype(jnp.bfloat16)
+    parts = dot_nt(everything, order_ref[...])
+    high, low = parts[:columns], parts[columns : 2 * columns]
+    rounded_out[...] = high.astype(jnp.bfloat16)
+    block_out[...] = high + low
+    whole = (parts[2 * columns + 8 : 2 * columns + 12] + parts[2 * columns + 4 : 2 * columns + 8]) + parts[
+        2 * columns : 2 * columns + 4
+    ]
     lane = lax.broadcasted_iota(jnp.int32, (1, local), 1)
     flags = jnp.zeros((1, local), jnp.float32)
     for offset in range(owner_ref.shape[1]):
         flags = jnp.where((lane == offset) & (owned_ref[0, offset] >= 0), 1.0, flags)
-    places_out[...] = jnp.concatenate([whole[columns : columns + 3], flags], axis=0)
+    own_out[...] = jnp.concatenate([whole, flags, jnp.zeros((3, local), jnp.float32)], axis=0)
+    places_out[...] = jnp.concatenate([whole[:3], flags], axis=0)
 
 
 def sort_region(first, tile_owner, near, far, near_error, far_error, block, other):
@@ -278,10 +288,9 @@
 
 
 def plan_blocks(
-    distance_ref, listed_ref, own_ref, far_ref, chunks, stage_ref, bounds_ref, ids_ref, count_ref, sem, prepare,
+    distance_ref, own_ref, far_ref, chunks, stage_ref, bounds_ref, ids_ref, count_ref, sem, prepare,
 ):
     places, local = far_ref.shape[0], own_ref.shape[1]
-    reach = listed_ref.shape[1]
     blocks = local // ROWS
     lane = lax.broadcasted_iota(jnp.int32, (1, LANES), 1)
 
@@ -303,9 +312,7 @@
         beyond = beyond + (low <= highest).astype(jnp.int32)
     distance = distance_ref[...]
     flags = jnp.where((lane == -distance) & (far_ref[:, 3, :LANES] > 0.0), 1.0, 0.0)
-    for offset in range(reach):
-        mine = jnp.where(listed_ref[0, offset] >= 0, 1.0, 0.0)
-        flags = flags + jnp.where((lane == offset) & (distance == offset), mine, 0.0)
+    flags = flags + jnp.where(lane == distance, own_ref[4:5, :LANES], 0.0)
     listed = jnp.sum(flags, axis=1, keepdims=True) > 0.0
     found = jnp.where(listed, jnp.maximum(beyond - first, 0), 0)
     stage_ref[...] = jnp.where(lane < blocks, first, found)
@@ -352,9 +359,9 @@
 
 
 def build_kernel(
-    kept, place_ref, distance_ref, listed_ref, own_ref, near_ref, other_ref,
+    place_ref, distance_ref, own_ref, near_ref, other_ref,
     ids_ref, count_ref, tiles_ref,
-    wide_ref, far_ref, stage_ref, bounds_ref, bounds_sem, *through,
+    wide_ref, far_ref, stage_ref, bounds_ref, bounds_sem,
 ):
     local = own_ref.shape[1]
     places = far_ref.shape[0]
@@ -371,24 +378,12 @@
             wide_ref[row] = jnp.broadcast_to(scale * column[:, row : row + 1], (local, LANES))
 
     plan_blocks(
-        distance_ref, listed_ref, own_ref, far_ref, 1 << chunk_bits,
+        distance_ref, own_ref, far_ref, 1 << chunk_bits,
         stage_ref, bounds_ref, ids_ref, count_ref, bounds_sem, prepare,
     )
     total = count_ref[0]
-    held_ref, sems = (tiles_ref, None) if kept else through
-
-    def copy_out(batch):
-        return pltpu.make_async_copy(
-            held_ref.at[batch], tiles_ref.at[batch], sems.at[lax.rem(batch, RING)]
-        )
 
     def build_batch(batch, carry):
-        if not kept:
-
-            @pl.when(batch >= RING)
-            def _():
-                copy_out(batch - RING).wait()
-
         for part in range(BATCH):
             real, place, lanes, rows = locate(ids_ref, batch, part, chunk_bits)
             far = far_ref[place, :, lanes]
@@ -397,22 +392,13 @@
             value = gaspari_cohn(across_x * across_x + across_y * across_y)
             spread = jnp.where(real, far[2:3, :], 0.0)
             value = wide_ref[2, rows, :] * spread * value
-            held_ref[batch, :, part * LANES : (part + 1) * LANES] = value.astype(jnp.bfloat16)
-        if not kept:
-            copy_out(batch).start()
+            tiles_ref[batch, :, part * LANES : (part + 1) * LANES] = value.astype(jnp.bfloat16)
         return carry
 
     lax.fori_loop(0, total, build_batch, 0)
-    if not kept:
-
-        def finish(batch, carry):
-            copy_out(batch).wait()
-            return carry
-
-        lax.fori_loop(jnp.maximum(total - RING, 0), total, finish, 0)
-
-
-def build_tiles(place, distance, tile_owner, own, near, far, capacity, kept):
+
+
+def build_tiles(place, distance, own, near, far, capacity):
     near, far = [piece.reshape((-1,) + piece.shape[2:]) for piece in (near, far)]
     places, local = place.shape[0], own.shape[1]
     smem = pl.BlockSpec(memory_space=pltpu.SMEM)
@@ -425,21 +411,19 @@
         pltpu.SMEM((places, LANES), jnp.int32),
         pltpu.SemaphoreType.DMA,
     ]
-    if not kept:
-        scratch += [pltpu.VMEM(shape, jnp.bfloat16), pltpu.SemaphoreType.DMA((RING,))]
     return pl.pallas_call(
-        functools.partial(build_kernel, kept),
+        build_kernel,
         out_shape=tuple(jax.ShapeDtypeStruct((size,), jnp.int32) for size in sizes)
-        + ((pltpu.VMEM if kept else pltpu.HBM)(shape, jnp.bfloat16),),
-        in_specs=[smem] + whole_vmem(1) + [smem] + whole_vmem(3),
-        out_specs=(smem,) * 2 + (pl.BlockSpec(memory_space=pltpu.VMEM if kept else pltpu.HBM),),
+        + (pltpu.VMEM(shape, jnp.bfloat16),),
+        in_specs=[smem] + whole_vmem(4),
+        out_specs=(smem,) * 2 + (pl.BlockSpec(memory_space=pltpu.VMEM),),
         scratch_shapes=scratch,
         compiler_params=pltpu.CompilerParams(vmem_limit_bytes=VMEM),
         cost_estimate=pl.CostEstimate(
             flops=2 * local * local * 16000, bytes_accessed=16 * local * local, transcendentals=0
         ),
-        name="build_kept" if kept else "build_passed",
-    )(place, distance, tile_owner, own, near, far)
+        name="build_tiles",
+    )(place, distance, own, near, far)
 
 
 def apply_kernel(started, last, grams, ids_ref, count_ref, near_ref, other_ref, tiles_ref, *refs):
@@ -448,45 +432,20 @@
     if last:
         first_ref = refs.pop(2) if grams else None
         block_ref, scale_ref, out_ref, rounded_ref = refs[:4]
-        all_ref, piece_sems, total_ref = refs[-3:]
-        held_ref = tiles_ref
+        total_ref = refs[-1]
     else:
-        total_ref, all_ref, piece_sems, held_ref, sems = refs
+        (total_ref,) = refs
     half, columns, local = near_ref.shape
     chunk_bits = (local // LANES).bit_length() - 1
     total = count_ref[0]
     groups = lax.div(total + UNROLL - 1, UNROLL)
 
-    copies = [
-        pltpu.make_async_copy(ref, all_ref.at[pl.ds(part * half, half)], piece_sems.at[part])
-        for part, ref in enumerate((near_ref, other_ref))
-    ]
-    for copy in copies:
-        copy.start()
-
-    def copy_in(group):
-        first = group * UNROLL
-        return pltpu.make_async_copy(
-            tiles_ref.at[pl.ds(first, UNROLL)], held_ref.at[pl.ds(first, UNROLL)], sems.at[group]
-        )
-
-    if not last:
-
-        def start_copy(group, carry):
-            copy_in(group).start()
-            return carry
-
-        lax.fori_loop(0, groups, start_copy, 0)
     if started:
         total_ref[...] = start_ref[...]
     else:
         total_ref[...] = jnp.zeros(total_ref.shape, jnp.float32)
-    for copy in copies:
-        copy.wait()
 
     def turn(group, carry):
-        if not last:
-            copy_in(group).wait()
         values = []
         for inner in range(UNROLL):
             batch = jnp.minimum(group * UNROLL + inner, total - 1)
@@ -495,12 +454,15 @@
                 sides = []
                 for part in range(pair * PAIR, (pair + 1) * PAIR):
                     _, place, chunk, rows = locate(ids_ref, batch, part, chunk_bits)
-                    sides.append(all_ref[place, :, chunk])
+                    inside = jnp.where(place < half, place, place - half)
+                    sides.append(
+                        jnp.where(place < half, near_ref[inside, :, chunk], other_ref[inside, :, chunk])
+                    )
                 side = jnp.concatenate(sides, axis=1)
                 if inner:
                     side = jnp.where(valid, side, jnp.zeros_like(side))
                 lanes = slice(pair * PAIR * LANES, (pair + 1) * PAIR * LANES)
-                values.append((rows, dot_nt(held_ref[batch, :, lanes], side)))
+                values.append((rows, dot_nt(tiles_ref[batch, :, lanes], side)))
         for rows, value in values:
             total_ref[rows, :] += value
         return carry
@@ -521,17 +483,12 @@
     last = finish is not None
     grams = last and len(finish) > 2
     smem = pl.BlockSpec(memory_space=pltpu.SMEM)
-    anywhere = pl.BlockSpec(memory_space=pl.ANY)
     operands = [*plan, near, far, tiles]
-    in_specs = [smem] * 2 + [anywhere] * 2
-    in_specs.append(pl.BlockSpec(memory_space=pltpu.VMEM if last else pltpu.HBM))
+    in_specs = [smem] * 2 + whole_vmem(3)
     if start is not None:
         operands.append(start)
         in_specs += whole_vmem(1)
-    scratch = [
-        pltpu.VMEM((2 * half, columns, local), jnp.bfloat16),
-        pltpu.SemaphoreType.DMA((2,)),
-    ]
+    scratch = []
     if last:
         operands += finish
         in_specs += whole_vmem(len(finish))
@@ -544,8 +501,6 @@
         scratch.append(pltpu.VMEM((local, columns), jnp.float32))
     else:
         out_shape = (jax.ShapeDtypeStruct((local, columns), jnp.float32),)
-        scratch.append(pltpu.VMEM(tiles.shape, jnp.bfloat16))
-        scratch.append(pltpu.SemaphoreType.DMA((tiles.shape[0] // UNROLL,)))
     return pl.pallas_call(
         functools.partial(apply_kernel, start is not None, last, grams),
         out_shape=out_shape,
@@ -706,8 +661,8 @@
     for part in range(2):
         inside = slot_region[:, part * half_regions : (part + 1) * half_regions]
         *plan, built = build_tiles(
-            (stack[:, None] + inside).reshape(-1), (inside - here).reshape(-1, 1), tile_owner, own,
-            near_places, far_places, capacity, part == 1,
+            (stack[:, None] + inside).reshape(-1), (inside - here).reshape(-1, 1), own,
+            near_places, far_places, capacity,
         )
         plans.append(plan)
         tiles.append(built)

time: 108 us -> 107 us (level); the launches traced: 109 us -> 106 us
  starting transfers between devices: 33 us -> 21.1 us
  waiting for transfers between devices: 37.5 us -> 49.2 us
  Pallas kernels: 34.4 us -> 32.7 us
    ppermute x12, waiting for transfers between devices: 27 us -> 38.2 us  [swap_regions(): return lax.ppermute(block, ('region', 'tile'), route)]
    ppermute x12, starting transfers between devices: 24.3 us -> 14.6 us  [swap_regions(): return lax.ppermute(block, ('region', 'tile'), route)]
    all_to_all x1, starting transfers between devices: 6.98 us -> 4.84 us  [shards(): everywhere = lax.all_to_all(everywhere, 'region', 0, 0)]
  transfers between devices with their start and end apart: 23 -> 23, of which waited for: 15 -> 16; matrix products, arithmetic and copies ran while one was open for 2% -> 2% of each run, Pallas kernels for 15% -> 14%
where the time goes in v9:
time: 107 us; the launch traced here: 106 us
  waiting for transfers between devices  49.2 us (46%)
  Pallas kernels  32.7 us (31%)
  starting transfers between devices  21.1 us (20%)
  other arithmetic  1.13 us (1%)
    ppermute x12, waiting for transfers between devices, swap_regions(): return lax.ppermute(block, ('region', 'tile'), route)  38.2 us
    ppermute x12, starting transfers between devices, swap_regions(): return lax.ppermute(block, ('region', 'tile'), route)  14.6 us
    pallas_call x2, Pallas kernels, build_tiles(): pl.pallas_call(build_kernel, out_shape=tuple((jax.ShapeDtypeStruct((size,...  9.73 us
    pallas_call x4, Pallas kernels, apply_tiles(): pl.pallas_call(functools.partial(apply_kernel, start is not None, last, g...  9.47 us
    pallas_call x1, Pallas kernels, last_step(): pl.pallas_call(last_kernel, out_shape=(jax.ShapeDtypeStruct(start.shape,...  7.52 us
    ppermute x10, waiting for transfers between devices, swapped(): lax.ppermute(block, axis, [(i, i ^ bit) for i in range(lax.axis_size(axis...  5.91 us
    all_to_all x1, waiting for transfers between devices, shards(): everywhere = lax.all_to_all(everywhere, 'region', 0, 0)  5.05 us
    all_to_all x1, starting transfers between devices, shards(): everywhere = lax.all_to_all(everywhere, 'region', 0, 0)  4.84 us
  transfers between devices with their start and end apart: 23, of which 16 were waited for; matrix products, arithmetic and copies ran while one was open for 2% of the time, Pallas kernels for 14%

profile of v9, /device:TPU:0, one launch (start us, length us, event | category | flops | bytes accessed | tf_op | source)
XLA Modules:
  0.0 106.0 jit_solution(14092176703075696803)
XLA Ops:
  0.6 0.5 collective-permute-start.2
  1.1 0.1 collective-permute-start
  1.2 0.4 collective-permute-start.1
  1.7 1.0 collective-permute-done.1.far_error_ref
  2.7 0.0 collective-permute-done.far_ref
  2.7 0.0 collective-permute-done.2.other_ref
  2.7 3.9 %sort_region.1 = (bf16[64,512]{1,0:T(8,128)(2,1)S(1)}, f32[4,512]{1,0:T(4,128)S(1)}, f32[8,512]{1,0:T(8,128)S(1)}, f32[64,512]{1,0:T(8,128)S(1)}, s32[1,512]{1,0:T(1,128)S(1)}) custom-call(s32[2]{0:T(128)S(1)} %fusion.2.first_ref, s32[1,7]{1,0:T(1,128)} %owner_ref.1, f32[1,3,512]{2,1,0:T(4,128)} %bitcast.41, f32[1,3,512]{2,1,0:T(4,128)S(1)} %collective-permute-done.far_ref, ...), custom_call_target="tpu_custom_call" | custom-call | flops 226492416 | bytes 2097152 | tf_op jit(solution)/shard_map/sort_region/pallas_call | solution.py:237
  6.7 4.0 %collective-permute-start.3 = (bf16[1,64,512]{2,1,0:T(8,128)(2,1)S(1)}, bf16[1,64,512]{2,1,0:T(8,128)(2,1)S(1)}, u32[]{:S(2)}, u32[]{:S(2)}) collective-permute-start(bf16[1,64,512]{2,1,0:T(8,128)(2,1)S(1)} %bitcast.18), channel_id=1, source_target_pairs={{0,16},{1,17},{2,18},{3,19},{4,20},{5,21},{6,22},{7,23},{8,24},{9,... | collective-permute-start | bytes 196616 | tf_op jit(solution)/shard_map/ppermute | solution.py:78
  10.6 0.7 broadcast_in_dim.61
  11.3 4.8 %all-to-all-start = ((f32[16,4,512]{2,1,0:T(4,128)}), f32[16,4,512]{2,1,0:T(4,128)S(1)}, u32[]{:S(2)}, u32[]{:S(2)}) async-start(f32[16,4,512]{2,1,0:T(4,128)} %broadcast_in_dim.61), calls=%async_computation | async-start | bytes 262144 | tf_op jit(solution)/shard_map/all_to_all | solution.py:652
  16.2 0.7 select_xor_fusion
  16.9 0.0 collective-permute-done.3
  16.9 2.0 %collective-permute-start.4 = (bf16[2,64,512]{2,1,0:T(8,128)(2,1)S(1)}, bf16[2,64,512]{2,1,0:T(8,128)(2,1)S(1)}, u32[]{:S(2)}, u32[]{:S(2)}) collective-permute-start(bf16[2,64,512]{2,1,0:T(8,128)(2,1)S(1)} %pad_maximum_fusion.5), channel_id=1, source_target_pairs={{0,8},{1,3},{2,10},{3,1},{4,12},{5,7},{6,14},{7,5},{8,0},{9,11},{1... | collective-permute-start | bytes 393224 | tf_op jit(solution)/shard_map/ppermute | solution.py:78
  18.9 5.0 %all-to-all-done.near_ref = f32[16,4,512]{2,1,0:T(4,128)S(1)} async-done(((f32[16,4,512]{2,1,0:T(4,128)}), f32[16,4,512]{2,1,0:T(4,128)S(1)}, u32[]{:S(2)}, u32[]{:S(2)}) %all-to-all-start) | async-done | bytes 131104 | tf_op jit(solution)/shard_map/all_to_all | solution.py:652
  24.0 0.0 collective-permute-start.7
  24.0 0.1 broadcast_subtract_fusion
  24.0 0.1 reshape.59.distance_ref
  24.1 0.1 reshape.53.place_ref
  24.2 0.1 reshape.58.distance_ref
  24.3 0.1 reshape.49.place_ref
  24.4 0.0 collective-permute-done.4
  24.4 0.8 collective-permute-start.5
  25.2 0.1 collective-permute-done.7
  25.3 5.1 %build_tiles.3 = (s32[532]{0:T(1024)S(1)}, s32[1]{0:T(128)}, bf16[132,64,512]{2,1,0:T(8,128)(2,1)S(1)}) custom-call(s32[16]{0:T(128)S(1)} %reshape.53.place_ref, s32[16,1]{1,0:T(8,128)S(1)} %reshape.59.distance_ref, f32[8,512]{1,0:T(8,128)S(1)} %get-tuple-element.27.own_ref, f32[16,4,512]{2,1,0:T(4,128)S(1)} %all-to-all-done.near_ref, f32[16,4,512]{2,1,0:T(4,128)S(1)} %bitcast.36), custom_call_target="tpu_custom_call" | custom-call | flops 8388608000 | bytes 4194304 | tf_op jit(solution)/shard_map/build_tiles/pallas_call | solution.py:414
  30.4 0.4 collective-permute-done.5
  30.8 0.1 pad_maximum_fusion.near_ref
  30.9 1.2 %collective-permute-start.6 = (bf16[8,64,512]{2,1,0:T(8,128)(2,1)S(1)}, bf16[8,64,512]{2,1,0:T(8,128)(2,1)S(1)}, u32[]{:S(2)}, u32[]{:S(2)}) collective-permute-start(bf16[8,64,512]{2,1,0:T(8,128)(2,1)S(1)} %pad_maximum_fusion.near_ref), channel_id=1, source_target_pairs={{0,2},{1,5},{2,0},{3,7},{4,6},{5,1},{6,4},{7,3},{8,10},{9,13},{10,... | collective-permute-start | bytes 1572872 | tf_op jit(solution)/shard_map/ppermute | solution.py:78
  32.1 0.0 collective-permute-start.9
  32.1 4.7 %build_tiles.2 = (s32[532]{0:T(1024)S(1)}, s32[1]{0:T(128)}, bf16[132,64,512]{2,1,0:T(8,128)(2,1)S(1)}) custom-call(s32[16]{0:T(128)S(1)} %reshape.49.place_ref, s32[16,1]{1,0:T(8,128)S(1)} %reshape.58.distance_ref, f32[8,512]{1,0:T(8,128)S(1)} %get-tuple-element.27.own_ref, f32[16,4,512]{2,1,0:T(4,128)S(1)} %all-to-all-done.near_ref, f32[16,4,512]{2,1,0:T(4,128)S(1)} %bitcast.37), custom_call_target="tpu_custom_call" | custom-call | flops 8388608000 | bytes 4194304 | tf_op jit(solution)/shard_map/build_tiles/pallas_call | solution.py:414
  36.7 3.4 %collective-permute-done.6.near_ref = bf16[8,64,512]{2,1,0:T(8,128)(2,1)S(1)} collective-permute-done((bf16[8,64,512]{2,1,0:T(8,128)(2,1)S(1)}, bf16[8,64,512]{2,1,0:T(8,128)(2,1)S(1)}, u32[]{:S(2)}, u32[]{:S(2)}) %collective-permute-start.6) | collective-permute-done | bytes 524320 | tf_op jit(solution)/shard_map/ppermute | solution.py:78
  40.1 0.0 collective-permute-start.8
  40.2 0.0 collective-permute-done.9
  40.2 2.2 %apply_first.2.refs_0_ = f32[512,64]{1,0:T(8,128)S(1)} custom-call(s32[532]{0:T(1024)S(1)} %get-tuple-element.37.ids_ref, s32[1]{0:T(128)} %get-tuple-element.38.count_ref, bf16[8,64,512]{2,1,0:T(8,128)(2,1)S(1)} %pad_maximum_fusion.near_ref, bf16[8,64,512]{2,1,0:T(8,128)(2,1)S(1)} %bitcast.32, bf16[132,64,512]{2,1,0:T(8,128)(2,1)S(1)} %get-tuple-element.40.tiles_ref), custom_call_target="tpu_custom_call" | custom-call | flops 3145728000 | bytes 4194304 | tf_op jit(solution)/shard_map/apply_first/pallas_call | solution.py:504
  42.4 0.0 collective-permute-done.8
  42.4 2.1 %apply_last.2 = (f32[64,512]{1,0:T(8,128)S(1)}, bf16[64,512]{1,0:T(8,128)(2,1)S(1)}) custom-call(s32[532]{0:T(1024)S(1)} %get-tuple-element.31.ids_ref, s32[1]{0:T(128)} %get-tuple-element.32.count_ref, bf16[8,64,512]{2,1,0:T(8,128)(2,1)S(1)} %collective-permute-done.6.near_ref, bf16[8,64,512]{2,1,0:T(8,128)(2,1)S(1)} %bitcast.33, ...), custom_call_target="tpu_custom_call" | custom-call | flops 3145728000 | bytes 4194304 | tf_op jit(solution)/shard_map/apply_last/pallas_call | solution.py:504
  44.6 3.8 %collective-permute-start.10 = (bf16[1,64,512]{2,1,0:T(8,128)(2,1)S(1)}, bf16[1,64,512]{2,1,0:T(8,128)(2,1)S(1)}, u32[]{:S(2)}, u32[]{:S(2)}) collective-permute-start(bf16[1,64,512]{2,1,0:T(8,128)(2,1)S(1)} %bitcast.22), channel_id=1, source_target_pairs={{0,16},{1,17},{2,18},{3,19},{4,20},{5,21},{6,22},{7,23},{8,24},{9,... | collective-permute-start | bytes 196616 | tf_op jit(solution)/shard_map/ppermute | solution.py:78
  48.4 0.7 first_grams.1.refs_3_
  49.0 3.5 %collective-permute-done.10 = bf16[1,64,512]{2,1,0:T(8,128)(2,1)S(1)} collective-permute-done((bf16[1,64,512]{2,1,0:T(8,128)(2,1)S(1)}, bf16[1,64,512]{2,1,0:T(8,128)(2,1)S(1)}, u32[]{:S(2)}, u32[]{:S(2)}) %collective-permute-start.10) | collective-permute-done | bytes 65568 | tf_op jit(solution)/shard_map/ppermute | solution.py:78
  52.5 0.3 collective-permute-start.11
  52.8 4.7 %collective-permute-done.11 = bf16[2,64,512]{2,1,0:T(8,128)(2,1)S(1)} collective-permute-done((bf16[2,64,512]{2,1,0:T(8,128)(2,1)S(1)}, bf16[2,64,512]{2,1,0:T(8,128)(2,1)S(1)}, u32[]{:S(2)}, u32[]{:S(2)}) %collective-permute-start.11) | collective-permute-done | bytes 131104 | tf_op jit(solution)/shard_map/ppermute | solution.py:78
  57.6 0.1 collective-permute-start.12
  57.7 6.4 %collective-permute-done.12 = bf16[4,64,512]{2,1,0:T(8,128)(2,1)S(1)} collective-permute-done((bf16[4,64,512]{2,1,0:T(8,128)(2,1)S(1)}, bf16[4,64,512]{2,1,0:T(8,128)(2,1)S(1)}, u32[]{:S(2)}, u32[]{:S(2)}) %collective-permute-start.12) | collective-permute-done | bytes 262176 | tf_op jit(solution)/shard_map/ppermute | solution.py:78
  64.0 0.1 fusion.3
  64.1 0.1 collective-permute-start.14
  64.2 0.1 collective-permute-start.13
  64.3 1.8 %collective-permute-done.14 = bf16[1,8,64,512]{3,2,1,0:T(8,128)(2,1)S(1)} collective-permute-done((bf16[1,8,64,512]{3,2,1,0:T(8,128)(2,1)S(1)}, bf16[1,8,64,512]{3,2,1,0:T(8,128)(2,1)S(1)}, u32[]{:S(2)}, u32[]{:S(2)}) %collective-permute-start.14) | collective-permute-done | bytes 524320 | tf_op jit(solution)/shard_map/ppermute | solution.py:60
  66.1 2.3 %apply_first.3.refs_0_ = f32[512,64]{1,0:T(8,128)S(1)} custom-call(s32[532]{0:T(1024)S(1)} %get-tuple-element.37.ids_ref, s32[1]{0:T(128)} %get-tuple-element.38.count_ref, bf16[8,64,512]{2,1,0:T(8,128)(2,1)S(1)} %get-tuple-element.51.near_ref, bf16[8,64,512]{2,1,0:T(8,128)(2,1)S(1)} %bitcast.35, bf16[132,64,512]{2,1,0:T(8,128)(2,1)S(1)} %get-tuple-element.40.tiles_ref), custom_call_target="tpu_custom_call" | custom-call | flops 3145728000 | bytes 4194304 | tf_op jit(solution)/shard_map/apply_first/pallas_call | solution.py:504
  68.4 0.0 copy-start
  68.4 5.1 %collective-permute-done.13.near_ref = bf16[8,64,512]{2,1,0:T(8,128)(2,1)S(1)} collective-permute-done((bf16[8,64,512]{2,1,0:T(8,128)(2,1)S(1)}, bf16[8,64,512]{2,1,0:T(8,128)(2,1)S(1)}, u32[]{:S(2)}, u32[]{:S(2)}) %collective-permute-start.13) | collective-permute-done | bytes 524320 | tf_op jit(solution)/shard_map/ppermute | solution.py:78
  73.5 0.0 collective-permute-start.15
  73.5 1.9 %collective-permute-done.15 = bf16[1,8,64,512]{3,2,1,0:T(8,128)(2,1)S(1)} collective-permute-done((bf16[1,8,64,512]{3,2,1,0:T(8,128)(2,1)S(1)}, bf16[1,8,64,512]{3,2,1,0:T(8,128)(2,1)S(1)}, u32[]{:S(2)}, u32[]{:S(2)}) %collective-permute-start.15) | collective-permute-done | bytes 524320 | tf_op jit(solution)/shard_map/ppermute | solution.py:60
  75.4 2.8 %apply_last.3 = (f32[64,512]{1,0:T(8,128)S(1)}, bf16[64,512]{1,0:T(8,128)(2,1)}, f32[72,128]{1,0:T(8,128)S(1)}) custom-call(s32[532]{0:T(1024)S(1)} %get-tuple-element.31.ids_ref, s32[1]{0:T(128)} %get-tuple-element.32.count_ref, bf16[8,64,512]{2,1,0:T(8,128)(2,1)S(1)} %collective-permute-done.13.near_ref, bf16[8,64,512]{2,1,0:T(8,128)(2,1)S(1)} %bitcast.34, ...), custom_call_target="tpu_custom_call" | custom-call | flops 3145728000 | bytes 4194304 | tf_op jit(solution)/shard_map/apply_last/pallas_call | solution.py:504
  78.2 0.2 collective-permute-start.21
  78.4 0.4 collective-permute-start.16
  78.8 1.1 %collective-permute-done.16 = f32[72,128]{1,0:T(8,128)S(1)} collective-permute-done((f32[72,128]{1,0:T(8,128)S(1)}, f32[72,128]{1,0:T(8,128)S(1)}, u32[]{:S(2)}, u32[]{:S(2)}) %collective-permute-start.16) | collective-permute-done | bytes 36896 | tf_op jit(solution)/shard_map/ppermute | solution.py:60
  79.9 2.0 %collective-permute-start.17 = (f32[72,128]{1,0:T(8,128)S(1)}, f32[72,128]{1,0:T(8,128)S(1)}, u32[]{:S(2)}, u32[]{:S(2)}) collective-permute-start(f32[72,128]{1,0:T(8,128)S(1)} %add.36), channel_id=1, source_target_pairs={{0,16},{1,5},{2,18},{3,7},{4,20},{5,1},{6,22},{7,3},{8,24},{9,13},... | collective-permute-start | bytes 110600 | tf_op jit(solution)/shard_map/ppermute | solution.py:78
  81.9 3.2 %collective-permute-done.17 = f32[72,128]{1,0:T(8,128)S(1)} collective-permute-done((f32[72,128]{1,0:T(8,128)S(1)}, f32[72,128]{1,0:T(8,128)S(1)}, u32[]{:S(2)}, u32[]{:S(2)}) %collective-permute-start.17) | collective-permute-done | bytes 36896 | tf_op jit(solution)/shard_map/ppermute | solution.py:78
  85.1 0.4 collective-permute-start.18
  85.6 3.5 %collective-permute-done.18 = f32[72,128]{1,0:T(8,128)S(1)} collective-permute-done((f32[72,128]{1,0:T(8,128)S(1)}, f32[72,128]{1,0:T(8,128)S(1)}, u32[]{:S(2)}, u32[]{:S(2)}) %collective-permute-start.18) | collective-permute-done | bytes 36896 | tf_op jit(solution)/shard_map/ppermute | solution.py:78
  89.1 3.9 %collective-permute-done.19 = f32[72,128]{1,0:T(8,128)S(1)} collective-permute-done((f32[72,128]{1,0:T(8,128)S(1)}, f32[72,128]{1,0:T(8,128)S(1)}, u32[]{:S(2)}, u32[]{:S(2)}) %collective-permute-start.19) | collective-permute-done | bytes 36896 | tf_op jit(solution)/shard_map/ppermute | solution.py:78
  93.1 0.0 collective-permute-start.20
  93.1 3.9 %collective-permute-done.20 = f32[72,128]{1,0:T(8,128)S(1)} collective-permute-done((f32[72,128]{1,0:T(8,128)S(1)}, f32[72,128]{1,0:T(8,128)S(1)}, u32[]{:S(2)}, u32[]{:S(2)}) %collective-permute-start.20) | collective-permute-done | bytes 36896 | tf_op jit(solution)/shard_map/ppermute | solution.py:78
  97.1 1.4 %unsort.1.images_ref = f32[128,512]{1,0:T(8,128)S(1)} custom-call(s32[2]{0:T(128)S(1)} %fusion.2.first_ref, s32[1,512]{1,0:T(1,128)S(1)} %get-tuple-element.48.rank_ref, f32[128,1024]{1,0:T(8,128)S(1)} %pad_maximum_fusion.2.block_ref), custom_call_target="tpu_custom_call" | custom-call | flops 402653184 | bytes 2097152 | tf_op jit(solution)/shard_map/unsort/pallas_call | solution.py:276
  98.5 7.5 %last_step.1 = (f32[64,512]{1,0:T(8,128)}, f32[64,512]{1,0:T(8,128)}) custom-call(f32[72,128]{1,0:T(8,128)S(1)} %add.40.grams_ref, f32[64,512]{1,0:T(8,128)S(1)} %copy-done, f32[128,512]{1,0:T(8,128)S(1)} %unsort.1.images_ref), custom_call_target="tpu_custom_call" | custom-call | tf_op jit(solution)/shard_map/last_step/pallas_call | solution.py:623
  (18 shorter events, 0.2 us)
Async XLA Ops:
  0.6 2.1 %collective-permute-start.2 = (f32[1,64,512]{2,1,0:T(8,128)}, f32[1,64,512]{2,1,0:T(8,128)S(1)}, u32[]{:S(2)}, u32[]{:S(2)}) collective-permute-start(f32[1,64,512]{2,1,0:T(8,128)} %bitcast.27), channel_id=1, source_target_pairs={{0,1},{1,0},{2,3},{3,2},{4,5},{5,4},{6,7},{7,6},{8,9},{9,8},{10,11... | collective-permute-start | bytes 393224 | tf_op jit(solution)/shard_map/ppermute | solution.py:60
  1.1 1.5 %collective-permute-start = (f32[1,3,512]{2,1,0:T(4,128)}, f32[1,3,512]{2,1,0:T(4,128)S(1)}, u32[]{:S(2)}, u32[]{:S(2)}) collective-permute-start(f32[1,3,512]{2,1,0:T(4,128)} %bitcast.40), channel_id=1, source_target_pairs={{0,1},{1,0},{2,3},{3,2},{4,5},{5,4},{6,7},{7,6},{8,9},{9,8},{10,11... | collective-permute-start | bytes 18440 | tf_op jit(solution)/shard_map/ppermute | solution.py:60
  1.2 1.5 %collective-permute-start.1 = (f32[1,1,512]{2,1,0:T(1,128)}, f32[1,1,512]{2,1,0:T(1,128)S(1)}, u32[]{:S(2)}, u32[]{:S(2)}) collective-permute-start(f32[1,1,512]{2,1,0:T(1,128)} %bitcast.42), channel_id=1, source_target_pairs={{0,1},{1,0},{2,3},{3,2},{4,5},{5,4},{6,7},{7,6},{8,9},{9,8},{10,11... | collective-permute-start | bytes 6152 | tf_op jit(solution)/shard_map/ppermute | solution.py:60
  6.7 10.3 %collective-permute-start.3 = (bf16[1,64,512]{2,1,0:T(8,128)(2,1)S(1)}, bf16[1,64,512]{2,1,0:T(8,128)(2,1)S(1)}, u32[]{:S(2)}, u32[]{:S(2)}) collective-permute-start(bf16[1,64,512]{2,1,0:T(8,128)(2,1)S(1)} %bitcast.18), channel_id=1, source_target_pairs={{0,16},{1,17},{2,18},{3,19},{4,20},{5,21},{6,22},{7,23},{8,24},{9,... | collective-permute-start | bytes 196616 | tf_op jit(solution)/shard_map/ppermute | solution.py:78
  11.3 12.7 %all-to-all-start = ((f32[16,4,512]{2,1,0:T(4,128)}), f32[16,4,512]{2,1,0:T(4,128)S(1)}, u32[]{:S(2)}, u32[]{:S(2)}) async-start(f32[16,4,512]{2,1,0:T(4,128)} %broadcast_in_dim.61), calls=%async_computation | async-start | bytes 262144 | tf_op jit(solution)/shard_map/all_to_all | solution.py:652
  16.9 7.4 %collective-permute-start.4 = (bf16[2,64,512]{2,1,0:T(8,128)(2,1)S(1)}, bf16[2,64,512]{2,1,0:T(8,128)(2,1)S(1)}, u32[]{:S(2)}, u32[]{:S(2)}) collective-permute-start(bf16[2,64,512]{2,1,0:T(8,128)(2,1)S(1)} %pad_maximum_fusion.5), channel_id=1, source_target_pairs={{0,8},{1,3},{2,10},{3,1},{4,12},{5,7},{6,14},{7,5},{8,0},{9,11},{1... | collective-permute-start | bytes 393224 | tf_op jit(solution)/shard_map/ppermute | solution.py:78
  24.0 1.3 %collective-permute-start.7 = (f32[1,16,4,512]{3,2,1,0:T(4,128)S(1)}, f32[1,16,4,512]{3,2,1,0:T(4,128)S(1)}, u32[]{:S(2)}, u32[]{:S(2)}) collective-permute-start(f32[1,16,4,512]{3,2,1,0:T(4,128)S(1)} %bitcast.29), channel_id=1, source_target_pairs={{0,1},{1,0},{2,3},{3,2},{4,5},{5,4},{6,7},{7,6},{8,9},{9,8},{10,11... | collective-permute-start | bytes 393224 | tf_op jit(solution)/shard_map/ppermute | solution.py:60
  24.4 6.4 %collective-permute-start.5 = (bf16[4,64,512]{2,1,0:T(8,128)(2,1)S(1)}, bf16[4,64,512]{2,1,0:T(8,128)(2,1)S(1)}, u32[]{:S(2)}, u32[]{:S(2)}) collective-permute-start(bf16[4,64,512]{2,1,0:T(8,128)(2,1)S(1)} %pad_maximum_fusion.3), channel_id=1, source_target_pairs={{0,4},{1,9},{2,6},{3,11},{4,0},{5,13},{6,2},{7,15},{8,12},{9,1},{1... | collective-permute-start | bytes 786440 | tf_op jit(solution)/shard_map/ppermute | solution.py:78
  30.9 9.2 %collective-permute-start.6 = (bf16[8,64,512]{2,1,0:T(8,128)(2,1)S(1)}, bf16[8,64,512]{2,1,0:T(8,128)(2,1)S(1)}, u32[]{:S(2)}, u32[]{:S(2)}) collective-permute-start(bf16[8,64,512]{2,1,0:T(8,128)(2,1)S(1)} %pad_maximum_fusion.near_ref), channel_id=1, source_target_pairs={{0,2},{1,5},{2,0},{3,7},{4,6},{5,1},{6,4},{7,3},{8,10},{9,13},{10,... | collective-permute-start | bytes 1572872 | tf_op jit(solution)/shard_map/ppermute | solution.py:78
  32.1 8.1 %collective-permute-start.9 = (bf16[1,8,64,512]{3,2,1,0:T(8,128)(2,1)S(1)}, bf16[1,8,64,512]{3,2,1,0:T(8,128)(2,1)S(1)}, u32[]{:S(2)}, u32[]{:S(2)}) collective-permute-start(bf16[1,8,64,512]{3,2,1,0:T(8,128)(2,1)S(1)} %bitcast.26), channel_id=1, source_target_pairs={{0,1},{1,0},{2,3},{3,2},{4,5},{5,4},{6,7},{7,6},{8,9},{9,8},{10,11... | collective-permute-start | bytes 1572872 | tf_op jit(solution)/shard_map/ppermute | solution.py:60
  40.1 2.3 %collective-permute-start.8 = (bf16[1,8,64,512]{3,2,1,0:T(8,128)(2,1)S(1)}, bf16[1,8,64,512]{3,2,1,0:T(8,128)(2,1)S(1)}, u32[]{:S(2)}, u32[]{:S(2)}) collective-permute-start(bf16[1,8,64,512]{3,2,1,0:T(8,128)(2,1)S(1)} %bitcast.30), channel_id=1, source_target_pairs={{0,1},{1,0},{2,3},{3,2},{4,5},{5,4},{6,7},{7,6},{8,9},{9,8},{10,11... | collective-permute-start | bytes 1572872 | tf_op jit(solution)/shard_map/ppermute | solution.py:60
  44.6 7.9 %collective-permute-start.10 = (bf16[1,64,512]{2,1,0:T(8,128)(2,1)S(1)}, bf16[1,64,512]{2,1,0:T(8,128)(2,1)S(1)}, u32[]{:S(2)}, u32[]{:S(2)}) collective-permute-start(bf16[1,64,512]{2,1,0:T(8,128)(2,1)S(1)} %bitcast.22), channel_id=1, source_target_pairs={{0,16},{1,17},{2,18},{3,19},{4,20},{5,21},{6,22},{7,23},{8,24},{9,... | collective-permute-start | bytes 196616 | tf_op jit(solution)/shard_map/ppermute | solution.py:78
  52.5 5.0 %collective-permute-start.11 = (bf16[2,64,512]{2,1,0:T(8,128)(2,1)S(1)}, bf16[2,64,512]{2,1,0:T(8,128)(2,1)S(1)}, u32[]{:S(2)}, u32[]{:S(2)}) collective-permute-start(bf16[2,64,512]{2,1,0:T(8,128)(2,1)S(1)} %pad_maximum_fusion.6), channel_id=1, source_target_pairs={{0,8},{1,3},{2,10},{3,1},{4,12},{5,7},{6,14},{7,5},{8,0},{9,11},{1... | collective-permute-start | bytes 393224 | tf_op jit(solution)/shard_map/ppermute | solution.py:78
  57.6 6.4 %collective-permute-start.12 = (bf16[4,64,512]{2,1,0:T(8,128)(2,1)S(1)}, bf16[4,64,512]{2,1,0:T(8,128)(2,1)S(1)}, u32[]{:S(2)}, u32[]{:S(2)}) collective-permute-start(bf16[4,64,512]{2,1,0:T(8,128)(2,1)S(1)} %pad_maximum_fusion.4), channel_id=1, source_target_pairs={{0,4},{1,9},{2,6},{3,11},{4,0},{5,13},{6,2},{7,15},{8,12},{9,1},{1... | collective-permute-start | bytes 786440 | tf_op jit(solution)/shard_map/ppermute | solution.py:78
  64.1 2.0 %collective-permute-start.14 = (bf16[1,8,64,512]{3,2,1,0:T(8,128)(2,1)S(1)}, bf16[1,8,64,512]{3,2,1,0:T(8,128)(2,1)S(1)}, u32[]{:S(2)}, u32[]{:S(2)}) collective-permute-start(bf16[1,8,64,512]{3,2,1,0:T(8,128)(2,1)S(1)} %get-tuple-element.50), channel_id=1, source_target_pairs={{0,1},{1,0},{2,3},{3,2},{4,5},{5,4},{6,7},{7,6},{8,9},{9,8},{10,11... | collective-permute-start | bytes 1572872 | tf_op jit(solution)/shard_map/ppermute | solution.py:60
  64.2 9.2 %collective-permute-start.13 = (bf16[8,64,512]{2,1,0:T(8,128)(2,1)S(1)}, bf16[8,64,512]{2,1,0:T(8,128)(2,1)S(1)}, u32[]{:S(2)}, u32[]{:S(2)}) collective-permute-start(bf16[8,64,512]{2,1,0:T(8,128)(2,1)S(1)} %get-tuple-element.51.near_ref), channel_id=1, source_target_pairs={{0,2},{1,5},{2,0},{3,7},{4,6},{5,1},{6,4},{7,3},{8,10},{9,13},{10,... | collective-permute-start | bytes 1572872 | tf_op jit(solution)/shard_map/ppermute | solution.py:78
  68.4 30.1 %copy-start = (f32[64,512]{1,0:T(8,128)S(1)}, f32[64,512]{1,0:T(8,128)}, u32[]{:S(2)}) copy-start(f32[64,512]{1,0:T(8,128)} %start_ref.1) | copy-start | bytes 393220
  73.5 1.9 %collective-permute-start.15 = (bf16[1,8,64,512]{3,2,1,0:T(8,128)(2,1)S(1)}, bf16[1,8,64,512]{3,2,1,0:T(8,128)(2,1)S(1)}, u32[]{:S(2)}, u32[]{:S(2)}) collective-permute-start(bf16[1,8,64,512]{3,2,1,0:T(8,128)(2,1)S(1)} %bitcast.31), channel_id=1, source_target_pairs={{0,1},{1,0},{2,3},{3,2},{4,5},{5,4},{6,7},{7,6},{8,9},{9,8},{10,11... | collective-permute-start | bytes 1572872 | tf_op jit(solution)/shard_map/ppermute | solution.py:60
  78.2 18.8 %collective-permute-start.21 = (f32[1,128,512]{2,1,0:T(8,128)S(1)}, f32[1,128,512]{2,1,0:T(8,128)S(1)}, u32[]{:S(2)}, u32[]{:S(2)}) collective-permute-start(f32[1,128,512]{2,1,0:T(8,128)S(1)} %bitcast.38), channel_id=1, source_target_pairs={{0,1},{1,0},{2,3},{3,2},{4,5},{5,4},{6,7},{7,6},{8,9},{9,8},{10,11... | collective-permute-start | bytes 786440 | tf_op jit(solution)/shard_map/ppermute | solution.py:60
  78.4 1.5 %collective-permute-start.16 = (f32[72,128]{1,0:T(8,128)S(1)}, f32[72,128]{1,0:T(8,128)S(1)}, u32[]{:S(2)}, u32[]{:S(2)}) collective-permute-start(f32[72,128]{1,0:T(8,128)S(1)} %get-tuple-element.47), channel_id=1, source_target_pairs={{0,1},{1,0},{2,3},{3,2},{4,5},{5,4},{6,7},{7,6},{8,9},{9,8},{10,11... | collective-permute-start | bytes 110600 | tf_op jit(solution)/shard_map/ppermute | solution.py:60
  79.9 5.3 %collective-permute-start.17 = (f32[72,128]{1,0:T(8,128)S(1)}, f32[72,128]{1,0:T(8,128)S(1)}, u32[]{:S(2)}, u32[]{:S(2)}) collective-permute-start(f32[72,128]{1,0:T(8,128)S(1)} %add.36), channel_id=1, source_target_pairs={{0,16},{1,5},{2,18},{3,7},{4,20},{5,1},{6,22},{7,3},{8,24},{9,13},... | collective-permute-start | bytes 110600 | tf_op jit(solution)/shard_map/ppermute | solution.py:78
  85.1 4.0 %collective-permute-start.18 = (f32[72,128]{1,0:T(8,128)S(1)}, f32[72,128]{1,0:T(8,128)S(1)}, u32[]{:S(2)}, u32[]{:S(2)}) collective-permute-start(f32[72,128]{1,0:T(8,128)S(1)} %add.37), channel_id=1, source_target_pairs={{0,8},{1,3},{2,10},{3,1},{4,12},{5,7},{6,14},{7,5},{8,0},{9,11},{1... | collective-permute-start | bytes 110600 | tf_op jit(solution)/shard_map/ppermute | solution.py:78
  89.1 4.0 %collective-permute-start.19 = (f32[72,128]{1,0:T(8,128)S(1)}, f32[72,128]{1,0:T(8,128)S(1)}, u32[]{:S(2)}, u32[]{:S(2)}) collective-permute-start(f32[72,128]{1,0:T(8,128)S(1)} %add.38), channel_id=1, source_target_pairs={{0,4},{1,17},{2,6},{3,19},{4,0},{5,21},{6,2},{7,23},{8,12},{9,25},... | collective-permute-start | bytes 110600 | tf_op jit(solution)/shard_map/ppermute | solution.py:78
  93.1 4.0 %collective-permute-start.20 = (f32[72,128]{1,0:T(8,128)S(1)}, f32[72,128]{1,0:T(8,128)S(1)}, u32[]{:S(2)}, u32[]{:S(2)}) collective-permute-start(f32[72,128]{1,0:T(8,128)S(1)} %add.39), channel_id=1, source_target_pairs={{0,2},{1,9},{2,0},{3,11},{4,6},{5,13},{6,4},{7,15},{8,10},{9,1},{1... | collective-permute-start | bytes 110600 | tf_op jit(solution)/shard_map/ppermute | solution.py:78

commit v10 on v9

--- a/solution.py
+++ b/solution.py
@@ -13,7 +13,7 @@
 ROWS = 64
 PAIR = 2
 BATCH = 2 * PAIR
-UNROLL = 4
+UNROLL = 8
 VMEM = 16 * 1024 * 1024
 HIGHEST = lax.Precision.HIGHEST
 
@@ -102,7 +102,7 @@
         for bit in bits:
             offsets = offsets + [offset ^ bit for offset in offsets]
         table.append(offsets)
-    return [jnp.array(offsets, jnp.int32) for offsets in table]
+    return table
 
 
 def exchange(block, *beside):
@@ -142,12 +142,13 @@
 
 
 def sort_kernel(
-    first_ref, owner_ref, near_ref, far_ref, near_error_ref, far_error_ref, block_ref, other_ref,
+    device_ref, owner_ref, near_ref, far_ref, near_error_ref, far_error_ref, block_ref, other_ref,
     rounded_out, places_out, own_out, block_out, rank_out,
     order_ref, column_ref, rank_ref, owned_ref, places_ref, errors_ref, blocks_ref, sems,
 ):
     columns, local = block_out.shape
     half = block_ref.shape[0]
+    tile = lax.rem(device_ref[0], 2 * half)
     pairs = [(owner_ref, owned_ref)]
     for sources, target in (
         ((near_ref, far_ref), places_ref),
@@ -170,7 +171,7 @@
     step = 64
     index = jnp.concatenate(
         [
-            (first_ref[i] + lax.broadcasted_iota(jnp.int32, (1, local), 1)).astype(jnp.float32)
+            ((tile ^ i) * local + lax.broadcasted_iota(jnp.int32, (1, local), 1)).astype(jnp.float32)
             for i in range(n // local)
         ],
         axis=1,
@@ -202,7 +203,7 @@
 
     rank = rank_ref[...]
     rank_out[...] = rank[:, :local]
-    fill_order(first_ref[0], rank, order_ref, 0, local)
+    fill_order(tile * local, rank, order_ref, 0, local)
     for copy in copies[5:]:
         copy.wait()
     block = jnp.concatenate([blocks_ref[i] for i in range(2 * half)], axis=1)
@@ -229,7 +230,7 @@
     places_out[...] = jnp.concatenate([whole[:3], flags], axis=0)
 
 
-def sort_region(first, tile_owner, near, far, near_error, far_error, block, other):
+def sort_region(device, tile_owner, near, far, near_error, far_error, block, other):
     local = near.shape[2]
     n = local * 2 * near.shape[0]
     columns = block.shape[1]
@@ -260,17 +261,18 @@
             flops=6 * n * local * (columns + 8), bytes_accessed=4 * n * local, transcendentals=0
         ),
         name="sort_region",
-    )(first, in_hbm(tile_owner), in_hbm(near), far, in_hbm(near_error), far_error, in_hbm(block), other)
-
-
-def unsort_kernel(first_ref, rank_ref, block_ref, block_out, order_ref):
+    )(device, in_hbm(tile_owner), in_hbm(near), far, in_hbm(near_error), far_error, in_hbm(block), other)
+
+
+def unsort_kernel(device_ref, rank_ref, block_ref, block_out, order_ref):
     n, local = order_ref.shape
+    tile = lax.rem(device_ref[0], n // local)
     for slot in range(n // local):
-        fill_order(first_ref[slot], rank_ref[...], order_ref, slot * local, local)
+        fill_order((tile ^ slot) * local, rank_ref[...], order_ref, slot * local, local)
     block_out[...] = add_parts(dot_nn(stacked_parts(block_ref[...]), order_ref[...]))
 
 
-def unsort(first, rank, block):
+def unsort(device, rank, block):
     n = block.shape[1]
     local = rank.shape[1]
     return pl.pallas_call(
@@ -284,7 +286,7 @@
             flops=6 * n * local * block.shape[0], bytes_accessed=4 * n * local, transcendentals=0
         ),
         name="unsort",
-    )(first, rank, block)
+    )(device, rank, block)
 
 
 def plan_blocks(
@@ -359,17 +361,25 @@
 
 
 def build_kernel(
-    place_ref, distance_ref, own_ref, near_ref, other_ref,
+    part, device_ref, own_ref, near_ref, other_ref,
     ids_ref, count_ref, tiles_ref,
-    wide_ref, far_ref, stage_ref, bounds_ref, bounds_sem,
+    wide_ref, far_ref, stage_ref, bounds_ref, bounds_sem, distance_ref,
 ):
     local = own_ref.shape[1]
     places = far_ref.shape[0]
     chunk_bits = (local // LANES).bit_length() - 1
     factor = jnp.where(lax.broadcasted_iota(jnp.int32, (4, 1), 0) < 2, 2.0, 1.0 / 12.0)
+    tiles, regions = 2 * near_ref.shape[0], near_ref.shape[1]
+    here, tile = lax.div(device_ref[0], tiles), lax.rem(device_ref[0], tiles)
+    even, odd = slot_offsets(regions)
+    size = regions // 2
     for index in range(places):
-        side_ref = near_ref if 2 * index < places else other_ref
-        far_ref[index, 0:4, :] = factor * side_ref[place_ref[index]]
+        other, slot = index // size, part * size + index % size
+        offset = jnp.where((tile ^ other) & 1 == 0, even[slot], odd[slot])
+        region = here ^ offset
+        side_ref = near_ref if 2 * other < tiles else other_ref
+        far_ref[index, 0:4, :] = factor * side_ref[other % (tiles // 2), region]
+        distance_ref[index : index + 1, :] = jnp.full((1, LANES), region - here, jnp.int32)
 
     def prepare():
         column = jnp.transpose(own_ref[...])
@@ -398,9 +408,8 @@
     lax.fori_loop(0, total, build_batch, 0)
 
 
-def build_tiles(place, distance, own, near, far, capacity):
-    near, far = [piece.reshape((-1,) + piece.shape[2:]) for piece in (near, far)]
-    places, local = place.shape[0], own.shape[1]
+def build_tiles(part, device, own, near, far, capacity):
+    places, local = near.shape[0] * near.shape[1], own.shape[1]
     smem = pl.BlockSpec(memory_space=pltpu.SMEM)
     sizes = (capacity * BATCH + local // LANES, 1)
     shape = (capacity, ROWS, BATCH * LANES)
@@ -410,12 +419,13 @@
         pltpu.VMEM((places, LANES), jnp.int32),
         pltpu.SMEM((places, LANES), jnp.int32),
         pltpu.SemaphoreType.DMA,
+        pltpu.VMEM((places, LANES), jnp.int32),
     ]
     return pl.pallas_call(
-        build_kernel,
+        functools.partial(build_kernel, part),
         out_shape=tuple(jax.ShapeDtypeStruct((size,), jnp.int32) for size in sizes)
         + (pltpu.VMEM(shape, jnp.bfloat16),),
-        in_specs=[smem] + whole_vmem(4),
+        in_specs=[smem] + whole_vmem(3),
         out_specs=(smem,) * 2 + (pl.BlockSpec(memory_space=pltpu.VMEM),),
         scratch_shapes=scratch,
         compiler_params=pltpu.CompilerParams(vmem_limit_bytes=VMEM),
@@ -423,7 +433,7 @@
             flops=2 * local * local * 16000, bytes_accessed=16 * local * local, transcendentals=0
         ),
         name="build_tiles",
-    )(place, distance, own, near, far)
+    )(device, own, near, far)
 
 
 def apply_kernel(started, last, grams, ids_ref, count_ref, near_ref, other_ref, tiles_ref, *refs):
@@ -633,15 +643,10 @@
 def shards(innovations, obs_geometry, obs_error, tile_owner):
     tiles_axis, regions = lax.axis_size("tile"), lax.axis_size("region")
     reach = tile_owner.shape[1]
-    here, tile = lax.axis_index("region"), lax.axis_index("tile")
     columns, local = innovations.shape
-    slot_tile = tile ^ jnp.arange(tiles_axis, dtype=jnp.int32)
-    first = slot_tile * local
-    even, odd = slot_offsets(regions)
-    slot_region = here ^ jnp.where((slot_tile % 2 == 0)[:, None], even, odd)
-
+    device = lax.axis_index(("region", "tile")).astype(jnp.int32).reshape(1)
     rounded, places, own, start, rank = sort_region(
-        first,
+        device,
         tile_owner,
         *halves(obs_geometry, "tile"),
         *halves(obs_error[None, :], "tile"),
@@ -656,14 +661,9 @@
     most = min(half_regions, 2 * reach - 1) * tiles_axis * (local // LANES)
     batches = -(-(local // ROWS) * -(-most // PAIR) * PAIR // BATCH) + 1
     capacity = -(-batches // UNROLL) * UNROLL
-    stack = jnp.arange(tiles_axis, dtype=jnp.int32) % (tiles_axis // 2) * regions
     plans, tiles = [], []
     for part in range(2):
-        inside = slot_region[:, part * half_regions : (part + 1) * half_regions]
-        *plan, built = build_tiles(
-            (stack[:, None] + inside).reshape(-1), (inside - here).reshape(-1, 1), own,
-            near_places, far_places, capacity,
-        )
+        *plan, built = build_tiles(part, device, own, near_places, far_places, capacity)
         plans.append(plan)
         tiles.append(built)
 
@@ -686,7 +686,7 @@
     second, _, grams = operate(image_rounded, image, first_grams(start, image))
     grams = sum_regions(sum_tiles(grams))
     near, far = halves(jnp.concatenate([image, second], axis=0), "tile")
-    images = unsort(first, rank, jnp.concatenate([*near, *far], axis=1))
+    images = unsort(device, rank, jnp.concatenate([*near, *far], axis=1))
     return last_step(grams, innovations, images)
 
 

time: 107 us -> 104 us (0.972)
  starting transfers between devices: 21.1 us -> 32.8 us
  waiting for transfers between devices: 49.2 us -> 38.8 us
  Pallas kernels: 32.7 us -> 30 us
    ppermute x12, starting transfers between devices: 14.6 us -> 27.2 us  [swap_regions(): return lax.ppermute(block, ('region', 'tile'), route)]
    ppermute x12, waiting for transfers between devices: 38.2 us -> 28.5 us  [swap_regions(): return lax.ppermute(block, ('region', 'tile'), route)]
    ppermute x10, waiting for transfers between devices: 5.91 us -> 4.51 us  [swapped(): lax.ppermute(block, axis, [(i, i ^ bit) for i in range(lax.axis_size(axis...]
  transfers between devices with their start and end apart: 23 -> 23, of which waited for: 16 -> 15; matrix products, arithmetic and copies ran while one was open for 2% -> 1% of each run, Pallas kernels for 14% -> 13%
where the time goes in v10:
time: 104 us; the launch traced here: 103 us
  waiting for transfers between devices  38.8 us (37%)
  starting transfers between devices  32.8 us (32%)
  Pallas kernels  30 us (29%)
    ppermute x12, waiting for transfers between devices, swap_regions(): return lax.ppermute(block, ('region', 'tile'), route)  28.5 us
    ppermute x12, starting transfers between devices, swap_regions(): return lax.ppermute(block, ('region', 'tile'), route)  27.2 us
    pallas_call x4, Pallas kernels, apply_tiles(): pl.pallas_call(functools.partial(apply_kernel, start is not None, last, g...  8.82 us
    pallas_call x2, Pallas kernels, build_tiles(): pl.pallas_call(functools.partial(build_kernel, part), out_shape=tuple((ja...  8.72 us
    pallas_call x1, Pallas kernels, last_step(): pl.pallas_call(last_kernel, out_shape=(jax.ShapeDtypeStruct(start.shape,...  7.52 us
    all_to_all x1, waiting for transfers between devices, shards(): everywhere = lax.all_to_all(everywhere, 'region', 0, 0)  5.78 us
    ppermute x10, waiting for transfers between devices, swapped(): lax.ppermute(block, axis, [(i, i ^ bit) for i in range(lax.axis_size(axis...  4.51 us
    all_to_all x1, starting transfers between devices, shards(): everywhere = lax.all_to_all(everywhere, 'region', 0, 0)  3.88 us
  transfers between devices with their start and end apart: 23, of which 15 were waited for; matrix products, arithmetic and copies ran while one was open for 1% of the time, Pallas kernels for 13%

profile of v10, /device:TPU:0, one launch (start us, length us, event | category | flops | bytes accessed | tf_op | source)
XLA Modules:
  0.0 103.4 jit_solution(2880372225024627083)
XLA Ops:
  0.6 0.5 collective-permute-start.2
  1.1 0.1 collective-permute-start
  1.2 0.4 collective-permute-start.1
  1.7 1.0 collective-permute-done.1.far_error_ref
  2.7 0.0 collective-permute-done.far_ref
  2.7 0.0 collective-permute-done.2.other_ref
  2.7 3.4 %sort_region.1 = (bf16[64,512]{1,0:T(8,128)(2,1)S(1)}, f32[4,512]{1,0:T(4,128)S(1)}, f32[8,512]{1,0:T(8,128)S(1)}, f32[64,512]{1,0:T(8,128)S(1)}, s32[1,512]{1,0:T(1,128)S(1)}) custom-call(s32[1]{0:T(128)} %bitcast.device_ref, s32[1,7]{1,0:T(1,128)} %owner_ref.1, f32[1,3,512]{2,1,0:T(4,128)} %bitcast.41, f32[1,3,512]{2,1,0:T(4,128)S(1)} %collective-permute-done.far_ref, ...), custom_call_target="tpu_custom_call" | custom-call | flops 226492416 | bytes 2097152 | tf_op jit(solution)/shard_map/sort_region/pallas_call | solution.py:238
  6.1 6.4 %collective-permute-start.3 = (bf16[1,64,512]{2,1,0:T(8,128)(2,1)S(1)}, bf16[1,64,512]{2,1,0:T(8,128)(2,1)S(1)}, u32[]{:S(2)}, u32[]{:S(2)}) collective-permute-start(bf16[1,64,512]{2,1,0:T(8,128)(2,1)S(1)} %bitcast.18), channel_id=1, source_target_pairs={{0,16},{1,17},{2,18},{3,19},{4,20},{5,21},{6,22},{7,23},{8,24},{9,... | collective-permute-start | bytes 196616 | tf_op jit(solution)/shard_map/ppermute | solution.py:78
  12.5 0.7 broadcast_in_dim.39
  13.1 3.9 %all-to-all-start = ((f32[16,4,512]{2,1,0:T(4,128)}), f32[16,4,512]{2,1,0:T(4,128)S(1)}, u32[]{:S(2)}, u32[]{:S(2)}) async-start(f32[16,4,512]{2,1,0:T(4,128)} %broadcast_in_dim.39), calls=%async_computation | async-start | bytes 262144 | tf_op jit(solution)/shard_map/all_to_all | solution.py:657
  17.0 0.0 collective-permute-done.3
  17.1 2.0 %collective-permute-start.4 = (bf16[2,64,512]{2,1,0:T(8,128)(2,1)S(1)}, bf16[2,64,512]{2,1,0:T(8,128)(2,1)S(1)}, u32[]{:S(2)}, u32[]{:S(2)}) collective-permute-start(bf16[2,64,512]{2,1,0:T(8,128)(2,1)S(1)} %pad_maximum_fusion.5), channel_id=1, source_target_pairs={{0,8},{1,3},{2,10},{3,1},{4,12},{5,7},{6,14},{7,5},{8,0},{9,11},{1... | collective-permute-start | bytes 393224 | tf_op jit(solution)/shard_map/ppermute | solution.py:78
  19.1 5.8 %all-to-all-done = f32[16,4,512]{2,1,0:T(4,128)S(1)} async-done(((f32[16,4,512]{2,1,0:T(4,128)}), f32[16,4,512]{2,1,0:T(4,128)S(1)}, u32[]{:S(2)}, u32[]{:S(2)}) %all-to-all-start) | async-done | bytes 131104 | tf_op jit(solution)/shard_map/all_to_all | solution.py:657
  24.8 0.0 collective-permute-start.7
  24.8 0.0 collective-permute-done.4
  24.9 0.8 collective-permute-start.5
  25.7 0.5 collective-permute-done.7.other_ref
  26.2 4.6 %build_tiles.3 = (s32[548]{0:T(1024)S(1)}, s32[1]{0:T(128)}, bf16[136,64,512]{2,1,0:T(8,128)(2,1)S(1)}) custom-call(s32[1]{0:T(128)} %bitcast.device_ref, f32[8,512]{1,0:T(8,128)S(1)} %get-tuple-element.27.own_ref, f32[1,16,4,512]{3,2,1,0:T(4,128)S(1)} %bitcast.30, f32[1,16,4,512]{3,2,1,0:T(4,128)S(1)} %collective-permute-done.7.other_ref), custom_call_target="tpu_custom_call" | custom-call | flops 8388608000 | bytes 4194304 | tf_op jit(solution)/shard_map/build_tiles/pallas_call | solution.py:424
  30.8 0.5 collective-permute-done.5
  31.3 0.1 pad_maximum_fusion.near_ref
  31.4 1.2 %collective-permute-start.6 = (bf16[8,64,512]{2,1,0:T(8,128)(2,1)S(1)}, bf16[8,64,512]{2,1,0:T(8,128)(2,1)S(1)}, u32[]{:S(2)}, u32[]{:S(2)}) collective-permute-start(bf16[8,64,512]{2,1,0:T(8,128)(2,1)S(1)} %pad_maximum_fusion.near_ref), channel_id=1, source_target_pairs={{0,2},{1,5},{2,0},{3,7},{4,6},{5,1},{6,4},{7,3},{8,10},{9,13},{10,... | collective-permute-start | bytes 1572872 | tf_op jit(solution)/shard_map/ppermute | solution.py:78
  32.5 0.0 collective-permute-start.9
  32.5 4.1 %build_tiles.2 = (s32[548]{0:T(1024)S(1)}, s32[1]{0:T(128)}, bf16[136,64,512]{2,1,0:T(8,128)(2,1)S(1)}) custom-call(s32[1]{0:T(128)} %bitcast.device_ref, f32[8,512]{1,0:T(8,128)S(1)} %get-tuple-element.27.own_ref, f32[1,16,4,512]{3,2,1,0:T(4,128)S(1)} %bitcast.31, f32[1,16,4,512]{3,2,1,0:T(4,128)S(1)} %collective-permute-done.7.other_ref), custom_call_target="tpu_custom_call" | custom-call | flops 8388608000 | bytes 4194304 | tf_op jit(solution)/shard_map/build_tiles/pallas_call | solution.py:424
  36.7 3.9 %collective-permute-done.6.near_ref = bf16[8,64,512]{2,1,0:T(8,128)(2,1)S(1)} collective-permute-done((bf16[8,64,512]{2,1,0:T(8,128)(2,1)S(1)}, bf16[8,64,512]{2,1,0:T(8,128)(2,1)S(1)}, u32[]{:S(2)}, u32[]{:S(2)}) %collective-permute-start.6) | collective-permute-done | bytes 524320 | tf_op jit(solution)/shard_map/ppermute | solution.py:78
  40.6 0.0 collective-permute-start.8
  40.6 0.0 collective-permute-done.9
  40.6 2.0 %apply_first.2.refs_0_ = f32[512,64]{1,0:T(8,128)S(1)} custom-call(s32[548]{0:T(1024)S(1)} %get-tuple-element.37.ids_ref, s32[1]{0:T(128)} %get-tuple-element.38.count_ref, bf16[8,64,512]{2,1,0:T(8,128)(2,1)S(1)} %pad_maximum_fusion.near_ref, bf16[8,64,512]{2,1,0:T(8,128)(2,1)S(1)} %bitcast.34, bf16[136,64,512]{2,1,0:T(8,128)(2,1)S(1)} %get-tuple-element.40.tiles_ref), custom_call_target="tpu_custom_call" | custom-call | flops 3145728000 | bytes 4194304 | tf_op jit(solution)/shard_map/apply_first/pallas_call | solution.py:514
  42.6 0.0 collective-permute-done.8
  42.6 2.1 %apply_last.2 = (f32[64,512]{1,0:T(8,128)S(1)}, bf16[64,512]{1,0:T(8,128)(2,1)S(1)}) custom-call(s32[548]{0:T(1024)S(1)} %get-tuple-element.31.ids_ref, s32[1]{0:T(128)} %get-tuple-element.32.count_ref, bf16[8,64,512]{2,1,0:T(8,128)(2,1)S(1)} %collective-permute-done.6.near_ref, bf16[8,64,512]{2,1,0:T(8,128)(2,1)S(1)} %bitcast.35, ...), custom_call_target="tpu_custom_call" | custom-call | flops 3145728000 | bytes 4194304 | tf_op jit(solution)/shard_map/apply_last/pallas_call | solution.py:514
  44.7 2.3 %collective-permute-start.10 = (bf16[1,64,512]{2,1,0:T(8,128)(2,1)S(1)}, bf16[1,64,512]{2,1,0:T(8,128)(2,1)S(1)}, u32[]{:S(2)}, u32[]{:S(2)}) collective-permute-start(bf16[1,64,512]{2,1,0:T(8,128)(2,1)S(1)} %bitcast.22), channel_id=1, source_target_pairs={{0,16},{1,17},{2,18},{3,19},{4,20},{5,21},{6,22},{7,23},{8,24},{9,... | collective-permute-start | bytes 196616 | tf_op jit(solution)/shard_map/ppermute | solution.py:78
  47.1 0.7 first_grams.1.refs_3_
  47.8 2.5 %collective-permute-done.10 = bf16[1,64,512]{2,1,0:T(8,128)(2,1)S(1)} collective-permute-done((bf16[1,64,512]{2,1,0:T(8,128)(2,1)S(1)}, bf16[1,64,512]{2,1,0:T(8,128)(2,1)S(1)}, u32[]{:S(2)}, u32[]{:S(2)}) %collective-permute-start.10) | collective-permute-done | bytes 65568 | tf_op jit(solution)/shard_map/ppermute | solution.py:78
  50.2 2.2 %collective-permute-start.11 = (bf16[2,64,512]{2,1,0:T(8,128)(2,1)S(1)}, bf16[2,64,512]{2,1,0:T(8,128)(2,1)S(1)}, u32[]{:S(2)}, u32[]{:S(2)}) collective-permute-start(bf16[2,64,512]{2,1,0:T(8,128)(2,1)S(1)} %pad_maximum_fusion.6), channel_id=1, source_target_pairs={{0,8},{1,3},{2,10},{3,1},{4,12},{5,7},{6,14},{7,5},{8,0},{9,11},{1... | collective-permute-start | bytes 393224 | tf_op jit(solution)/shard_map/ppermute | solution.py:78
  52.4 2.9 %collective-permute-done.11 = bf16[2,64,512]{2,1,0:T(8,128)(2,1)S(1)} collective-permute-done((bf16[2,64,512]{2,1,0:T(8,128)(2,1)S(1)}, bf16[2,64,512]{2,1,0:T(8,128)(2,1)S(1)}, u32[]{:S(2)}, u32[]{:S(2)}) %collective-permute-start.11) | collective-permute-done | bytes 131104 | tf_op jit(solution)/shard_map/ppermute | solution.py:78
  55.4 1.7 %collective-permute-start.12 = (bf16[4,64,512]{2,1,0:T(8,128)(2,1)S(1)}, bf16[4,64,512]{2,1,0:T(8,128)(2,1)S(1)}, u32[]{:S(2)}, u32[]{:S(2)}) collective-permute-start(bf16[4,64,512]{2,1,0:T(8,128)(2,1)S(1)} %pad_maximum_fusion.4), channel_id=1, source_target_pairs={{0,4},{1,9},{2,6},{3,11},{4,0},{5,13},{6,2},{7,15},{8,12},{9,1},{1... | collective-permute-start | bytes 786440 | tf_op jit(solution)/shard_map/ppermute | solution.py:78
  57.0 4.8 %collective-permute-done.12 = bf16[4,64,512]{2,1,0:T(8,128)(2,1)S(1)} collective-permute-done((bf16[4,64,512]{2,1,0:T(8,128)(2,1)S(1)}, bf16[4,64,512]{2,1,0:T(8,128)(2,1)S(1)}, u32[]{:S(2)}, u32[]{:S(2)}) %collective-permute-start.12) | collective-permute-done | bytes 262176 | tf_op jit(solution)/shard_map/ppermute | solution.py:78
  61.8 0.1 fusion
  61.9 0.1 collective-permute-start.14
  62.0 2.5 %collective-permute-start.13 = (bf16[8,64,512]{2,1,0:T(8,128)(2,1)S(1)}, bf16[8,64,512]{2,1,0:T(8,128)(2,1)S(1)}, u32[]{:S(2)}, u32[]{:S(2)}) collective-permute-start(bf16[8,64,512]{2,1,0:T(8,128)(2,1)S(1)} %get-tuple-element.51.near_ref), channel_id=1, source_target_pairs={{0,2},{1,5},{2,0},{3,7},{4,6},{5,1},{6,4},{7,3},{8,10},{9,13},{10,... | collective-permute-start | bytes 1572872 | tf_op jit(solution)/shard_map/ppermute | solution.py:78
  64.5 0.0 collective-permute-done.14
  64.5 2.0 %apply_first.3.refs_0_ = f32[512,64]{1,0:T(8,128)S(1)} custom-call(s32[548]{0:T(1024)S(1)} %get-tuple-element.37.ids_ref, s32[1]{0:T(128)} %get-tuple-element.38.count_ref, bf16[8,64,512]{2,1,0:T(8,128)(2,1)S(1)} %get-tuple-element.51.near_ref, bf16[8,64,512]{2,1,0:T(8,128)(2,1)S(1)} %bitcast.37, bf16[136,64,512]{2,1,0:T(8,128)(2,1)S(1)} %get-tuple-element.40.tiles_ref), custom_call_target="tpu_custom_call" | custom-call | flops 3145728000 | bytes 4194304 | tf_op jit(solution)/shard_map/apply_first/pallas_call | solution.py:514
  66.4 0.0 copy-start
  66.5 5.2 %collective-permute-done.13.near_ref = bf16[8,64,512]{2,1,0:T(8,128)(2,1)S(1)} collective-permute-done((bf16[8,64,512]{2,1,0:T(8,128)(2,1)S(1)}, bf16[8,64,512]{2,1,0:T(8,128)(2,1)S(1)}, u32[]{:S(2)}, u32[]{:S(2)}) %collective-permute-start.13) | collective-permute-done | bytes 524320 | tf_op jit(solution)/shard_map/ppermute | solution.py:78
  71.6 0.0 collective-permute-start.15
  71.6 1.9 %collective-permute-done.15 = bf16[1,8,64,512]{3,2,1,0:T(8,128)(2,1)S(1)} collective-permute-done((bf16[1,8,64,512]{3,2,1,0:T(8,128)(2,1)S(1)}, bf16[1,8,64,512]{3,2,1,0:T(8,128)(2,1)S(1)}, u32[]{:S(2)}, u32[]{:S(2)}) %collective-permute-start.15) | collective-permute-done | bytes 524320 | tf_op jit(solution)/shard_map/ppermute | solution.py:60
  73.5 2.8 %apply_last.3 = (f32[64,512]{1,0:T(8,128)S(1)}, bf16[64,512]{1,0:T(8,128)(2,1)}, f32[72,128]{1,0:T(8,128)S(1)}) custom-call(s32[548]{0:T(1024)S(1)} %get-tuple-element.31.ids_ref, s32[1]{0:T(128)} %get-tuple-element.32.count_ref, bf16[8,64,512]{2,1,0:T(8,128)(2,1)S(1)} %collective-permute-done.13.near_ref, bf16[8,64,512]{2,1,0:T(8,128)(2,1)S(1)} %bitcast.36, ...), custom_call_target="tpu_custom_call" | custom-call | flops 3145728000 | bytes 4194304 | tf_op jit(solution)/shard_map/apply_last/pallas_call | solution.py:514
  76.3 0.2 collective-permute-start.21
  76.5 0.4 collective-permute-start.16
  76.9 1.1 %collective-permute-done.16 = f32[72,128]{1,0:T(8,128)S(1)} collective-permute-done((f32[72,128]{1,0:T(8,128)S(1)}, f32[72,128]{1,0:T(8,128)S(1)}, u32[]{:S(2)}, u32[]{:S(2)}) %collective-permute-start.16) | collective-permute-done | bytes 36896 | tf_op jit(solution)/shard_map/ppermute | solution.py:60
  78.0 2.3 %collective-permute-start.17 = (f32[72,128]{1,0:T(8,128)S(1)}, f32[72,128]{1,0:T(8,128)S(1)}, u32[]{:S(2)}, u32[]{:S(2)}) collective-permute-start(f32[72,128]{1,0:T(8,128)S(1)} %add.19), channel_id=1, source_target_pairs={{0,16},{1,5},{2,18},{3,7},{4,20},{5,1},{6,22},{7,3},{8,24},{9,13},... | collective-permute-start | bytes 110600 | tf_op jit(solution)/shard_map/ppermute | solution.py:78
  80.3 2.6 %collective-permute-done.17 = f32[72,128]{1,0:T(8,128)S(1)} collective-permute-done((f32[72,128]{1,0:T(8,128)S(1)}, f32[72,128]{1,0:T(8,128)S(1)}, u32[]{:S(2)}, u32[]{:S(2)}) %collective-permute-start.17) | collective-permute-done | bytes 36896 | tf_op jit(solution)/shard_map/ppermute | solution.py:78
  82.8 2.0 %collective-permute-start.18 = (f32[72,128]{1,0:T(8,128)S(1)}, f32[72,128]{1,0:T(8,128)S(1)}, u32[]{:S(2)}, u32[]{:S(2)}) collective-permute-start(f32[72,128]{1,0:T(8,128)S(1)} %add.20), channel_id=1, source_target_pairs={{0,8},{1,3},{2,10},{3,1},{4,12},{5,7},{6,14},{7,5},{8,0},{9,11},{1... | collective-permute-start | bytes 110600 | tf_op jit(solution)/shard_map/ppermute | solution.py:78
  84.8 2.0 %collective-permute-done.18 = f32[72,128]{1,0:T(8,128)S(1)} collective-permute-done((f32[72,128]{1,0:T(8,128)S(1)}, f32[72,128]{1,0:T(8,128)S(1)}, u32[]{:S(2)}, u32[]{:S(2)}) %collective-permute-start.18) | collective-permute-done | bytes 36896 | tf_op jit(solution)/shard_map/ppermute | solution.py:78
  86.8 1.7 %collective-permute-start.19 = (f32[72,128]{1,0:T(8,128)S(1)}, f32[72,128]{1,0:T(8,128)S(1)}, u32[]{:S(2)}, u32[]{:S(2)}) collective-permute-start(f32[72,128]{1,0:T(8,128)S(1)} %add.21), channel_id=1, source_target_pairs={{0,4},{1,17},{2,6},{3,19},{4,0},{5,21},{6,2},{7,23},{8,12},{9,25},... | collective-permute-start | bytes 110600 | tf_op jit(solution)/shard_map/ppermute | solution.py:78
  88.5 2.2 %collective-permute-done.19 = f32[72,128]{1,0:T(8,128)S(1)} collective-permute-done((f32[72,128]{1,0:T(8,128)S(1)}, f32[72,128]{1,0:T(8,128)S(1)}, u32[]{:S(2)}, u32[]{:S(2)}) %collective-permute-start.19) | collective-permute-done | bytes 36896 | tf_op jit(solution)/shard_map/ppermute | solution.py:78
  90.8 2.2 %collective-permute-start.20 = (f32[72,128]{1,0:T(8,128)S(1)}, f32[72,128]{1,0:T(8,128)S(1)}, u32[]{:S(2)}, u32[]{:S(2)}) collective-permute-start(f32[72,128]{1,0:T(8,128)S(1)} %add.22), channel_id=1, source_target_pairs={{0,2},{1,9},{2,0},{3,11},{4,6},{5,13},{6,4},{7,15},{8,10},{9,1},{1... | collective-permute-start | bytes 110600 | tf_op jit(solution)/shard_map/ppermute | solution.py:78
  93.0 1.9 %collective-permute-done.20 = f32[72,128]{1,0:T(8,128)S(1)} collective-permute-done((f32[72,128]{1,0:T(8,128)S(1)}, f32[72,128]{1,0:T(8,128)S(1)}, u32[]{:S(2)}, u32[]{:S(2)}) %collective-permute-start.20) | collective-permute-done | bytes 36896 | tf_op jit(solution)/shard_map/ppermute | solution.py:78
  95.0 0.0 collective-permute-done.21
  95.0 0.8 unsort.1.images_ref
  95.8 0.0 copy-done
  95.8 7.5 %last_step.1 = (f32[64,512]{1,0:T(8,128)}, f32[64,512]{1,0:T(8,128)}) custom-call(f32[72,128]{1,0:T(8,128)S(1)} %add.23.grams_ref, f32[64,512]{1,0:T(8,128)S(1)} %copy-done, f32[128,512]{1,0:T(8,128)S(1)} %unsort.1.images_ref), custom_call_target="tpu_custom_call" | custom-call | tf_op jit(solution)/shard_map/last_step/pallas_call | solution.py:633
  (13 shorter events, 0.2 us)
Async XLA Ops:
  0.6 2.1 %collective-permute-start.2 = (f32[1,64,512]{2,1,0:T(8,128)}, f32[1,64,512]{2,1,0:T(8,128)S(1)}, u32[]{:S(2)}, u32[]{:S(2)}) collective-permute-start(f32[1,64,512]{2,1,0:T(8,128)} %bitcast.27), channel_id=1, source_target_pairs={{0,1},{1,0},{2,3},{3,2},{4,5},{5,4},{6,7},{7,6},{8,9},{9,8},{10,11... | collective-permute-start | bytes 393224 | tf_op jit(solution)/shard_map/ppermute | solution.py:60
  1.1 1.5 %collective-permute-start = (f32[1,3,512]{2,1,0:T(4,128)}, f32[1,3,512]{2,1,0:T(4,128)S(1)}, u32[]{:S(2)}, u32[]{:S(2)}) collective-permute-start(f32[1,3,512]{2,1,0:T(4,128)} %bitcast.40), channel_id=1, source_target_pairs={{0,1},{1,0},{2,3},{3,2},{4,5},{5,4},{6,7},{7,6},{8,9},{9,8},{10,11... | collective-permute-start | bytes 18440 | tf_op jit(solution)/shard_map/ppermute | solution.py:60
  1.2 1.5 %collective-permute-start.1 = (f32[1,1,512]{2,1,0:T(1,128)}, f32[1,1,512]{2,1,0:T(1,128)S(1)}, u32[]{:S(2)}, u32[]{:S(2)}) collective-permute-start(f32[1,1,512]{2,1,0:T(1,128)} %bitcast.42), channel_id=1, source_target_pairs={{0,1},{1,0},{2,3},{3,2},{4,5},{5,4},{6,7},{7,6},{8,9},{9,8},{10,11... | collective-permute-start | bytes 6152 | tf_op jit(solution)/shard_map/ppermute | solution.py:60
  6.1 10.9 %collective-permute-start.3 = (bf16[1,64,512]{2,1,0:T(8,128)(2,1)S(1)}, bf16[1,64,512]{2,1,0:T(8,128)(2,1)S(1)}, u32[]{:S(2)}, u32[]{:S(2)}) collective-permute-start(bf16[1,64,512]{2,1,0:T(8,128)(2,1)S(1)} %bitcast.18), channel_id=1, source_target_pairs={{0,16},{1,17},{2,18},{3,19},{4,20},{5,21},{6,22},{7,23},{8,24},{9,... | collective-permute-start | bytes 196616 | tf_op jit(solution)/shard_map/ppermute | solution.py:78
  13.1 11.7 %all-to-all-start = ((f32[16,4,512]{2,1,0:T(4,128)}), f32[16,4,512]{2,1,0:T(4,128)S(1)}, u32[]{:S(2)}, u32[]{:S(2)}) async-start(f32[16,4,512]{2,1,0:T(4,128)} %broadcast_in_dim.39), calls=%async_computation | async-start | bytes 262144 | tf_op jit(solution)/shard_map/all_to_all | solution.py:657
  17.1 7.8 %collective-permute-start.4 = (bf16[2,64,512]{2,1,0:T(8,128)(2,1)S(1)}, bf16[2,64,512]{2,1,0:T(8,128)(2,1)S(1)}, u32[]{:S(2)}, u32[]{:S(2)}) collective-permute-start(bf16[2,64,512]{2,1,0:T(8,128)(2,1)S(1)} %pad_maximum_fusion.5), channel_id=1, source_target_pairs={{0,8},{1,3},{2,10},{3,1},{4,12},{5,7},{6,14},{7,5},{8,0},{9,11},{1... | collective-permute-start | bytes 393224 | tf_op jit(solution)/shard_map/ppermute | solution.py:78
  24.8 1.3 %collective-permute-start.7 = (f32[1,16,4,512]{3,2,1,0:T(4,128)S(1)}, f32[1,16,4,512]{3,2,1,0:T(4,128)S(1)}, u32[]{:S(2)}, u32[]{:S(2)}) collective-permute-start(f32[1,16,4,512]{3,2,1,0:T(4,128)S(1)} %bitcast.29), channel_id=1, source_target_pairs={{0,1},{1,0},{2,3},{3,2},{4,5},{5,4},{6,7},{7,6},{8,9},{9,8},{10,11... | collective-permute-start | bytes 393224 | tf_op jit(solution)/shard_map/ppermute | solution.py:60
  24.9 6.4 %collective-permute-start.5 = (bf16[4,64,512]{2,1,0:T(8,128)(2,1)S(1)}, bf16[4,64,512]{2,1,0:T(8,128)(2,1)S(1)}, u32[]{:S(2)}, u32[]{:S(2)}) collective-permute-start(bf16[4,64,512]{2,1,0:T(8,128)(2,1)S(1)} %pad_maximum_fusion.3), channel_id=1, source_target_pairs={{0,4},{1,9},{2,6},{3,11},{4,0},{5,13},{6,2},{7,15},{8,12},{9,1},{1... | collective-permute-start | bytes 786440 | tf_op jit(solution)/shard_map/ppermute | solution.py:78
  31.4 9.2 %collective-permute-start.6 = (bf16[8,64,512]{2,1,0:T(8,128)(2,1)S(1)}, bf16[8,64,512]{2,1,0:T(8,128)(2,1)S(1)}, u32[]{:S(2)}, u32[]{:S(2)}) collective-permute-start(bf16[8,64,512]{2,1,0:T(8,128)(2,1)S(1)} %pad_maximum_fusion.near_ref), channel_id=1, source_target_pairs={{0,2},{1,5},{2,0},{3,7},{4,6},{5,1},{6,4},{7,3},{8,10},{9,13},{10,... | collective-permute-start | bytes 1572872 | tf_op jit(solution)/shard_map/ppermute | solution.py:78
  32.5 8.1 %collective-permute-start.9 = (bf16[1,8,64,512]{3,2,1,0:T(8,128)(2,1)S(1)}, bf16[1,8,64,512]{3,2,1,0:T(8,128)(2,1)S(1)}, u32[]{:S(2)}, u32[]{:S(2)}) collective-permute-start(bf16[1,8,64,512]{3,2,1,0:T(8,128)(2,1)S(1)} %bitcast.26), channel_id=1, source_target_pairs={{0,1},{1,0},{2,3},{3,2},{4,5},{5,4},{6,7},{7,6},{8,9},{9,8},{10,11... | collective-permute-start | bytes 1572872 | tf_op jit(solution)/shard_map/ppermute | solution.py:60
  40.6 2.0 %collective-permute-start.8 = (bf16[1,8,64,512]{3,2,1,0:T(8,128)(2,1)S(1)}, bf16[1,8,64,512]{3,2,1,0:T(8,128)(2,1)S(1)}, u32[]{:S(2)}, u32[]{:S(2)}) collective-permute-start(bf16[1,8,64,512]{3,2,1,0:T(8,128)(2,1)S(1)} %bitcast.32), channel_id=1, source_target_pairs={{0,1},{1,0},{2,3},{3,2},{4,5},{5,4},{6,7},{7,6},{8,9},{9,8},{10,11... | collective-permute-start | bytes 1572872 | tf_op jit(solution)/shard_map/ppermute | solution.py:60
  44.7 5.5 %collective-permute-start.10 = (bf16[1,64,512]{2,1,0:T(8,128)(2,1)S(1)}, bf16[1,64,512]{2,1,0:T(8,128)(2,1)S(1)}, u32[]{:S(2)}, u32[]{:S(2)}) collective-permute-start(bf16[1,64,512]{2,1,0:T(8,128)(2,1)S(1)} %bitcast.22), channel_id=1, source_target_pairs={{0,16},{1,17},{2,18},{3,19},{4,20},{5,21},{6,22},{7,23},{8,24},{9,... | collective-permute-start | bytes 196616 | tf_op jit(solution)/shard_map/ppermute | solution.py:78
  50.2 5.1 %collective-permute-start.11 = (bf16[2,64,512]{2,1,0:T(8,128)(2,1)S(1)}, bf16[2,64,512]{2,1,0:T(8,128)(2,1)S(1)}, u32[]{:S(2)}, u32[]{:S(2)}) collective-permute-start(bf16[2,64,512]{2,1,0:T(8,128)(2,1)S(1)} %pad_maximum_fusion.6), channel_id=1, source_target_pairs={{0,8},{1,3},{2,10},{3,1},{4,12},{5,7},{6,14},{7,5},{8,0},{9,11},{1... | collective-permute-start | bytes 393224 | tf_op jit(solution)/shard_map/ppermute | solution.py:78
  55.4 6.4 %collective-permute-start.12 = (bf16[4,64,512]{2,1,0:T(8,128)(2,1)S(1)}, bf16[4,64,512]{2,1,0:T(8,128)(2,1)S(1)}, u32[]{:S(2)}, u32[]{:S(2)}) collective-permute-start(bf16[4,64,512]{2,1,0:T(8,128)(2,1)S(1)} %pad_maximum_fusion.4), channel_id=1, source_target_pairs={{0,4},{1,9},{2,6},{3,11},{4,0},{5,13},{6,2},{7,15},{8,12},{9,1},{1... | collective-permute-start | bytes 786440 | tf_op jit(solution)/shard_map/ppermute | solution.py:78
  61.9 2.6 %collective-permute-start.14 = (bf16[1,8,64,512]{3,2,1,0:T(8,128)(2,1)S(1)}, bf16[1,8,64,512]{3,2,1,0:T(8,128)(2,1)S(1)}, u32[]{:S(2)}, u32[]{:S(2)}) collective-permute-start(bf16[1,8,64,512]{3,2,1,0:T(8,128)(2,1)S(1)} %get-tuple-element.50), channel_id=1, source_target_pairs={{0,1},{1,0},{2,3},{3,2},{4,5},{5,4},{6,7},{7,6},{8,9},{9,8},{10,11... | collective-permute-start | bytes 1572872 | tf_op jit(solution)/shard_map/ppermute | solution.py:60
  62.0 9.6 %collective-permute-start.13 = (bf16[8,64,512]{2,1,0:T(8,128)(2,1)S(1)}, bf16[8,64,512]{2,1,0:T(8,128)(2,1)S(1)}, u32[]{:S(2)}, u32[]{:S(2)}) collective-permute-start(bf16[8,64,512]{2,1,0:T(8,128)(2,1)S(1)} %get-tuple-element.51.near_ref), channel_id=1, source_target_pairs={{0,2},{1,5},{2,0},{3,7},{4,6},{5,1},{6,4},{7,3},{8,10},{9,13},{10,... | collective-permute-start | bytes 1572872 | tf_op jit(solution)/shard_map/ppermute | solution.py:78
  66.4 29.4 %copy-start = (f32[64,512]{1,0:T(8,128)S(1)}, f32[64,512]{1,0:T(8,128)}, u32[]{:S(2)}) copy-start(f32[64,512]{1,0:T(8,128)} %start_ref.1) | copy-start | bytes 393220
  71.6 1.9 %collective-permute-start.15 = (bf16[1,8,64,512]{3,2,1,0:T(8,128)(2,1)S(1)}, bf16[1,8,64,512]{3,2,1,0:T(8,128)(2,1)S(1)}, u32[]{:S(2)}, u32[]{:S(2)}) collective-permute-start(bf16[1,8,64,512]{3,2,1,0:T(8,128)(2,1)S(1)} %bitcast.33), channel_id=1, source_target_pairs={{0,1},{1,0},{2,3},{3,2},{4,5},{5,4},{6,7},{7,6},{8,9},{9,8},{10,11... | collective-permute-start | bytes 1572872 | tf_op jit(solution)/shard_map/ppermute | solution.py:60
  76.3 18.6 %collective-permute-start.21 = (f32[1,128,512]{2,1,0:T(8,128)S(1)}, f32[1,128,512]{2,1,0:T(8,128)S(1)}, u32[]{:S(2)}, u32[]{:S(2)}) collective-permute-start(f32[1,128,512]{2,1,0:T(8,128)S(1)} %bitcast.38), channel_id=1, source_target_pairs={{0,1},{1,0},{2,3},{3,2},{4,5},{5,4},{6,7},{7,6},{8,9},{9,8},{10,11... | collective-permute-start | bytes 786440 | tf_op jit(solution)/shard_map/ppermute | solution.py:60
  76.5 1.4 %collective-permute-start.16 = (f32[72,128]{1,0:T(8,128)S(1)}, f32[72,128]{1,0:T(8,128)S(1)}, u32[]{:S(2)}, u32[]{:S(2)}) collective-permute-start(f32[72,128]{1,0:T(8,128)S(1)} %get-tuple-element.47), channel_id=1, source_target_pairs={{0,1},{1,0},{2,3},{3,2},{4,5},{5,4},{6,7},{7,6},{8,9},{9,8},{10,11... | collective-permute-start | bytes 110600 | tf_op jit(solution)/shard_map/ppermute | solution.py:60
  78.0 4.9 %collective-permute-start.17 = (f32[72,128]{1,0:T(8,128)S(1)}, f32[72,128]{1,0:T(8,128)S(1)}, u32[]{:S(2)}, u32[]{:S(2)}) collective-permute-start(f32[72,128]{1,0:T(8,128)S(1)} %add.19), channel_id=1, source_target_pairs={{0,16},{1,5},{2,18},{3,7},{4,20},{5,1},{6,22},{7,3},{8,24},{9,13},... | collective-permute-start | bytes 110600 | tf_op jit(solution)/shard_map/ppermute | solution.py:78
  82.8 4.0 %collective-permute-start.18 = (f32[72,128]{1,0:T(8,128)S(1)}, f32[72,128]{1,0:T(8,128)S(1)}, u32[]{:S(2)}, u32[]{:S(2)}) collective-permute-start(f32[72,128]{1,0:T(8,128)S(1)} %add.20), channel_id=1, source_target_pairs={{0,8},{1,3},{2,10},{3,1},{4,12},{5,7},{6,14},{7,5},{8,0},{9,11},{1... | collective-permute-start | bytes 110600 | tf_op jit(solution)/shard_map/ppermute | solution.py:78
  86.8 4.0 %collective-permute-start.19 = (f32[72,128]{1,0:T(8,128)S(1)}, f32[72,128]{1,0:T(8,128)S(1)}, u32[]{:S(2)}, u32[]{:S(2)}) collective-permute-start(f32[72,128]{1,0:T(8,128)S(1)} %add.21), channel_id=1, source_target_pairs={{0,4},{1,17},{2,6},{3,19},{4,0},{5,21},{6,2},{7,23},{8,12},{9,25},... | collective-permute-start | bytes 110600 | tf_op jit(solution)/shard_map/ppermute | solution.py:78
  90.8 4.2 %collective-permute-start.20 = (f32[72,128]{1,0:T(8,128)S(1)}, f32[72,128]{1,0:T(8,128)S(1)}, u32[]{:S(2)}, u32[]{:S(2)}) collective-permute-start(f32[72,128]{1,0:T(8,128)S(1)} %add.22), channel_id=1, source_target_pairs={{0,2},{1,9},{2,0},{3,11},{4,6},{5,13},{6,4},{7,15},{8,10},{9,1},{1... | collective-permute-start | bytes 110600 | tf_op jit(solution)/shard_map/ppermute | solution.py:78

commit v11 on v10

--- a/solution.py
+++ b/solution.py
@@ -78,12 +78,14 @@
     return lax.ppermute(block, ("region", "tile"), route)
 
 
-def sum_regions(block):
+def sum_regions(block, later):
     bits, _ = region_orders(lax.axis_size("region"))
     middle = len(bits) // 2
-    for even, odd in zip(bits, bits[middle:] + bits[:middle]):
+    for step, (even, odd) in enumerate(zip(bits, bits[middle:] + bits[:middle])):
+        if step == len(bits) - 1:
+            block, later = lax.optimization_barrier((block, later))
         block = block + swap_regions(block, even, odd)
-    return block
+    return block, later
 
 
 def region_orders(count):
@@ -283,7 +285,7 @@
         scratch_shapes=[pltpu.VMEM((n, local), jnp.bfloat16)],
         compiler_params=pltpu.CompilerParams(vmem_limit_bytes=VMEM),
         cost_estimate=pl.CostEstimate(
-            flops=6 * n * local * block.shape[0], bytes_accessed=4 * n * local, transcendentals=0
+            flops=20 * n * local * block.shape[0], bytes_accessed=4 * n * local, transcendentals=0
         ),
         name="unsort",
     )(device, rank, block)
@@ -565,11 +567,6 @@
     )(left, right)
 
 
-def reciprocal(value):
-    root = lax.rsqrt(value)
-    return root * root
-
-
 def small_product(left, right):
     return [[sum(l * r[j] for l, r in zip(row, right)) for j in range(len(right[0]))] for row in left]
 
@@ -580,7 +577,7 @@
 
 def small_inverse(matrix):
     (a, b), (c, d) = matrix
-    scale = reciprocal(a * d - b * c)
+    scale = 1.0 / (a * d - b * c)
     return [[d * scale, -b * scale], [-c * scale, a * scale]]
 
 
@@ -684,10 +681,10 @@
 
     image, image_rounded = operate(rounded, start)
     second, _, grams = operate(image_rounded, image, first_grams(start, image))
-    grams = sum_regions(sum_tiles(grams))
     near, far = halves(jnp.concatenate([image, second], axis=0), "tile")
-    images = unsort(device, rank, jnp.concatenate([*near, *far], axis=1))
-    return last_step(grams, innovations, images)
+    images = jnp.concatenate([*near, *far], axis=1)
+    grams, images = sum_regions(sum_tiles(grams), images)
+    return last_step(grams, innovations, unsort(device, rank, images))
 
 
 def solution(mesh):

time: 104 us -> 103 us (level)
  starting transfers between devices: 32.8 us -> 21.3 us
  waiting for transfers between devices: 38.8 us -> 49.9 us
    ppermute x12, starting transfers between devices: 27.2 us -> 13.4 us  [swap_regions(): return lax.ppermute(block, ('region', 'tile'), route)]
    ppermute x12, waiting for transfers between devices: 28.5 us -> 38.9 us  [swap_regions(): return lax.ppermute(block, ('region', 'tile'), route)]
    all_to_all x1, starting transfers between devices: 3.88 us -> 6.2 us  [shards(): everywhere = lax.all_to_all(everywhere, 'region', 0, 0)]
  transfers between devices with their start and end apart: 23 -> 23, of which waited for: 15 -> 16; matrix products, arithmetic and copies ran while one was open for 1% -> 1% of each run, Pallas kernels for 13% -> 14%
where the time goes in v11:
time: 103 us
  waiting for transfers between devices  49.9 us (48%)
  Pallas kernels  30.3 us (29%)
  starting transfers between devices  21.3 us (21%)
    ppermute x12, waiting for transfers between devices, swap_regions(): return lax.ppermute(block, ('region', 'tile'), route)  38.9 us
    ppermute x12, starting transfers between devices, swap_regions(): return lax.ppermute(block, ('region', 'tile'), route)  13.4 us
    pallas_call x2, Pallas kernels, build_tiles(): pl.pallas_call(functools.partial(build_kernel, part), out_shape=tuple((ja...  9 us
    pallas_call x4, Pallas kernels, apply_tiles(): pl.pallas_call(functools.partial(apply_kernel, start is not None, last, g...  8.9 us
    pallas_call x1, Pallas kernels, last_step(): pl.pallas_call(last_kernel, out_shape=(jax.ShapeDtypeStruct(start.shape,...  7.55 us
    all_to_all x1, starting transfers between devices, shards(): everywhere = lax.all_to_all(everywhere, 'region', 0, 0)  6.2 us
    all_to_all x1, waiting for transfers between devices, shards(): everywhere = lax.all_to_all(everywhere, 'region', 0, 0)  5.78 us
    ppermute x10, waiting for transfers between devices, swapped(): lax.ppermute(block, axis, [(i, i ^ bit) for i in range(lax.axis_size(axis...  5.23 us
  transfers between devices with their start and end apart: 23, of which 16 were waited for; matrix products, arithmetic and copies ran while one was open for 1% of the time, Pallas kernels for 14%

profile of v11, /device:TPU:0, one launch (start us, length us, event | category | flops | bytes accessed | tf_op | source)
XLA Modules:
  0.0 103.3 jit_solution(13629927718749386430)
XLA Ops:
  0.6 0.5 collective-permute-start.2
  1.1 0.1 collective-permute-start
  1.2 0.4 collective-permute-start.1
  1.7 1.0 collective-permute-done.1.far_error_ref
  2.7 0.0 collective-permute-done.far_ref
  2.7 0.0 collective-permute-done.2.other_ref
  2.7 3.4 %sort_region.1 = (bf16[64,512]{1,0:T(8,128)(2,1)S(1)}, f32[4,512]{1,0:T(4,128)S(1)}, f32[8,512]{1,0:T(8,128)S(1)}, f32[64,512]{1,0:T(8,128)S(1)}, s32[1,512]{1,0:T(1,128)S(1)}) custom-call(s32[1]{0:T(128)} %bitcast.device_ref, s32[1,7]{1,0:T(1,128)} %owner_ref.1, f32[1,3,512]{2,1,0:T(4,128)} %bitcast.41, f32[1,3,512]{2,1,0:T(4,128)S(1)} %collective-permute-done.far_ref, ...), custom_call_target="tpu_custom_call" | custom-call | flops 226492416 | bytes 2097152 | tf_op jit(solution)/shard_map/sort_region/pallas_call | solution.py:240
  6.1 4.0 %collective-permute-start.3 = (bf16[1,64,512]{2,1,0:T(8,128)(2,1)S(1)}, bf16[1,64,512]{2,1,0:T(8,128)(2,1)S(1)}, u32[]{:S(2)}, u32[]{:S(2)}) collective-permute-start(bf16[1,64,512]{2,1,0:T(8,128)(2,1)S(1)} %bitcast.18), channel_id=1, source_target_pairs={{0,16},{1,17},{2,18},{3,19},{4,20},{5,21},{6,22},{7,23},{8,24},{9,... | collective-permute-start | bytes 196616 | tf_op jit(solution)/shard_map/ppermute | solution.py:78
  10.1 0.7 broadcast_in_dim.39
  10.8 6.2 %all-to-all-start = ((f32[16,4,512]{2,1,0:T(4,128)}), f32[16,4,512]{2,1,0:T(4,128)S(1)}, u32[]{:S(2)}, u32[]{:S(2)}) async-start(f32[16,4,512]{2,1,0:T(4,128)} %broadcast_in_dim.39), calls=%async_computation | async-start | bytes 262144 | tf_op jit(solution)/shard_map/all_to_all | solution.py:654
  17.0 0.0 collective-permute-done.3
  17.0 2.0 %collective-permute-start.4 = (bf16[2,64,512]{2,1,0:T(8,128)(2,1)S(1)}, bf16[2,64,512]{2,1,0:T(8,128)(2,1)S(1)}, u32[]{:S(2)}, u32[]{:S(2)}) collective-permute-start(bf16[2,64,512]{2,1,0:T(8,128)(2,1)S(1)} %pad_maximum_fusion.5), channel_id=1, source_target_pairs={{0,8},{1,3},{2,10},{3,1},{4,12},{5,7},{6,14},{7,5},{8,0},{9,11},{1... | collective-permute-start | bytes 393224 | tf_op jit(solution)/shard_map/ppermute | solution.py:78
  19.0 5.8 %all-to-all-done = f32[16,4,512]{2,1,0:T(4,128)S(1)} async-done(((f32[16,4,512]{2,1,0:T(4,128)}), f32[16,4,512]{2,1,0:T(4,128)S(1)}, u32[]{:S(2)}, u32[]{:S(2)}) %all-to-all-start) | async-done | bytes 131104 | tf_op jit(solution)/shard_map/all_to_all | solution.py:654
  24.8 0.0 collective-permute-start.7
  24.8 0.0 collective-permute-done.4
  24.8 0.8 collective-permute-start.5
  25.6 0.5 collective-permute-done.7.other_ref
  26.1 4.7 %build_tiles.3 = (s32[548]{0:T(1024)S(1)}, s32[1]{0:T(128)}, bf16[136,64,512]{2,1,0:T(8,128)(2,1)S(1)}) custom-call(s32[1]{0:T(128)} %bitcast.device_ref, f32[8,512]{1,0:T(8,128)S(1)} %get-tuple-element.29.own_ref, f32[1,16,4,512]{3,2,1,0:T(4,128)S(1)} %bitcast.30, f32[1,16,4,512]{3,2,1,0:T(4,128)S(1)} %collective-permute-done.7.other_ref), custom_call_target="tpu_custom_call" | custom-call | flops 8388608000 | bytes 4194304 | tf_op jit(solution)/shard_map/build_tiles/pallas_call | solution.py:426
  30.9 0.4 collective-permute-done.5
  31.3 0.1 pad_maximum_fusion.near_ref
  31.3 1.2 %collective-permute-start.6 = (bf16[8,64,512]{2,1,0:T(8,128)(2,1)S(1)}, bf16[8,64,512]{2,1,0:T(8,128)(2,1)S(1)}, u32[]{:S(2)}, u32[]{:S(2)}) collective-permute-start(bf16[8,64,512]{2,1,0:T(8,128)(2,1)S(1)} %pad_maximum_fusion.near_ref), channel_id=1, source_target_pairs={{0,2},{1,5},{2,0},{3,7},{4,6},{5,1},{6,4},{7,3},{8,10},{9,13},{10,... | collective-permute-start | bytes 1572872 | tf_op jit(solution)/shard_map/ppermute | solution.py:78
  32.5 0.0 collective-permute-start.9
  32.5 4.3 %build_tiles.2 = (s32[548]{0:T(1024)S(1)}, s32[1]{0:T(128)}, bf16[136,64,512]{2,1,0:T(8,128)(2,1)S(1)}) custom-call(s32[1]{0:T(128)} %bitcast.device_ref, f32[8,512]{1,0:T(8,128)S(1)} %get-tuple-element.29.own_ref, f32[1,16,4,512]{3,2,1,0:T(4,128)S(1)} %bitcast.31, f32[1,16,4,512]{3,2,1,0:T(4,128)S(1)} %collective-permute-done.7.other_ref), custom_call_target="tpu_custom_call" | custom-call | flops 8388608000 | bytes 4194304 | tf_op jit(solution)/shard_map/build_tiles/pallas_call | solution.py:426
  36.8 3.8 %collective-permute-done.6.near_ref = bf16[8,64,512]{2,1,0:T(8,128)(2,1)S(1)} collective-permute-done((bf16[8,64,512]{2,1,0:T(8,128)(2,1)S(1)}, bf16[8,64,512]{2,1,0:T(8,128)(2,1)S(1)}, u32[]{:S(2)}, u32[]{:S(2)}) %collective-permute-start.6) | collective-permute-done | bytes 524320 | tf_op jit(solution)/shard_map/ppermute | solution.py:78
  40.6 0.0 collective-permute-start.8
  40.6 0.0 collective-permute-done.9
  40.6 2.0 %apply_first.2.refs_0_ = f32[512,64]{1,0:T(8,128)S(1)} custom-call(s32[548]{0:T(1024)S(1)} %get-tuple-element.39.ids_ref, s32[1]{0:T(128)} %get-tuple-element.40.count_ref, bf16[8,64,512]{2,1,0:T(8,128)(2,1)S(1)} %pad_maximum_fusion.near_ref, bf16[8,64,512]{2,1,0:T(8,128)(2,1)S(1)} %bitcast.34, bf16[136,64,512]{2,1,0:T(8,128)(2,1)S(1)} %get-tuple-element.42.tiles_ref), custom_call_target="tpu_custom_call" | custom-call | flops 3145728000 | bytes 4194304 | tf_op jit(solution)/shard_map/apply_first/pallas_call | solution.py:516
  42.6 0.0 collective-permute-done.8
  42.6 2.1 %apply_last.2 = (f32[64,512]{1,0:T(8,128)S(1)}, bf16[64,512]{1,0:T(8,128)(2,1)S(1)}) custom-call(s32[548]{0:T(1024)S(1)} %get-tuple-element.33.ids_ref, s32[1]{0:T(128)} %get-tuple-element.34.count_ref, bf16[8,64,512]{2,1,0:T(8,128)(2,1)S(1)} %collective-permute-done.6.near_ref, bf16[8,64,512]{2,1,0:T(8,128)(2,1)S(1)} %bitcast.35, ...), custom_call_target="tpu_custom_call" | custom-call | flops 3145728000 | bytes 4194304 | tf_op jit(solution)/shard_map/apply_last/pallas_call | solution.py:516
  44.7 1.9 %collective-permute-start.10 = (bf16[1,64,512]{2,1,0:T(8,128)(2,1)S(1)}, bf16[1,64,512]{2,1,0:T(8,128)(2,1)S(1)}, u32[]{:S(2)}, u32[]{:S(2)}) collective-permute-start(bf16[1,64,512]{2,1,0:T(8,128)(2,1)S(1)} %bitcast.22), channel_id=1, source_target_pairs={{0,16},{1,17},{2,18},{3,19},{4,20},{5,21},{6,22},{7,23},{8,24},{9,... | collective-permute-start | bytes 196616 | tf_op jit(solution)/shard_map/ppermute | solution.py:78
  46.7 0.7 first_grams.1.refs_3_
  47.3 4.3 %collective-permute-done.10 = bf16[1,64,512]{2,1,0:T(8,128)(2,1)S(1)} collective-permute-done((bf16[1,64,512]{2,1,0:T(8,128)(2,1)S(1)}, bf16[1,64,512]{2,1,0:T(8,128)(2,1)S(1)}, u32[]{:S(2)}, u32[]{:S(2)}) %collective-permute-start.10) | collective-permute-done | bytes 65568 | tf_op jit(solution)/shard_map/ppermute | solution.py:78
  51.6 0.1 collective-permute-start.11
  51.7 5.0 %collective-permute-done.11 = bf16[2,64,512]{2,1,0:T(8,128)(2,1)S(1)} collective-permute-done((bf16[2,64,512]{2,1,0:T(8,128)(2,1)S(1)}, bf16[2,64,512]{2,1,0:T(8,128)(2,1)S(1)}, u32[]{:S(2)}, u32[]{:S(2)}) %collective-permute-start.11) | collective-permute-done | bytes 131104 | tf_op jit(solution)/shard_map/ppermute | solution.py:78
  56.7 0.1 collective-permute-start.12
  56.7 6.4 %collective-permute-done.12 = bf16[4,64,512]{2,1,0:T(8,128)(2,1)S(1)} collective-permute-done((bf16[4,64,512]{2,1,0:T(8,128)(2,1)S(1)}, bf16[4,64,512]{2,1,0:T(8,128)(2,1)S(1)}, u32[]{:S(2)}, u32[]{:S(2)}) %collective-permute-start.12) | collective-permute-done | bytes 262176 | tf_op jit(solution)/shard_map/ppermute | solution.py:78
  63.1 0.1 fusion
  63.2 0.1 collective-permute-start.14
  63.3 1.2 %collective-permute-start.13 = (bf16[8,64,512]{2,1,0:T(8,128)(2,1)S(1)}, bf16[8,64,512]{2,1,0:T(8,128)(2,1)S(1)}, u32[]{:S(2)}, u32[]{:S(2)}) collective-permute-start(bf16[8,64,512]{2,1,0:T(8,128)(2,1)S(1)} %get-tuple-element.55.near_ref), channel_id=1, source_target_pairs={{0,2},{1,5},{2,0},{3,7},{4,6},{5,1},{6,4},{7,3},{8,10},{9,13},{10,... | collective-permute-start | bytes 1572872 | tf_op jit(solution)/shard_map/ppermute | solution.py:78
  64.4 0.7 collective-permute-done.14
  65.2 2.0 %apply_first.3.refs_0_ = f32[512,64]{1,0:T(8,128)S(1)} custom-call(s32[548]{0:T(1024)S(1)} %get-tuple-element.39.ids_ref, s32[1]{0:T(128)} %get-tuple-element.40.count_ref, bf16[8,64,512]{2,1,0:T(8,128)(2,1)S(1)} %get-tuple-element.55.near_ref, bf16[8,64,512]{2,1,0:T(8,128)(2,1)S(1)} %bitcast.37, bf16[136,64,512]{2,1,0:T(8,128)(2,1)S(1)} %get-tuple-element.42.tiles_ref), custom_call_target="tpu_custom_call" | custom-call | flops 3145728000 | bytes 4194304 | tf_op jit(solution)/shard_map/apply_first/pallas_call | solution.py:516
  67.2 5.4 %collective-permute-done.13.near_ref = bf16[8,64,512]{2,1,0:T(8,128)(2,1)S(1)} collective-permute-done((bf16[8,64,512]{2,1,0:T(8,128)(2,1)S(1)}, bf16[8,64,512]{2,1,0:T(8,128)(2,1)S(1)}, u32[]{:S(2)}, u32[]{:S(2)}) %collective-permute-start.13) | collective-permute-done | bytes 524320 | tf_op jit(solution)/shard_map/ppermute | solution.py:78
  72.5 0.0 collective-permute-start.15
  72.5 1.9 %collective-permute-done.15 = bf16[1,8,64,512]{3,2,1,0:T(8,128)(2,1)S(1)} collective-permute-done((bf16[1,8,64,512]{3,2,1,0:T(8,128)(2,1)S(1)}, bf16[1,8,64,512]{3,2,1,0:T(8,128)(2,1)S(1)}, u32[]{:S(2)}, u32[]{:S(2)}) %collective-permute-start.15) | collective-permute-done | bytes 524320 | tf_op jit(solution)/shard_map/ppermute | solution.py:60
  74.4 0.0 copy-start
  74.4 2.8 %apply_last.3 = (f32[64,512]{1,0:T(8,128)S(1)}, bf16[64,512]{1,0:T(8,128)(2,1)}, f32[72,128]{1,0:T(8,128)S(1)}) custom-call(s32[548]{0:T(1024)S(1)} %get-tuple-element.33.ids_ref, s32[1]{0:T(128)} %get-tuple-element.34.count_ref, bf16[8,64,512]{2,1,0:T(8,128)(2,1)S(1)} %collective-permute-done.13.near_ref, bf16[8,64,512]{2,1,0:T(8,128)(2,1)S(1)} %bitcast.36, ...), custom_call_target="tpu_custom_call" | custom-call | flops 3145728000 | bytes 4194304 | tf_op jit(solution)/shard_map/apply_last/pallas_call | solution.py:516
  77.3 0.2 collective-permute-start.20
  77.5 0.4 collective-permute-start.16
  77.8 1.1 %collective-permute-done.16 = f32[72,128]{1,0:T(8,128)S(1)} collective-permute-done((f32[72,128]{1,0:T(8,128)S(1)}, f32[72,128]{1,0:T(8,128)S(1)}, u32[]{:S(2)}, u32[]{:S(2)}) %collective-permute-start.16) | collective-permute-done | bytes 36896 | tf_op jit(solution)/shard_map/ppermute | solution.py:60
  78.9 0.8 collective-permute-start.17
  79.8 4.0 %collective-permute-done.17 = f32[72,128]{1,0:T(8,128)S(1)} collective-permute-done((f32[72,128]{1,0:T(8,128)S(1)}, f32[72,128]{1,0:T(8,128)S(1)}, u32[]{:S(2)}, u32[]{:S(2)}) %collective-permute-start.17) | collective-permute-done | bytes 36896 | tf_op jit(solution)/shard_map/ppermute | solution.py:78
  83.8 0.0 collective-permute-start.18
  83.8 3.9 %collective-permute-done.18 = f32[72,128]{1,0:T(8,128)S(1)} collective-permute-done((f32[72,128]{1,0:T(8,128)S(1)}, f32[72,128]{1,0:T(8,128)S(1)}, u32[]{:S(2)}, u32[]{:S(2)}) %collective-permute-start.18) | collective-permute-done | bytes 36896 | tf_op jit(solution)/shard_map/ppermute | solution.py:78
  87.7 0.0 collective-permute-start.19
  87.8 3.9 %collective-permute-done.19 = f32[72,128]{1,0:T(8,128)S(1)} collective-permute-done((f32[72,128]{1,0:T(8,128)S(1)}, f32[72,128]{1,0:T(8,128)S(1)}, u32[]{:S(2)}, u32[]{:S(2)}) %collective-permute-start.19) | collective-permute-done | bytes 36896 | tf_op jit(solution)/shard_map/ppermute | solution.py:78
  91.7 0.0 collective-permute-done.20
  91.8 1.4 %collective-permute-start.21 = (f32[72,128]{1,0:T(8,128)S(1)}, f32[72,128]{1,0:T(8,128)S(1)}, u32[]{:S(2)}, u32[]{:S(2)}) collective-permute-start(f32[72,128]{1,0:T(8,128)S(1)} %add.22), channel_id=1, source_target_pairs={{0,2},{1,9},{2,0},{3,11},{4,6},{5,13},{6,4},{7,15},{8,10},{9,1},{1... | collective-permute-start | bytes 110600 | tf_op jit(solution)/shard_map/ppermute | solution.py:78
  93.1 0.8 unsort.1.images_ref
  94.0 1.8 %collective-permute-done.21 = f32[72,128]{1,0:T(8,128)S(1)} collective-permute-done((f32[72,128]{1,0:T(8,128)S(1)}, f32[72,128]{1,0:T(8,128)S(1)}, u32[]{:S(2)}, u32[]{:S(2)}) %collective-permute-start.21) | collective-permute-done | bytes 36896 | tf_op jit(solution)/shard_map/ppermute | solution.py:78
  95.8 0.0 copy-done
  95.8 7.5 %last_step.1 = (f32[64,512]{1,0:T(8,128)}, f32[64,512]{1,0:T(8,128)}) custom-call(f32[72,128]{1,0:T(8,128)S(1)} %add.23.grams_ref, f32[64,512]{1,0:T(8,128)S(1)} %copy-done, f32[128,512]{1,0:T(8,128)S(1)} %unsort.1.images_ref), custom_call_target="tpu_custom_call" | custom-call | tf_op jit(solution)/shard_map/last_step/pallas_call | solution.py:630
  (13 shorter events, 0.2 us)
Async XLA Ops:
  0.6 2.1 %collective-permute-start.2 = (f32[1,64,512]{2,1,0:T(8,128)}, f32[1,64,512]{2,1,0:T(8,128)S(1)}, u32[]{:S(2)}, u32[]{:S(2)}) collective-permute-start(f32[1,64,512]{2,1,0:T(8,128)} %bitcast.27), channel_id=1, source_target_pairs={{0,1},{1,0},{2,3},{3,2},{4,5},{5,4},{6,7},{7,6},{8,9},{9,8},{10,11... | collective-permute-start | bytes 393224 | tf_op jit(solution)/shard_map/ppermute | solution.py:60
  1.1 1.5 %collective-permute-start = (f32[1,3,512]{2,1,0:T(4,128)}, f32[1,3,512]{2,1,0:T(4,128)S(1)}, u32[]{:S(2)}, u32[]{:S(2)}) collective-permute-start(f32[1,3,512]{2,1,0:T(4,128)} %bitcast.40), channel_id=1, source_target_pairs={{0,1},{1,0},{2,3},{3,2},{4,5},{5,4},{6,7},{7,6},{8,9},{9,8},{10,11... | collective-permute-start | bytes 18440 | tf_op jit(solution)/shard_map/ppermute | solution.py:60
  1.2 1.5 %collective-permute-start.1 = (f32[1,1,512]{2,1,0:T(1,128)}, f32[1,1,512]{2,1,0:T(1,128)S(1)}, u32[]{:S(2)}, u32[]{:S(2)}) collective-permute-start(f32[1,1,512]{2,1,0:T(1,128)} %bitcast.42), channel_id=1, source_target_pairs={{0,1},{1,0},{2,3},{3,2},{4,5},{5,4},{6,7},{7,6},{8,9},{9,8},{10,11... | collective-permute-start | bytes 6152 | tf_op jit(solution)/shard_map/ppermute | solution.py:60
  6.1 10.9 %collective-permute-start.3 = (bf16[1,64,512]{2,1,0:T(8,128)(2,1)S(1)}, bf16[1,64,512]{2,1,0:T(8,128)(2,1)S(1)}, u32[]{:S(2)}, u32[]{:S(2)}) collective-permute-start(bf16[1,64,512]{2,1,0:T(8,128)(2,1)S(1)} %bitcast.18), channel_id=1, source_target_pairs={{0,16},{1,17},{2,18},{3,19},{4,20},{5,21},{6,22},{7,23},{8,24},{9,... | collective-permute-start | bytes 196616 | tf_op jit(solution)/shard_map/ppermute | solution.py:78
  10.8 14.0 %all-to-all-start = ((f32[16,4,512]{2,1,0:T(4,128)}), f32[16,4,512]{2,1,0:T(4,128)S(1)}, u32[]{:S(2)}, u32[]{:S(2)}) async-start(f32[16,4,512]{2,1,0:T(4,128)} %broadcast_in_dim.39), calls=%async_computation | async-start | bytes 262144 | tf_op jit(solution)/shard_map/all_to_all | solution.py:654
  17.0 7.8 %collective-permute-start.4 = (bf16[2,64,512]{2,1,0:T(8,128)(2,1)S(1)}, bf16[2,64,512]{2,1,0:T(8,128)(2,1)S(1)}, u32[]{:S(2)}, u32[]{:S(2)}) collective-permute-start(bf16[2,64,512]{2,1,0:T(8,128)(2,1)S(1)} %pad_maximum_fusion.5), channel_id=1, source_target_pairs={{0,8},{1,3},{2,10},{3,1},{4,12},{5,7},{6,14},{7,5},{8,0},{9,11},{1... | collective-permute-start | bytes 393224 | tf_op jit(solution)/shard_map/ppermute | solution.py:78
  24.8 1.3 %collective-permute-start.7 = (f32[1,16,4,512]{3,2,1,0:T(4,128)S(1)}, f32[1,16,4,512]{3,2,1,0:T(4,128)S(1)}, u32[]{:S(2)}, u32[]{:S(2)}) collective-permute-start(f32[1,16,4,512]{3,2,1,0:T(4,128)S(1)} %bitcast.29), channel_id=1, source_target_pairs={{0,1},{1,0},{2,3},{3,2},{4,5},{5,4},{6,7},{7,6},{8,9},{9,8},{10,11... | collective-permute-start | bytes 393224 | tf_op jit(solution)/shard_map/ppermute | solution.py:60
  24.8 6.4 %collective-permute-start.5 = (bf16[4,64,512]{2,1,0:T(8,128)(2,1)S(1)}, bf16[4,64,512]{2,1,0:T(8,128)(2,1)S(1)}, u32[]{:S(2)}, u32[]{:S(2)}) collective-permute-start(bf16[4,64,512]{2,1,0:T(8,128)(2,1)S(1)} %pad_maximum_fusion.3), channel_id=1, source_target_pairs={{0,4},{1,9},{2,6},{3,11},{4,0},{5,13},{6,2},{7,15},{8,12},{9,1},{1... | collective-permute-start | bytes 786440 | tf_op jit(solution)/shard_map/ppermute | solution.py:78
  31.3 9.2 %collective-permute-start.6 = (bf16[8,64,512]{2,1,0:T(8,128)(2,1)S(1)}, bf16[8,64,512]{2,1,0:T(8,128)(2,1)S(1)}, u32[]{:S(2)}, u32[]{:S(2)}) collective-permute-start(bf16[8,64,512]{2,1,0:T(8,128)(2,1)S(1)} %pad_maximum_fusion.near_ref), channel_id=1, source_target_pairs={{0,2},{1,5},{2,0},{3,7},{4,6},{5,1},{6,4},{7,3},{8,10},{9,13},{10,... | collective-permute-start | bytes 1572872 | tf_op jit(solution)/shard_map/ppermute | solution.py:78
  32.5 8.1 %collective-permute-start.9 = (bf16[1,8,64,512]{3,2,1,0:T(8,128)(2,1)S(1)}, bf16[1,8,64,512]{3,2,1,0:T(8,128)(2,1)S(1)}, u32[]{:S(2)}, u32[]{:S(2)}) collective-permute-start(bf16[1,8,64,512]{3,2,1,0:T(8,128)(2,1)S(1)} %bitcast.26), channel_id=1, source_target_pairs={{0,1},{1,0},{2,3},{3,2},{4,5},{5,4},{6,7},{7,6},{8,9},{9,8},{10,11... | collective-permute-start | bytes 1572872 | tf_op jit(solution)/shard_map/ppermute | solution.py:60
  40.6 2.0 %collective-permute-start.8 = (bf16[1,8,64,512]{3,2,1,0:T(8,128)(2,1)S(1)}, bf16[1,8,64,512]{3,2,1,0:T(8,128)(2,1)S(1)}, u32[]{:S(2)}, u32[]{:S(2)}) collective-permute-start(bf16[1,8,64,512]{3,2,1,0:T(8,128)(2,1)S(1)} %bitcast.32), channel_id=1, source_target_pairs={{0,1},{1,0},{2,3},{3,2},{4,5},{5,4},{6,7},{7,6},{8,9},{9,8},{10,11... | collective-permute-start | bytes 1572872 | tf_op jit(solution)/shard_map/ppermute | solution.py:60
  44.7 6.9 %collective-permute-start.10 = (bf16[1,64,512]{2,1,0:T(8,128)(2,1)S(1)}, bf16[1,64,512]{2,1,0:T(8,128)(2,1)S(1)}, u32[]{:S(2)}, u32[]{:S(2)}) collective-permute-start(bf16[1,64,512]{2,1,0:T(8,128)(2,1)S(1)} %bitcast.22), channel_id=1, source_target_pairs={{0,16},{1,17},{2,18},{3,19},{4,20},{5,21},{6,22},{7,23},{8,24},{9,... | collective-permute-start | bytes 196616 | tf_op jit(solution)/shard_map/ppermute | solution.py:78
  51.6 5.0 %collective-permute-start.11 = (bf16[2,64,512]{2,1,0:T(8,128)(2,1)S(1)}, bf16[2,64,512]{2,1,0:T(8,128)(2,1)S(1)}, u32[]{:S(2)}, u32[]{:S(2)}) collective-permute-start(bf16[2,64,512]{2,1,0:T(8,128)(2,1)S(1)} %pad_maximum_fusion.6), channel_id=1, source_target_pairs={{0,8},{1,3},{2,10},{3,1},{4,12},{5,7},{6,14},{7,5},{8,0},{9,11},{1... | collective-permute-start | bytes 393224 | tf_op jit(solution)/shard_map/ppermute | solution.py:78
  56.7 6.4 %collective-permute-start.12 = (bf16[4,64,512]{2,1,0:T(8,128)(2,1)S(1)}, bf16[4,64,512]{2,1,0:T(8,128)(2,1)S(1)}, u32[]{:S(2)}, u32[]{:S(2)}) collective-permute-start(bf16[4,64,512]{2,1,0:T(8,128)(2,1)S(1)} %pad_maximum_fusion.4), channel_id=1, source_target_pairs={{0,4},{1,9},{2,6},{3,11},{4,0},{5,13},{6,2},{7,15},{8,12},{9,1},{1... | collective-permute-start | bytes 786440 | tf_op jit(solution)/shard_map/ppermute | solution.py:78
  63.2 2.0 %collective-permute-start.14 = (bf16[1,8,64,512]{3,2,1,0:T(8,128)(2,1)S(1)}, bf16[1,8,64,512]{3,2,1,0:T(8,128)(2,1)S(1)}, u32[]{:S(2)}, u32[]{:S(2)}) collective-permute-start(bf16[1,8,64,512]{3,2,1,0:T(8,128)(2,1)S(1)} %get-tuple-element.54), channel_id=1, source_target_pairs={{0,1},{1,0},{2,3},{3,2},{4,5},{5,4},{6,7},{7,6},{8,9},{9,8},{10,11... | collective-permute-start | bytes 1572872 | tf_op jit(solution)/shard_map/ppermute | solution.py:60
  63.3 9.2 %collective-permute-start.13 = (bf16[8,64,512]{2,1,0:T(8,128)(2,1)S(1)}, bf16[8,64,512]{2,1,0:T(8,128)(2,1)S(1)}, u32[]{:S(2)}, u32[]{:S(2)}) collective-permute-start(bf16[8,64,512]{2,1,0:T(8,128)(2,1)S(1)} %get-tuple-element.55.near_ref), channel_id=1, source_target_pairs={{0,2},{1,5},{2,0},{3,7},{4,6},{5,1},{6,4},{7,3},{8,10},{9,13},{10,... | collective-permute-start | bytes 1572872 | tf_op jit(solution)/shard_map/ppermute | solution.py:78
  72.5 1.9 %collective-permute-start.15 = (bf16[1,8,64,512]{3,2,1,0:T(8,128)(2,1)S(1)}, bf16[1,8,64,512]{3,2,1,0:T(8,128)(2,1)S(1)}, u32[]{:S(2)}, u32[]{:S(2)}) collective-permute-start(bf16[1,8,64,512]{3,2,1,0:T(8,128)(2,1)S(1)} %bitcast.33), channel_id=1, source_target_pairs={{0,1},{1,0},{2,3},{3,2},{4,5},{5,4},{6,7},{7,6},{8,9},{9,8},{10,11... | collective-permute-start | bytes 1572872 | tf_op jit(solution)/shard_map/ppermute | solution.py:60
  74.4 21.4 %copy-start = (f32[64,512]{1,0:T(8,128)S(1)}, f32[64,512]{1,0:T(8,128)}, u32[]{:S(2)}) copy-start(f32[64,512]{1,0:T(8,128)} %start_ref.1) | copy-start | bytes 393220
  77.3 14.5 %collective-permute-start.20 = (f32[1,128,512]{2,1,0:T(8,128)S(1)}, f32[1,128,512]{2,1,0:T(8,128)S(1)}, u32[]{:S(2)}, u32[]{:S(2)}) collective-permute-start(f32[1,128,512]{2,1,0:T(8,128)S(1)} %bitcast.38), channel_id=1, source_target_pairs={{0,1},{1,0},{2,3},{3,2},{4,5},{5,4},{6,7},{7,6},{8,9},{9,8},{10,11... | collective-permute-start | bytes 786440 | tf_op jit(solution)/shard_map/ppermute | solution.py:60
  77.5 1.4 %collective-permute-start.16 = (f32[72,128]{1,0:T(8,128)S(1)}, f32[72,128]{1,0:T(8,128)S(1)}, u32[]{:S(2)}, u32[]{:S(2)}) collective-permute-start(f32[72,128]{1,0:T(8,128)S(1)} %get-tuple-element.49), channel_id=1, source_target_pairs={{0,1},{1,0},{2,3},{3,2},{4,5},{5,4},{6,7},{7,6},{8,9},{9,8},{10,11... | collective-permute-start | bytes 110600 | tf_op jit(solution)/shard_map/ppermute | solution.py:60
  78.9 4.9 %collective-permute-start.17 = (f32[72,128]{1,0:T(8,128)S(1)}, f32[72,128]{1,0:T(8,128)S(1)}, u32[]{:S(2)}, u32[]{:S(2)}) collective-permute-start(f32[72,128]{1,0:T(8,128)S(1)} %add.19), channel_id=1, source_target_pairs={{0,16},{1,5},{2,18},{3,7},{4,20},{5,1},{6,22},{7,3},{8,24},{9,13},... | collective-permute-start | bytes 110600 | tf_op jit(solution)/shard_map/ppermute | solution.py:78
  83.8 4.0 %collective-permute-start.18 = (f32[72,128]{1,0:T(8,128)S(1)}, f32[72,128]{1,0:T(8,128)S(1)}, u32[]{:S(2)}, u32[]{:S(2)}) collective-permute-start(f32[72,128]{1,0:T(8,128)S(1)} %add.20), channel_id=1, source_target_pairs={{0,8},{1,3},{2,10},{3,1},{4,12},{5,7},{6,14},{7,5},{8,0},{9,11},{1... | collective-permute-start | bytes 110600 | tf_op jit(solution)/shard_map/ppermute | solution.py:78
  87.7 4.0 %collective-permute-start.19 = (f32[72,128]{1,0:T(8,128)S(1)}, f32[72,128]{1,0:T(8,128)S(1)}, u32[]{:S(2)}, u32[]{:S(2)}) collective-permute-start(f32[72,128]{1,0:T(8,128)S(1)} %add.21), channel_id=1, source_target_pairs={{0,4},{1,17},{2,6},{3,19},{4,0},{5,21},{6,2},{7,23},{8,12},{9,25},... | collective-permute-start | bytes 110600 | tf_op jit(solution)/shard_map/ppermute | solution.py:78
  91.8 4.0 %collective-permute-start.21 = (f32[72,128]{1,0:T(8,128)S(1)}, f32[72,128]{1,0:T(8,128)S(1)}, u32[]{:S(2)}, u32[]{:S(2)}) collective-permute-start(f32[72,128]{1,0:T(8,128)S(1)} %add.22), channel_id=1, source_target_pairs={{0,2},{1,9},{2,0},{3,11},{4,6},{5,13},{6,4},{7,15},{8,10},{9,1},{1... | collective-permute-start | bytes 110600 | tf_op jit(solution)/shard_map/ppermute | solution.py:78

commit v12 on v11

--- a/solution.py
+++ b/solution.py
@@ -81,7 +81,7 @@
 def sum_regions(block, later):
     bits, _ = region_orders(lax.axis_size("region"))
     middle = len(bits) // 2
-    for step, (even, odd) in enumerate(zip(bits, bits[middle:] + bits[:middle])):
+    for step, (even, odd) in enumerate(zip(bits[::-1], (bits[middle:] + bits[:middle])[::-1])):
         if step == len(bits) - 1:
             block, later = lax.optimization_barrier((block, later))
         block = block + swap_regions(block, even, odd)
@@ -444,6 +444,7 @@
     if last:
         first_ref = refs.pop(2) if grams else None
         block_ref, scale_ref, out_ref, rounded_ref = refs[:4]
+        gram_ref = rounded_ref
         total_ref = refs[-1]
     else:
         (total_ref,) = refs
@@ -484,9 +485,10 @@
         block = block_ref[...]
         result = jnp.transpose(total_ref[...]) + scale_ref[...] * block
         out_ref[...] = result
-        rounded_ref[...] = result.astype(jnp.bfloat16)
-        if grams:
-            refs[4][...] = jnp.concatenate([first_ref[...], packed_grams(block, result)], axis=1)
+        if not grams:
+            rounded_ref[...] = result.astype(jnp.bfloat16)
+        else:
+            gram_ref[...] = jnp.concatenate([first_ref[...], packed_grams(block, result)], axis=1)
 
 
 def apply_tiles(plan, near, far, tiles, start, finish):
@@ -506,10 +508,10 @@
         in_specs += whole_vmem(len(finish))
         out_shape = (
             jax.ShapeDtypeStruct((columns, local), jnp.float32),
-            jax.ShapeDtypeStruct((columns, local), jnp.bfloat16),
+            jax.ShapeDtypeStruct((columns + 8, 2 * columns), jnp.float32)
+            if grams
+            else jax.ShapeDtypeStruct((columns, local), jnp.bfloat16),
         )
-        if grams:
-            out_shape += (jax.ShapeDtypeStruct((columns + 8, 2 * columns), jnp.float32),)
         scratch.append(pltpu.VMEM((local, columns), jnp.float32))
     else:
         out_shape = (jax.ShapeDtypeStruct((local, columns), jnp.float32),)
@@ -680,7 +682,7 @@
         return results
 
     image, image_rounded = operate(rounded, start)
-    second, _, grams = operate(image_rounded, image, first_grams(start, image))
+    second, grams = operate(image_rounded, image, first_grams(start, image))
     near, far = halves(jnp.concatenate([image, second], axis=0), "tile")
     images = jnp.concatenate([*near, *far], axis=1)
     grams, images = sum_regions(sum_tiles(grams), images)

time: 103 us -> 104 us (level); the launches traced: 103 us -> 102 us
    all_to_all x1, starting transfers between devices: 6.2 us -> 5.04 us  [shards(): everywhere = lax.all_to_all(everywhere, 'region', 0, 0)]
where the time goes in v12:
time: 104 us; the launch traced here: 102 us
  waiting for transfers between devices  49.6 us (48%)
  Pallas kernels  30 us (29%)
  starting transfers between devices  20.8 us (20%)
    ppermute x12, waiting for transfers between devices, swap_regions(): return lax.ppermute(block, ('region', 'tile'), route)  38.6 us
    ppermute x12, starting transfers between devices, swap_regions(): return lax.ppermute(block, ('region', 'tile'), route)  14 us
    pallas_call x4, Pallas kernels, apply_tiles(): pl.pallas_call(functools.partial(apply_kernel, start is not None, last, g...  8.89 us
    pallas_call x2, Pallas kernels, build_tiles(): pl.pallas_call(functools.partial(build_kernel, part), out_shape=tuple((ja...  8.72 us
    pallas_call x1, Pallas kernels, last_step(): pl.pallas_call(last_kernel, out_shape=(jax.ShapeDtypeStruct(start.shape,...  7.55 us
    all_to_all x1, waiting for transfers between devices, shards(): everywhere = lax.all_to_all(everywhere, 'region', 0, 0)  5.78 us
    ppermute x10, waiting for transfers between devices, swapped(): lax.ppermute(block, axis, [(i, i ^ bit) for i in range(lax.axis_size(axis...  5.25 us
    all_to_all x1, starting transfers between devices, shards(): everywhere = lax.all_to_all(everywhere, 'region', 0, 0)  5.04 us
  transfers between devices with their start and end apart: 23, of which 16 were waited for; matrix products, arithmetic and copies ran while one was open for 1% of the time, Pallas kernels for 14%

profile of v12, /device:TPU:0, one launch (start us, length us, event | category | flops | bytes accessed | tf_op | source)
XLA Modules:
  0.0 102.2 jit_solution(5410590195503085671)
XLA Ops:
  0.6 0.5 collective-permute-start.2
  1.1 0.1 collective-permute-start
  1.2 0.4 collective-permute-start.1
  1.7 1.0 %collective-permute-done.1.far_error_ref = f32[1,1,512]{2,1,0:T(1,128)S(1)} collective-permute-done((f32[1,1,512]{2,1,0:T(1,128)}, f32[1,1,512]{2,1,0:T(1,128)S(1)}, u32[]{:S(2)}, u32[]{:S(2)}) %collective-permute-start.1) | collective-permute-done | bytes 2080 | tf_op jit(solution)/shard_map/ppermute | solution.py:60
  2.7 0.0 collective-permute-done.far_ref
  2.7 0.0 collective-permute-done.2.other_ref
  2.7 3.4 %sort_region.1 = (bf16[64,512]{1,0:T(8,128)(2,1)S(1)}, f32[4,512]{1,0:T(4,128)S(1)}, f32[8,512]{1,0:T(8,128)S(1)}, f32[64,512]{1,0:T(8,128)S(1)}, s32[1,512]{1,0:T(1,128)S(1)}) custom-call(s32[1]{0:T(128)} %bitcast.device_ref, s32[1,7]{1,0:T(1,128)} %owner_ref.1, f32[1,3,512]{2,1,0:T(4,128)} %bitcast.41, f32[1,3,512]{2,1,0:T(4,128)S(1)} %collective-permute-done.far_ref, ...), custom_call_target="tpu_custom_call" | custom-call | flops 226492416 | bytes 2097152 | tf_op jit(solution)/shard_map/sort_region/pallas_call | solution.py:240
  6.1 4.0 %collective-permute-start.3 = (bf16[1,64,512]{2,1,0:T(8,128)(2,1)S(1)}, bf16[1,64,512]{2,1,0:T(8,128)(2,1)S(1)}, u32[]{:S(2)}, u32[]{:S(2)}) collective-permute-start(bf16[1,64,512]{2,1,0:T(8,128)(2,1)S(1)} %bitcast.18), channel_id=1, source_target_pairs={{0,16},{1,17},{2,18},{3,19},{4,20},{5,21},{6,22},{7,23},{8,24},{9,... | collective-permute-start | bytes 196616 | tf_op jit(solution)/shard_map/ppermute | solution.py:78
  10.1 0.7 broadcast_in_dim.39
  10.8 5.0 %all-to-all-start = ((f32[16,4,512]{2,1,0:T(4,128)}), f32[16,4,512]{2,1,0:T(4,128)S(1)}, u32[]{:S(2)}, u32[]{:S(2)}) async-start(f32[16,4,512]{2,1,0:T(4,128)} %broadcast_in_dim.39), calls=%async_computation | async-start | bytes 262144 | tf_op jit(solution)/shard_map/all_to_all | solution.py:656
  15.8 0.0 collective-permute-done.3
  15.9 2.0 %collective-permute-start.4 = (bf16[2,64,512]{2,1,0:T(8,128)(2,1)S(1)}, bf16[2,64,512]{2,1,0:T(8,128)(2,1)S(1)}, u32[]{:S(2)}, u32[]{:S(2)}) collective-permute-start(bf16[2,64,512]{2,1,0:T(8,128)(2,1)S(1)} %pad_maximum_fusion.5), channel_id=1, source_target_pairs={{0,8},{1,3},{2,10},{3,1},{4,12},{5,7},{6,14},{7,5},{8,0},{9,11},{1... | collective-permute-start | bytes 393224 | tf_op jit(solution)/shard_map/ppermute | solution.py:78
  17.8 5.8 %all-to-all-done = f32[16,4,512]{2,1,0:T(4,128)S(1)} async-done(((f32[16,4,512]{2,1,0:T(4,128)}), f32[16,4,512]{2,1,0:T(4,128)S(1)}, u32[]{:S(2)}, u32[]{:S(2)}) %all-to-all-start) | async-done | bytes 131104 | tf_op jit(solution)/shard_map/all_to_all | solution.py:656
  23.6 0.0 collective-permute-start.7
  23.6 0.0 collective-permute-done.4
  23.7 0.8 collective-permute-start.5
  24.5 0.5 collective-permute-done.7.other_ref
  25.0 4.6 %build_tiles.3 = (s32[548]{0:T(1024)S(1)}, s32[1]{0:T(128)}, bf16[136,64,512]{2,1,0:T(8,128)(2,1)S(1)}) custom-call(s32[1]{0:T(128)} %bitcast.device_ref, f32[8,512]{1,0:T(8,128)S(1)} %get-tuple-element.29.own_ref, f32[1,16,4,512]{3,2,1,0:T(4,128)S(1)} %bitcast.30, f32[1,16,4,512]{3,2,1,0:T(4,128)S(1)} %collective-permute-done.7.other_ref), custom_call_target="tpu_custom_call" | custom-call | flops 8388608000 | bytes 4194304 | tf_op jit(solution)/shard_map/build_tiles/pallas_call | solution.py:426
  29.6 0.5 collective-permute-done.5
  30.1 0.1 pad_maximum_fusion.near_ref
  30.2 1.2 %collective-permute-start.6 = (bf16[8,64,512]{2,1,0:T(8,128)(2,1)S(1)}, bf16[8,64,512]{2,1,0:T(8,128)(2,1)S(1)}, u32[]{:S(2)}, u32[]{:S(2)}) collective-permute-start(bf16[8,64,512]{2,1,0:T(8,128)(2,1)S(1)} %pad_maximum_fusion.near_ref), channel_id=1, source_target_pairs={{0,2},{1,5},{2,0},{3,7},{4,6},{5,1},{6,4},{7,3},{8,10},{9,13},{10,... | collective-permute-start | bytes 1572872 | tf_op jit(solution)/shard_map/ppermute | solution.py:78
  31.3 0.0 collective-permute-start.9
  31.3 4.1 %build_tiles.2 = (s32[548]{0:T(1024)S(1)}, s32[1]{0:T(128)}, bf16[136,64,512]{2,1,0:T(8,128)(2,1)S(1)}) custom-call(s32[1]{0:T(128)} %bitcast.device_ref, f32[8,512]{1,0:T(8,128)S(1)} %get-tuple-element.29.own_ref, f32[1,16,4,512]{3,2,1,0:T(4,128)S(1)} %bitcast.31, f32[1,16,4,512]{3,2,1,0:T(4,128)S(1)} %collective-permute-done.7.other_ref), custom_call_target="tpu_custom_call" | custom-call | flops 8388608000 | bytes 4194304 | tf_op jit(solution)/shard_map/build_tiles/pallas_call | solution.py:426
  35.5 3.9 %collective-permute-done.6.near_ref = bf16[8,64,512]{2,1,0:T(8,128)(2,1)S(1)} collective-permute-done((bf16[8,64,512]{2,1,0:T(8,128)(2,1)S(1)}, bf16[8,64,512]{2,1,0:T(8,128)(2,1)S(1)}, u32[]{:S(2)}, u32[]{:S(2)}) %collective-permute-start.6) | collective-permute-done | bytes 524320 | tf_op jit(solution)/shard_map/ppermute | solution.py:78
  39.4 0.0 collective-permute-start.8
  39.4 0.0 collective-permute-done.9
  39.4 2.0 %apply_first.2.refs_0_ = f32[512,64]{1,0:T(8,128)S(1)} custom-call(s32[548]{0:T(1024)S(1)} %get-tuple-element.39.ids_ref, s32[1]{0:T(128)} %get-tuple-element.40.count_ref, bf16[8,64,512]{2,1,0:T(8,128)(2,1)S(1)} %pad_maximum_fusion.near_ref, bf16[8,64,512]{2,1,0:T(8,128)(2,1)S(1)} %bitcast.34, bf16[136,64,512]{2,1,0:T(8,128)(2,1)S(1)} %get-tuple-element.42.tiles_ref), custom_call_target="tpu_custom_call" | custom-call | flops 3145728000 | bytes 4194304 | tf_op jit(solution)/shard_map/apply_first/pallas_call | solution.py:518
  41.4 0.0 collective-permute-done.8
  41.4 2.1 %apply_last.2 = (f32[64,512]{1,0:T(8,128)S(1)}, bf16[64,512]{1,0:T(8,128)(2,1)S(1)}) custom-call(s32[548]{0:T(1024)S(1)} %get-tuple-element.33.ids_ref, s32[1]{0:T(128)} %get-tuple-element.34.count_ref, bf16[8,64,512]{2,1,0:T(8,128)(2,1)S(1)} %collective-permute-done.6.near_ref, bf16[8,64,512]{2,1,0:T(8,128)(2,1)S(1)} %bitcast.35, ...), custom_call_target="tpu_custom_call" | custom-call | flops 3145728000 | bytes 4194304 | tf_op jit(solution)/shard_map/apply_last/pallas_call | solution.py:518
  43.6 2.4 %collective-permute-start.10 = (bf16[1,64,512]{2,1,0:T(8,128)(2,1)S(1)}, bf16[1,64,512]{2,1,0:T(8,128)(2,1)S(1)}, u32[]{:S(2)}, u32[]{:S(2)}) collective-permute-start(bf16[1,64,512]{2,1,0:T(8,128)(2,1)S(1)} %bitcast.22), channel_id=1, source_target_pairs={{0,16},{1,17},{2,18},{3,19},{4,20},{5,21},{6,22},{7,23},{8,24},{9,... | collective-permute-start | bytes 196616 | tf_op jit(solution)/shard_map/ppermute | solution.py:78
  45.9 0.7 first_grams.1.refs_3_
  46.6 3.8 %collective-permute-done.10 = bf16[1,64,512]{2,1,0:T(8,128)(2,1)S(1)} collective-permute-done((bf16[1,64,512]{2,1,0:T(8,128)(2,1)S(1)}, bf16[1,64,512]{2,1,0:T(8,128)(2,1)S(1)}, u32[]{:S(2)}, u32[]{:S(2)}) %collective-permute-start.10) | collective-permute-done | bytes 65568 | tf_op jit(solution)/shard_map/ppermute | solution.py:78
  50.5 0.1 collective-permute-start.11
  50.5 5.0 %collective-permute-done.11 = bf16[2,64,512]{2,1,0:T(8,128)(2,1)S(1)} collective-permute-done((bf16[2,64,512]{2,1,0:T(8,128)(2,1)S(1)}, bf16[2,64,512]{2,1,0:T(8,128)(2,1)S(1)}, u32[]{:S(2)}, u32[]{:S(2)}) %collective-permute-start.11) | collective-permute-done | bytes 131104 | tf_op jit(solution)/shard_map/ppermute | solution.py:78
  55.5 0.1 collective-permute-start.12
  55.6 6.4 %collective-permute-done.12 = bf16[4,64,512]{2,1,0:T(8,128)(2,1)S(1)} collective-permute-done((bf16[4,64,512]{2,1,0:T(8,128)(2,1)S(1)}, bf16[4,64,512]{2,1,0:T(8,128)(2,1)S(1)}, u32[]{:S(2)}, u32[]{:S(2)}) %collective-permute-start.12) | collective-permute-done | bytes 262176 | tf_op jit(solution)/shard_map/ppermute | solution.py:78
  62.0 0.1 fusion
  62.0 0.1 collective-permute-start.14
  62.1 1.2 %collective-permute-start.13 = (bf16[8,64,512]{2,1,0:T(8,128)(2,1)S(1)}, bf16[8,64,512]{2,1,0:T(8,128)(2,1)S(1)}, u32[]{:S(2)}, u32[]{:S(2)}) collective-permute-start(bf16[8,64,512]{2,1,0:T(8,128)(2,1)S(1)} %get-tuple-element.55.near_ref), channel_id=1, source_target_pairs={{0,2},{1,5},{2,0},{3,7},{4,6},{5,1},{6,4},{7,3},{8,10},{9,13},{10,... | collective-permute-start | bytes 1572872 | tf_op jit(solution)/shard_map/ppermute | solution.py:78
  63.3 0.7 collective-permute-done.14
  64.0 1.9 %apply_first.3.refs_0_ = f32[512,64]{1,0:T(8,128)S(1)} custom-call(s32[548]{0:T(1024)S(1)} %get-tuple-element.39.ids_ref, s32[1]{0:T(128)} %get-tuple-element.40.count_ref, bf16[8,64,512]{2,1,0:T(8,128)(2,1)S(1)} %get-tuple-element.55.near_ref, bf16[8,64,512]{2,1,0:T(8,128)(2,1)S(1)} %bitcast.37, bf16[136,64,512]{2,1,0:T(8,128)(2,1)S(1)} %get-tuple-element.42.tiles_ref), custom_call_target="tpu_custom_call" | custom-call | flops 3145728000 | bytes 4194304 | tf_op jit(solution)/shard_map/apply_first/pallas_call | solution.py:518
  66.0 5.4 %collective-permute-done.13.near_ref = bf16[8,64,512]{2,1,0:T(8,128)(2,1)S(1)} collective-permute-done((bf16[8,64,512]{2,1,0:T(8,128)(2,1)S(1)}, bf16[8,64,512]{2,1,0:T(8,128)(2,1)S(1)}, u32[]{:S(2)}, u32[]{:S(2)}) %collective-permute-start.13) | collective-permute-done | bytes 524320 | tf_op jit(solution)/shard_map/ppermute | solution.py:78
  71.4 0.0 collective-permute-start.15
  71.4 1.9 %collective-permute-done.15 = bf16[1,8,64,512]{3,2,1,0:T(8,128)(2,1)S(1)} collective-permute-done((bf16[1,8,64,512]{3,2,1,0:T(8,128)(2,1)S(1)}, bf16[1,8,64,512]{3,2,1,0:T(8,128)(2,1)S(1)}, u32[]{:S(2)}, u32[]{:S(2)}) %collective-permute-start.15) | collective-permute-done | bytes 524320 | tf_op jit(solution)/shard_map/ppermute | solution.py:60
  73.3 0.0 copy-start
  73.3 2.8 %apply_last.3 = (f32[64,512]{1,0:T(8,128)S(1)}, f32[72,128]{1,0:T(8,128)S(1)}) custom-call(s32[548]{0:T(1024)S(1)} %get-tuple-element.33.ids_ref, s32[1]{0:T(128)} %get-tuple-element.34.count_ref, bf16[8,64,512]{2,1,0:T(8,128)(2,1)S(1)} %collective-permute-done.13.near_ref, bf16[8,64,512]{2,1,0:T(8,128)(2,1)S(1)} %bitcast.36, ...), custom_call_target="tpu_custom_call" | custom-call | flops 3145728000 | bytes 4194304 | tf_op jit(solution)/shard_map/apply_last/pallas_call | solution.py:518
  76.1 0.2 collective-permute-start.20
  76.4 0.4 collective-permute-start.16
  76.7 1.1 %collective-permute-done.16 = f32[72,128]{1,0:T(8,128)S(1)} collective-permute-done((f32[72,128]{1,0:T(8,128)S(1)}, f32[72,128]{1,0:T(8,128)S(1)}, u32[]{:S(2)}, u32[]{:S(2)}) %collective-permute-start.16) | collective-permute-done | bytes 36896 | tf_op jit(solution)/shard_map/ppermute | solution.py:60
  77.8 1.1 %collective-permute-start.17 = (f32[72,128]{1,0:T(8,128)S(1)}, f32[72,128]{1,0:T(8,128)S(1)}, u32[]{:S(2)}, u32[]{:S(2)}) collective-permute-start(f32[72,128]{1,0:T(8,128)S(1)} %add.19), channel_id=1, source_target_pairs={{0,2},{1,9},{2,0},{3,11},{4,6},{5,13},{6,4},{7,15},{8,10},{9,1},{1... | collective-permute-start | bytes 110600 | tf_op jit(solution)/shard_map/ppermute | solution.py:78
  78.9 2.9 %collective-permute-done.17 = f32[72,128]{1,0:T(8,128)S(1)} collective-permute-done((f32[72,128]{1,0:T(8,128)S(1)}, f32[72,128]{1,0:T(8,128)S(1)}, u32[]{:S(2)}, u32[]{:S(2)}) %collective-permute-start.17) | collective-permute-done | bytes 36896 | tf_op jit(solution)/shard_map/ppermute | solution.py:78
  81.8 0.0 collective-permute-start.18
  81.8 3.9 %collective-permute-done.18 = f32[72,128]{1,0:T(8,128)S(1)} collective-permute-done((f32[72,128]{1,0:T(8,128)S(1)}, f32[72,128]{1,0:T(8,128)S(1)}, u32[]{:S(2)}, u32[]{:S(2)}) %collective-permute-start.18) | collective-permute-done | bytes 36896 | tf_op jit(solution)/shard_map/ppermute | solution.py:78
  85.7 0.0 collective-permute-start.19
  85.7 3.9 %collective-permute-done.19 = f32[72,128]{1,0:T(8,128)S(1)} collective-permute-done((f32[72,128]{1,0:T(8,128)S(1)}, f32[72,128]{1,0:T(8,128)S(1)}, u32[]{:S(2)}, u32[]{:S(2)}) %collective-permute-start.19) | collective-permute-done | bytes 36896 | tf_op jit(solution)/shard_map/ppermute | solution.py:78
  89.7 0.0 collective-permute-done.20
  89.7 1.3 %collective-permute-start.21 = (f32[72,128]{1,0:T(8,128)S(1)}, f32[72,128]{1,0:T(8,128)S(1)}, u32[]{:S(2)}, u32[]{:S(2)}) collective-permute-start(f32[72,128]{1,0:T(8,128)S(1)} %add.22), channel_id=1, source_target_pairs={{0,16},{1,5},{2,18},{3,7},{4,20},{5,1},{6,22},{7,3},{8,24},{9,13},... | collective-permute-start | bytes 110600 | tf_op jit(solution)/shard_map/ppermute | solution.py:78
  91.1 0.8 unsort.1.images_ref
  91.9 2.8 %collective-permute-done.21 = f32[72,128]{1,0:T(8,128)S(1)} collective-permute-done((f32[72,128]{1,0:T(8,128)S(1)}, f32[72,128]{1,0:T(8,128)S(1)}, u32[]{:S(2)}, u32[]{:S(2)}) %collective-permute-start.21) | collective-permute-done | bytes 36896 | tf_op jit(solution)/shard_map/ppermute | solution.py:78
  94.7 0.0 copy-done
  94.7 7.5 %last_step.1 = (f32[64,512]{1,0:T(8,128)}, f32[64,512]{1,0:T(8,128)}) custom-call(f32[72,128]{1,0:T(8,128)S(1)} %add.23.grams_ref, f32[64,512]{1,0:T(8,128)S(1)} %copy-done, f32[128,512]{1,0:T(8,128)S(1)} %unsort.1.images_ref), custom_call_target="tpu_custom_call" | custom-call | tf_op jit(solution)/shard_map/last_step/pallas_call | solution.py:632
  (13 shorter events, 0.2 us)
Async XLA Ops:
  0.6 2.1 %collective-permute-start.2 = (f32[1,64,512]{2,1,0:T(8,128)}, f32[1,64,512]{2,1,0:T(8,128)S(1)}, u32[]{:S(2)}, u32[]{:S(2)}) collective-permute-start(f32[1,64,512]{2,1,0:T(8,128)} %bitcast.27), channel_id=1, source_target_pairs={{0,1},{1,0},{2,3},{3,2},{4,5},{5,4},{6,7},{7,6},{8,9},{9,8},{10,11... | collective-permute-start | bytes 393224 | tf_op jit(solution)/shard_map/ppermute | solution.py:60
  1.1 1.5 %collective-permute-start = (f32[1,3,512]{2,1,0:T(4,128)}, f32[1,3,512]{2,1,0:T(4,128)S(1)}, u32[]{:S(2)}, u32[]{:S(2)}) collective-permute-start(f32[1,3,512]{2,1,0:T(4,128)} %bitcast.40), channel_id=1, source_target_pairs={{0,1},{1,0},{2,3},{3,2},{4,5},{5,4},{6,7},{7,6},{8,9},{9,8},{10,11... | collective-permute-start | bytes 18440 | tf_op jit(solution)/shard_map/ppermute | solution.py:60
  1.2 1.5 %collective-permute-start.1 = (f32[1,1,512]{2,1,0:T(1,128)}, f32[1,1,512]{2,1,0:T(1,128)S(1)}, u32[]{:S(2)}, u32[]{:S(2)}) collective-permute-start(f32[1,1,512]{2,1,0:T(1,128)} %bitcast.42), channel_id=1, source_target_pairs={{0,1},{1,0},{2,3},{3,2},{4,5},{5,4},{6,7},{7,6},{8,9},{9,8},{10,11... | collective-permute-start | bytes 6152 | tf_op jit(solution)/shard_map/ppermute | solution.py:60
  6.1 9.7 %collective-permute-start.3 = (bf16[1,64,512]{2,1,0:T(8,128)(2,1)S(1)}, bf16[1,64,512]{2,1,0:T(8,128)(2,1)S(1)}, u32[]{:S(2)}, u32[]{:S(2)}) collective-permute-start(bf16[1,64,512]{2,1,0:T(8,128)(2,1)S(1)} %bitcast.18), channel_id=1, source_target_pairs={{0,16},{1,17},{2,18},{3,19},{4,20},{5,21},{6,22},{7,23},{8,24},{9,... | collective-permute-start | bytes 196616 | tf_op jit(solution)/shard_map/ppermute | solution.py:78
  10.8 12.9 %all-to-all-start = ((f32[16,4,512]{2,1,0:T(4,128)}), f32[16,4,512]{2,1,0:T(4,128)S(1)}, u32[]{:S(2)}, u32[]{:S(2)}) async-start(f32[16,4,512]{2,1,0:T(4,128)} %broadcast_in_dim.39), calls=%async_computation | async-start | bytes 262144 | tf_op jit(solution)/shard_map/all_to_all | solution.py:656
  15.9 7.8 %collective-permute-start.4 = (bf16[2,64,512]{2,1,0:T(8,128)(2,1)S(1)}, bf16[2,64,512]{2,1,0:T(8,128)(2,1)S(1)}, u32[]{:S(2)}, u32[]{:S(2)}) collective-permute-start(bf16[2,64,512]{2,1,0:T(8,128)(2,1)S(1)} %pad_maximum_fusion.5), channel_id=1, source_target_pairs={{0,8},{1,3},{2,10},{3,1},{4,12},{5,7},{6,14},{7,5},{8,0},{9,11},{1... | collective-permute-start | bytes 393224 | tf_op jit(solution)/shard_map/ppermute | solution.py:78
  23.6 1.3 %collective-permute-start.7 = (f32[1,16,4,512]{3,2,1,0:T(4,128)S(1)}, f32[1,16,4,512]{3,2,1,0:T(4,128)S(1)}, u32[]{:S(2)}, u32[]{:S(2)}) collective-permute-start(f32[1,16,4,512]{3,2,1,0:T(4,128)S(1)} %bitcast.29), channel_id=1, source_target_pairs={{0,1},{1,0},{2,3},{3,2},{4,5},{5,4},{6,7},{7,6},{8,9},{9,8},{10,11... | collective-permute-start | bytes 393224 | tf_op jit(solution)/shard_map/ppermute | solution.py:60
  23.7 6.4 %collective-permute-start.5 = (bf16[4,64,512]{2,1,0:T(8,128)(2,1)S(1)}, bf16[4,64,512]{2,1,0:T(8,128)(2,1)S(1)}, u32[]{:S(2)}, u32[]{:S(2)}) collective-permute-start(bf16[4,64,512]{2,1,0:T(8,128)(2,1)S(1)} %pad_maximum_fusion.3), channel_id=1, source_target_pairs={{0,4},{1,9},{2,6},{3,11},{4,0},{5,13},{6,2},{7,15},{8,12},{9,1},{1... | collective-permute-start | bytes 786440 | tf_op jit(solution)/shard_map/ppermute | solution.py:78
  30.2 9.2 %collective-permute-start.6 = (bf16[8,64,512]{2,1,0:T(8,128)(2,1)S(1)}, bf16[8,64,512]{2,1,0:T(8,128)(2,1)S(1)}, u32[]{:S(2)}, u32[]{:S(2)}) collective-permute-start(bf16[8,64,512]{2,1,0:T(8,128)(2,1)S(1)} %pad_maximum_fusion.near_ref), channel_id=1, source_target_pairs={{0,2},{1,5},{2,0},{3,7},{4,6},{5,1},{6,4},{7,3},{8,10},{9,13},{10,... | collective-permute-start | bytes 1572872 | tf_op jit(solution)/shard_map/ppermute | solution.py:78
  31.3 8.1 %collective-permute-start.9 = (bf16[1,8,64,512]{3,2,1,0:T(8,128)(2,1)S(1)}, bf16[1,8,64,512]{3,2,1,0:T(8,128)(2,1)S(1)}, u32[]{:S(2)}, u32[]{:S(2)}) collective-permute-start(bf16[1,8,64,512]{3,2,1,0:T(8,128)(2,1)S(1)} %bitcast.26), channel_id=1, source_target_pairs={{0,1},{1,0},{2,3},{3,2},{4,5},{5,4},{6,7},{7,6},{8,9},{9,8},{10,11... | collective-permute-start | bytes 1572872 | tf_op jit(solution)/shard_map/ppermute | solution.py:60
  39.4 2.0 %collective-permute-start.8 = (bf16[1,8,64,512]{3,2,1,0:T(8,128)(2,1)S(1)}, bf16[1,8,64,512]{3,2,1,0:T(8,128)(2,1)S(1)}, u32[]{:S(2)}, u32[]{:S(2)}) collective-permute-start(bf16[1,8,64,512]{3,2,1,0:T(8,128)(2,1)S(1)} %bitcast.32), channel_id=1, source_target_pairs={{0,1},{1,0},{2,3},{3,2},{4,5},{5,4},{6,7},{7,6},{8,9},{9,8},{10,11... | collective-permute-start | bytes 1572872 | tf_op jit(solution)/shard_map/ppermute | solution.py:60
  43.6 6.9 %collective-permute-start.10 = (bf16[1,64,512]{2,1,0:T(8,128)(2,1)S(1)}, bf16[1,64,512]{2,1,0:T(8,128)(2,1)S(1)}, u32[]{:S(2)}, u32[]{:S(2)}) collective-permute-start(bf16[1,64,512]{2,1,0:T(8,128)(2,1)S(1)} %bitcast.22), channel_id=1, source_target_pairs={{0,16},{1,17},{2,18},{3,19},{4,20},{5,21},{6,22},{7,23},{8,24},{9,... | collective-permute-start | bytes 196616 | tf_op jit(solution)/shard_map/ppermute | solution.py:78
  50.5 5.0 %collective-permute-start.11 = (bf16[2,64,512]{2,1,0:T(8,128)(2,1)S(1)}, bf16[2,64,512]{2,1,0:T(8,128)(2,1)S(1)}, u32[]{:S(2)}, u32[]{:S(2)}) collective-permute-start(bf16[2,64,512]{2,1,0:T(8,128)(2,1)S(1)} %pad_maximum_fusion.6), channel_id=1, source_target_pairs={{0,8},{1,3},{2,10},{3,1},{4,12},{5,7},{6,14},{7,5},{8,0},{9,11},{1... | collective-permute-start | bytes 393224 | tf_op jit(solution)/shard_map/ppermute | solution.py:78
  55.5 6.4 %collective-permute-start.12 = (bf16[4,64,512]{2,1,0:T(8,128)(2,1)S(1)}, bf16[4,64,512]{2,1,0:T(8,128)(2,1)S(1)}, u32[]{:S(2)}, u32[]{:S(2)}) collective-permute-start(bf16[4,64,512]{2,1,0:T(8,128)(2,1)S(1)} %pad_maximum_fusion.4), channel_id=1, source_target_pairs={{0,4},{1,9},{2,6},{3,11},{4,0},{5,13},{6,2},{7,15},{8,12},{9,1},{1... | collective-permute-start | bytes 786440 | tf_op jit(solution)/shard_map/ppermute | solution.py:78
  62.0 2.0 %collective-permute-start.14 = (bf16[1,8,64,512]{3,2,1,0:T(8,128)(2,1)S(1)}, bf16[1,8,64,512]{3,2,1,0:T(8,128)(2,1)S(1)}, u32[]{:S(2)}, u32[]{:S(2)}) collective-permute-start(bf16[1,8,64,512]{3,2,1,0:T(8,128)(2,1)S(1)} %get-tuple-element.54), channel_id=1, source_target_pairs={{0,1},{1,0},{2,3},{3,2},{4,5},{5,4},{6,7},{7,6},{8,9},{9,8},{10,11... | collective-permute-start | bytes 1572872 | tf_op jit(solution)/shard_map/ppermute | solution.py:60
  62.1 9.2 %collective-permute-start.13 = (bf16[8,64,512]{2,1,0:T(8,128)(2,1)S(1)}, bf16[8,64,512]{2,1,0:T(8,128)(2,1)S(1)}, u32[]{:S(2)}, u32[]{:S(2)}) collective-permute-start(bf16[8,64,512]{2,1,0:T(8,128)(2,1)S(1)} %get-tuple-element.55.near_ref), channel_id=1, source_target_pairs={{0,2},{1,5},{2,0},{3,7},{4,6},{5,1},{6,4},{7,3},{8,10},{9,13},{10,... | collective-permute-start | bytes 1572872 | tf_op jit(solution)/shard_map/ppermute | solution.py:78
  71.4 1.9 %collective-permute-start.15 = (bf16[1,8,64,512]{3,2,1,0:T(8,128)(2,1)S(1)}, bf16[1,8,64,512]{3,2,1,0:T(8,128)(2,1)S(1)}, u32[]{:S(2)}, u32[]{:S(2)}) collective-permute-start(bf16[1,8,64,512]{3,2,1,0:T(8,128)(2,1)S(1)} %bitcast.33), channel_id=1, source_target_pairs={{0,1},{1,0},{2,3},{3,2},{4,5},{5,4},{6,7},{7,6},{8,9},{9,8},{10,11... | collective-permute-start | bytes 1572872 | tf_op jit(solution)/shard_map/ppermute | solution.py:60
  73.3 21.4 %copy-start = (f32[64,512]{1,0:T(8,128)S(1)}, f32[64,512]{1,0:T(8,128)}, u32[]{:S(2)}) copy-start(f32[64,512]{1,0:T(8,128)} %start_ref.1) | copy-start | bytes 393220
  76.1 13.6 %collective-permute-start.20 = (f32[1,128,512]{2,1,0:T(8,128)S(1)}, f32[1,128,512]{2,1,0:T(8,128)S(1)}, u32[]{:S(2)}, u32[]{:S(2)}) collective-permute-start(f32[1,128,512]{2,1,0:T(8,128)S(1)} %bitcast.38), channel_id=1, source_target_pairs={{0,1},{1,0},{2,3},{3,2},{4,5},{5,4},{6,7},{7,6},{8,9},{9,8},{10,11... | collective-permute-start | bytes 786440 | tf_op jit(solution)/shard_map/ppermute | solution.py:60
  76.4 1.4 %collective-permute-start.16 = (f32[72,128]{1,0:T(8,128)S(1)}, f32[72,128]{1,0:T(8,128)S(1)}, u32[]{:S(2)}, u32[]{:S(2)}) collective-permute-start(f32[72,128]{1,0:T(8,128)S(1)} %get-tuple-element.49), channel_id=1, source_target_pairs={{0,1},{1,0},{2,3},{3,2},{4,5},{5,4},{6,7},{7,6},{8,9},{9,8},{10,11... | collective-permute-start | bytes 110600 | tf_op jit(solution)/shard_map/ppermute | solution.py:60
  77.8 4.0 %collective-permute-start.17 = (f32[72,128]{1,0:T(8,128)S(1)}, f32[72,128]{1,0:T(8,128)S(1)}, u32[]{:S(2)}, u32[]{:S(2)}) collective-permute-start(f32[72,128]{1,0:T(8,128)S(1)} %add.19), channel_id=1, source_target_pairs={{0,2},{1,9},{2,0},{3,11},{4,6},{5,13},{6,4},{7,15},{8,10},{9,1},{1... | collective-permute-start | bytes 110600 | tf_op jit(solution)/shard_map/ppermute | solution.py:78
  81.8 4.0 %collective-permute-start.18 = (f32[72,128]{1,0:T(8,128)S(1)}, f32[72,128]{1,0:T(8,128)S(1)}, u32[]{:S(2)}, u32[]{:S(2)}) collective-permute-start(f32[72,128]{1,0:T(8,128)S(1)} %add.20), channel_id=1, source_target_pairs={{0,4},{1,17},{2,6},{3,19},{4,0},{5,21},{6,2},{7,23},{8,12},{9,25},... | collective-permute-start | bytes 110600 | tf_op jit(solution)/shard_map/ppermute | solution.py:78
  85.7 4.0 %collective-permute-start.19 = (f32[72,128]{1,0:T(8,128)S(1)}, f32[72,128]{1,0:T(8,128)S(1)}, u32[]{:S(2)}, u32[]{:S(2)}) collective-permute-start(f32[72,128]{1,0:T(8,128)S(1)} %add.21), channel_id=1, source_target_pairs={{0,8},{1,3},{2,10},{3,1},{4,12},{5,7},{6,14},{7,5},{8,0},{9,11},{1... | collective-permute-start | bytes 110600 | tf_op jit(solution)/shard_map/ppermute | solution.py:78
  89.7 4.9 %collective-permute-start.21 = (f32[72,128]{1,0:T(8,128)S(1)}, f32[72,128]{1,0:T(8,128)S(1)}, u32[]{:S(2)}, u32[]{:S(2)}) collective-permute-start(f32[72,128]{1,0:T(8,128)S(1)} %add.22), channel_id=1, source_target_pairs={{0,16},{1,5},{2,18},{3,7},{4,20},{5,1},{6,22},{7,3},{8,24},{9,13},... | collective-permute-start | bytes 110600 | tf_op jit(solution)/shard_map/ppermute | solution.py:78

commit v13 on v11

--- a/solution.py
+++ b/solution.py
@@ -13,7 +13,7 @@
 ROWS = 64
 PAIR = 2
 BATCH = 2 * PAIR
-UNROLL = 8
+UNROLL = 16
 VMEM = 16 * 1024 * 1024
 HIGHEST = lax.Precision.HIGHEST
 

time: 103 us -> 102 us (level)
  transfers between devices with their start and end apart: 23 -> 23, of which waited for: 16 -> 17; matrix products, arithmetic and copies ran while one was open for 1% -> 1% of each run, Pallas kernels for 14% -> 13%
where the time goes in v13:
time: 102 us; the launch traced here: 103 us
  waiting for transfers between devices  50.1 us (49%)
  Pallas kernels  29.4 us (29%)
  starting transfers between devices  21.7 us (21%)
    ppermute x12, waiting for transfers between devices, swap_regions(): return lax.ppermute(block, ('region', 'tile'), route)  39.2 us
    ppermute x12, starting transfers between devices, swap_regions(): return lax.ppermute(block, ('region', 'tile'), route)  13.7 us
    pallas_call x2, Pallas kernels, build_tiles(): pl.pallas_call(functools.partial(build_kernel, part), out_shape=tuple((ja...  8.72 us
    pallas_call x4, Pallas kernels, apply_tiles(): pl.pallas_call(functools.partial(apply_kernel, start is not None, last, g...  8.2 us
    pallas_call x1, Pallas kernels, last_step(): pl.pallas_call(last_kernel, out_shape=(jax.ShapeDtypeStruct(start.shape,...  7.55 us
    all_to_all x1, starting transfers between devices, shards(): everywhere = lax.all_to_all(everywhere, 'region', 0, 0)  6.29 us
    all_to_all x1, waiting for transfers between devices, shards(): everywhere = lax.all_to_all(everywhere, 'region', 0, 0)  5.78 us
    ppermute x10, waiting for transfers between devices, swapped(): lax.ppermute(block, axis, [(i, i ^ bit) for i in range(lax.axis_size(axis...  5.11 us
  transfers between devices with their start and end apart: 23, of which 17 were waited for; matrix products, arithmetic and copies ran while one was open for 1% of the time, Pallas kernels for 13%

profile of v13, /device:TPU:0, one launch (start us, length us, event | category | flops | bytes accessed | tf_op | source)
XLA Modules:
  0.0 102.9 jit_solution(1816573879182985490)
XLA Ops:
  0.6 0.5 collective-permute-start.2
  1.1 0.1 collective-permute-start
  1.2 0.4 collective-permute-start.1
  1.7 1.0 %collective-permute-done.1.far_error_ref = f32[1,1,512]{2,1,0:T(1,128)S(1)} collective-permute-done((f32[1,1,512]{2,1,0:T(1,128)}, f32[1,1,512]{2,1,0:T(1,128)S(1)}, u32[]{:S(2)}, u32[]{:S(2)}) %collective-permute-start.1) | collective-permute-done | bytes 2080 | tf_op jit(solution)/shard_map/ppermute | solution.py:60
  2.7 0.0 collective-permute-done.far_ref
  2.7 0.0 collective-permute-done.2.other_ref
  2.7 3.4 %sort_region.1 = (bf16[64,512]{1,0:T(8,128)(2,1)S(1)}, f32[4,512]{1,0:T(4,128)S(1)}, f32[8,512]{1,0:T(8,128)S(1)}, f32[64,512]{1,0:T(8,128)S(1)}, s32[1,512]{1,0:T(1,128)S(1)}) custom-call(s32[1]{0:T(128)} %bitcast.device_ref, s32[1,7]{1,0:T(1,128)} %owner_ref.1, f32[1,3,512]{2,1,0:T(4,128)} %bitcast.41, f32[1,3,512]{2,1,0:T(4,128)S(1)} %collective-permute-done.far_ref, ...), custom_call_target="tpu_custom_call" | custom-call | flops 226492416 | bytes 2097152 | tf_op jit(solution)/shard_map/sort_region/pallas_call | solution.py:240
  6.1 4.0 %collective-permute-start.3 = (bf16[1,64,512]{2,1,0:T(8,128)(2,1)S(1)}, bf16[1,64,512]{2,1,0:T(8,128)(2,1)S(1)}, u32[]{:S(2)}, u32[]{:S(2)}) collective-permute-start(bf16[1,64,512]{2,1,0:T(8,128)(2,1)S(1)} %bitcast.18), channel_id=1, source_target_pairs={{0,16},{1,17},{2,18},{3,19},{4,20},{5,21},{6,22},{7,23},{8,24},{9,... | collective-permute-start | bytes 196616 | tf_op jit(solution)/shard_map/ppermute | solution.py:78
  10.1 0.7 broadcast_in_dim.39
  10.8 6.3 %all-to-all-start = ((f32[16,4,512]{2,1,0:T(4,128)}), f32[16,4,512]{2,1,0:T(4,128)S(1)}, u32[]{:S(2)}, u32[]{:S(2)}) async-start(f32[16,4,512]{2,1,0:T(4,128)} %broadcast_in_dim.39), calls=%async_computation | async-start | bytes 262144 | tf_op jit(solution)/shard_map/all_to_all | solution.py:654
  17.1 0.0 collective-permute-done.3
  17.1 2.0 %collective-permute-start.4 = (bf16[2,64,512]{2,1,0:T(8,128)(2,1)S(1)}, bf16[2,64,512]{2,1,0:T(8,128)(2,1)S(1)}, u32[]{:S(2)}, u32[]{:S(2)}) collective-permute-start(bf16[2,64,512]{2,1,0:T(8,128)(2,1)S(1)} %pad_maximum_fusion.5), channel_id=1, source_target_pairs={{0,8},{1,3},{2,10},{3,1},{4,12},{5,7},{6,14},{7,5},{8,0},{9,11},{1... | collective-permute-start | bytes 393224 | tf_op jit(solution)/shard_map/ppermute | solution.py:78
  19.1 5.8 %all-to-all-done = f32[16,4,512]{2,1,0:T(4,128)S(1)} async-done(((f32[16,4,512]{2,1,0:T(4,128)}), f32[16,4,512]{2,1,0:T(4,128)S(1)}, u32[]{:S(2)}, u32[]{:S(2)}) %all-to-all-start) | async-done | bytes 131104 | tf_op jit(solution)/shard_map/all_to_all | solution.py:654
  24.9 0.0 collective-permute-start.7
  24.9 0.0 collective-permute-done.4
  24.9 0.8 collective-permute-start.5
  25.7 0.5 collective-permute-done.7.other_ref
  26.2 4.6 %build_tiles.3 = (s32[580]{0:T(1024)S(1)}, s32[1]{0:T(128)}, bf16[144,64,512]{2,1,0:T(8,128)(2,1)S(1)}) custom-call(s32[1]{0:T(128)} %bitcast.device_ref, f32[8,512]{1,0:T(8,128)S(1)} %get-tuple-element.29.own_ref, f32[1,16,4,512]{3,2,1,0:T(4,128)S(1)} %bitcast.30, f32[1,16,4,512]{3,2,1,0:T(4,128)S(1)} %collective-permute-done.7.other_ref), custom_call_target="tpu_custom_call" | custom-call | flops 8388608000 | bytes 4194304 | tf_op jit(solution)/shard_map/build_tiles/pallas_call | solution.py:426
  30.8 0.5 collective-permute-done.5
  31.3 0.1 pad_maximum_fusion.near_ref
  31.4 1.2 %collective-permute-start.6 = (bf16[8,64,512]{2,1,0:T(8,128)(2,1)S(1)}, bf16[8,64,512]{2,1,0:T(8,128)(2,1)S(1)}, u32[]{:S(2)}, u32[]{:S(2)}) collective-permute-start(bf16[8,64,512]{2,1,0:T(8,128)(2,1)S(1)} %pad_maximum_fusion.near_ref), channel_id=1, source_target_pairs={{0,2},{1,5},{2,0},{3,7},{4,6},{5,1},{6,4},{7,3},{8,10},{9,13},{10,... | collective-permute-start | bytes 1572872 | tf_op jit(solution)/shard_map/ppermute | solution.py:78
  32.6 0.0 collective-permute-start.9
  32.6 4.1 %build_tiles.2 = (s32[580]{0:T(1024)S(1)}, s32[1]{0:T(128)}, bf16[144,64,512]{2,1,0:T(8,128)(2,1)S(1)}) custom-call(s32[1]{0:T(128)} %bitcast.device_ref, f32[8,512]{1,0:T(8,128)S(1)} %get-tuple-element.29.own_ref, f32[1,16,4,512]{3,2,1,0:T(4,128)S(1)} %bitcast.31, f32[1,16,4,512]{3,2,1,0:T(4,128)S(1)} %collective-permute-done.7.other_ref), custom_call_target="tpu_custom_call" | custom-call | flops 8388608000 | bytes 4194304 | tf_op jit(solution)/shard_map/build_tiles/pallas_call | solution.py:426
  36.7 3.9 %collective-permute-done.6.near_ref = bf16[8,64,512]{2,1,0:T(8,128)(2,1)S(1)} collective-permute-done((bf16[8,64,512]{2,1,0:T(8,128)(2,1)S(1)}, bf16[8,64,512]{2,1,0:T(8,128)(2,1)S(1)}, u32[]{:S(2)}, u32[]{:S(2)}) %collective-permute-start.6) | collective-permute-done | bytes 524320 | tf_op jit(solution)/shard_map/ppermute | solution.py:78
  40.7 0.0 collective-permute-start.8
  40.7 0.0 collective-permute-done.9
  40.7 1.8 %apply_first.2.refs_0_ = f32[512,64]{1,0:T(8,128)S(1)} custom-call(s32[580]{0:T(1024)S(1)} %get-tuple-element.39.ids_ref, s32[1]{0:T(128)} %get-tuple-element.40.count_ref, bf16[8,64,512]{2,1,0:T(8,128)(2,1)S(1)} %pad_maximum_fusion.near_ref, bf16[8,64,512]{2,1,0:T(8,128)(2,1)S(1)} %bitcast.34, bf16[144,64,512]{2,1,0:T(8,128)(2,1)S(1)} %get-tuple-element.42.tiles_ref), custom_call_target="tpu_custom_call" | custom-call | flops 3145728000 | bytes 4194304 | tf_op jit(solution)/shard_map/apply_first/pallas_call | solution.py:516
  42.5 0.1 collective-permute-done.8
  42.6 1.9 %apply_last.2 = (f32[64,512]{1,0:T(8,128)S(1)}, bf16[64,512]{1,0:T(8,128)(2,1)S(1)}) custom-call(s32[580]{0:T(1024)S(1)} %get-tuple-element.33.ids_ref, s32[1]{0:T(128)} %get-tuple-element.34.count_ref, bf16[8,64,512]{2,1,0:T(8,128)(2,1)S(1)} %collective-permute-done.6.near_ref, bf16[8,64,512]{2,1,0:T(8,128)(2,1)S(1)} %bitcast.35, ...), custom_call_target="tpu_custom_call" | custom-call | flops 3145728000 | bytes 4194304 | tf_op jit(solution)/shard_map/apply_last/pallas_call | solution.py:516
  44.5 1.5 %collective-permute-start.10 = (bf16[1,64,512]{2,1,0:T(8,128)(2,1)S(1)}, bf16[1,64,512]{2,1,0:T(8,128)(2,1)S(1)}, u32[]{:S(2)}, u32[]{:S(2)}) collective-permute-start(bf16[1,64,512]{2,1,0:T(8,128)(2,1)S(1)} %bitcast.22), channel_id=1, source_target_pairs={{0,16},{1,17},{2,18},{3,19},{4,20},{5,21},{6,22},{7,23},{8,24},{9,... | collective-permute-start | bytes 196616 | tf_op jit(solution)/shard_map/ppermute | solution.py:78
  46.0 0.7 first_grams.1.refs_3_
  46.7 4.6 %collective-permute-done.10 = bf16[1,64,512]{2,1,0:T(8,128)(2,1)S(1)} collective-permute-done((bf16[1,64,512]{2,1,0:T(8,128)(2,1)S(1)}, bf16[1,64,512]{2,1,0:T(8,128)(2,1)S(1)}, u32[]{:S(2)}, u32[]{:S(2)}) %collective-permute-start.10) | collective-permute-done | bytes 65568 | tf_op jit(solution)/shard_map/ppermute | solution.py:78
  51.3 0.3 collective-permute-start.11
  51.6 4.8 %collective-permute-done.11 = bf16[2,64,512]{2,1,0:T(8,128)(2,1)S(1)} collective-permute-done((bf16[2,64,512]{2,1,0:T(8,128)(2,1)S(1)}, bf16[2,64,512]{2,1,0:T(8,128)(2,1)S(1)}, u32[]{:S(2)}, u32[]{:S(2)}) %collective-permute-start.11) | collective-permute-done | bytes 131104 | tf_op jit(solution)/shard_map/ppermute | solution.py:78
  56.4 0.1 collective-permute-start.12
  56.5 6.4 %collective-permute-done.12 = bf16[4,64,512]{2,1,0:T(8,128)(2,1)S(1)} collective-permute-done((bf16[4,64,512]{2,1,0:T(8,128)(2,1)S(1)}, bf16[4,64,512]{2,1,0:T(8,128)(2,1)S(1)}, u32[]{:S(2)}, u32[]{:S(2)}) %collective-permute-start.12) | collective-permute-done | bytes 262176 | tf_op jit(solution)/shard_map/ppermute | solution.py:78
  62.8 0.1 fusion
  62.9 0.1 collective-permute-start.14
  63.0 1.3 %collective-permute-start.13 = (bf16[8,64,512]{2,1,0:T(8,128)(2,1)S(1)}, bf16[8,64,512]{2,1,0:T(8,128)(2,1)S(1)}, u32[]{:S(2)}, u32[]{:S(2)}) collective-permute-start(bf16[8,64,512]{2,1,0:T(8,128)(2,1)S(1)} %get-tuple-element.55.near_ref), channel_id=1, source_target_pairs={{0,2},{1,5},{2,0},{3,7},{4,6},{5,1},{6,4},{7,3},{8,10},{9,13},{10,... | collective-permute-start | bytes 1572872 | tf_op jit(solution)/shard_map/ppermute | solution.py:78
  64.4 0.6 collective-permute-done.14
  64.9 1.8 %apply_first.3.refs_0_ = f32[512,64]{1,0:T(8,128)S(1)} custom-call(s32[580]{0:T(1024)S(1)} %get-tuple-element.39.ids_ref, s32[1]{0:T(128)} %get-tuple-element.40.count_ref, bf16[8,64,512]{2,1,0:T(8,128)(2,1)S(1)} %get-tuple-element.55.near_ref, bf16[8,64,512]{2,1,0:T(8,128)(2,1)S(1)} %bitcast.37, bf16[144,64,512]{2,1,0:T(8,128)(2,1)S(1)} %get-tuple-element.42.tiles_ref), custom_call_target="tpu_custom_call" | custom-call | flops 3145728000 | bytes 4194304 | tf_op jit(solution)/shard_map/apply_first/pallas_call | solution.py:516
  66.7 0.0 copy-start
  66.7 5.5 %collective-permute-done.13.near_ref = bf16[8,64,512]{2,1,0:T(8,128)(2,1)S(1)} collective-permute-done((bf16[8,64,512]{2,1,0:T(8,128)(2,1)S(1)}, bf16[8,64,512]{2,1,0:T(8,128)(2,1)S(1)}, u32[]{:S(2)}, u32[]{:S(2)}) %collective-permute-start.13) | collective-permute-done | bytes 524320 | tf_op jit(solution)/shard_map/ppermute | solution.py:78
  72.3 0.0 collective-permute-start.15
  72.3 1.9 %collective-permute-done.15 = bf16[1,8,64,512]{3,2,1,0:T(8,128)(2,1)S(1)} collective-permute-done((bf16[1,8,64,512]{3,2,1,0:T(8,128)(2,1)S(1)}, bf16[1,8,64,512]{3,2,1,0:T(8,128)(2,1)S(1)}, u32[]{:S(2)}, u32[]{:S(2)}) %collective-permute-start.15) | collective-permute-done | bytes 524320 | tf_op jit(solution)/shard_map/ppermute | solution.py:60
  74.2 2.6 %apply_last.3 = (f32[64,512]{1,0:T(8,128)S(1)}, bf16[64,512]{1,0:T(8,128)(2,1)}, f32[72,128]{1,0:T(8,128)S(1)}) custom-call(s32[580]{0:T(1024)S(1)} %get-tuple-element.33.ids_ref, s32[1]{0:T(128)} %get-tuple-element.34.count_ref, bf16[8,64,512]{2,1,0:T(8,128)(2,1)S(1)} %collective-permute-done.13.near_ref, bf16[8,64,512]{2,1,0:T(8,128)(2,1)S(1)} %bitcast.36, ...), custom_call_target="tpu_custom_call" | custom-call | flops 3145728000 | bytes 4194304 | tf_op jit(solution)/shard_map/apply_last/pallas_call | solution.py:516
  76.8 0.2 collective-permute-start.20
  77.0 0.4 collective-permute-start.16
  77.4 1.1 %collective-permute-done.16 = f32[72,128]{1,0:T(8,128)S(1)} collective-permute-done((f32[72,128]{1,0:T(8,128)S(1)}, f32[72,128]{1,0:T(8,128)S(1)}, u32[]{:S(2)}, u32[]{:S(2)}) %collective-permute-start.16) | collective-permute-done | bytes 36896 | tf_op jit(solution)/shard_map/ppermute | solution.py:60
  78.5 0.2 collective-permute-start.17
  78.7 4.7 %collective-permute-done.17 = f32[72,128]{1,0:T(8,128)S(1)} collective-permute-done((f32[72,128]{1,0:T(8,128)S(1)}, f32[72,128]{1,0:T(8,128)S(1)}, u32[]{:S(2)}, u32[]{:S(2)}) %collective-permute-start.17) | collective-permute-done | bytes 36896 | tf_op jit(solution)/shard_map/ppermute | solution.py:78
  83.4 0.2 collective-permute-start.18
  83.5 3.8 %collective-permute-done.18 = f32[72,128]{1,0:T(8,128)S(1)} collective-permute-done((f32[72,128]{1,0:T(8,128)S(1)}, f32[72,128]{1,0:T(8,128)S(1)}, u32[]{:S(2)}, u32[]{:S(2)}) %collective-permute-start.18) | collective-permute-done | bytes 36896 | tf_op jit(solution)/shard_map/ppermute | solution.py:78
  87.3 0.4 collective-permute-start.19
  87.8 3.5 %collective-permute-done.19 = f32[72,128]{1,0:T(8,128)S(1)} collective-permute-done((f32[72,128]{1,0:T(8,128)S(1)}, f32[72,128]{1,0:T(8,128)S(1)}, u32[]{:S(2)}, u32[]{:S(2)}) %collective-permute-start.19) | collective-permute-done | bytes 36896 | tf_op jit(solution)/shard_map/ppermute | solution.py:78
  91.3 0.0 collective-permute-done.20
  91.3 1.7 %collective-permute-start.21 = (f32[72,128]{1,0:T(8,128)S(1)}, f32[72,128]{1,0:T(8,128)S(1)}, u32[]{:S(2)}, u32[]{:S(2)}) collective-permute-start(f32[72,128]{1,0:T(8,128)S(1)} %add.22), channel_id=1, source_target_pairs={{0,2},{1,9},{2,0},{3,11},{4,6},{5,13},{6,4},{7,15},{8,10},{9,1},{1... | collective-permute-start | bytes 110600 | tf_op jit(solution)/shard_map/ppermute | solution.py:78
  93.1 0.8 unsort.1.images_ref
  93.9 1.5 %collective-permute-done.21 = f32[72,128]{1,0:T(8,128)S(1)} collective-permute-done((f32[72,128]{1,0:T(8,128)S(1)}, f32[72,128]{1,0:T(8,128)S(1)}, u32[]{:S(2)}, u32[]{:S(2)}) %collective-permute-start.21) | collective-permute-done | bytes 36896 | tf_op jit(solution)/shard_map/ppermute | solution.py:78
  95.4 0.0 copy-done
  95.4 7.5 %last_step.1 = (f32[64,512]{1,0:T(8,128)}, f32[64,512]{1,0:T(8,128)}) custom-call(f32[72,128]{1,0:T(8,128)S(1)} %add.23.grams_ref, f32[64,512]{1,0:T(8,128)S(1)} %copy-done, f32[128,512]{1,0:T(8,128)S(1)} %unsort.1.images_ref), custom_call_target="tpu_custom_call" | custom-call | tf_op jit(solution)/shard_map/last_step/pallas_call | solution.py:630
  (13 shorter events, 0.2 us)
Async XLA Ops:
  0.6 2.1 %collective-permute-start.2 = (f32[1,64,512]{2,1,0:T(8,128)}, f32[1,64,512]{2,1,0:T(8,128)S(1)}, u32[]{:S(2)}, u32[]{:S(2)}) collective-permute-start(f32[1,64,512]{2,1,0:T(8,128)} %bitcast.27), channel_id=1, source_target_pairs={{0,1},{1,0},{2,3},{3,2},{4,5},{5,4},{6,7},{7,6},{8,9},{9,8},{10,11... | collective-permute-start | bytes 393224 | tf_op jit(solution)/shard_map/ppermute | solution.py:60
  1.1 1.5 %collective-permute-start = (f32[1,3,512]{2,1,0:T(4,128)}, f32[1,3,512]{2,1,0:T(4,128)S(1)}, u32[]{:S(2)}, u32[]{:S(2)}) collective-permute-start(f32[1,3,512]{2,1,0:T(4,128)} %bitcast.40), channel_id=1, source_target_pairs={{0,1},{1,0},{2,3},{3,2},{4,5},{5,4},{6,7},{7,6},{8,9},{9,8},{10,11... | collective-permute-start | bytes 18440 | tf_op jit(solution)/shard_map/ppermute | solution.py:60
  1.2 1.5 %collective-permute-start.1 = (f32[1,1,512]{2,1,0:T(1,128)}, f32[1,1,512]{2,1,0:T(1,128)S(1)}, u32[]{:S(2)}, u32[]{:S(2)}) collective-permute-start(f32[1,1,512]{2,1,0:T(1,128)} %bitcast.42), channel_id=1, source_target_pairs={{0,1},{1,0},{2,3},{3,2},{4,5},{5,4},{6,7},{7,6},{8,9},{9,8},{10,11... | collective-permute-start | bytes 6152 | tf_op jit(solution)/shard_map/ppermute | solution.py:60
  6.1 11.0 %collective-permute-start.3 = (bf16[1,64,512]{2,1,0:T(8,128)(2,1)S(1)}, bf16[1,64,512]{2,1,0:T(8,128)(2,1)S(1)}, u32[]{:S(2)}, u32[]{:S(2)}) collective-permute-start(bf16[1,64,512]{2,1,0:T(8,128)(2,1)S(1)} %bitcast.18), channel_id=1, source_target_pairs={{0,16},{1,17},{2,18},{3,19},{4,20},{5,21},{6,22},{7,23},{8,24},{9,... | collective-permute-start | bytes 196616 | tf_op jit(solution)/shard_map/ppermute | solution.py:78
  10.8 14.1 %all-to-all-start = ((f32[16,4,512]{2,1,0:T(4,128)}), f32[16,4,512]{2,1,0:T(4,128)S(1)}, u32[]{:S(2)}, u32[]{:S(2)}) async-start(f32[16,4,512]{2,1,0:T(4,128)} %broadcast_in_dim.39), calls=%async_computation | async-start | bytes 262144 | tf_op jit(solution)/shard_map/all_to_all | solution.py:654
  17.1 7.8 %collective-permute-start.4 = (bf16[2,64,512]{2,1,0:T(8,128)(2,1)S(1)}, bf16[2,64,512]{2,1,0:T(8,128)(2,1)S(1)}, u32[]{:S(2)}, u32[]{:S(2)}) collective-permute-start(bf16[2,64,512]{2,1,0:T(8,128)(2,1)S(1)} %pad_maximum_fusion.5), channel_id=1, source_target_pairs={{0,8},{1,3},{2,10},{3,1},{4,12},{5,7},{6,14},{7,5},{8,0},{9,11},{1... | collective-permute-start | bytes 393224 | tf_op jit(solution)/shard_map/ppermute | solution.py:78
  24.9 1.3 %collective-permute-start.7 = (f32[1,16,4,512]{3,2,1,0:T(4,128)S(1)}, f32[1,16,4,512]{3,2,1,0:T(4,128)S(1)}, u32[]{:S(2)}, u32[]{:S(2)}) collective-permute-start(f32[1,16,4,512]{3,2,1,0:T(4,128)S(1)} %bitcast.29), channel_id=1, source_target_pairs={{0,1},{1,0},{2,3},{3,2},{4,5},{5,4},{6,7},{7,6},{8,9},{9,8},{10,11... | collective-permute-start | bytes 393224 | tf_op jit(solution)/shard_map/ppermute | solution.py:60
  24.9 6.4 %collective-permute-start.5 = (bf16[4,64,512]{2,1,0:T(8,128)(2,1)S(1)}, bf16[4,64,512]{2,1,0:T(8,128)(2,1)S(1)}, u32[]{:S(2)}, u32[]{:S(2)}) collective-permute-start(bf16[4,64,512]{2,1,0:T(8,128)(2,1)S(1)} %pad_maximum_fusion.3), channel_id=1, source_target_pairs={{0,4},{1,9},{2,6},{3,11},{4,0},{5,13},{6,2},{7,15},{8,12},{9,1},{1... | collective-permute-start | bytes 786440 | tf_op jit(solution)/shard_map/ppermute | solution.py:78
  31.4 9.2 %collective-permute-start.6 = (bf16[8,64,512]{2,1,0:T(8,128)(2,1)S(1)}, bf16[8,64,512]{2,1,0:T(8,128)(2,1)S(1)}, u32[]{:S(2)}, u32[]{:S(2)}) collective-permute-start(bf16[8,64,512]{2,1,0:T(8,128)(2,1)S(1)} %pad_maximum_fusion.near_ref), channel_id=1, source_target_pairs={{0,2},{1,5},{2,0},{3,7},{4,6},{5,1},{6,4},{7,3},{8,10},{9,13},{10,... | collective-permute-start | bytes 1572872 | tf_op jit(solution)/shard_map/ppermute | solution.py:78
  32.6 8.1 %collective-permute-start.9 = (bf16[1,8,64,512]{3,2,1,0:T(8,128)(2,1)S(1)}, bf16[1,8,64,512]{3,2,1,0:T(8,128)(2,1)S(1)}, u32[]{:S(2)}, u32[]{:S(2)}) collective-permute-start(bf16[1,8,64,512]{3,2,1,0:T(8,128)(2,1)S(1)} %bitcast.26), channel_id=1, source_target_pairs={{0,1},{1,0},{2,3},{3,2},{4,5},{5,4},{6,7},{7,6},{8,9},{9,8},{10,11... | collective-permute-start | bytes 1572872 | tf_op jit(solution)/shard_map/ppermute | solution.py:60
  40.7 1.9 %collective-permute-start.8 = (bf16[1,8,64,512]{3,2,1,0:T(8,128)(2,1)S(1)}, bf16[1,8,64,512]{3,2,1,0:T(8,128)(2,1)S(1)}, u32[]{:S(2)}, u32[]{:S(2)}) collective-permute-start(bf16[1,8,64,512]{3,2,1,0:T(8,128)(2,1)S(1)} %bitcast.32), channel_id=1, source_target_pairs={{0,1},{1,0},{2,3},{3,2},{4,5},{5,4},{6,7},{7,6},{8,9},{9,8},{10,11... | collective-permute-start | bytes 1572872 | tf_op jit(solution)/shard_map/ppermute | solution.py:60
  44.5 6.8 %collective-permute-start.10 = (bf16[1,64,512]{2,1,0:T(8,128)(2,1)S(1)}, bf16[1,64,512]{2,1,0:T(8,128)(2,1)S(1)}, u32[]{:S(2)}, u32[]{:S(2)}) collective-permute-start(bf16[1,64,512]{2,1,0:T(8,128)(2,1)S(1)} %bitcast.22), channel_id=1, source_target_pairs={{0,16},{1,17},{2,18},{3,19},{4,20},{5,21},{6,22},{7,23},{8,24},{9,... | collective-permute-start | bytes 196616 | tf_op jit(solution)/shard_map/ppermute | solution.py:78
  51.3 5.0 %collective-permute-start.11 = (bf16[2,64,512]{2,1,0:T(8,128)(2,1)S(1)}, bf16[2,64,512]{2,1,0:T(8,128)(2,1)S(1)}, u32[]{:S(2)}, u32[]{:S(2)}) collective-permute-start(bf16[2,64,512]{2,1,0:T(8,128)(2,1)S(1)} %pad_maximum_fusion.6), channel_id=1, source_target_pairs={{0,8},{1,3},{2,10},{3,1},{4,12},{5,7},{6,14},{7,5},{8,0},{9,11},{1... | collective-permute-start | bytes 393224 | tf_op jit(solution)/shard_map/ppermute | solution.py:78
  56.4 6.4 %collective-permute-start.12 = (bf16[4,64,512]{2,1,0:T(8,128)(2,1)S(1)}, bf16[4,64,512]{2,1,0:T(8,128)(2,1)S(1)}, u32[]{:S(2)}, u32[]{:S(2)}) collective-permute-start(bf16[4,64,512]{2,1,0:T(8,128)(2,1)S(1)} %pad_maximum_fusion.4), channel_id=1, source_target_pairs={{0,4},{1,9},{2,6},{3,11},{4,0},{5,13},{6,2},{7,15},{8,12},{9,1},{1... | collective-permute-start | bytes 786440 | tf_op jit(solution)/shard_map/ppermute | solution.py:78
  62.9 2.0 %collective-permute-start.14 = (bf16[1,8,64,512]{3,2,1,0:T(8,128)(2,1)S(1)}, bf16[1,8,64,512]{3,2,1,0:T(8,128)(2,1)S(1)}, u32[]{:S(2)}, u32[]{:S(2)}) collective-permute-start(bf16[1,8,64,512]{3,2,1,0:T(8,128)(2,1)S(1)} %get-tuple-element.54), channel_id=1, source_target_pairs={{0,1},{1,0},{2,3},{3,2},{4,5},{5,4},{6,7},{7,6},{8,9},{9,8},{10,11... | collective-permute-start | bytes 1572872 | tf_op jit(solution)/shard_map/ppermute | solution.py:60
  63.0 9.2 %collective-permute-start.13 = (bf16[8,64,512]{2,1,0:T(8,128)(2,1)S(1)}, bf16[8,64,512]{2,1,0:T(8,128)(2,1)S(1)}, u32[]{:S(2)}, u32[]{:S(2)}) collective-permute-start(bf16[8,64,512]{2,1,0:T(8,128)(2,1)S(1)} %get-tuple-element.55.near_ref), channel_id=1, source_target_pairs={{0,2},{1,5},{2,0},{3,7},{4,6},{5,1},{6,4},{7,3},{8,10},{9,13},{10,... | collective-permute-start | bytes 1572872 | tf_op jit(solution)/shard_map/ppermute | solution.py:78
  66.7 28.7 %copy-start = (f32[64,512]{1,0:T(8,128)S(1)}, f32[64,512]{1,0:T(8,128)}, u32[]{:S(2)}) copy-start(f32[64,512]{1,0:T(8,128)} %start_ref.1) | copy-start | bytes 393220
  72.3 1.9 %collective-permute-start.15 = (bf16[1,8,64,512]{3,2,1,0:T(8,128)(2,1)S(1)}, bf16[1,8,64,512]{3,2,1,0:T(8,128)(2,1)S(1)}, u32[]{:S(2)}, u32[]{:S(2)}) collective-permute-start(bf16[1,8,64,512]{3,2,1,0:T(8,128)(2,1)S(1)} %bitcast.33), channel_id=1, source_target_pairs={{0,1},{1,0},{2,3},{3,2},{4,5},{5,4},{6,7},{7,6},{8,9},{9,8},{10,11... | collective-permute-start | bytes 1572872 | tf_op jit(solution)/shard_map/ppermute | solution.py:60
  76.8 14.5 %collective-permute-start.20 = (f32[1,128,512]{2,1,0:T(8,128)S(1)}, f32[1,128,512]{2,1,0:T(8,128)S(1)}, u32[]{:S(2)}, u32[]{:S(2)}) collective-permute-start(f32[1,128,512]{2,1,0:T(8,128)S(1)} %bitcast.38), channel_id=1, source_target_pairs={{0,1},{1,0},{2,3},{3,2},{4,5},{5,4},{6,7},{7,6},{8,9},{9,8},{10,11... | collective-permute-start | bytes 786440 | tf_op jit(solution)/shard_map/ppermute | solution.py:60
  77.0 1.4 %collective-permute-start.16 = (f32[72,128]{1,0:T(8,128)S(1)}, f32[72,128]{1,0:T(8,128)S(1)}, u32[]{:S(2)}, u32[]{:S(2)}) collective-permute-start(f32[72,128]{1,0:T(8,128)S(1)} %get-tuple-element.49), channel_id=1, source_target_pairs={{0,1},{1,0},{2,3},{3,2},{4,5},{5,4},{6,7},{7,6},{8,9},{9,8},{10,11... | collective-permute-start | bytes 110600 | tf_op jit(solution)/shard_map/ppermute | solution.py:60
  78.5 4.9 %collective-permute-start.17 = (f32[72,128]{1,0:T(8,128)S(1)}, f32[72,128]{1,0:T(8,128)S(1)}, u32[]{:S(2)}, u32[]{:S(2)}) collective-permute-start(f32[72,128]{1,0:T(8,128)S(1)} %add.19), channel_id=1, source_target_pairs={{0,16},{1,5},{2,18},{3,7},{4,20},{5,1},{6,22},{7,3},{8,24},{9,13},... | collective-permute-start | bytes 110600 | tf_op jit(solution)/shard_map/ppermute | solution.py:78
  83.4 4.0 %collective-permute-start.18 = (f32[72,128]{1,0:T(8,128)S(1)}, f32[72,128]{1,0:T(8,128)S(1)}, u32[]{:S(2)}, u32[]{:S(2)}) collective-permute-start(f32[72,128]{1,0:T(8,128)S(1)} %add.20), channel_id=1, source_target_pairs={{0,8},{1,3},{2,10},{3,1},{4,12},{5,7},{6,14},{7,5},{8,0},{9,11},{1... | collective-permute-start | bytes 110600 | tf_op jit(solution)/shard_map/ppermute | solution.py:78
  87.3 4.0 %collective-permute-start.19 = (f32[72,128]{1,0:T(8,128)S(1)}, f32[72,128]{1,0:T(8,128)S(1)}, u32[]{:S(2)}, u32[]{:S(2)}) collective-permute-start(f32[72,128]{1,0:T(8,128)S(1)} %add.21), channel_id=1, source_target_pairs={{0,4},{1,17},{2,6},{3,19},{4,0},{5,21},{6,2},{7,23},{8,12},{9,25},... | collective-permute-start | bytes 110600 | tf_op jit(solution)/shard_map/ppermute | solution.py:78
  91.3 4.0 %collective-permute-start.21 = (f32[72,128]{1,0:T(8,128)S(1)}, f32[72,128]{1,0:T(8,128)S(1)}, u32[]{:S(2)}, u32[]{:S(2)}) collective-permute-start(f32[72,128]{1,0:T(8,128)S(1)} %add.22), channel_id=1, source_target_pairs={{0,2},{1,9},{2,0},{3,11},{4,6},{5,13},{6,4},{7,15},{8,10},{9,1},{1... | collective-permute-start | bytes 110600 | tf_op jit(solution)/shard_map/ppermute | solution.py:78

commit v14 on v13

--- a/solution.py
+++ b/solution.py
@@ -110,10 +110,12 @@
 def exchange(block, *beside):
     regions = lax.axis_size("region")
     block = block[None]
+    steps = []
     for even, odd in zip(*region_orders(regions)):
         other = swap_regions(block, even, odd)
+        steps.append(other)
         if 2 * block.shape[0] == regions:
-            return block, other
+            return block, *steps[-1:-4:-1]
         other, *beside = lax.optimization_barrier((other, *beside))
         block = jnp.concatenate([block, other], axis=0)
 
@@ -652,6 +654,8 @@
     scale = own[3:4]
     everywhere = jnp.broadcast_to(places[None], (regions,) + places.shape)
     everywhere = lax.all_to_all(everywhere, "region", 0, 0)
+    *groups, _, before_third = exchange(rounded)
+    everywhere, _ = lax.optimization_barrier((everywhere, before_third))
     near_places, far_places = halves(everywhere, "tile")
 
     half_regions = regions // 2
@@ -664,10 +668,10 @@
         plans.append(plan)
         tiles.append(built)
 
-    def operate(sent, block, *grams):
+    def operate(groups, block, *grams):
         building = not grams
         total = None
-        for part, group in enumerate(exchange(sent, *grams)):
+        for part, group in enumerate(groups):
             if building:
                 group, plans[part] = lax.optimization_barrier((group, plans[part]))
             elif part:
@@ -679,8 +683,9 @@
             total = results[0]
         return results
 
-    image, image_rounded = operate(rounded, start)
-    second, _, grams = operate(image_rounded, image, first_grams(start, image))
+    image, image_rounded = operate(groups, start)
+    grams = first_grams(start, image)
+    second, _, grams = operate(exchange(image_rounded, grams)[:2], image, grams)
     near, far = halves(jnp.concatenate([image, second], axis=0), "tile")
     images = jnp.concatenate([*near, *far], axis=1)
     grams, images = sum_regions(sum_tiles(grams), images)

time: 102 us -> 102 us (level); the launches traced: 103 us -> 102 us
  waiting for transfers between devices: 50.1 us -> 47.3 us
  starting transfers between devices: 21.7 us -> 23 us
    all_to_all x1, waiting for transfers between devices: 5.78 us -> 1.26 us  [shards(): everywhere = lax.all_to_all(everywhere, 'region', 0, 0)]
    ppermute x12, starting transfers between devices: 13.7 us -> 16.5 us  [swap_regions(): return lax.ppermute(block, ('region', 'tile'), route)]
    ppermute x12, waiting for transfers between devices: 39.2 us -> 41.2 us  [swap_regions(): return lax.ppermute(block, ('region', 'tile'), route)]
    all_to_all x1, starting transfers between devices: 6.29 us -> 4.84 us  [shards(): everywhere = lax.all_to_all(everywhere, 'region', 0, 0)]
  transfers between devices with their start and end apart: 23 -> 23, of which waited for: 17 -> 18; matrix products, arithmetic and copies ran while one was open for 1% -> 1% of each run, Pallas kernels for 13% -> 14%
where the time goes in v14:
time: 102 us
  waiting for transfers between devices  47.3 us (46%)
  Pallas kernels  29.4 us (29%)
  starting transfers between devices  23 us (23%)
    ppermute x12, waiting for transfers between devices, swap_regions(): return lax.ppermute(block, ('region', 'tile'), route)  41.2 us
    ppermute x12, starting transfers between devices, swap_regions(): return lax.ppermute(block, ('region', 'tile'), route)  16.5 us
    pallas_call x2, Pallas kernels, build_tiles(): pl.pallas_call(functools.partial(build_kernel, part), out_shape=tuple((ja...  8.72 us
    pallas_call x4, Pallas kernels, apply_tiles(): pl.pallas_call(functools.partial(apply_kernel, start is not None, last, g...  8.2 us
    pallas_call x1, Pallas kernels, last_step(): pl.pallas_call(last_kernel, out_shape=(jax.ShapeDtypeStruct(start.shape,...  7.55 us
    ppermute x10, waiting for transfers between devices, swapped(): lax.ppermute(block, axis, [(i, i ^ bit) for i in range(lax.axis_size(axis...  4.92 us
    all_to_all x1, starting transfers between devices, shards(): everywhere = lax.all_to_all(everywhere, 'region', 0, 0)  4.84 us
    pallas_call x1, Pallas kernels, sort_region(): pl.pallas_call(sort_kernel, out_shape=(jax.ShapeDtypeStruct((columns, loc...  3.41 us
  transfers between devices with their start and end apart: 23, of which 18 were waited for; matrix products, arithmetic and copies ran while one was open for 1% of the time, Pallas kernels for 14%

profile of v14, /device:TPU:0, one launch (start us, length us, event | category | flops | bytes accessed | tf_op | source)
XLA Modules:
  0.0 101.5 jit_solution(5274779914260775934)
XLA Ops:
  0.6 0.5 collective-permute-start.2
  1.1 0.1 collective-permute-start
  1.2 0.4 collective-permute-start.1
  1.7 1.0 %collective-permute-done.1.far_error_ref = f32[1,1,512]{2,1,0:T(1,128)S(1)} collective-permute-done((f32[1,1,512]{2,1,0:T(1,128)}, f32[1,1,512]{2,1,0:T(1,128)S(1)}, u32[]{:S(2)}, u32[]{:S(2)}) %collective-permute-start.1) | collective-permute-done | bytes 2080 | tf_op jit(solution)/shard_map/ppermute | solution.py:60
  2.7 0.0 collective-permute-done.far_ref
  2.7 0.0 collective-permute-done.2.other_ref
  2.7 3.4 %sort_region.1 = (bf16[64,512]{1,0:T(8,128)(2,1)S(1)}, f32[4,512]{1,0:T(4,128)S(1)}, f32[8,512]{1,0:T(8,128)S(1)}, f32[64,512]{1,0:T(8,128)S(1)}, s32[1,512]{1,0:T(1,128)S(1)}) custom-call(s32[1]{0:T(128)} %bitcast.device_ref, s32[1,7]{1,0:T(1,128)} %owner_ref.1, f32[1,3,512]{2,1,0:T(4,128)} %bitcast.41, f32[1,3,512]{2,1,0:T(4,128)S(1)} %collective-permute-done.far_ref, ...), custom_call_target="tpu_custom_call" | custom-call | flops 226492416 | bytes 2097152 | tf_op jit(solution)/shard_map/sort_region/pallas_call | solution.py:242
  6.1 4.0 %collective-permute-start.3 = (bf16[1,64,512]{2,1,0:T(8,128)(2,1)S(1)}, bf16[1,64,512]{2,1,0:T(8,128)(2,1)S(1)}, u32[]{:S(2)}, u32[]{:S(2)}) collective-permute-start(bf16[1,64,512]{2,1,0:T(8,128)(2,1)S(1)} %bitcast.18), channel_id=1, source_target_pairs={{0,16},{1,17},{2,18},{3,19},{4,20},{5,21},{6,22},{7,23},{8,24},{9,... | collective-permute-start | bytes 196616 | tf_op jit(solution)/shard_map/ppermute | solution.py:78
  10.1 0.7 broadcast_in_dim.39
  10.8 4.8 %all-to-all-start = ((f32[16,4,512]{2,1,0:T(4,128)}), f32[16,4,512]{2,1,0:T(4,128)S(1)}, u32[]{:S(2)}, u32[]{:S(2)}) async-start(f32[16,4,512]{2,1,0:T(4,128)} %broadcast_in_dim.39), calls=%async_computation | async-start | bytes 262144 | tf_op jit(solution)/shard_map/all_to_all | solution.py:656
  15.6 0.0 collective-permute-done.3
  15.7 2.0 %collective-permute-start.4 = (bf16[2,64,512]{2,1,0:T(8,128)(2,1)S(1)}, bf16[2,64,512]{2,1,0:T(8,128)(2,1)S(1)}, u32[]{:S(2)}, u32[]{:S(2)}) collective-permute-start(bf16[2,64,512]{2,1,0:T(8,128)(2,1)S(1)} %pad_maximum_fusion.5), channel_id=1, source_target_pairs={{0,8},{1,3},{2,10},{3,1},{4,12},{5,7},{6,14},{7,5},{8,0},{9,11},{1... | collective-permute-start | bytes 393224 | tf_op jit(solution)/shard_map/ppermute | solution.py:78
  17.6 4.5 %collective-permute-done.4 = bf16[2,64,512]{2,1,0:T(8,128)(2,1)S(1)} collective-permute-done((bf16[2,64,512]{2,1,0:T(8,128)(2,1)S(1)}, bf16[2,64,512]{2,1,0:T(8,128)(2,1)S(1)}, u32[]{:S(2)}, u32[]{:S(2)}) %collective-permute-start.4) | collective-permute-done | bytes 131104 | tf_op jit(solution)/shard_map/ppermute | solution.py:78
  22.2 1.3 %all-to-all-done = f32[16,4,512]{2,1,0:T(4,128)S(1)} async-done(((f32[16,4,512]{2,1,0:T(4,128)}), f32[16,4,512]{2,1,0:T(4,128)S(1)}, u32[]{:S(2)}, u32[]{:S(2)}) %all-to-all-start) | async-done | bytes 131104 | tf_op jit(solution)/shard_map/all_to_all | solution.py:656
  23.4 0.0 collective-permute-start.7
  23.5 0.8 collective-permute-start.5
  24.3 0.5 collective-permute-done.7.other_ref
  24.8 4.6 %build_tiles.3 = (s32[580]{0:T(1024)S(1)}, s32[1]{0:T(128)}, bf16[144,64,512]{2,1,0:T(8,128)(2,1)S(1)}) custom-call(s32[1]{0:T(128)} %bitcast.device_ref, f32[8,512]{1,0:T(8,128)S(1)} %get-tuple-element.30.own_ref, f32[1,16,4,512]{3,2,1,0:T(4,128)S(1)} %bitcast.30, f32[1,16,4,512]{3,2,1,0:T(4,128)S(1)} %collective-permute-done.7.other_ref), custom_call_target="tpu_custom_call" | custom-call | flops 8388608000 | bytes 4194304 | tf_op jit(solution)/shard_map/build_tiles/pallas_call | solution.py:428
  29.4 0.5 collective-permute-done.5
  29.9 0.1 pad_maximum_fusion.near_ref
  30.0 1.2 %collective-permute-start.6 = (bf16[8,64,512]{2,1,0:T(8,128)(2,1)S(1)}, bf16[8,64,512]{2,1,0:T(8,128)(2,1)S(1)}, u32[]{:S(2)}, u32[]{:S(2)}) collective-permute-start(bf16[8,64,512]{2,1,0:T(8,128)(2,1)S(1)} %pad_maximum_fusion.near_ref), channel_id=1, source_target_pairs={{0,2},{1,5},{2,0},{3,7},{4,6},{5,1},{6,4},{7,3},{8,10},{9,13},{10,... | collective-permute-start | bytes 1572872 | tf_op jit(solution)/shard_map/ppermute | solution.py:78
  31.1 0.0 collective-permute-start.9
  31.1 4.1 %build_tiles.2 = (s32[580]{0:T(1024)S(1)}, s32[1]{0:T(128)}, bf16[144,64,512]{2,1,0:T(8,128)(2,1)S(1)}) custom-call(s32[1]{0:T(128)} %bitcast.device_ref, f32[8,512]{1,0:T(8,128)S(1)} %get-tuple-element.30.own_ref, f32[1,16,4,512]{3,2,1,0:T(4,128)S(1)} %bitcast.31, f32[1,16,4,512]{3,2,1,0:T(4,128)S(1)} %collective-permute-done.7.other_ref), custom_call_target="tpu_custom_call" | custom-call | flops 8388608000 | bytes 4194304 | tf_op jit(solution)/shard_map/build_tiles/pallas_call | solution.py:428
  35.3 3.9 %collective-permute-done.6.near_ref = bf16[8,64,512]{2,1,0:T(8,128)(2,1)S(1)} collective-permute-done((bf16[8,64,512]{2,1,0:T(8,128)(2,1)S(1)}, bf16[8,64,512]{2,1,0:T(8,128)(2,1)S(1)}, u32[]{:S(2)}, u32[]{:S(2)}) %collective-permute-start.6) | collective-permute-done | bytes 524320 | tf_op jit(solution)/shard_map/ppermute | solution.py:78
  39.2 0.0 collective-permute-start.8
  39.2 0.0 collective-permute-done.9
  39.2 1.8 %apply_first.2.refs_0_ = f32[512,64]{1,0:T(8,128)S(1)} custom-call(s32[580]{0:T(1024)S(1)} %get-tuple-element.41.ids_ref, s32[1]{0:T(128)} %get-tuple-element.42.count_ref, bf16[8,64,512]{2,1,0:T(8,128)(2,1)S(1)} %pad_maximum_fusion.near_ref, bf16[8,64,512]{2,1,0:T(8,128)(2,1)S(1)} %bitcast.34, bf16[144,64,512]{2,1,0:T(8,128)(2,1)S(1)} %get-tuple-element.44.tiles_ref), custom_call_target="tpu_custom_call" | custom-call | flops 3145728000 | bytes 4194304 | tf_op jit(solution)/shard_map/apply_first/pallas_call | solution.py:518
  41.1 0.1 collective-permute-done.8
  41.1 1.9 %apply_last.2 = (f32[64,512]{1,0:T(8,128)S(1)}, bf16[64,512]{1,0:T(8,128)(2,1)S(1)}) custom-call(s32[580]{0:T(1024)S(1)} %get-tuple-element.35.ids_ref, s32[1]{0:T(128)} %get-tuple-element.36.count_ref, bf16[8,64,512]{2,1,0:T(8,128)(2,1)S(1)} %collective-permute-done.6.near_ref, bf16[8,64,512]{2,1,0:T(8,128)(2,1)S(1)} %bitcast.35, ...), custom_call_target="tpu_custom_call" | custom-call | flops 3145728000 | bytes 4194304 | tf_op jit(solution)/shard_map/apply_last/pallas_call | solution.py:518
  43.1 2.7 %collective-permute-start.10 = (bf16[1,64,512]{2,1,0:T(8,128)(2,1)S(1)}, bf16[1,64,512]{2,1,0:T(8,128)(2,1)S(1)}, u32[]{:S(2)}, u32[]{:S(2)}) collective-permute-start(bf16[1,64,512]{2,1,0:T(8,128)(2,1)S(1)} %bitcast.22), channel_id=1, source_target_pairs={{0,16},{1,17},{2,18},{3,19},{4,20},{5,21},{6,22},{7,23},{8,24},{9,... | collective-permute-start | bytes 196616 | tf_op jit(solution)/shard_map/ppermute | solution.py:78
  45.8 0.7 first_grams.1.refs_3_
  46.4 3.5 %collective-permute-done.10 = bf16[1,64,512]{2,1,0:T(8,128)(2,1)S(1)} collective-permute-done((bf16[1,64,512]{2,1,0:T(8,128)(2,1)S(1)}, bf16[1,64,512]{2,1,0:T(8,128)(2,1)S(1)}, u32[]{:S(2)}, u32[]{:S(2)}) %collective-permute-start.10) | collective-permute-done | bytes 65568 | tf_op jit(solution)/shard_map/ppermute | solution.py:78
  50.0 0.1 collective-permute-start.11
  50.0 5.0 %collective-permute-done.11 = bf16[2,64,512]{2,1,0:T(8,128)(2,1)S(1)} collective-permute-done((bf16[2,64,512]{2,1,0:T(8,128)(2,1)S(1)}, bf16[2,64,512]{2,1,0:T(8,128)(2,1)S(1)}, u32[]{:S(2)}, u32[]{:S(2)}) %collective-permute-start.11) | collective-permute-done | bytes 131104 | tf_op jit(solution)/shard_map/ppermute | solution.py:78
  55.0 0.1 collective-permute-start.12
  55.1 6.4 %collective-permute-done.12 = bf16[4,64,512]{2,1,0:T(8,128)(2,1)S(1)} collective-permute-done((bf16[4,64,512]{2,1,0:T(8,128)(2,1)S(1)}, bf16[4,64,512]{2,1,0:T(8,128)(2,1)S(1)}, u32[]{:S(2)}, u32[]{:S(2)}) %collective-permute-start.12) | collective-permute-done | bytes 262176 | tf_op jit(solution)/shard_map/ppermute | solution.py:78
  61.5 0.1 fusion
  61.5 0.1 collective-permute-start.14
  61.6 1.5 %collective-permute-start.13 = (bf16[8,64,512]{2,1,0:T(8,128)(2,1)S(1)}, bf16[8,64,512]{2,1,0:T(8,128)(2,1)S(1)}, u32[]{:S(2)}, u32[]{:S(2)}) collective-permute-start(bf16[8,64,512]{2,1,0:T(8,128)(2,1)S(1)} %get-tuple-element.57.near_ref), channel_id=1, source_target_pairs={{0,2},{1,5},{2,0},{3,7},{4,6},{5,1},{6,4},{7,3},{8,10},{9,13},{10,... | collective-permute-start | bytes 1572872 | tf_op jit(solution)/shard_map/ppermute | solution.py:78
  63.2 0.4 collective-permute-done.14
  63.5 1.8 %apply_first.3.refs_0_ = f32[512,64]{1,0:T(8,128)S(1)} custom-call(s32[580]{0:T(1024)S(1)} %get-tuple-element.41.ids_ref, s32[1]{0:T(128)} %get-tuple-element.42.count_ref, bf16[8,64,512]{2,1,0:T(8,128)(2,1)S(1)} %get-tuple-element.57.near_ref, bf16[8,64,512]{2,1,0:T(8,128)(2,1)S(1)} %bitcast.37, bf16[144,64,512]{2,1,0:T(8,128)(2,1)S(1)} %get-tuple-element.44.tiles_ref), custom_call_target="tpu_custom_call" | custom-call | flops 3145728000 | bytes 4194304 | tf_op jit(solution)/shard_map/apply_first/pallas_call | solution.py:518
  65.3 0.0 copy-start
  65.4 5.5 %collective-permute-done.13.near_ref = bf16[8,64,512]{2,1,0:T(8,128)(2,1)S(1)} collective-permute-done((bf16[8,64,512]{2,1,0:T(8,128)(2,1)S(1)}, bf16[8,64,512]{2,1,0:T(8,128)(2,1)S(1)}, u32[]{:S(2)}, u32[]{:S(2)}) %collective-permute-start.13) | collective-permute-done | bytes 524320 | tf_op jit(solution)/shard_map/ppermute | solution.py:78
  70.9 0.0 collective-permute-start.15
  70.9 1.9 %collective-permute-done.15 = bf16[1,8,64,512]{3,2,1,0:T(8,128)(2,1)S(1)} collective-permute-done((bf16[1,8,64,512]{3,2,1,0:T(8,128)(2,1)S(1)}, bf16[1,8,64,512]{3,2,1,0:T(8,128)(2,1)S(1)}, u32[]{:S(2)}, u32[]{:S(2)}) %collective-permute-start.15) | collective-permute-done | bytes 524320 | tf_op jit(solution)/shard_map/ppermute | solution.py:60
  72.8 2.6 %apply_last.3 = (f32[64,512]{1,0:T(8,128)S(1)}, bf16[64,512]{1,0:T(8,128)(2,1)}, f32[72,128]{1,0:T(8,128)S(1)}) custom-call(s32[580]{0:T(1024)S(1)} %get-tuple-element.35.ids_ref, s32[1]{0:T(128)} %get-tuple-element.36.count_ref, bf16[8,64,512]{2,1,0:T(8,128)(2,1)S(1)} %collective-permute-done.13.near_ref, bf16[8,64,512]{2,1,0:T(8,128)(2,1)S(1)} %bitcast.36, ...), custom_call_target="tpu_custom_call" | custom-call | flops 3145728000 | bytes 4194304 | tf_op jit(solution)/shard_map/apply_last/pallas_call | solution.py:518
  75.4 0.2 collective-permute-start.20
  75.6 0.4 collective-permute-start.16
  76.0 1.1 %collective-permute-done.16 = f32[72,128]{1,0:T(8,128)S(1)} collective-permute-done((f32[72,128]{1,0:T(8,128)S(1)}, f32[72,128]{1,0:T(8,128)S(1)}, u32[]{:S(2)}, u32[]{:S(2)}) %collective-permute-start.16) | collective-permute-done | bytes 36896 | tf_op jit(solution)/shard_map/ppermute | solution.py:60
  77.1 1.8 %collective-permute-start.17 = (f32[72,128]{1,0:T(8,128)S(1)}, f32[72,128]{1,0:T(8,128)S(1)}, u32[]{:S(2)}, u32[]{:S(2)}) collective-permute-start(f32[72,128]{1,0:T(8,128)S(1)} %add.19), channel_id=1, source_target_pairs={{0,16},{1,5},{2,18},{3,7},{4,20},{5,1},{6,22},{7,3},{8,24},{9,13},... | collective-permute-start | bytes 110600 | tf_op jit(solution)/shard_map/ppermute | solution.py:78
  78.9 3.0 %collective-permute-done.17 = f32[72,128]{1,0:T(8,128)S(1)} collective-permute-done((f32[72,128]{1,0:T(8,128)S(1)}, f32[72,128]{1,0:T(8,128)S(1)}, u32[]{:S(2)}, u32[]{:S(2)}) %collective-permute-start.17) | collective-permute-done | bytes 36896 | tf_op jit(solution)/shard_map/ppermute | solution.py:78
  81.9 0.0 collective-permute-start.18
  81.9 3.9 %collective-permute-done.18 = f32[72,128]{1,0:T(8,128)S(1)} collective-permute-done((f32[72,128]{1,0:T(8,128)S(1)}, f32[72,128]{1,0:T(8,128)S(1)}, u32[]{:S(2)}, u32[]{:S(2)}) %collective-permute-start.18) | collective-permute-done | bytes 36896 | tf_op jit(solution)/shard_map/ppermute | solution.py:78
  85.9 0.4 collective-permute-start.19
  86.3 3.6 %collective-permute-done.19 = f32[72,128]{1,0:T(8,128)S(1)} collective-permute-done((f32[72,128]{1,0:T(8,128)S(1)}, f32[72,128]{1,0:T(8,128)S(1)}, u32[]{:S(2)}, u32[]{:S(2)}) %collective-permute-start.19) | collective-permute-done | bytes 36896 | tf_op jit(solution)/shard_map/ppermute | solution.py:78
  89.9 0.0 collective-permute-done.20
  89.9 1.9 %collective-permute-start.21 = (f32[72,128]{1,0:T(8,128)S(1)}, f32[72,128]{1,0:T(8,128)S(1)}, u32[]{:S(2)}, u32[]{:S(2)}) collective-permute-start(f32[72,128]{1,0:T(8,128)S(1)} %add.22), channel_id=1, source_target_pairs={{0,2},{1,9},{2,0},{3,11},{4,6},{5,13},{6,4},{7,15},{8,10},{9,1},{1... | collective-permute-start | bytes 110600 | tf_op jit(solution)/shard_map/ppermute | solution.py:78
  91.9 0.8 unsort.1.images_ref
  92.7 1.3 %collective-permute-done.21 = f32[72,128]{1,0:T(8,128)S(1)} collective-permute-done((f32[72,128]{1,0:T(8,128)S(1)}, f32[72,128]{1,0:T(8,128)S(1)}, u32[]{:S(2)}, u32[]{:S(2)}) %collective-permute-start.21) | collective-permute-done | bytes 36896 | tf_op jit(solution)/shard_map/ppermute | solution.py:78
  94.0 0.0 copy-done
  94.0 7.5 %last_step.1 = (f32[64,512]{1,0:T(8,128)}, f32[64,512]{1,0:T(8,128)}) custom-call(f32[72,128]{1,0:T(8,128)S(1)} %add.23.grams_ref, f32[64,512]{1,0:T(8,128)S(1)} %copy-done, f32[128,512]{1,0:T(8,128)S(1)} %unsort.1.images_ref), custom_call_target="tpu_custom_call" | custom-call | tf_op jit(solution)/shard_map/last_step/pallas_call | solution.py:632
  (13 shorter events, 0.2 us)
Async XLA Ops:
  0.6 2.1 %collective-permute-start.2 = (f32[1,64,512]{2,1,0:T(8,128)}, f32[1,64,512]{2,1,0:T(8,128)S(1)}, u32[]{:S(2)}, u32[]{:S(2)}) collective-permute-start(f32[1,64,512]{2,1,0:T(8,128)} %bitcast.27), channel_id=1, source_target_pairs={{0,1},{1,0},{2,3},{3,2},{4,5},{5,4},{6,7},{7,6},{8,9},{9,8},{10,11... | collective-permute-start | bytes 393224 | tf_op jit(solution)/shard_map/ppermute | solution.py:60
  1.1 1.5 %collective-permute-start = (f32[1,3,512]{2,1,0:T(4,128)}, f32[1,3,512]{2,1,0:T(4,128)S(1)}, u32[]{:S(2)}, u32[]{:S(2)}) collective-permute-start(f32[1,3,512]{2,1,0:T(4,128)} %bitcast.40), channel_id=1, source_target_pairs={{0,1},{1,0},{2,3},{3,2},{4,5},{5,4},{6,7},{7,6},{8,9},{9,8},{10,11... | collective-permute-start | bytes 18440 | tf_op jit(solution)/shard_map/ppermute | solution.py:60
  1.2 1.5 %collective-permute-start.1 = (f32[1,1,512]{2,1,0:T(1,128)}, f32[1,1,512]{2,1,0:T(1,128)S(1)}, u32[]{:S(2)}, u32[]{:S(2)}) collective-permute-start(f32[1,1,512]{2,1,0:T(1,128)} %bitcast.42), channel_id=1, source_target_pairs={{0,1},{1,0},{2,3},{3,2},{4,5},{5,4},{6,7},{7,6},{8,9},{9,8},{10,11... | collective-permute-start | bytes 6152 | tf_op jit(solution)/shard_map/ppermute | solution.py:60
  6.1 9.5 %collective-permute-start.3 = (bf16[1,64,512]{2,1,0:T(8,128)(2,1)S(1)}, bf16[1,64,512]{2,1,0:T(8,128)(2,1)S(1)}, u32[]{:S(2)}, u32[]{:S(2)}) collective-permute-start(bf16[1,64,512]{2,1,0:T(8,128)(2,1)S(1)} %bitcast.18), channel_id=1, source_target_pairs={{0,16},{1,17},{2,18},{3,19},{4,20},{5,21},{6,22},{7,23},{8,24},{9,... | collective-permute-start | bytes 196616 | tf_op jit(solution)/shard_map/ppermute | solution.py:78
  10.8 12.7 %all-to-all-start = ((f32[16,4,512]{2,1,0:T(4,128)}), f32[16,4,512]{2,1,0:T(4,128)S(1)}, u32[]{:S(2)}, u32[]{:S(2)}) async-start(f32[16,4,512]{2,1,0:T(4,128)} %broadcast_in_dim.39), calls=%async_computation | async-start | bytes 262144 | tf_op jit(solution)/shard_map/all_to_all | solution.py:656
  15.7 6.5 %collective-permute-start.4 = (bf16[2,64,512]{2,1,0:T(8,128)(2,1)S(1)}, bf16[2,64,512]{2,1,0:T(8,128)(2,1)S(1)}, u32[]{:S(2)}, u32[]{:S(2)}) collective-permute-start(bf16[2,64,512]{2,1,0:T(8,128)(2,1)S(1)} %pad_maximum_fusion.5), channel_id=1, source_target_pairs={{0,8},{1,3},{2,10},{3,1},{4,12},{5,7},{6,14},{7,5},{8,0},{9,11},{1... | collective-permute-start | bytes 393224 | tf_op jit(solution)/shard_map/ppermute | solution.py:78
  23.4 1.3 %collective-permute-start.7 = (f32[1,16,4,512]{3,2,1,0:T(4,128)S(1)}, f32[1,16,4,512]{3,2,1,0:T(4,128)S(1)}, u32[]{:S(2)}, u32[]{:S(2)}) collective-permute-start(f32[1,16,4,512]{3,2,1,0:T(4,128)S(1)} %bitcast.29), channel_id=1, source_target_pairs={{0,1},{1,0},{2,3},{3,2},{4,5},{5,4},{6,7},{7,6},{8,9},{9,8},{10,11... | collective-permute-start | bytes 393224 | tf_op jit(solution)/shard_map/ppermute | solution.py:60
  23.5 6.4 %collective-permute-start.5 = (bf16[4,64,512]{2,1,0:T(8,128)(2,1)S(1)}, bf16[4,64,512]{2,1,0:T(8,128)(2,1)S(1)}, u32[]{:S(2)}, u32[]{:S(2)}) collective-permute-start(bf16[4,64,512]{2,1,0:T(8,128)(2,1)S(1)} %pad_maximum_fusion.3), channel_id=1, source_target_pairs={{0,4},{1,9},{2,6},{3,11},{4,0},{5,13},{6,2},{7,15},{8,12},{9,1},{1... | collective-permute-start | bytes 786440 | tf_op jit(solution)/shard_map/ppermute | solution.py:78
  30.0 9.2 %collective-permute-start.6 = (bf16[8,64,512]{2,1,0:T(8,128)(2,1)S(1)}, bf16[8,64,512]{2,1,0:T(8,128)(2,1)S(1)}, u32[]{:S(2)}, u32[]{:S(2)}) collective-permute-start(bf16[8,64,512]{2,1,0:T(8,128)(2,1)S(1)} %pad_maximum_fusion.near_ref), channel_id=1, source_target_pairs={{0,2},{1,5},{2,0},{3,7},{4,6},{5,1},{6,4},{7,3},{8,10},{9,13},{10,... | collective-permute-start | bytes 1572872 | tf_op jit(solution)/shard_map/ppermute | solution.py:78
  31.1 8.1 %collective-permute-start.9 = (bf16[1,8,64,512]{3,2,1,0:T(8,128)(2,1)S(1)}, bf16[1,8,64,512]{3,2,1,0:T(8,128)(2,1)S(1)}, u32[]{:S(2)}, u32[]{:S(2)}) collective-permute-start(bf16[1,8,64,512]{3,2,1,0:T(8,128)(2,1)S(1)} %bitcast.26), channel_id=1, source_target_pairs={{0,1},{1,0},{2,3},{3,2},{4,5},{5,4},{6,7},{7,6},{8,9},{9,8},{10,11... | collective-permute-start | bytes 1572872 | tf_op jit(solution)/shard_map/ppermute | solution.py:60
  39.2 1.9 %collective-permute-start.8 = (bf16[1,8,64,512]{3,2,1,0:T(8,128)(2,1)S(1)}, bf16[1,8,64,512]{3,2,1,0:T(8,128)(2,1)S(1)}, u32[]{:S(2)}, u32[]{:S(2)}) collective-permute-start(bf16[1,8,64,512]{3,2,1,0:T(8,128)(2,1)S(1)} %bitcast.32), channel_id=1, source_target_pairs={{0,1},{1,0},{2,3},{3,2},{4,5},{5,4},{6,7},{7,6},{8,9},{9,8},{10,11... | collective-permute-start | bytes 1572872 | tf_op jit(solution)/shard_map/ppermute | solution.py:60
  43.1 6.9 %collective-permute-start.10 = (bf16[1,64,512]{2,1,0:T(8,128)(2,1)S(1)}, bf16[1,64,512]{2,1,0:T(8,128)(2,1)S(1)}, u32[]{:S(2)}, u32[]{:S(2)}) collective-permute-start(bf16[1,64,512]{2,1,0:T(8,128)(2,1)S(1)} %bitcast.22), channel_id=1, source_target_pairs={{0,16},{1,17},{2,18},{3,19},{4,20},{5,21},{6,22},{7,23},{8,24},{9,... | collective-permute-start | bytes 196616 | tf_op jit(solution)/shard_map/ppermute | solution.py:78
  50.0 5.0 %collective-permute-start.11 = (bf16[2,64,512]{2,1,0:T(8,128)(2,1)S(1)}, bf16[2,64,512]{2,1,0:T(8,128)(2,1)S(1)}, u32[]{:S(2)}, u32[]{:S(2)}) collective-permute-start(bf16[2,64,512]{2,1,0:T(8,128)(2,1)S(1)} %pad_maximum_fusion.6), channel_id=1, source_target_pairs={{0,8},{1,3},{2,10},{3,1},{4,12},{5,7},{6,14},{7,5},{8,0},{9,11},{1... | collective-permute-start | bytes 393224 | tf_op jit(solution)/shard_map/ppermute | solution.py:78
  55.0 6.4 %collective-permute-start.12 = (bf16[4,64,512]{2,1,0:T(8,128)(2,1)S(1)}, bf16[4,64,512]{2,1,0:T(8,128)(2,1)S(1)}, u32[]{:S(2)}, u32[]{:S(2)}) collective-permute-start(bf16[4,64,512]{2,1,0:T(8,128)(2,1)S(1)} %pad_maximum_fusion.4), channel_id=1, source_target_pairs={{0,4},{1,9},{2,6},{3,11},{4,0},{5,13},{6,2},{7,15},{8,12},{9,1},{1... | collective-permute-start | bytes 786440 | tf_op jit(solution)/shard_map/ppermute | solution.py:78
  61.5 2.0 %collective-permute-start.14 = (bf16[1,8,64,512]{3,2,1,0:T(8,128)(2,1)S(1)}, bf16[1,8,64,512]{3,2,1,0:T(8,128)(2,1)S(1)}, u32[]{:S(2)}, u32[]{:S(2)}) collective-permute-start(bf16[1,8,64,512]{3,2,1,0:T(8,128)(2,1)S(1)} %get-tuple-element.56), channel_id=1, source_target_pairs={{0,1},{1,0},{2,3},{3,2},{4,5},{5,4},{6,7},{7,6},{8,9},{9,8},{10,11... | collective-permute-start | bytes 1572872 | tf_op jit(solution)/shard_map/ppermute | solution.py:60
  61.6 9.2 %collective-permute-start.13 = (bf16[8,64,512]{2,1,0:T(8,128)(2,1)S(1)}, bf16[8,64,512]{2,1,0:T(8,128)(2,1)S(1)}, u32[]{:S(2)}, u32[]{:S(2)}) collective-permute-start(bf16[8,64,512]{2,1,0:T(8,128)(2,1)S(1)} %get-tuple-element.57.near_ref), channel_id=1, source_target_pairs={{0,2},{1,5},{2,0},{3,7},{4,6},{5,1},{6,4},{7,3},{8,10},{9,13},{10,... | collective-permute-start | bytes 1572872 | tf_op jit(solution)/shard_map/ppermute | solution.py:78
  65.3 28.6 %copy-start = (f32[64,512]{1,0:T(8,128)S(1)}, f32[64,512]{1,0:T(8,128)}, u32[]{:S(2)}) copy-start(f32[64,512]{1,0:T(8,128)} %start_ref.1) | copy-start | bytes 393220
  70.9 1.9 %collective-permute-start.15 = (bf16[1,8,64,512]{3,2,1,0:T(8,128)(2,1)S(1)}, bf16[1,8,64,512]{3,2,1,0:T(8,128)(2,1)S(1)}, u32[]{:S(2)}, u32[]{:S(2)}) collective-permute-start(bf16[1,8,64,512]{3,2,1,0:T(8,128)(2,1)S(1)} %bitcast.33), channel_id=1, source_target_pairs={{0,1},{1,0},{2,3},{3,2},{4,5},{5,4},{6,7},{7,6},{8,9},{9,8},{10,11... | collective-permute-start | bytes 1572872 | tf_op jit(solution)/shard_map/ppermute | solution.py:60
  75.4 14.5 %collective-permute-start.20 = (f32[1,128,512]{2,1,0:T(8,128)S(1)}, f32[1,128,512]{2,1,0:T(8,128)S(1)}, u32[]{:S(2)}, u32[]{:S(2)}) collective-permute-start(f32[1,128,512]{2,1,0:T(8,128)S(1)} %bitcast.38), channel_id=1, source_target_pairs={{0,1},{1,0},{2,3},{3,2},{4,5},{5,4},{6,7},{7,6},{8,9},{9,8},{10,11... | collective-permute-start | bytes 786440 | tf_op jit(solution)/shard_map/ppermute | solution.py:60
  75.6 1.5 %collective-permute-start.16 = (f32[72,128]{1,0:T(8,128)S(1)}, f32[72,128]{1,0:T(8,128)S(1)}, u32[]{:S(2)}, u32[]{:S(2)}) collective-permute-start(f32[72,128]{1,0:T(8,128)S(1)} %get-tuple-element.51), channel_id=1, source_target_pairs={{0,1},{1,0},{2,3},{3,2},{4,5},{5,4},{6,7},{7,6},{8,9},{9,8},{10,11... | collective-permute-start | bytes 110600 | tf_op jit(solution)/shard_map/ppermute | solution.py:60
  77.1 4.9 %collective-permute-start.17 = (f32[72,128]{1,0:T(8,128)S(1)}, f32[72,128]{1,0:T(8,128)S(1)}, u32[]{:S(2)}, u32[]{:S(2)}) collective-permute-start(f32[72,128]{1,0:T(8,128)S(1)} %add.19), channel_id=1, source_target_pairs={{0,16},{1,5},{2,18},{3,7},{4,20},{5,1},{6,22},{7,3},{8,24},{9,13},... | collective-permute-start | bytes 110600 | tf_op jit(solution)/shard_map/ppermute | solution.py:78
  81.9 4.0 %collective-permute-start.18 = (f32[72,128]{1,0:T(8,128)S(1)}, f32[72,128]{1,0:T(8,128)S(1)}, u32[]{:S(2)}, u32[]{:S(2)}) collective-permute-start(f32[72,128]{1,0:T(8,128)S(1)} %add.20), channel_id=1, source_target_pairs={{0,8},{1,3},{2,10},{3,1},{4,12},{5,7},{6,14},{7,5},{8,0},{9,11},{1... | collective-permute-start | bytes 110600 | tf_op jit(solution)/shard_map/ppermute | solution.py:78
  85.9 4.0 %collective-permute-start.19 = (f32[72,128]{1,0:T(8,128)S(1)}, f32[72,128]{1,0:T(8,128)S(1)}, u32[]{:S(2)}, u32[]{:S(2)}) collective-permute-start(f32[72,128]{1,0:T(8,128)S(1)} %add.21), channel_id=1, source_target_pairs={{0,4},{1,17},{2,6},{3,19},{4,0},{5,21},{6,2},{7,23},{8,12},{9,25},... | collective-permute-start | bytes 110600 | tf_op jit(solution)/shard_map/ppermute | solution.py:78
  89.9 4.0 %collective-permute-start.21 = (f32[72,128]{1,0:T(8,128)S(1)}, f32[72,128]{1,0:T(8,128)S(1)}, u32[]{:S(2)}, u32[]{:S(2)}) collective-permute-start(f32[72,128]{1,0:T(8,128)S(1)} %add.22), channel_id=1, source_target_pairs={{0,2},{1,9},{2,0},{3,11},{4,6},{5,13},{6,4},{7,15},{8,10},{9,1},{1... | collective-permute-start | bytes 110600 | tf_op jit(solution)/shard_map/ppermute | solution.py:78
